TPU v7x, 32 devices: a whole 2x2x4 slice. The times are simulated.
32 devices in a mesh: grp: 2 (over x), row: 8 (over z, y), col: 2 (over core).
Axes of the slice: x: 2, y: 2, z: 4, core: 2. Of those that a mesh axis runs over, the one named last changes fastest.
Arguments:
- pair_rep: bfloat16 [512, 256, 128], P(('grp', 'row'), 'col'), parts along dimension 0, may hold values from -6 to 6
- cotangent: bfloat16 [512, 256, 128], P(('grp', 'row'), 'col'), parts along dimension 0, may hold values from -6 to 6
- residue_mask: int32 [512], P('grp'), parts along dimension 0, may hold values 0 or 1
- chain_ids: int32 [512], P('grp'), parts along dimension 0, may hold values from 0 to 5, never falling along the last dimension, each value on 1 to 64 neighbouring positions
- proj_weight: bfloat16 [2, 128, 640], replicated, may hold values from -0.5 to 0.5
- out_weight: bfloat16 [2, 128, 128], replicated, may hold values from -0.5 to 0.5
- input_gain: float32 [2, 128], replicated, may hold values from 0.25 to 1.75
- input_bias: float32 [2, 128], replicated, may hold values from -3 to 3
- hidden_gain: float32 [2, 128], replicated, may hold values from 0.25 to 1.75
- hidden_bias: float32 [2, 128], replicated, may hold values from -3 to 3
- chain_bias: float32 [2, 128], replicated, may hold values from -4 to 4
Outputs:
- grad_pair: bfloat16 [512, 256, 128], P(('grp', 'row'), 'col'), parts along dimension 0
- grad_proj: float32 [4, 128, 640], P('grp'), parts along dimension 0
- grad_output_weight: float32 [4, 128, 128], P('grp'), parts along dimension 0
- grad_input_norm: float32 [4, 2, 128], P('grp'), parts along dimension 0
- grad_hidden_norm: float32 [4, 2, 128], P('grp'), parts along dimension 0
- grad_chain: float32 [4, 128], P('grp'), parts along dimension 0
There are 2 independent parts, one for each index of `grp`. A program takes and returns all parts, laid end to end along the dimension named above; an argument that names none is the same for every part. Nothing has to cross between parts.
Inputs may be any that keep to these rules, and one draw needn't show every extreme that they name: `chain_ids`: chain numbers never fall along the residues.
All inputs are finite; a program needn't handle non-finite values.
Results may differ from a plain program's by a relative error of at most 0.018.
Values may be sent and summed in bfloat16 or wider, within the bound.
No kernel may reach another device: no remote copies, remote signals or barrier semaphores. Data moves between devices by JAX's collectives and lax.ppermute only.
A program may use at most 128 MiB of HBM per device.

v0:
```python
import jax
import jax.numpy as jnp
from jax import lax
from jax.sharding import PartitionSpec as P

EPSILON = 1e-05
FORWARD_FORMS = ("cik,cjk->cij", "cki,ckj->cij")


def norm_forward(values, norm_gain, norm_bias):
    average = jnp.mean(values, -1, keepdims=True)
    centred = values - average
    inv_std = lax.rsqrt(jnp.mean(centred * centred, -1, keepdims=True) + EPSILON)
    normed = centred * inv_std
    return (normed, inv_std, normed * norm_gain + norm_bias)


def norm_backward(grad_scaled, normed, inv_std, norm_gain):
    grad_normed = grad_scaled * norm_gain
    first_mean = jnp.mean(grad_normed, -1, keepdims=True)
    second_mean = jnp.mean(grad_normed * normed, -1, keepdims=True)
    grad_values = (grad_normed - first_mean - normed * second_mean) * inv_std
    return (grad_values, jnp.sum(grad_scaled * normed, 0), jnp.sum(grad_scaled, 0))


def edge_forward(cells, weight, norm_gain, norm_bias, pair_mask, same_chain, chain_vec, hidden):
    normed, inv_std, scaled = norm_forward(cells, norm_gain, norm_bias)
    lowered = scaled.astype(jnp.bfloat16)
    projected = jnp.dot(lowered, weight, preferred_element_type=jnp.float32)
    left_edge = (
        projected[:, :hidden]
        * jax.nn.sigmoid(projected[:, hidden : 2 * hidden])
        * pair_mask[:, None]
    )
    right_edge = (
        projected[:, 2 * hidden : 3 * hidden]
        * jax.nn.sigmoid(projected[:, 3 * hidden : 4 * hidden])
        * pair_mask[:, None]
    )
    logits = projected[:, 4 * hidden :] + same_chain[:, None] * chain_vec
    return (
        left_edge.astype(jnp.bfloat16),
        right_edge.astype(jnp.bfloat16),
        logits,
        (normed, inv_std, lowered, projected),
    )


def edge_backward(
    grad_left, grad_right, grad_logits, stored, weight, norm_gain, pair_mask, same_chain, hidden
):
    normed, inv_std, lowered, projected = stored
    left_sig = jax.nn.sigmoid(projected[:, hidden : 2 * hidden])
    right_sig = jax.nn.sigmoid(projected[:, 3 * hidden : 4 * hidden])
    masked_left = grad_left * pair_mask[:, None]
    masked_right = grad_right * pair_mask[:, None]
    grad_projected = jnp.concatenate(
        [
            masked_left * left_sig,
            masked_left * projected[:, :hidden] * left_sig * (1.0 - left_sig),
            masked_right * right_sig,
            masked_right * projected[:, 2 * hidden : 3 * hidden] * right_sig * (1.0 - right_sig),
            grad_logits,
        ],
        1,
    ).astype(jnp.bfloat16)
    grad_weight = lax.dot_general(
        lowered, grad_projected, (((0,), (0,)), ((), ())), preferred_element_type=jnp.float32
    )
    grad_scaled = lax.dot_general(
        grad_projected, weight, (((1,), (1,)), ((), ())), preferred_element_type=jnp.float32
    )
    grad_cells, grad_gain, grad_bias = norm_backward(grad_scaled, normed, inv_std, norm_gain)
    grad_chain = jnp.sum(grad_logits * same_chain[:, None], 0)
    return (grad_cells, grad_weight, grad_gain, grad_bias, grad_chain)


def mix_forward(product_cells, logits, weight, norm_gain, norm_bias):
    normed, inv_std, scaled = norm_forward(product_cells.astype(jnp.float32), norm_gain, norm_bias)
    lowered = scaled.astype(jnp.bfloat16)
    mixed = jnp.dot(lowered, weight, preferred_element_type=jnp.float32)
    gate_vals = jax.nn.sigmoid(logits)
    return (gate_vals * mixed, (normed, inv_std, lowered, mixed, gate_vals))


def mix_backward(upstream, stored, weight, norm_gain):
    normed, inv_std, lowered, mixed, gate_vals = stored
    grad_logits = upstream * mixed * gate_vals * (1.0 - gate_vals)
    grad_mixed = (upstream * gate_vals).astype(jnp.bfloat16)
    grad_weight = lax.dot_general(
        lowered, grad_mixed, (((0,), (0,)), ((), ())), preferred_element_type=jnp.float32
    )
    grad_scaled = lax.dot_general(
        grad_mixed, weight, (((1,), (1,)), ((), ())), preferred_element_type=jnp.float32
    )
    grad_product, grad_gain, grad_bias = norm_backward(grad_scaled, normed, inv_std, norm_gain)
    return (grad_product.astype(jnp.bfloat16), grad_logits, grad_weight, grad_gain, grad_bias)


def tri_product(formula, first_edge, second_edge):
    return jnp.einsum(formula, first_edge, second_edge, preferred_element_type=jnp.float32).astype(
        jnp.bfloat16
    )


def joint_to_full(received, row_count, col_count):
    row_devices = lax.axis_size("row")
    col_devices = lax.axis_size("col")
    per_device = received.shape[0]
    shaped = received.reshape(per_device, row_devices, col_devices, row_count, col_count)
    return shaped.transpose(0, 1, 3, 2, 4).reshape(
        per_device, row_devices * row_count, col_devices * col_count
    )


def full_to_joint(channels, row_count, col_count):
    row_devices = lax.axis_size("row")
    col_devices = lax.axis_size("col")
    per_device = channels.shape[0]
    shaped = channels.reshape(per_device, row_devices, row_count, col_devices, col_count)
    return shaped.transpose(1, 3, 0, 2, 4).reshape(
        row_devices * col_devices * per_device, row_count, col_count
    )


def cells_to_block(edge, row_count, col_count):
    return edge.T.reshape(edge.shape[1], row_count, col_count)


def block_to_cells(block):
    return block.reshape(block.shape[0], -1).T


def edges_to_channels(left_edge, right_edge, row_count, col_count):
    left_block = cells_to_block(left_edge, row_count, col_count)
    right_block = cells_to_block(right_edge, row_count, col_count)
    left_got, right_got = (
        lax.all_to_all(left_block, ("row", "col"), split_axis=0, concat_axis=1, tiled=True),
        lax.all_to_all(right_block, ("row", "col"), split_axis=0, concat_axis=1, tiled=True),
    )
    return (
        joint_to_full(left_got, row_count, col_count),
        joint_to_full(right_got, row_count, col_count),
    )


def grads_to_cells(grad_left, grad_right, row_count, col_count):
    left_got, right_got = (
        lax.all_to_all(
            full_to_joint(grad_left, row_count, col_count),
            ("row", "col"),
            split_axis=0,
            concat_axis=0,
            tiled=True,
        ),
        lax.all_to_all(
            full_to_joint(grad_right, row_count, col_count),
            ("row", "col"),
            split_axis=0,
            concat_axis=0,
            tiled=True,
        ),
    )
    return (block_to_cells(left_got), block_to_cells(right_got))


def shards(
    pair_rep,
    cotangent,
    residue_mask,
    chain_ids,
    proj_weight,
    out_weight,
    input_gain,
    input_bias,
    hidden_gain,
    hidden_bias,
    chain_bias,
):
    row_count, col_count, width = pair_rep.shape
    hidden = out_weight.shape[1]
    length = row_count * lax.axis_size("row")
    row_start = lax.axis_index("row") * row_count
    col_start = lax.axis_index("col") * col_count
    mask_rows = lax.dynamic_slice_in_dim(residue_mask, row_start, row_count)
    mask_cols = lax.dynamic_slice_in_dim(residue_mask, col_start, col_count)
    chain_rows = lax.dynamic_slice_in_dim(chain_ids, row_start, row_count)
    chain_cols = lax.dynamic_slice_in_dim(chain_ids, col_start, col_count)
    pair_mask = (mask_rows[:, None] * mask_cols[None, :]).astype(jnp.float32).reshape(-1)
    same_chain = (chain_rows[:, None] == chain_cols[None, :]).astype(jnp.float32).reshape(-1)
    cells = pair_rep.reshape(-1, width).astype(jnp.float32)
    records = []
    for layer_no in range(2):
        left_edge, right_edge, logits, edge_store = edge_forward(
            cells,
            proj_weight[layer_no],
            input_gain[layer_no],
            input_bias[layer_no],
            pair_mask,
            same_chain,
            chain_bias[layer_no],
            hidden,
        )
        left_chan, right_chan = edges_to_channels(left_edge, right_edge, row_count, col_count)
        product = tri_product(FORWARD_FORMS[layer_no], left_chan, right_chan)
        product_got = lax.all_to_all(
            full_to_joint(product, row_count, col_count),
            ("row", "col"),
            split_axis=0,
            concat_axis=0,
            tiled=True,
        )
        mixed_out, mix_store = mix_forward(
            block_to_cells(product_got),
            logits,
            out_weight[layer_no],
            hidden_gain[layer_no],
            hidden_bias[layer_no],
        )
        records.append((left_chan, right_chan, edge_store, mix_store))
        cells = cells + mixed_out
    upstream = cotangent.reshape(-1, width).astype(jnp.float32)
    grads = [None, None]
    for layer_no in (1, 0):
        left_chan, right_chan, edge_store, mix_store = records[layer_no]
        grad_prod, grad_logits, grad_outw, grad_hgain, grad_hbias = mix_backward(
            upstream, mix_store, out_weight[layer_no], hidden_gain[layer_no]
        )
        grad_got = lax.all_to_all(
            cells_to_block(grad_prod, row_count, col_count),
            ("row", "col"),
            split_axis=0,
            concat_axis=1,
            tiled=True,
        )
        grad_chan = joint_to_full(grad_got, row_count, col_count)
        if layer_no == 0:
            grad_left = tri_product("cij,cjk->cik", grad_chan, right_chan)
            grad_right = tri_product("cij,cik->cjk", grad_chan, left_chan)
        else:
            grad_left = tri_product("ckj,cij->cki", right_chan, grad_chan)
            grad_right = tri_product("cki,cij->ckj", left_chan, grad_chan)
        left_cells, right_cells = grads_to_cells(grad_left, grad_right, row_count, col_count)
        grad_cells, grad_weight, grad_gain, grad_bias, grad_chain = edge_backward(
            left_cells.astype(jnp.float32),
            right_cells.astype(jnp.float32),
            grad_logits,
            edge_store,
            proj_weight[layer_no],
            input_gain[layer_no],
            pair_mask,
            same_chain,
            hidden,
        )
        upstream = upstream + grad_cells
        grads[layer_no] = (
            grad_weight,
            grad_outw,
            jnp.stack([grad_gain, grad_bias]),
            jnp.stack([grad_hgain, grad_hbias]),
            grad_chain,
        )
    stacked = [jnp.stack([grads[0][member], grads[1][member]]) for member in range(5)]
    summed = (
        lax.psum(stacked[0].astype(jnp.bfloat16), ("row", "col")).astype(jnp.float32),
        lax.psum(stacked[1].astype(jnp.bfloat16), ("row", "col")).astype(jnp.float32),
        lax.psum(stacked[2].astype(jnp.bfloat16), ("row", "col")).astype(jnp.float32),
        lax.psum(stacked[3].astype(jnp.bfloat16), ("row", "col")).astype(jnp.float32),
        lax.psum(stacked[4].astype(jnp.bfloat16), ("row", "col")).astype(jnp.float32),
    )
    factor = 1.0 / length
    grad_pair = upstream.reshape(row_count, col_count, width).astype(jnp.bfloat16)
    return (
        grad_pair,
        summed[0] * factor,
        summed[1] * factor,
        summed[2] * factor,
        summed[3] * factor,
        summed[4] * factor,
    )


def solution(mesh):
    placed = (
        P(("grp", "row"), "col", None),
        P(("grp", "row"), "col", None),
        P("grp"),
        P("grp"),
        P(),
        P(),
        P(),
        P(),
        P(),
        P(),
        P(),
    )
    return jax.shard_map(
        shards,
        mesh=mesh,
        in_specs=placed,
        out_specs=(
            P(("grp", "row"), "col", None),
            P("grp", None, None),
            P("grp", None, None),
            P("grp", None, None),
            P("grp", None, None),
            P("grp", None),
        ),
        check_vma=False,
    )
```

profile of v0, /device:TPU:0, one launch (start us, length us, event | category | flops | bytes accessed | tf_op | source)
XLA Modules:
  0.0 655.0 jit_solution(14678695638551496291)
XLA Ops:
  23.1 7.4 %all-to-all-start = ((bf16[128,32,128]{2,1,0:T(8,128)(2,1)}), bf16[128,32,128]{2,1,0:T(8,128)(2,1)S(1)}, u32[]{:S(2)}, u32[]{:S(2)}) async-start(bf16[128,32,128]{2,1,0:T(8,128)(2,1)} %copy.24), calls=%async_computation | async-start | bytes 2097152 | tf_op jit(solution)/shard_map/all_to_all | solution.py:138
  32.3 21.2 %all-to-all-done = bf16[128,32,128]{2,1,0:T(8,128)(2,1)S(1)} async-done(((bf16[128,32,128]{2,1,0:T(8,128)(2,1)}), bf16[128,32,128]{2,1,0:T(8,128)(2,1)S(1)}, u32[]{:S(2)}, u32[]{:S(2)}) %all-to-all-start) | async-done | bytes 1048608 | tf_op jit(solution)/shard_map/all_to_all | solution.py:138
  53.5 6.9 %all-to-all-start.1 = ((bf16[128,32,128]{2,1,0:T(8,128)(2,1)}), bf16[128,32,128]{2,1,0:T(8,128)(2,1)}, u32[]{:S(2)}, u32[]{:S(2)}) async-start(bf16[128,32,128]{2,1,0:T(8,128)(2,1)} %copy.27), calls=%async_computation.1 | async-start | bytes 2097152 | tf_op jit(solution)/shard_map/all_to_all | solution.py:139
  64.2 19.2 %all-to-all-done.1 = bf16[128,32,128]{2,1,0:T(8,128)(2,1)} async-done(((bf16[128,32,128]{2,1,0:T(8,128)(2,1)}), bf16[128,32,128]{2,1,0:T(8,128)(2,1)}, u32[]{:S(2)}, u32[]{:S(2)}) %all-to-all-start.1) | async-done | bytes 1048608 | tf_op jit(solution)/shard_map/all_to_all | solution.py:139
  92.5 7.3 %all-to-all-start.2 = ((bf16[128,32,128]{2,1,0:T(8,128)(2,1)}), bf16[128,32,128]{2,1,0:T(8,128)(2,1)S(1)}, u32[]{:S(2)}, u32[]{:S(2)}) async-start(bf16[128,32,128]{2,1,0:T(8,128)(2,1)} %bitcast.368), calls=%async_computation.2 | async-start | bytes 2097152 | tf_op jit(solution)/shard_map/all_to_all | solution.py:206
  101.1 21.6 %all-to-all-done.2 = bf16[128,32,128]{2,1,0:T(8,128)(2,1)S(1)} async-done(((bf16[128,32,128]{2,1,0:T(8,128)(2,1)}), bf16[128,32,128]{2,1,0:T(8,128)(2,1)S(1)}, u32[]{:S(2)}, u32[]{:S(2)}) %all-to-all-start.2) | async-done | bytes 1048608 | tf_op jit(solution)/shard_map/all_to_all | solution.py:206
  127.5 5.1 fusion.103
  135.8 4.9 multiply_convert_fusion.2
  143.3 6.9 %all-to-all-start.4 = ((bf16[128,32,128]{2,1,0:T(8,128)(2,1)}), bf16[128,32,128]{2,1,0:T(8,128)(2,1)}, u32[]{:S(2)}, u32[]{:S(2)}) async-start(bf16[128,32,128]{2,1,0:T(8,128)(2,1)} %copy.35), calls=%async_computation.4 | async-start | bytes 2097152 | tf_op jit(solution)/shard_map/all_to_all | solution.py:138
  153.0 20.3 %all-to-all-done.4 = bf16[128,32,128]{2,1,0:T(8,128)(2,1)} async-done(((bf16[128,32,128]{2,1,0:T(8,128)(2,1)}), bf16[128,32,128]{2,1,0:T(8,128)(2,1)}, u32[]{:S(2)}, u32[]{:S(2)}) %all-to-all-start.4) | async-done | bytes 1048608 | tf_op jit(solution)/shard_map/all_to_all | solution.py:138
  173.3 6.9 %all-to-all-start.3 = ((bf16[128,32,128]{2,1,0:T(8,128)(2,1)}), bf16[128,32,128]{2,1,0:T(8,128)(2,1)}, u32[]{:S(2)}, u32[]{:S(2)}) async-start(bf16[128,32,128]{2,1,0:T(8,128)(2,1)} %copy.32), calls=%async_computation.3 | async-start | bytes 2097152 | tf_op jit(solution)/shard_map/all_to_all | solution.py:139
  186.0 17.2 %all-to-all-done.3 = bf16[128,32,128]{2,1,0:T(8,128)(2,1)} async-done(((bf16[128,32,128]{2,1,0:T(8,128)(2,1)}), bf16[128,32,128]{2,1,0:T(8,128)(2,1)}, u32[]{:S(2)}, u32[]{:S(2)}) %all-to-all-start.3) | async-done | bytes 1048608 | tf_op jit(solution)/shard_map/all_to_all | solution.py:139
  215.7 31.7 %all_to_all.120 = bf16[128,32,128]{2,1,0:T(8,128)(2,1)S(1)} all-to-all(bf16[128,32,128]{2,1,0:T(8,128)(2,1)S(1)} %bitcast.373), channel_id=1, replica_groups=mesh['grp'=2,'row'=8,'col'=2] {'row','col'}, dimensions={0} | all-to-all | bytes 2097152 | tf_op jit(solution)/shard_map/all_to_all | solution.py:206
  263.0 29.8 %all_to_all.121 = bf16[128,32,128]{2,1,0:T(8,128)(2,1)S(1)} all-to-all(bf16[128,32,128]{2,1,0:T(8,128)(2,1)} %copy.41), channel_id=1, replica_groups=mesh['grp'=2,'row'=8,'col'=2] {'row','col'}, dimensions={0} | all-to-all | bytes 2097152 | tf_op jit(solution)/shard_map/all_to_all | solution.py:229
  305.0 5.0 all-to-all-start.7
  317.5 15.5 %all-to-all-done.7 = bf16[128,32,128]{2,1,0:T(8,128)(2,1)} async-done(((bf16[128,32,128]{2,1,0:T(8,128)(2,1)}), bf16[128,32,128]{2,1,0:T(8,128)(2,1)}, u32[]{:S(2)}, u32[]{:S(2)}) %all-to-all-start.7) | async-done | bytes 1048608 | tf_op jit(solution)/shard_map/all_to_all | solution.py:149
  333.0 7.1 %all-to-all-start.8 = ((bf16[128,32,128]{2,1,0:T(8,128)(2,1)}), bf16[128,32,128]{2,1,0:T(8,128)(2,1)}, u32[]{:S(2)}, u32[]{:S(2)}) async-start(bf16[128,32,128]{2,1,0:T(8,128)(2,1)} %bitcast.371), calls=%async_computation.8 | async-start | bytes 2097152 | tf_op jit(solution)/shard_map/all_to_all | solution.py:156
  343.1 20.1 %all-to-all-done.8 = bf16[128,32,128]{2,1,0:T(8,128)(2,1)} async-done(((bf16[128,32,128]{2,1,0:T(8,128)(2,1)}), bf16[128,32,128]{2,1,0:T(8,128)(2,1)}, u32[]{:S(2)}, u32[]{:S(2)}) %all-to-all-start.8) | async-done | bytes 1048608 | tf_op jit(solution)/shard_map/all_to_all | solution.py:156
  366.0 5.7 fusion.36
  380.9 6.3 multiply_reduce_fusion.1
  392.6 3.7 fusion.32
  398.9 31.7 %all_to_all.122 = bf16[128,32,128]{2,1,0:T(8,128)(2,1)S(1)} all-to-all(bf16[128,32,128]{2,1,0:T(8,128)(2,1)} %copy.48), channel_id=1, replica_groups=mesh['grp'=2,'row'=8,'col'=2] {'row','col'}, dimensions={0} | all-to-all | bytes 2097152 | tf_op jit(solution)/shard_map/all_to_all | solution.py:229
  442.7 5.0 all-to-all-start.10
  455.4 15.4 %all-to-all-done.10 = bf16[128,32,128]{2,1,0:T(8,128)(2,1)} async-done(((bf16[128,32,128]{2,1,0:T(8,128)(2,1)}), bf16[128,32,128]{2,1,0:T(8,128)(2,1)}, u32[]{:S(2)}, u32[]{:S(2)}) %all-to-all-start.10) | async-done | bytes 1048608 | tf_op jit(solution)/shard_map/all_to_all | solution.py:149
  470.8 6.9 %all-to-all-start.11 = ((bf16[128,32,128]{2,1,0:T(8,128)(2,1)}), bf16[128,32,128]{2,1,0:T(8,128)(2,1)}, u32[]{:S(2)}, u32[]{:S(2)}) async-start(bf16[128,32,128]{2,1,0:T(8,128)(2,1)} %bitcast.367), calls=%async_computation.11 | async-start | bytes 2097152 | tf_op jit(solution)/shard_map/all_to_all | solution.py:156
  483.3 5.8 fusion.71
  491.0 9.6 %all-to-all-done.11 = bf16[128,32,128]{2,1,0:T(8,128)(2,1)} async-done(((bf16[128,32,128]{2,1,0:T(8,128)(2,1)}), bf16[128,32,128]{2,1,0:T(8,128)(2,1)}, u32[]{:S(2)}, u32[]{:S(2)}) %all-to-all-start.11) | async-done | bytes 1048608 | tf_op jit(solution)/shard_map/all_to_all | solution.py:156
  503.6 5.1 fusion.26
  513.9 3.8 fusion.69
  518.8 35.5 %all-reduce = (bf16[2,2,128]{2,1,0:T(2,128)(2,1)S(1)}, bf16[2,2,128]{2,1,0:T(2,128)(2,1)S(1)}, bf16[2,128]{1,0:T(2,128)(2,1)}) all-reduce(bf16[2,2,128]{2,1,0:T(2,128)(2,1)S(1)} %pad_maximum_fusion.2, bf16[2,2,128]{2,1,0:T(2,128)(2,1)S(1)} %pad_maximum_fusion.3, ...), channel_id=1, replica_groups=mesh['grp'=2,'row'=8,'col'=2] {'row','col'}, use_global_device_ids=true, to_apply=%region_22.0 | all-reduce | flops 1280 | bytes 5120 | tf_op jit(solution)/shard_map/psum | solution.py:267
  556.3 4.8 fusion.66
  561.7 82.6 %all-reduce.4.cloned.1.call-done = (bf16[2,128,640]{2,1,0:T(8,128)(2,1)}, bf16[2,128,128]{2,1,0:T(8,128)(2,1)}) async-done(((bf16[2,128,640]{2,1,0:T(8,128)(2,1)}, bf16[2,128,128]{2,1,0:T(8,128)(2,1)}), (bf16[2,128,640]{2,1,0:T(8,128)(2,1)}, bf16[2,128,128]{2,1,0:T(8,128)(2,1)})) %all-reduce.4.cloned.1.call-update) | async-done | bytes 393232 | tf_op jit(solution)/shard_map/psum | solution.py:265
  (242 shorter events, 163.3 us)
Async XLA Ops:
  7.2 7.5 %copy-start.9 = (bf16[32,128,128]{2,1,0:T(8,128)(2,1)S(1)}, bf16[32,128,128]{2,1,0:T(8,128)(2,1)}, u32[]{:S(2)}) copy-start(bf16[32,128,128]{2,1,0:T(8,128)(2,1)} %param.11) | copy-start | bytes 3145732
  7.2 6.8 %copy-start.55 = (f32[2,128]{1,0:T(2,128)S(1)}, f32[2,128]{1,0:T(2,128)}, u32[]{:S(2)}) copy-start(f32[2,128]{1,0:T(2,128)} %param.18) | copy-start | bytes 3076
  7.2 6.8 %copy-start.56 = (f32[2,128]{1,0:T(2,128)S(1)}, f32[2,128]{1,0:T(2,128)}, u32[]{:S(2)}) copy-start(f32[2,128]{1,0:T(2,128)} %param.17) | copy-start | bytes 3076
  8.8 7.1 %copy-start.21 = (bf16[2,128,640]{2,1,0:T(8,128)(2,1)S(1)}, bf16[2,128,640]{2,1,0:T(8,128)(2,1)}, u32[]{:S(2)}) copy-start(bf16[2,128,640]{2,1,0:T(8,128)(2,1)} %param.15) | copy-start | bytes 983044
  17.4 4.0 copy-start
  23.1 30.3 %all-to-all-start = ((bf16[128,32,128]{2,1,0:T(8,128)(2,1)}), bf16[128,32,128]{2,1,0:T(8,128)(2,1)S(1)}, u32[]{:S(2)}, u32[]{:S(2)}) async-start(bf16[128,32,128]{2,1,0:T(8,128)(2,1)} %copy.24), calls=%async_computation | async-start | bytes 2097152 | tf_op jit(solution)/shard_map/all_to_all | solution.py:138
  53.5 29.9 %all-to-all-start.1 = ((bf16[128,32,128]{2,1,0:T(8,128)(2,1)}), bf16[128,32,128]{2,1,0:T(8,128)(2,1)}, u32[]{:S(2)}, u32[]{:S(2)}) async-start(bf16[128,32,128]{2,1,0:T(8,128)(2,1)} %copy.27), calls=%async_computation.1 | async-start | bytes 2097152 | tf_op jit(solution)/shard_map/all_to_all | solution.py:139
  64.2 24.2 %copy-start.10 = (bf16[8,256,256]{2,1,0:T(8,128)(2,1)}, bf16[8,256,256]{2,1,0:T(8,128)(2,1)S(1)}, u32[]{:S(2)}) copy-start(bf16[8,256,256]{2,1,0:T(8,128)(2,1)S(1)} %reshape.302) | copy-start | bytes 3145732
  91.2 8.6 %copy-start.61 = (s32[256]{0:T(256)S(1)}, s32[256]{0:T(256)}, u32[]{:S(2)}) copy-start(s32[256]{0:T(256)} %param.14) | copy-start | bytes 3076
  91.2 8.7 %copy-start.54 = (f32[2,128]{1,0:T(2,128)S(1)}, f32[2,128]{1,0:T(2,128)}, u32[]{:S(2)}) copy-start(f32[2,128]{1,0:T(2,128)} %param.19) | copy-start | bytes 3076
  91.2 9.3 %copy-start.57 = (f32[2,128]{1,0:T(2,128)S(1)}, f32[2,128]{1,0:T(2,128)}, u32[]{:S(2)}) copy-start(f32[2,128]{1,0:T(2,128)} %param.20) | copy-start | bytes 3076
  91.3 9.3 %copy-start.58 = (f32[2,128]{1,0:T(2,128)S(1)}, f32[2,128]{1,0:T(2,128)}, u32[]{:S(2)}) copy-start(f32[2,128]{1,0:T(2,128)} %param.21) | copy-start | bytes 3076
  92.5 30.3 %all-to-all-start.2 = ((bf16[128,32,128]{2,1,0:T(8,128)(2,1)}), bf16[128,32,128]{2,1,0:T(8,128)(2,1)S(1)}, u32[]{:S(2)}, u32[]{:S(2)}) async-start(bf16[128,32,128]{2,1,0:T(8,128)(2,1)} %bitcast.368), calls=%async_computation.2 | async-start | bytes 2097152 | tf_op jit(solution)/shard_map/all_to_all | solution.py:206
  100.5 26.9 %copy-start.36 = (f32[128]{0:T(128)}, f32[128]{0:T(128)S(1)}, u32[]{:S(2)}) copy-start(f32[128]{0:T(128)S(1)} %get-tuple-element.61) | copy-start | bytes 1540
  101.0 26.4 %copy-start.41 = (f32[128]{0:T(128)}, f32[128]{0:T(128)S(1)}, u32[]{:S(2)}) copy-start(f32[128]{0:T(128)S(1)} %get-tuple-element.77) | copy-start | bytes 1540
  101.0 26.4 %copy-start.46 = (f32[128]{0:T(128)}, f32[128]{0:T(128)S(1)}, u32[]{:S(2)}) copy-start(f32[128]{0:T(128)S(1)} %get-tuple-element.63) | copy-start | bytes 1540
  127.4 5.1 copy-start.2
  135.7 4.9 copy-start.1
  143.3 29.9 %all-to-all-start.4 = ((bf16[128,32,128]{2,1,0:T(8,128)(2,1)}), bf16[128,32,128]{2,1,0:T(8,128)(2,1)}, u32[]{:S(2)}, u32[]{:S(2)}) async-start(bf16[128,32,128]{2,1,0:T(8,128)(2,1)} %copy.35), calls=%async_computation.4 | async-start | bytes 2097152 | tf_op jit(solution)/shard_map/all_to_all | solution.py:138
  173.3 29.9 %all-to-all-start.3 = ((bf16[128,32,128]{2,1,0:T(8,128)(2,1)}), bf16[128,32,128]{2,1,0:T(8,128)(2,1)}, u32[]{:S(2)}, u32[]{:S(2)}) async-start(bf16[128,32,128]{2,1,0:T(8,128)(2,1)} %copy.32), calls=%async_computation.3 | async-start | bytes 2097152 | tf_op jit(solution)/shard_map/all_to_all | solution.py:139
  305.0 28.1 %all-to-all-start.7 = ((bf16[128,32,128]{2,1,0:T(8,128)(2,1)}), bf16[128,32,128]{2,1,0:T(8,128)(2,1)}, u32[]{:S(2)}, u32[]{:S(2)}) async-start(bf16[128,32,128]{2,1,0:T(8,128)(2,1)} %bitcast.370), calls=%async_computation.7 | async-start | bytes 2097152 | tf_op jit(solution)/shard_map/all_to_all | solution.py:149
  333.0 30.1 %all-to-all-start.8 = ((bf16[128,32,128]{2,1,0:T(8,128)(2,1)}), bf16[128,32,128]{2,1,0:T(8,128)(2,1)}, u32[]{:S(2)}, u32[]{:S(2)}) async-start(bf16[128,32,128]{2,1,0:T(8,128)(2,1)} %bitcast.371), calls=%async_computation.8 | async-start | bytes 2097152 | tf_op jit(solution)/shard_map/all_to_all | solution.py:156
  442.7 28.0 %all-to-all-start.10 = ((bf16[128,32,128]{2,1,0:T(8,128)(2,1)}), bf16[128,32,128]{2,1,0:T(8,128)(2,1)}, u32[]{:S(2)}, u32[]{:S(2)}) async-start(bf16[128,32,128]{2,1,0:T(8,128)(2,1)} %bitcast.372), calls=%async_computation.10 | async-start | bytes 2097152 | tf_op jit(solution)/shard_map/all_to_all | solution.py:149
  452.9 24.9 %copy-start.59 = (bf16[128]{0:T(256)(128)(2,1)S(1)}, bf16[128]{0:T(256)(128)(2,1)}, u32[]{:S(2)}) copy-start(bf16[128]{0:T(256)(128)(2,1)} %get-tuple-element.10) | copy-start | bytes 772
  452.9 24.9 %copy-start.60 = (bf16[128]{0:T(256)(128)(2,1)S(1)}, bf16[128]{0:T(256)(128)(2,1)}, u32[]{:S(2)}) copy-start(bf16[128]{0:T(256)(128)(2,1)} %get-tuple-element.19) | copy-start | bytes 772
  452.9 24.9 %copy-start.25 = (f32[4096]{0:T(1024)S(1)}, f32[4096]{0:T(1024)}, u32[]{:S(2)}) copy-start(f32[4096]{0:T(1024)} %copy-done.23) | copy-start | bytes 49156
  452.9 24.9 %copy-start.40 = (f32[128]{0:T(128)S(1)}, f32[128]{0:T(128)}, u32[]{:S(2)}) copy-start(f32[128]{0:T(128)} %get-tuple-element.60) | copy-start | bytes 1540
  452.9 24.9 %copy-start.49 = (f32[128]{0:T(128)S(1)}, f32[128]{0:T(128)}, u32[]{:S(2)}) copy-start(f32[128]{0:T(128)} %get-tuple-element.62) | copy-start | bytes 1540
  470.8 29.9 %all-to-all-start.11 = ((bf16[128,32,128]{2,1,0:T(8,128)(2,1)}), bf16[128,32,128]{2,1,0:T(8,128)(2,1)}, u32[]{:S(2)}, u32[]{:S(2)}) async-start(bf16[128,32,128]{2,1,0:T(8,128)(2,1)} %bitcast.367), calls=%async_computation.11 | async-start | bytes 2097152 | tf_op jit(solution)/shard_map/all_to_all | solution.py:156
  477.7 3.8 copy-start.47
  477.7 166.6 %all-reduce.4.cloned.1.call-start = ((), (), s32[]{:S(2)}) async-start(), calls=%async_computation.12 | async-start | bytes 786432 | tf_op jit(solution)/shard_map/psum | solution.py:265
  556.3 4.8 copy-start.62
  (43 other events, 98.2 us)
Sparse Core Ops, SparseCore 0:
  556.4 87.8 all-reduce.3
where the time goes:
time: 664 us; the launch traced here: 655 us
  waiting for transfers between devices  243 us (37%)
  blocking collectives  129 us (19%)
  local copies, waits for them, and re-layouts  97.5 us (15%)
  other arithmetic  61.1 us (9%)
  starting transfers between devices  59.7 us (9%)
  matrix products  49.7 us (7%)
  between operations  15.6 us (2%)
    psum x1, waiting for transfers between devices, shards(): lax.psum(stacked[0].astype(jnp.bfloat16), ('row', 'col'))  82.6 us
    all_to_all x2, blocking collectives, shards(): lax.all_to_all(cells_to_block(grad_prod, row_count, col_count), ('row', '...  61.5 us
    all_to_all x2, waiting for transfers between devices, edges_to_channels(): lax.all_to_all(left_block, ('row', 'col'), split_axis=0, concat_axis=1, t...  41.5 us
    all_to_all x2, waiting for transfers between devices, edges_to_channels(): lax.all_to_all(right_block, ('row', 'col'), split_axis=0, concat_axis=1,...  36.4 us
    psum x1, blocking collectives, shards(): lax.psum(stacked[2].astype(jnp.bfloat16), ('row', 'col'))  35.5 us
    all_to_all x1, blocking collectives, shards(): lax.all_to_all(full_to_joint(product, row_count, col_count), ('row', 'col...  31.7 us
    all_to_all x2, waiting for transfers between devices, grads_to_cells(): lax.all_to_all(full_to_joint(grad_left, row_count, col_count), ('row', 'c...  30.9 us
    all_to_all x2, waiting for transfers between devices, grads_to_cells(): lax.all_to_all(full_to_joint(grad_right, row_count, col_count), ('row', '...  29.7 us
  transfers between devices with their start and end apart: 10, of which 10 were waited for; matrix products, arithmetic and copies ran while one was open for 8% of the time, Pallas kernels for 0%

commit v1 on v0

v1 whole, which is shorter than its diff:
```python
import functools

import jax
import jax.numpy as jnp
from jax import lax
from jax.experimental import pallas as pl
from jax.experimental.pallas import tpu as pltpu
from jax.sharding import PartitionSpec as P

EPSILON = 1e-05
AXES = ("row", "col")
F32 = jnp.float32
BF16 = jnp.bfloat16
VMEM_BYTES = 50 * 1024 * 1024


def dot(a, b, ca, cb):
    return lax.dot_general(a, b, (((ca,), (cb,)), ((), ())), preferred_element_type=F32)


def sigmoid(x):
    return 0.5 * jnp.tanh(0.5 * x) + 0.5


def columns(vectors, width):
    c = vectors.shape[1]
    square = jnp.broadcast_to(vectors, (c, c)).T
    return jnp.concatenate([square] * (width // c), 1)


def norm(x):
    centred = x - jnp.mean(x, 0, keepdims=True)
    inv = lax.rsqrt(jnp.mean(centred * centred, 0, keepdims=True) + EPSILON)
    return centred * inv, inv


def norm_grad(grad_scaled, normed, inv, gain):
    g = grad_scaled * gain
    first = jnp.mean(g, 0, keepdims=True)
    second = jnp.mean(g * normed, 0, keepdims=True)
    return (g - first - normed * second) * inv


def unpack(block, cpd):
    devices, rows, cols = block.shape
    values = block.astype(F32)
    parts = []
    for a in range(rows // cpd):
        if cpd % 8 == 0:
            parts.append(values[:, a * cpd : (a + 1) * cpd, :].reshape(devices * cpd, cols))
        else:
            parts.append(
                jnp.concatenate([values[d, a * cpd : (a + 1) * cpd, :] for d in range(devices)], 0)
            )
    return jnp.concatenate(parts, 1)


def pack(tile, cpd, cols):
    channels, lanes = tile.shape
    devices = channels // cpd
    parts = [tile[:, a * cols : (a + 1) * cols] for a in range(lanes // cols)]
    if cpd % 8 == 0:
        return jnp.concatenate([p.reshape(devices, cpd, cols) for p in parts], 1).astype(BF16)
    return jnp.stack(
        [
            jnp.concatenate([p[d * cpd : (d + 1) * cpd, :] for p in parts], 0)
            for d in range(devices)
        ]
    ).astype(BF16)


def fold(tile, width):
    return sum(tile[:, a : a + width] for a in range(0, tile.shape[1], width))


def project(cells, wt_ref, gain, bias, hidden, blocks):
    normed, inv = norm(cells)
    lowered = (normed * gain + bias).astype(BF16)
    projected = dot(wt_ref[: blocks * hidden, :], lowered, 1, 0)
    return normed, inv, lowered, projected


def emit_edges(cells, wt_ref, gain, bias, chain, mask, same, hidden, cpd, cols):
    _, _, _, projected = project(cells, wt_ref, gain, bias, hidden, 5)
    part = [projected[n * hidden : (n + 1) * hidden] for n in range(5)]
    left = part[0] * sigmoid(part[1]) * mask
    right = part[2] * sigmoid(part[3]) * mask
    gate = sigmoid(part[4] + same * chain)
    return pack(left, cpd, cols), pack(right, cpd, cols), gate


def edge_first_kernel(
    cpd, q, mask_smem, chain_smem, start_smem, pair_ref, cot_ref, maskc_ref, chainc_ref, wt_ref,
    gain_ref, bias_ref, chain_ref, edges_ref, z_ref, up_ref, gate_ref, flags_ref, vec,
):
    tiles, channels, lanes = z_ref.shape
    hidden = wt_ref.shape[0] // 5
    cols = lanes // q
    step = pl.program_id(0)

    @pl.when(step == 0)
    def _():
        vec[0] = columns(gain_ref[0:1, :], lanes)
        vec[1] = columns(bias_ref[0:1, :], lanes)
        vec[2] = columns(chain_ref[0:1, :], lanes)

    for t in range(tiles):
        z_parts, u_parts, m_parts, s_parts = [], [], [], []
        for a in range(q):
            row = t * q + a
            z_parts.append(pair_ref[row].astype(F32).T)
            u_parts.append(cot_ref[row].astype(F32).T)
            whole = start_smem[0] + step * (tiles * q) + row
            m_parts.append(maskc_ref[pl.ds(start_smem[1], 1), :] * mask_smem[whole])
            s_parts.append((chainc_ref[pl.ds(start_smem[1], 1), :] == chain_smem[whole]).astype(F32))
        cells = jnp.concatenate(z_parts, 1)
        mask = jnp.concatenate(m_parts, 1).astype(F32)
        same = jnp.concatenate(s_parts, 1)
        left, right, gate = emit_edges(
            cells, wt_ref, vec[0], vec[1], vec[2], mask, same, hidden, cpd, cols
        )
        edges_ref[:, 0, t * q * cpd : (t + 1) * q * cpd, :] = left
        edges_ref[:, 1, t * q * cpd : (t + 1) * q * cpd, :] = right
        z_ref[t] = cells.astype(BF16)
        up_ref[t] = jnp.concatenate(u_parts, 1).astype(BF16)
        gate_ref[t] = gate
        flags_ref[t] = jnp.concatenate([mask, same], 0)


def mix_edge_kernel(
    cpd, q, layer, prod_ref, z_ref, gate_ref, flags_ref, owt_ref, hgain_ref, hbias_ref, wt_ref,
    gain_ref, bias_ref, chain_ref, edges_ref, znext_ref, gatenext_ref, vec,
):
    tiles, channels, lanes = z_ref.shape
    hidden = wt_ref.shape[0] // 5
    cols = lanes // q
    rows = q * cpd

    @pl.when(pl.program_id(0) == 0)
    def _():
        vec[0] = columns(hgain_ref[layer : layer + 1, :], lanes)
        vec[1] = columns(hbias_ref[layer : layer + 1, :], lanes)
        vec[2] = columns(gain_ref[layer + 1 : layer + 2, :], lanes)
        vec[3] = columns(bias_ref[layer + 1 : layer + 2, :], lanes)
        vec[4] = columns(chain_ref[layer + 1 : layer + 2, :], lanes)

    for t in range(tiles):
        mask, same = flags_ref[t, 0:1, :], flags_ref[t, 1:2, :]
        hnormed, _ = norm(unpack(prod_ref[:, t * rows : (t + 1) * rows, :], cpd))
        hscaled = (hnormed * vec[0] + vec[1]).astype(BF16)
        cells = z_ref[t].astype(F32) + gate_ref[t] * dot(owt_ref[...], hscaled, 1, 0)
        left, right, gate = emit_edges(
            cells, wt_ref, vec[2], vec[3], vec[4], mask, same, hidden, cpd, cols
        )
        edges_ref[:, 0, t * rows : (t + 1) * rows, :] = left
        edges_ref[:, 1, t * rows : (t + 1) * rows, :] = right
        znext_ref[t] = cells
        gatenext_ref[t] = gate


def mix_back(upstream, product, gate, same, ow_ref, owt_ref, hgain, hbias, acc_ow, acc_hg, acc_hb, acc_ch):
    width = acc_hg.shape[1]
    hnormed, hinv = norm(product)
    hscaled = (hnormed * hgain + hbias).astype(BF16)
    mixed = dot(owt_ref[...], hscaled, 1, 0)
    grad_gate = upstream * gate
    grad_logits = grad_gate * mixed * (1.0 - gate)
    grad_mixed = grad_gate.astype(BF16)
    acc_ow[...] += dot(hscaled, grad_mixed, 1, 1)
    grad_hscaled = dot(ow_ref[...], grad_mixed, 1, 0)
    acc_hg[...] += fold(grad_hscaled * hnormed, width)
    acc_hb[...] += fold(grad_hscaled, width)
    acc_ch[...] += fold(grad_logits * same, width)
    return norm_grad(grad_hscaled, hnormed, hinv, hgain), grad_logits


def row_of(acc):
    return jnp.sum(acc.T, 0, keepdims=True)


def finish_mix(out_ref, acc_ow, acc_hg, acc_hb, acc_ch):
    hidden = acc_ow.shape[0]
    out_ref[:hidden, :] = acc_ow[...]
    rows = [row_of(acc_hg[...]), row_of(acc_hb[...]), row_of(acc_ch[...])]
    rows.append(jnp.zeros((out_ref.shape[0] - hidden - 3, hidden), F32))
    out_ref[hidden:, :] = jnp.concatenate(rows, 0)


def mix_back_kernel(
    cpd, q, layer, prod_ref, up_ref, gate_ref, flags_ref, ow_ref, owt_ref, hgain_ref, hbias_ref,
    gp_ref, glog_ref, terms_ref, vec, acc_ow, acc_hg, acc_hb, acc_ch,
):
    tiles, channels, lanes = up_ref.shape
    cols = lanes // q
    rows = q * cpd

    @pl.when(pl.program_id(0) == 0)
    def _():
        vec[0] = columns(hgain_ref[layer : layer + 1, :], lanes)
        vec[1] = columns(hbias_ref[layer : layer + 1, :], lanes)
        for acc in (acc_ow, acc_hg, acc_hb, acc_ch):
            acc[...] = jnp.zeros_like(acc)

    for t in range(tiles):
        grad_product, grad_logits = mix_back(
            up_ref[t].astype(F32),
            unpack(prod_ref[:, t * rows : (t + 1) * rows, :], cpd),
            gate_ref[t], flags_ref[t, 1:2, :], ow_ref, owt_ref, vec[0], vec[1],
            acc_ow, acc_hg, acc_hb, acc_ch,
        )
        gp_ref[:, t * rows : (t + 1) * rows, :] = pack(grad_product, cpd, cols)
        glog_ref[t] = grad_logits.astype(BF16)

    @pl.when(pl.program_id(0) == pl.num_programs(0) - 1)
    def _():
        finish_mix(terms_ref, acc_ow, acc_hg, acc_hb, acc_ch)


def edge_back(
    cells, upstream, grad_left, grad_right, glog, mask, wt_ref, w_ref, gain, bias, hidden, acc_w, acc_g, acc_b
):
    width = acc_g.shape[1]
    normed, inv, lowered, projected = project(cells, wt_ref, gain, bias, hidden, 4)
    part = [projected[n * hidden : (n + 1) * hidden] for n in range(4)]
    blocks = []
    for grad, value, logit in ((grad_left, part[0], part[1]), (grad_right, part[2], part[3])):
        sig = sigmoid(logit)
        opened = grad * mask * sig
        blocks += [opened.astype(BF16), (opened * value * (1.0 - sig)).astype(BF16)]
    grad_projected = jnp.concatenate(blocks + [glog], 0)
    acc_w[...] += dot(lowered, grad_projected, 1, 1)
    grad_scaled = dot(w_ref[...], grad_projected, 1, 0)
    acc_g[...] += fold(grad_scaled * normed, width)
    acc_b[...] += fold(grad_scaled, width)
    return upstream + norm_grad(grad_scaled, normed, inv, gain)


def finish_edge(out_ref, mix_ref, acc_w, acc_g, acc_b):
    hidden = acc_w.shape[0]
    for n in range(5):
        out_ref[n * hidden : (n + 1) * hidden, :] = acc_w[:, n * hidden : (n + 1) * hidden].astype(BF16)
    out_ref[5 * hidden : 6 * hidden, :] = mix_ref[:hidden, :].astype(BF16)
    rows = [
        row_of(acc_g[...]), row_of(acc_b[...]), mix_ref[hidden : hidden + 3, :],
        jnp.zeros((out_ref.shape[0] - 6 * hidden - 5, hidden), F32),
    ]
    out_ref[6 * hidden :, :] = jnp.concatenate(rows, 0).astype(BF16)


def edge_mix_back_kernel(
    cpd, q, layer, grads_ref, z_ref, glog_ref, up_ref, flags_ref, wt_ref, w_ref, gain_ref, bias_ref,
    terms_in_ref, prod_ref, gate_ref, ow_ref, owt_ref, hgain_ref, hbias_ref,
    upnext_ref, gp_ref, glognext_ref, all_ref, terms_ref,
    vec, acc_w, acc_g, acc_b, acc_ow, acc_hg, acc_hb, acc_ch,
):
    tiles, channels, lanes = z_ref.shape
    hidden = wt_ref.shape[0] // 5
    cols = lanes // q
    rows = q * cpd

    @pl.when(pl.program_id(0) == 0)
    def _():
        vec[0] = columns(gain_ref[layer : layer + 1, :], lanes)
        vec[1] = columns(bias_ref[layer : layer + 1, :], lanes)
        vec[2] = columns(hgain_ref[layer - 1 : layer, :], lanes)
        vec[3] = columns(hbias_ref[layer - 1 : layer, :], lanes)
        for acc in (acc_w, acc_g, acc_b, acc_ow, acc_hg, acc_hb, acc_ch):
            acc[...] = jnp.zeros_like(acc)

    for t in range(tiles):
        here = slice(t * rows, (t + 1) * rows)
        upstream = edge_back(
            z_ref[t], up_ref[t].astype(F32), unpack(grads_ref[:, 0, here, :], cpd),
            unpack(grads_ref[:, 1, here, :], cpd), glog_ref[t], flags_ref[t, 0:1, :],
            wt_ref, w_ref, vec[0], vec[1], hidden, acc_w, acc_g, acc_b,
        )
        upnext_ref[t] = upstream
        grad_product, grad_logits = mix_back(
            upstream, unpack(prod_ref[:, here, :], cpd), gate_ref[t], flags_ref[t, 1:2, :],
            ow_ref, owt_ref, vec[2], vec[3], acc_ow, acc_hg, acc_hb, acc_ch,
        )
        gp_ref[:, here, :] = pack(grad_product, cpd, cols)
        glognext_ref[t] = grad_logits.astype(BF16)

    @pl.when(pl.program_id(0) == pl.num_programs(0) - 1)
    def _():
        finish_edge(all_ref, terms_in_ref, acc_w, acc_g, acc_b)
        finish_mix(terms_ref, acc_ow, acc_hg, acc_hb, acc_ch)


def edge_back_kernel(
    cpd, q, layer, grads_ref, z_ref, glog_ref, up_ref, flags_ref, wt_ref, w_ref, gain_ref, bias_ref,
    terms_in_ref, pair_ref, all_ref, vec, acc_w, acc_g, acc_b,
):
    tiles, channels, lanes = z_ref.shape
    hidden = wt_ref.shape[0] // 5
    cols = lanes // q
    rows = q * cpd

    @pl.when(pl.program_id(0) == 0)
    def _():
        vec[0] = columns(gain_ref[layer : layer + 1, :], lanes)
        vec[1] = columns(bias_ref[layer : layer + 1, :], lanes)
        for acc in (acc_w, acc_g, acc_b):
            acc[...] = jnp.zeros_like(acc)

    for t in range(tiles):
        here = slice(t * rows, (t + 1) * rows)
        upstream = edge_back(
            z_ref[t].astype(F32), up_ref[t], unpack(grads_ref[:, 0, here, :], cpd),
            unpack(grads_ref[:, 1, here, :], cpd), glog_ref[t], flags_ref[t, 0:1, :],
            wt_ref, w_ref, vec[0], vec[1], hidden, acc_w, acc_g, acc_b,
        )
        for a in range(q):
            pair_ref[t * q + a] = upstream[:, a * cols : (a + 1) * cols].T.astype(BF16)

    @pl.when(pl.program_id(0) == pl.num_programs(0) - 1)
    def _():
        finish_edge(all_ref, terms_in_ref, acc_w, acc_g, acc_b)


def cell_call(kernel, steps, ins, outs, scratch, prefetch=(), flops=0):
    def spec(shape, how):
        if how is None:
            return pl.BlockSpec(shape, lambda *s: (0,) * len(shape))
        block = tuple(n // steps if axis == how else n for axis, n in enumerate(shape))
        return pl.BlockSpec(
            block, lambda *s: tuple(s[0] if axis == how else 0 for axis in range(len(shape)))
        )

    moved = sum(a.size * a.dtype.itemsize for a, _ in ins)
    moved += sum(functools.reduce(lambda x, y: x * y, s, 1) * jnp.dtype(t).itemsize for (s, t), _ in outs)
    return pl.pallas_call(
        kernel,
        grid_spec=pltpu.PrefetchScalarGridSpec(
            num_scalar_prefetch=len(prefetch),
            grid=(steps,),
            in_specs=[spec(a.shape, how) for a, how in ins],
            out_specs=[spec(s, how) for (s, _), how in outs],
            scratch_shapes=scratch,
        ),
        out_shape=[jax.ShapeDtypeStruct(s, t) for (s, t), _ in outs],
        compiler_params=pltpu.CompilerParams(vmem_limit_bytes=VMEM_BYTES),
        cost_estimate=pl.CostEstimate(flops=flops, bytes_accessed=int(moved), transcendentals=0),
    )(*prefetch, *[a for a, _ in ins])


def widen(src_ref, dst):
    devices, cols = src_ref.shape[0], src_ref.shape[-1]
    per = dst.shape[0] // devices
    for d in range(devices):
        dst[d * per : (d + 1) * per, :] = src_ref[d].astype(F32).reshape(per, cols)


def narrow(src, dst_ref):
    devices = dst_ref.shape[0]
    per = src.shape[0] // devices
    for d in range(devices):
        dst_ref[d] = src[d * per : (d + 1) * per, :].astype(BF16).reshape(dst_ref.shape[1:])


def get_channel(src, ch, sub, subs, dims):
    row_devs, col_devs, rows, cpd, cols = dims
    halves = []
    for s in range(col_devs):
        parts = []
        for r in range(row_devs):
            base = ((r * col_devs + s) * subs + sub) * rows * cpd
            parts.append(src[pl.ds(base + ch, rows, stride=cpd), :])
        halves.append(jnp.concatenate(parts, 0))
    return jnp.concatenate(halves, 1).astype(BF16)


def put_channel(dst, value, ch, sub, subs, dims):
    row_devs, col_devs, rows, cpd, cols = dims
    for s in range(col_devs):
        for r in range(row_devs):
            base = ((r * col_devs + s) * subs + sub) * rows * cpd
            dst[pl.ds(base + ch, rows, stride=cpd), :] = value[
                r * rows : (r + 1) * rows, s * cols : (s + 1) * cols
            ]


def product_kernel(dims, outgoing, edges_ref, out_ref, edges, result):
    widen(edges_ref, edges)
    for ch in range(dims[3]):
        left = get_channel(edges, ch, 0, 2, dims)
        right = get_channel(edges, ch, 1, 2, dims)
        value = dot(left, right, 1, 1) if outgoing else dot(left, right, 0, 0)
        put_channel(result, value, ch, 0, 1, dims)
    narrow(result, out_ref)


def product_grad_kernel(dims, outgoing, edges_ref, grad_ref, out_ref, edges, grad, result):
    widen(edges_ref, edges)
    widen(grad_ref, grad)
    for ch in range(dims[3]):
        left = get_channel(edges, ch, 0, 2, dims)
        right = get_channel(edges, ch, 1, 2, dims)
        gp = get_channel(grad, ch, 0, 1, dims)
        if outgoing:
            grad_left = dot(gp, right, 1, 0)
            grad_right = dot(gp, left, 0, 0)
        else:
            grad_left = dot(right, gp, 1, 1)
            grad_right = dot(left, gp, 1, 0)
        put_channel(result, grad_left, ch, 0, 2, dims)
        put_channel(result, grad_right, ch, 1, 2, dims)
    narrow(result, out_ref)


def channel_call(kernel, ins, out_shape, flops):
    cols = out_shape[-1]

    def rows_of(shape):
        return functools.reduce(lambda x, y: x * y, shape[:-1], 1)

    moved = sum(a.size * 2 for a in ins) + 2 * cols * rows_of(out_shape)
    return pl.pallas_call(
        kernel,
        in_specs=[pl.BlockSpec(memory_space=pltpu.VMEM)] * len(ins),
        out_specs=pl.BlockSpec(memory_space=pltpu.VMEM),
        out_shape=jax.ShapeDtypeStruct(out_shape, BF16),
        scratch_shapes=[pltpu.VMEM((rows_of(a.shape), cols), F32) for a in ins]
        + [pltpu.VMEM((rows_of(out_shape), cols), F32)],
        compiler_params=pltpu.CompilerParams(vmem_limit_bytes=VMEM_BYTES),
        cost_estimate=pl.CostEstimate(flops=flops, bytes_accessed=int(moved), transcendentals=0),
    )(*ins)


def exchange(array):
    return lax.all_to_all(array, AXES, split_axis=0, concat_axis=0, tiled=True)


def shards(
    pair_rep, cotangent, residue_mask, chain_ids, proj_weight, out_weight,
    input_gain, input_bias, hidden_gain, hidden_bias, chain_bias,
):
    rows, cols, width = pair_rep.shape
    hidden = out_weight.shape[1]
    row_devs, col_devs = lax.axis_size("row"), lax.axis_size("col")
    devices = row_devs * col_devs
    length = rows * row_devs
    cpd = hidden // devices
    q = max(1, 16 // cpd)
    tiles = rows // q
    lanes = q * cols
    steps = max(1, tiles // 2)
    dims = (row_devs, col_devs, rows, cpd, cols)
    side = rows * cpd

    starts = jnp.stack([lax.axis_index("row") * rows, lax.axis_index("col")]).astype(jnp.int32)
    wt = jnp.swapaxes(proj_weight, 1, 2)
    owt = jnp.swapaxes(out_weight, 1, 2)
    tile = (tiles, width, lanes)
    edge_shape = (devices, 2, side, cols)
    cell_shape = (devices, side, cols)
    vec = lambda n: pltpu.VMEM((n, width, lanes), F32)
    acc = lambda n: pltpu.VMEM((width, n), F32)
    cell_flops = 2 * rows * cols * width * hidden
    tri_flops = 2 * cpd * length**3

    def product(edges, outgoing):
        return channel_call(
            functools.partial(product_kernel, dims, outgoing), [edges], cell_shape, tri_flops
        )

    def product_grad(edges, grad, outgoing):
        return channel_call(
            functools.partial(product_grad_kernel, dims, outgoing), [edges, grad], edge_shape, 2 * tri_flops
        )

    edges0, z0, up, gate0, flags = cell_call(
        functools.partial(edge_first_kernel, cpd, q),
        steps,
        [
            (pair_rep, 0), (cotangent, 0), (residue_mask.reshape(col_devs, cols), None),
            (chain_ids.reshape(col_devs, cols), None), (wt[0], None),
            (input_gain, None), (input_bias, None), (chain_bias, None),
        ],
        [
            ((edge_shape, BF16), 2), ((tile, BF16), 0), ((tile, BF16), 0), ((tile, F32), 0),
            (((tiles, 2, lanes), F32), 0),
        ],
        [vec(3)],
        prefetch=(residue_mask, chain_ids, starts),
        flops=5 * cell_flops,
    )
    edges0 = exchange(edges0)
    prod0 = exchange(product(edges0, True))
    edges1, z1, gate1 = cell_call(
        functools.partial(mix_edge_kernel, cpd, q, 0),
        steps,
        [
            (prod0, 1), (z0, 0), (gate0, 0), (flags, 0), (owt[0], None), (hidden_gain, None),
            (hidden_bias, None), (wt[1], None), (input_gain, None), (input_bias, None), (chain_bias, None),
        ],
        [((edge_shape, BF16), 2), ((tile, F32), 0), ((tile, F32), 0)],
        [vec(5)],
        flops=6 * cell_flops,
    )
    edges1 = exchange(edges1)
    prod1 = exchange(product(edges1, False))
    terms_shape = (hidden + 8, hidden)
    grad1, glog1, terms1 = cell_call(
        functools.partial(mix_back_kernel, cpd, q, 1),
        steps,
        [
            (prod1, 1), (up, 0), (gate1, 0), (flags, 0), (out_weight[1], None), (owt[1], None),
            (hidden_gain, None), (hidden_bias, None),
        ],
        [((cell_shape, BF16), 1), ((tile, BF16), 0), ((terms_shape, F32), None)],
        [vec(2), acc(hidden), acc(cols), acc(cols), acc(cols)],
        flops=3 * cell_flops,
    )
    grads1 = exchange(product_grad(edges1, exchange(grad1), False))
    per_device = -(-(6 * hidden + 5) * 2 // (devices * 16)) * 16
    all_shape = (devices * per_device // 2, hidden)
    up0, grad0, glog0, all1, terms0 = cell_call(
        functools.partial(edge_mix_back_kernel, cpd, q, 1),
        steps,
        [
            (grads1, 2), (z1, 0), (glog1, 0), (up, 0), (flags, 0), (wt[1], None), (proj_weight[1], None),
            (input_gain, None), (input_bias, None), (terms1, None), (prod0, 1), (gate0, 0),
            (out_weight[0], None), (owt[0], None), (hidden_gain, None), (hidden_bias, None),
        ],
        [
            ((tile, F32), 0), ((cell_shape, BF16), 1), ((tile, BF16), 0), ((all_shape, BF16), None),
            ((terms_shape, F32), None),
        ],
        [vec(4), acc(5 * hidden), acc(cols), acc(cols), acc(hidden), acc(cols), acc(cols), acc(cols)],
        flops=17 * cell_flops,
    )
    grads0 = exchange(product_grad(edges0, exchange(grad0), True))
    grad_pair, all0 = cell_call(
        functools.partial(edge_back_kernel, cpd, q, 0),
        steps,
        [
            (grads0, 2), (z0, 0), (glog0, 0), (up0, 0), (flags, 0), (wt[0], None), (proj_weight[0], None),
            (input_gain, None), (input_bias, None), (terms0, None),
        ],
        [((pair_rep.shape, BF16), 0), ((all_shape, BF16), None)],
        [vec(2), acc(5 * hidden), acc(cols), acc(cols)],
        flops=14 * cell_flops,
    )
    mine = exchange(jnp.stack([all0, all1]).reshape(devices, per_device, hidden))
    mine = (jnp.sum(mine.astype(F32), 0) * (1.0 / length)).astype(BF16)
    total = lax.all_gather(mine, AXES, axis=0, tiled=True).reshape(2, -1, hidden).astype(F32)
    proj = total[:, : 5 * hidden].reshape(2, 5, width, hidden).transpose(0, 2, 1, 3)
    vectors = total[:, 6 * hidden : 6 * hidden + 5]
    return (
        grad_pair,
        proj.reshape(2, width, 5 * hidden),
        total[:, 5 * hidden : 6 * hidden],
        vectors[:, 0:2],
        vectors[:, 2:4],
        vectors[:, 4],
    )


def solution(mesh):
    cells = P(("grp", "row"), "col", None)
    return jax.shard_map(
        shards,
        mesh=mesh,
        in_specs=(cells, cells, P("grp"), P("grp")) + (P(),) * 7,
        out_specs=(
            cells, P("grp", None, None), P("grp", None, None), P("grp", None, None),
            P("grp", None, None), P("grp", None),
        ),
        check_vma=False,
    )
```

time: 664 us -> 447 us (0.67); the launches traced: 655 us -> 445 us
  waiting for transfers between devices: 243 us -> 84.6 us
  blocking collectives: 129 us -> 268 us
  local copies, waits for them, and re-layouts: 97.5 us -> 15.4 us
  Pallas kernels: 0 us -> 61 us
  other arithmetic: 61.1 us -> 0.19 us
  matrix products: 49.7 us -> 0 us
  starting transfers between devices: 59.7 us -> 15.4 us
  between operations: 15.6 us -> 0.83 us
    all_to_all x3 -> x6, blocking collectives: 93.2 us -> 247 us  [exchange(): return lax.all_to_all(array, AXES, split_axis=0, concat_axis=0, tiled=True)]
    psum x1 -> x0, waiting for transfers between devices: 82.6 us -> none  [shards(): lax.psum(stacked[0].astype(jnp.bfloat16), ('row', 'col'))]
    all_to_all x9 -> x3, waiting for transfers between devices: 160 us -> 84.6 us  [exchange(): return lax.all_to_all(array, AXES, split_axis=0, concat_axis=0, tiled=True)]
    pallas_call x0 -> x9, Pallas kernels: none -> 61 us  [the longest x5 48.1 us: cell_call(): pl.pallas_call(kernel, grid_spec=pltpu.PrefetchScalarGridSpec(num_scalar_...]
    reshape x24 -> x1, local copies, waits for them, and re-layouts: 52.2 us -> 0.23 us  [shards(): total[:, :5 * hidden].reshape(2, 5, width, hidden).transpose(0, 2, 1, 3)]
    dot_general x18 -> x0, matrix products: 49.7 us -> none  [the longest x6 16.3 us: tri_product(): jnp.einsum(formula, first_edge, second_edge, preferred_element_type=jnp.f...]
    all_to_all x9 -> x3, starting transfers between devices: 59.6 us -> 15.4 us  [exchange(): return lax.all_to_all(array, AXES, split_axis=0, concat_axis=0, tiled=True)]
    psum x1 -> x0, blocking collectives: 35.5 us -> none  [shards(): lax.psum(stacked[2].astype(jnp.bfloat16), ('row', 'col'))]
  transfers between devices with their start and end apart: 10 -> 3, of which waited for: 10 -> 3; matrix products, arithmetic and copies ran while one was open for 8% -> 1% of each run, Pallas kernels for 0% -> 0%
where the time goes in v1:
time: 447 us; the launch traced here: 445 us
  blocking collectives  268 us (60%)
  waiting for transfers between devices  84.6 us (19%)
  Pallas kernels  61 us (14%)
  local copies, waits for them, and re-layouts  15.4 us (3%)
  starting transfers between devices  15.4 us (3%)
    all_to_all x6, blocking collectives, exchange(): return lax.all_to_all(array, AXES, split_axis=0, concat_axis=0, tiled=True)  247 us
    all_to_all x3, waiting for transfers between devices, exchange(): return lax.all_to_all(array, AXES, split_axis=0, concat_axis=0, tiled=True)  84.6 us
    pallas_call x5, Pallas kernels, cell_call(): pl.pallas_call(kernel, grid_spec=pltpu.PrefetchScalarGridSpec(num_scalar_...  48.1 us
    all_gather x1, blocking collectives, shards(): lax.all_gather(mine, AXES, axis=0, tiled=True).reshape(2, -1, hidden)  20.9 us
    all_to_all x3, starting transfers between devices, exchange(): return lax.all_to_all(array, AXES, split_axis=0, concat_axis=0, tiled=True)  15.4 us
    pallas_call x4, Pallas kernels, channel_call(): pl.pallas_call(kernel, in_specs=[pl.BlockSpec(memory_space=pltpu.VMEM)] *...  12.9 us
    unnamed x45, local copies, waits for them, and re-layouts  11.9 us
  transfers between devices with their start and end apart: 3, of which 3 were waited for; matrix products, arithmetic and copies ran while one was open for 1% of the time, Pallas kernels for 0%

profile of v1, /device:TPU:0, one launch (start us, length us, event | category | flops | bytes accessed | tf_op | source)
XLA Modules:
  0.0 445.1 jit_solution(11836492955768106775)
XLA Ops:
  0.6 1.2 copy.23
  1.9 0.7 copy-done.11
  2.6 0.7 copy-done.13
  4.0 1.2 copy-done.17
  6.6 8.6 %shard_map.154 = (bf16[16,2,256,128]{3,2,1,0:T(8,128)(2,1)}, bf16[16,128,256]{2,1,0:T(8,128)(2,1)S(1)}, bf16[16,128,256]{2,1,0:T(8,128)(2,1)S(1)}, f32[16,128,256]{2,1,0:T(8,128)}, f32[16,2,256]{2,1,0:T(2,128)S(1)}) custom-call(s32[256]{0:T(256)S(1)} %copy-done.18, s32[256]{0:T(256)S(1)} %copy-done.19, s32[2]{0:T(128)S(1)} %pad_add_fusion.start_smem, ...), custom_call_target="tpu_custom_call" | custom-call | flops 671088640 | bytes 8590336 | tf_op jit(solution)/shard_map/pallas_call | solution.py:333
  15.2 54.7 %all_to_all.45.edges_ref = bf16[16,2,256,128]{3,2,1,0:T(8,128)(2,1)S(1)} all-to-all(bf16[16,2,256,128]{3,2,1,0:T(8,128)(2,1)} %get-tuple-element.24), channel_id=1, replica_groups=mesh['grp'=2,'row'=8,'col'=2] {'row','col'}, dimensions={0} | all-to-all | bytes 4194304 | tf_op jit(solution)/shard_map/all_to_all | solution.py:432
  69.9 1.3 shard_map.155
  71.2 1.0 copy-done.3
  72.2 5.1 %all-to-all-start.1 = ((bf16[16,256,128]{2,1,0:T(8,128)(2,1)}), bf16[16,256,128]{2,1,0:T(8,128)(2,1)S(1)}, u32[]{:S(2)}, u32[]{:S(2)}) async-start(bf16[16,256,128]{2,1,0:T(8,128)(2,1)} %copy-done.3), calls=%async_computation.1 | async-start | bytes 2097152 | tf_op jit(solution)/shard_map/all_to_all | solution.py:432
  77.3 1.0 copy.24
  78.9 21.4 %all-to-all-done.1.prod_ref = bf16[16,256,128]{2,1,0:T(8,128)(2,1)S(1)} async-done(((bf16[16,256,128]{2,1,0:T(8,128)(2,1)}), bf16[16,256,128]{2,1,0:T(8,128)(2,1)S(1)}, u32[]{:S(2)}, u32[]{:S(2)}) %all-to-all-start.1) | async-done | bytes 1048608 | tf_op jit(solution)/shard_map/all_to_all | solution.py:432
  100.3 1.6 copy-done.6
  102.5 9.3 %shard_map.156 = (bf16[16,2,256,128]{3,2,1,0:T(8,128)(2,1)}, f32[16,128,256]{2,1,0:T(8,128)}, f32[16,128,256]{2,1,0:T(8,128)}) custom-call(bf16[16,256,128]{2,1,0:T(8,128)(2,1)S(1)} %all-to-all-done.1.prod_ref, bf16[16,128,256]{2,1,0:T(8,128)(2,1)S(1)} %copy-done.6, f32[16,128,256]{2,1,0:T(8,128)} %get-tuple-element.26.gate_ref, ...), custom_call_target="tpu_custom_call" | custom-call | flops 805306368 | bytes 10720256 | tf_op jit(solution)/shard_map/pallas_call | solution.py:333
  111.8 54.2 %all_to_all.46.edges_ref = bf16[16,2,256,128]{3,2,1,0:T(8,128)(2,1)S(1)} all-to-all(bf16[16,2,256,128]{3,2,1,0:T(8,128)(2,1)} %get-tuple-element.28), channel_id=1, replica_groups=mesh['grp'=2,'row'=8,'col'=2] {'row','col'}, dimensions={0} | all-to-all | bytes 4194304 | tf_op jit(solution)/shard_map/all_to_all | solution.py:432
  166.0 2.3 shard_map.157
  168.3 5.1 %all-to-all-start.3 = ((bf16[16,256,128]{2,1,0:T(8,128)(2,1)}), bf16[16,256,128]{2,1,0:T(8,128)(2,1)S(1)}, u32[]{:S(2)}, u32[]{:S(2)}) async-start(bf16[16,256,128]{2,1,0:T(8,128)(2,1)} %shard_map.157), calls=%async_computation.3 | async-start | bytes 2097152 | tf_op jit(solution)/shard_map/all_to_all | solution.py:432
  173.4 0.8 slice_bitcast_fusion.6
  174.2 22.2 %all-to-all-done.3.prod_ref = bf16[16,256,128]{2,1,0:T(8,128)(2,1)S(1)} async-done(((bf16[16,256,128]{2,1,0:T(8,128)(2,1)}), bf16[16,256,128]{2,1,0:T(8,128)(2,1)S(1)}, u32[]{:S(2)}, u32[]{:S(2)}) %all-to-all-start.3) | async-done | bytes 1048608 | tf_op jit(solution)/shard_map/all_to_all | solution.py:432
  196.4 0.8 copy-done.8
  197.1 6.6 %shard_map.158 = (bf16[16,256,128]{2,1,0:T(8,128)(2,1)S(1)}, bf16[16,128,256]{2,1,0:T(8,128)(2,1)S(1)}, f32[136,128]{1,0:T(8,128)S(1)}) custom-call(bf16[16,256,128]{2,1,0:T(8,128)(2,1)S(1)} %all-to-all-done.3.prod_ref, bf16[16,128,256]{2,1,0:T(8,128)(2,1)} %copy-done.4, f32[16,128,256]{2,1,0:T(8,128)} %get-tuple-element.30.gate_ref, ...), custom_call_target="tpu_custom_call" | custom-call | flops 402653184 | bytes 6461440 | tf_op jit(solution)/shard_map/pallas_call | solution.py:333
  203.7 31.5 %all_to_all.47.grad_ref = bf16[16,256,128]{2,1,0:T(8,128)(2,1)S(1)} all-to-all(bf16[16,256,128]{2,1,0:T(8,128)(2,1)S(1)} %get-tuple-element.31), channel_id=1, replica_groups=mesh['grp'=2,'row'=8,'col'=2] {'row','col'}, dimensions={0} | all-to-all | bytes 2097152 | tf_op jit(solution)/shard_map/all_to_all | solution.py:432
  235.3 5.2 %shard_map.159 = bf16[16,2,256,128]{3,2,1,0:T(8,128)(2,1)} custom-call(bf16[16,2,256,128]{3,2,1,0:T(8,128)(2,1)} %copy-done.1, bf16[16,256,128]{2,1,0:T(8,128)(2,1)S(1)} %all_to_all.47.grad_ref), custom_call_target="tpu_custom_call" | custom-call | flops 536870912 | bytes 5242880 | tf_op jit(solution)/shard_map/pallas_call | solution.py:419
  240.4 5.2 %all-to-all-start.5 = ((bf16[16,2,256,128]{3,2,1,0:T(8,128)(2,1)}), bf16[16,2,256,128]{3,2,1,0:T(8,128)(2,1)}, u32[]{:S(2)}, u32[]{:S(2)}) async-start(bf16[16,2,256,128]{3,2,1,0:T(8,128)(2,1)} %shard_map.159), calls=%async_computation.5 | async-start | bytes 4194304 | tf_op jit(solution)/shard_map/all_to_all | solution.py:432
  245.7 41.1 %all-to-all-done.5.grads_ref = bf16[16,2,256,128]{3,2,1,0:T(8,128)(2,1)} async-done(((bf16[16,2,256,128]{3,2,1,0:T(8,128)(2,1)}), bf16[16,2,256,128]{3,2,1,0:T(8,128)(2,1)}, u32[]{:S(2)}, u32[]{:S(2)}) %all-to-all-start.5) | async-done | bytes 2097184 | tf_op jit(solution)/shard_map/all_to_all | solution.py:432
  286.8 13.6 %shard_map.160 = (f32[16,128,256]{2,1,0:T(8,128)}, bf16[16,256,128]{2,1,0:T(8,128)(2,1)S(1)}, bf16[16,128,256]{2,1,0:T(8,128)(2,1)S(1)}, bf16[896,128]{1,0:T(8,128)(2,1)S(1)}, f32[136,128]{1,0:T(8,128)S(1)}) custom-call(bf16[16,2,256,128]{3,2,1,0:T(8,128)(2,1)} %all-to-all-done.5.grads_ref, f32[16,128,256]{2,1,0:T(8,128)} %get-tuple-element.32.z_ref, ...), custom_call_target="tpu_custom_call" | custom-call | flops 2281701376 | bytes 14430208 | tf_op jit(solution)/shard_map/pallas_call | solution.py:333
  300.4 35.8 %all_to_all.48.grad_ref = bf16[16,256,128]{2,1,0:T(8,128)(2,1)S(1)} all-to-all(bf16[16,256,128]{2,1,0:T(8,128)(2,1)S(1)} %get-tuple-element.35), channel_id=1, replica_groups=mesh['grp'=2,'row'=8,'col'=2] {'row','col'}, dimensions={0} | all-to-all | bytes 2097152 | tf_op jit(solution)/shard_map/all_to_all | solution.py:432
  336.3 4.2 shard_map.161
  340.5 52.4 %all_to_all.49.grads_ref = bf16[16,2,256,128]{3,2,1,0:T(8,128)(2,1)} all-to-all(bf16[16,2,256,128]{3,2,1,0:T(8,128)(2,1)S(1)} %shard_map.161), channel_id=1, replica_groups=mesh['grp'=2,'row'=8,'col'=2] {'row','col'}, dimensions={0} | all-to-all | bytes 4194304 | tf_op jit(solution)/shard_map/all_to_all | solution.py:432
  392.8 9.9 %shard_map.162 = (bf16[32,128,128]{2,1,0:T(8,128)(2,1)}, bf16[896,128]{1,0:T(8,128)(2,1)S(1)}) custom-call(bf16[16,2,256,128]{3,2,1,0:T(8,128)(2,1)} %all_to_all.49.grads_ref, bf16[16,128,256]{2,1,0:T(8,128)(2,1)S(1)} %copy-done.7, bf16[16,128,256]{2,1,0:T(8,128)(2,1)S(1)} %get-tuple-element.36.glog_ref, f32[16,128,256]{2,1,0:T(8,128)} %get-tuple-element.37.up_ref, ...), custom_call_target="tpu_custom_call" | custom-call | flops 1879048192 | bytes 8001536 | tf_op jit(solution)/shard_map/pallas_call | solution.py:333
  402.8 18.2 %all_to_all.50 = bf16[16,112,128]{2,1,0:T(8,128)(2,1)S(1)} all-to-all(bf16[16,112,128]{2,1,0:T(8,128)(2,1)S(1)} %bitcast.42), channel_id=1, replica_groups=mesh['grp'=2,'row'=8,'col'=2] {'row','col'}, dimensions={0} | all-to-all | bytes 917504 | tf_op jit(solution)/shard_map/all_to_all | solution.py:432
  421.0 20.9 %all_gather.3 = bf16[1792,128]{1,0:T(8,128)(2,1)S(1)} all-gather(bf16[112,128]{1,0:T(8,128)(2,1)S(1)} %multiply_convert_fusion), channel_id=1, replica_groups=mesh['grp'=2,'row'=8,'col'=2] {'row','col'}, dimensions={0}, use_global_device_ids=true | all-gather | bytes 487424 | tf_op jit(solution)/shard_map/all_gather | solution.py:548
  444.0 1.1 copy.26
  (48 shorter events, 5.7 us)
Async XLA Ops:
  1.9 0.7 copy-start.11
  2.6 0.7 copy-start.13
  3.3 0.7 copy-start.15
  4.0 1.2 copy-start.17
  5.2 0.7 copy-start.18
  5.9 0.7 copy-start.19
  15.2 54.7 %copy-start.4 = (bf16[16,128,256]{2,1,0:T(8,128)(2,1)}, bf16[16,128,256]{2,1,0:T(8,128)(2,1)S(1)}, u32[]{:S(2)}) copy-start(bf16[16,128,256]{2,1,0:T(8,128)(2,1)S(1)} %get-tuple-element.29.up_ref) | copy-start | bytes 3145732
  15.2 54.7 %copy-start.5 = (bf16[16,128,256]{2,1,0:T(8,128)(2,1)}, bf16[16,128,256]{2,1,0:T(8,128)(2,1)S(1)}, u32[]{:S(2)}) copy-start(bf16[16,128,256]{2,1,0:T(8,128)(2,1)S(1)} %get-tuple-element.25.z_ref) | copy-start | bytes 3145732
  69.9 2.3 copy-start
  69.9 30.3 %copy-start.9 = (f32[2,128]{1,0:T(2,128)S(1)}, f32[2,128]{1,0:T(2,128)}, u32[]{:S(2)}) copy-start(f32[2,128]{1,0:T(2,128)} %hgain_ref.5) | copy-start | bytes 3076
  69.9 30.3 %copy-start.10 = (f32[2,128]{1,0:T(2,128)S(1)}, f32[2,128]{1,0:T(2,128)}, u32[]{:S(2)}) copy-start(f32[2,128]{1,0:T(2,128)} %hbias_ref.5) | copy-start | bytes 3076
  69.9 30.3 %copy-start.12 = (f32[2,128]{1,0:T(2,128)S(1)}, f32[2,128]{1,0:T(2,128)}, u32[]{:S(2)}) copy-start(f32[2,128]{1,0:T(2,128)} %gain_ref.7) | copy-start | bytes 3076
  69.9 30.3 %copy-start.14 = (f32[2,128]{1,0:T(2,128)S(1)}, f32[2,128]{1,0:T(2,128)}, u32[]{:S(2)}) copy-start(f32[2,128]{1,0:T(2,128)} %bias_ref.7) | copy-start | bytes 3076
  71.2 1.0 copy-start.3
  72.2 28.1 %all-to-all-start.1 = ((bf16[16,256,128]{2,1,0:T(8,128)(2,1)}), bf16[16,256,128]{2,1,0:T(8,128)(2,1)S(1)}, u32[]{:S(2)}, u32[]{:S(2)}) async-start(bf16[16,256,128]{2,1,0:T(8,128)(2,1)} %copy-done.3), calls=%async_computation.1 | async-start | bytes 2097152 | tf_op jit(solution)/shard_map/all_to_all | solution.py:432
  100.2 11.6 %copy-start.2 = (bf16[16,256,128]{2,1,0:T(8,128)(2,1)}, bf16[16,256,128]{2,1,0:T(8,128)(2,1)S(1)}, u32[]{:S(2)}) copy-start(bf16[16,256,128]{2,1,0:T(8,128)(2,1)S(1)} %all-to-all-done.1.prod_ref) | copy-start | bytes 3145732
  100.2 1.6 copy-start.6
  101.9 0.7 copy-start.16
  166.0 2.3 copy-start.1
  168.3 28.1 %all-to-all-start.3 = ((bf16[16,256,128]{2,1,0:T(8,128)(2,1)}), bf16[16,256,128]{2,1,0:T(8,128)(2,1)S(1)}, u32[]{:S(2)}, u32[]{:S(2)}) async-start(bf16[16,256,128]{2,1,0:T(8,128)(2,1)} %shard_map.157), calls=%async_computation.3 | async-start | bytes 2097152 | tf_op jit(solution)/shard_map/all_to_all | solution.py:432
  196.4 0.8 copy-start.8
  240.4 5.2 %copy-start.20 = (bf16[2,128,640]{2,1,0:T(8,128)(2,1)S(1)}, bf16[2,128,640]{2,1,0:T(8,128)(2,1)}, u32[]{:S(2)}) copy-start(bf16[2,128,640]{2,1,0:T(8,128)(2,1)} %param.15) | copy-start | bytes 983044
  240.4 46.3 %all-to-all-start.5 = ((bf16[16,2,256,128]{3,2,1,0:T(8,128)(2,1)}), bf16[16,2,256,128]{3,2,1,0:T(8,128)(2,1)}, u32[]{:S(2)}, u32[]{:S(2)}) async-start(bf16[16,2,256,128]{3,2,1,0:T(8,128)(2,1)} %shard_map.159), calls=%async_computation.5 | async-start | bytes 4194304 | tf_op jit(solution)/shard_map/all_to_all | solution.py:432
  340.5 52.4 %copy-start.7 = (bf16[16,128,256]{2,1,0:T(8,128)(2,1)S(1)}, bf16[16,128,256]{2,1,0:T(8,128)(2,1)}, u32[]{:S(2)}) copy-start(bf16[16,128,256]{2,1,0:T(8,128)(2,1)} %copy-done.5) | copy-start | bytes 3145732

commit v2 on v1

v2 whole, which is shorter than its diff:
```python
import functools

import jax
import jax.numpy as jnp
from jax import lax
from jax.experimental import pallas as pl
from jax.experimental.pallas import tpu as pltpu
from jax.sharding import PartitionSpec as P

EPSILON = 1e-05
AXES = ("row", "col")
F32 = jnp.float32
BF16 = jnp.bfloat16
VMEM_BYTES = 50 * 1024 * 1024


def dot(a, b, ca, cb):
    return lax.dot_general(a, b, (((ca,), (cb,)), ((), ())), preferred_element_type=F32)


def sigmoid(x):
    return 0.5 * jnp.tanh(0.5 * x) + 0.5


def columns(vectors, width):
    c = vectors.shape[1]
    square = jnp.broadcast_to(vectors, (c, c)).T
    return jnp.concatenate([square] * (width // c), 1)


def norm(x):
    centred = x - jnp.mean(x, 0, keepdims=True)
    inv = lax.rsqrt(jnp.mean(centred * centred, 0, keepdims=True) + EPSILON)
    return centred * inv, inv


def norm_grad(grad_scaled, normed, inv, gain):
    g = grad_scaled * gain
    first = jnp.mean(g, 0, keepdims=True)
    second = jnp.mean(g * normed, 0, keepdims=True)
    return (g - first - normed * second) * inv


def unpack(block, cpd):
    devices, rows, cols = block.shape
    values = block.astype(F32)
    parts = []
    for a in range(rows // cpd):
        if cpd % 8 == 0:
            parts.append(values[:, a * cpd : (a + 1) * cpd, :].reshape(devices * cpd, cols))
        else:
            parts.append(
                jnp.concatenate([values[d, a * cpd : (a + 1) * cpd, :] for d in range(devices)], 0)
            )
    return jnp.concatenate(parts, 1)


def pack(tile, cpd, cols):
    channels, lanes = tile.shape
    devices = channels // cpd
    parts = [tile[:, a * cols : (a + 1) * cols] for a in range(lanes // cols)]
    if cpd % 8 == 0:
        return jnp.concatenate([p.reshape(devices, cpd, cols) for p in parts], 1).astype(BF16)
    return jnp.stack(
        [
            jnp.concatenate([p[d * cpd : (d + 1) * cpd, :] for p in parts], 0)
            for d in range(devices)
        ]
    ).astype(BF16)


def fold(tile, width):
    return sum(tile[:, a : a + width] for a in range(0, tile.shape[1], width))


def project(cells, wt_ref, gain, bias, first, last):
    normed, _ = norm(cells)
    lowered = (normed * gain + bias).astype(BF16)
    hidden = wt_ref.shape[0] // 5
    projected = dot(wt_ref[first * hidden : last * hidden, :], lowered, 1, 0)
    return [projected[n * hidden : (n + 1) * hidden] for n in range(last - first)]


def emit_edges(edges_ref, here, cells, wt_ref, gain, bias, mask, cpd, cols):
    part = project(cells, wt_ref, gain, bias, 0, 4)
    edges_ref[:, 0, here, :] = pack(part[0] * sigmoid(part[1]) * mask, cpd, cols)
    edges_ref[:, 1, here, :] = pack(part[2] * sigmoid(part[3]) * mask, cpd, cols)


def first_step(fill):
    pl.when(pl.program_id(0) == 0)(fill)


def last_step(fill):
    pl.when(pl.program_id(0) == pl.num_programs(0) - 1)(fill)


def load_columns(vec, *rows):
    @first_step
    def _():
        for n, (ref, layer) in enumerate(rows):
            vec[n] = columns(ref[layer : layer + 1, :], vec.shape[2])


def clear(*accs):
    @first_step
    def _():
        for acc in accs:
            acc[...] = jnp.zeros_like(acc)


def turned(ref, t, q):
    return jnp.concatenate([ref[t * q + a].astype(F32).T for a in range(q)], 1)


def row_flags(row, mask_smem, chain_smem, start_smem, maskc_ref, chainc_ref):
    whole = start_smem[0] + row
    here = pl.ds(start_smem[1], 1)
    mask = (maskc_ref[here, :] * mask_smem[whole]).astype(F32)
    return mask, (chainc_ref[here, :] == chain_smem[whole]).astype(F32)


def edge_first_kernel(
    cpd, q, mask_smem, chain_smem, start_smem, pair_ref, maskc_ref, chainc_ref, wt_ref, gain_ref, bias_ref,
    edges_ref, vec,
):
    rows, cols, _ = pair_ref.shape
    load_columns(vec, (gain_ref, 0), (bias_ref, 0))
    for t in range(rows // q):
        first = pl.program_id(0) * rows + t * q
        mask = jnp.concatenate(
            [
                row_flags(first + a, mask_smem, chain_smem, start_smem, maskc_ref, chainc_ref)[0]
                for a in range(q)
            ],
            1,
        )
        here = slice(t * q * cpd, (t + 1) * q * cpd)
        emit_edges(edges_ref, here, turned(pair_ref, t, q), wt_ref, vec[0], vec[1], mask, cpd, cols)


def keep_factors(fac_ref, gate_ref, t, cells, wt_ref, gain, bias, chain, mask, same):
    hidden = wt_ref.shape[0] // 5
    part = project(cells, wt_ref, gain, bias, 0, 5)
    for n in (0, 2):
        sig = sigmoid(part[n + 1]) * mask
        fac_ref[t, n * hidden : (n + 1) * hidden, :] = sig.astype(BF16)
        fac_ref[t, (n + 1) * hidden : (n + 2) * hidden, :] = (
            part[n] * sig * (1.0 - sig)
        ).astype(BF16)
    gate_ref[t] = sigmoid(part[4] + same * chain)


def first_keep_kernel(
    q, mask_smem, chain_smem, start_smem, pair_ref, cot_ref, maskc_ref, chainc_ref, wt_ref, gain_ref,
    bias_ref, chain_ref, z_ref, up_ref, gate_ref, flags_ref, fac_ref, vec,
):
    load_columns(vec, (gain_ref, 0), (bias_ref, 0), (chain_ref, 0))
    tiles = z_ref.shape[0]
    for t in range(tiles):
        flags = [
            row_flags(
                (pl.program_id(0) * tiles + t) * q + a, mask_smem, chain_smem, start_smem, maskc_ref, chainc_ref
            )
            for a in range(q)
        ]
        mask = jnp.concatenate([f[0] for f in flags], 1)
        same = jnp.concatenate([f[1] for f in flags], 1)
        cells = turned(pair_ref, t, q)
        z_ref[t] = cells.astype(BF16)
        up_ref[t] = turned(cot_ref, t, q).astype(BF16)
        flags_ref[t] = jnp.concatenate([mask, same], 0)
        keep_factors(fac_ref, gate_ref, t, cells, wt_ref, vec[0], vec[1], vec[2], mask, same)


def keep_kernel(layer, z_ref, flags_ref, wt_ref, gain_ref, bias_ref, chain_ref, gate_ref, fac_ref, vec):
    load_columns(vec, (gain_ref, layer), (bias_ref, layer), (chain_ref, layer))
    for t in range(z_ref.shape[0]):
        keep_factors(
            fac_ref, gate_ref, t, z_ref[t], wt_ref, vec[0], vec[1], vec[2],
            flags_ref[t, 0:1, :], flags_ref[t, 1:2, :],
        )


def mix_edge_kernel(
    cpd, q, layer, prod_ref, z_ref, gate_ref, flags_ref, owt_ref, hgain_ref, hbias_ref, wt_ref,
    gain_ref, bias_ref, edges_ref, znext_ref, vec,
):
    tiles, _, lanes = z_ref.shape
    rows = q * cpd
    load_columns(vec, (hgain_ref, layer), (hbias_ref, layer), (gain_ref, layer + 1), (bias_ref, layer + 1))
    for t in range(tiles):
        here = slice(t * rows, (t + 1) * rows)
        hnormed, _ = norm(unpack(prod_ref[:, here, :], cpd))
        hscaled = (hnormed * vec[0] + vec[1]).astype(BF16)
        cells = z_ref[t].astype(F32) + gate_ref[t] * dot(owt_ref[...], hscaled, 1, 0)
        znext_ref[t] = cells
        emit_edges(
            edges_ref, here, cells, wt_ref, vec[2], vec[3], flags_ref[t, 0:1, :], cpd, lanes // q
        )


def mix_grad(upstream, product, gate, ow_ref, hgain):
    hnormed, hinv = norm(product)
    grad_hscaled = dot(ow_ref[...], (upstream * gate).astype(BF16), 1, 0)
    return norm_grad(grad_hscaled, hnormed, hinv, hgain)


def mix_back_kernel(cpd, q, layer, prod_ref, up_ref, gate_ref, ow_ref, hgain_ref, gp_ref, vec):
    tiles, _, lanes = up_ref.shape
    rows = q * cpd
    load_columns(vec, (hgain_ref, layer))
    for t in range(tiles):
        here = slice(t * rows, (t + 1) * rows)
        grad = mix_grad(
            up_ref[t].astype(F32), unpack(prod_ref[:, here, :], cpd), gate_ref[t], ow_ref, vec[0]
        )
        gp_ref[:, here, :] = pack(grad, cpd, lanes // q)


def mix_terms(upstream, product, gate, same, ow_ref, owt_ref, hgain, hbias, acc_ow, acc_hg, acc_hb, acc_ch):
    width = acc_hg.shape[1]
    hnormed, _ = norm(product)
    hscaled = (hnormed * hgain + hbias).astype(BF16)
    mixed = dot(owt_ref[...], hscaled, 1, 0)
    grad_gate = upstream * gate
    grad_logits = grad_gate * mixed * (1.0 - gate)
    grad_mixed = grad_gate.astype(BF16)
    acc_ow[...] += dot(hscaled, grad_mixed, 1, 1)
    grad_hscaled = dot(ow_ref[...], grad_mixed, 1, 0)
    acc_hg[...] += fold(grad_hscaled * hnormed, width)
    acc_hb[...] += fold(grad_hscaled, width)
    acc_ch[...] += fold(grad_logits * same, width)
    return grad_logits


def row_of(acc):
    return jnp.sum(acc.T, 0, keepdims=True)


def mix_terms_kernel(
    cpd, q, layer, prod_ref, up_ref, gate_ref, flags_ref, ow_ref, owt_ref, hgain_ref, hbias_ref,
    glog_ref, terms_ref, vec, acc_ow, acc_hg, acc_hb, acc_ch,
):
    rows = q * cpd
    load_columns(vec, (hgain_ref, layer), (hbias_ref, layer))
    clear(acc_ow, acc_hg, acc_hb, acc_ch)
    for t in range(up_ref.shape[0]):
        grad_logits = mix_terms(
            up_ref[t].astype(F32), unpack(prod_ref[:, t * rows : (t + 1) * rows, :], cpd),
            gate_ref[t], flags_ref[t, 1:2, :], ow_ref, owt_ref, vec[0], vec[1],
            acc_ow, acc_hg, acc_hb, acc_ch,
        )
        glog_ref[t] = grad_logits.astype(BF16)

    @last_step
    def _():
        hidden = acc_ow.shape[0]
        terms_ref[:hidden, :] = acc_ow[...]
        vectors = [row_of(acc_hg[...]), row_of(acc_hb[...]), row_of(acc_ch[...])]
        vectors.append(jnp.zeros((terms_ref.shape[0] - hidden - 3, hidden), F32))
        terms_ref[hidden:, :] = jnp.concatenate(vectors, 0)


def project_grad(grads, fac_ref, t, gproj_ref):
    hidden = fac_ref.shape[1] // 4
    for n in range(4):
        block = slice(n * hidden, (n + 1) * hidden)
        gproj_ref[t, block, :] = (grads[n // 2] * fac_ref[t, block, :].astype(F32)).astype(BF16)


def input_grad(cells, gproj_ref, glog_ref, t, w_ref, gain):
    hidden = gproj_ref.shape[1] // 4
    normed, inv = norm(cells)
    grad_scaled = dot(w_ref[:, : 4 * hidden], gproj_ref[t], 1, 0) + dot(
        w_ref[:, 4 * hidden :], glog_ref[t], 1, 0
    )
    return norm_grad(grad_scaled, normed, inv, gain)


def edge_mix_back_kernel(
    cpd, q, layer, left_ref, right_ref, fac_ref, z_ref, glog_ref, up_ref, w_ref, gain_ref,
    prod_ref, gate_ref, ow_ref, hgain_ref, upnext_ref, gp_ref, gproj_ref, vec,
):
    tiles, _, lanes = z_ref.shape
    rows = q * cpd
    load_columns(vec, (gain_ref, layer), (hgain_ref, layer - 1))
    for t in range(tiles):
        here = slice(t * rows, (t + 1) * rows)
        grads = (unpack(left_ref[:, here, :], cpd), unpack(right_ref[:, here, :], cpd))
        project_grad(grads, fac_ref, t, gproj_ref)
        upstream = up_ref[t].astype(F32) + input_grad(z_ref[t], gproj_ref, glog_ref, t, w_ref, vec[0])
        upnext_ref[t] = upstream
        grad = mix_grad(upstream, unpack(prod_ref[:, here, :], cpd), gate_ref[t], ow_ref, vec[1])
        gp_ref[:, here, :] = pack(grad, cpd, lanes // q)


def edge_terms(cells, gproj_ref, glog_ref, t, gain, bias, acc_w):
    hidden = gproj_ref.shape[1] // 4
    normed, _ = norm(cells)
    lowered = (normed * gain + bias).astype(BF16)
    ones = jnp.ones((16, cells.shape[1]), BF16)
    sides = jnp.concatenate([lowered, normed.astype(BF16), ones], 0)
    acc_w[:, : 4 * hidden] += dot(sides, gproj_ref[t], 1, 1)
    acc_w[:, 4 * hidden :] += dot(sides, glog_ref[t], 1, 1)


def finish_edge(out_ref, acc_w, w_ref):
    width = w_ref.shape[0]
    for n in range(acc_w.shape[1] // width):
        out_ref[n * width : (n + 1) * width, :] = acc_w[:width, n * width : (n + 1) * width].astype(BF16)
    weight = w_ref[...].astype(F32)
    gain = row_of(fold(weight * acc_w[width : 2 * width, :], width))
    bias = row_of(fold(weight * acc_w[2 * width : 2 * width + 1, :], width))
    return [gain, bias]


def finish_rows(out_ref, first, vectors):
    pad = jnp.zeros((out_ref.shape[0] - first - sum(v.shape[0] for v in vectors), out_ref.shape[1]), F32)
    out_ref[first:, :] = jnp.concatenate(vectors + [pad], 0).astype(BF16)


def late_terms_kernel(
    cpd, q, layer, z_ref, gproj_ref, glog_ref, w_ref, gain_ref, bias_ref, terms_ref,
    prod_ref, up_ref, gate_ref, flags_ref, ow_ref, owt_ref, hgain_ref, hbias_ref,
    glognext_ref, all_ref, vec, acc_w, acc_ow, acc_hg, acc_hb, acc_ch,
):
    rows = q * cpd
    load_columns(vec, (gain_ref, layer), (bias_ref, layer), (hgain_ref, layer - 1), (hbias_ref, layer - 1))
    clear(acc_w, acc_ow, acc_hg, acc_hb, acc_ch)
    for t in range(z_ref.shape[0]):
        edge_terms(z_ref[t], gproj_ref, glog_ref, t, vec[0], vec[1], acc_w)
        grad_logits = mix_terms(
            up_ref[t], unpack(prod_ref[:, t * rows : (t + 1) * rows, :], cpd), gate_ref[t],
            flags_ref[t, 1:2, :], ow_ref, owt_ref, vec[2], vec[3], acc_ow, acc_hg, acc_hb, acc_ch,
        )
        glognext_ref[t] = grad_logits.astype(BF16)

    @last_step
    def _():
        hidden = acc_ow.shape[0]
        vectors = finish_edge(all_ref, acc_w, w_ref)
        all_ref[5 * hidden : 6 * hidden, :] = terms_ref[:hidden, :].astype(BF16)
        all_ref[6 * hidden : 7 * hidden, :] = acc_ow[...].astype(BF16)
        vectors += [terms_ref[hidden : hidden + 3, :]]
        vectors += [row_of(acc_hg[...]), row_of(acc_hb[...]), row_of(acc_ch[...])]
        finish_rows(all_ref, 7 * hidden, vectors)


def last_terms_kernel(
    cpd, q, layer, left_ref, right_ref, fac_ref, z_ref, glog_ref, w_ref, gain_ref, bias_ref,
    gproj_ref, all_ref, vec, acc_w,
):
    rows = q * cpd
    load_columns(vec, (gain_ref, layer), (bias_ref, layer))
    clear(acc_w)
    for t in range(z_ref.shape[0]):
        here = slice(t * rows, (t + 1) * rows)
        grads = (unpack(left_ref[:, here, :], cpd), unpack(right_ref[:, here, :], cpd))
        project_grad(grads, fac_ref, t, gproj_ref)
        edge_terms(z_ref[t].astype(F32), gproj_ref, glog_ref, t, vec[0], vec[1], acc_w)

    @last_step
    def _():
        finish_rows(all_ref, acc_w.shape[1], finish_edge(all_ref, acc_w, w_ref))


def pair_grad_kernel(q, layer, gproj_ref, glog_ref, z_ref, up_ref, w_ref, gain_ref, pair_ref, vec):
    tiles, _, lanes = z_ref.shape
    cols = lanes // q
    load_columns(vec, (gain_ref, layer))
    for t in range(tiles):
        upstream = up_ref[t] + input_grad(z_ref[t].astype(F32), gproj_ref, glog_ref, t, w_ref, vec[0])
        for a in range(q):
            pair_ref[t * q + a] = upstream[:, a * cols : (a + 1) * cols].T.astype(BF16)


def spread_kernel(factor, early_ref, late_ref, out_ref):
    early = (jnp.sum(early_ref[...].astype(F32), 0) * factor).astype(BF16)
    late = (jnp.sum(late_ref[...].astype(F32), 0) * factor).astype(BF16)
    out_ref[...] = jnp.broadcast_to(jnp.concatenate([early, late], 0)[None], out_ref.shape)


def unpack_kernel(early_rows, got_ref, proj_ref, ow_ref, inorm_ref, hnorm_ref, chain_ref):
    width = ow_ref.shape[1]
    early = got_ref[:, :early_rows, :].astype(F32).reshape(-1, width)
    late = got_ref[:, early_rows:, :].astype(F32).reshape(-1, width)
    for n in range(5):
        rows, lanes = slice(n * width, (n + 1) * width), slice(n * width, (n + 1) * width)
        proj_ref[0, :, lanes] = late[rows]
        proj_ref[1, :, lanes] = early[rows]
    ow_ref[1] = early[5 * width : 6 * width]
    ow_ref[0] = early[6 * width : 7 * width]
    inorm_ref[0] = late[5 * width : 5 * width + 2]
    vectors = early[7 * width : 7 * width + 8]
    inorm_ref[1] = vectors[0:2]
    hnorm_ref[1] = vectors[2:4]
    hnorm_ref[0] = vectors[5:7]
    chain_ref[...] = jnp.concatenate([vectors[7:8], vectors[4:5]], 0)


def cell_call(kernel, steps, ins, outs, scratch, prefetch=(), flops=0):
    def spec(shape, how):
        if how is None:
            return pl.BlockSpec(shape, lambda *s: (0,) * len(shape))
        axis, first, size = how if isinstance(how, tuple) else (how, 0, shape[how] // steps)
        block = tuple(size if n == axis else length for n, length in enumerate(shape))
        return pl.BlockSpec(
            block, lambda *s: tuple(s[0] + first if n == axis else 0 for n in range(len(shape)))
        )

    moved = sum(a.size * a.dtype.itemsize for a, _ in ins)
    moved += sum(functools.reduce(lambda x, y: x * y, s, 1) * jnp.dtype(t).itemsize for (s, t), _ in outs)
    return pl.pallas_call(
        kernel,
        grid_spec=pltpu.PrefetchScalarGridSpec(
            num_scalar_prefetch=len(prefetch),
            grid=(steps,),
            in_specs=[spec(a.shape, how) for a, how in ins],
            out_specs=[spec(s, how) for (s, _), how in outs],
            scratch_shapes=scratch,
        ),
        out_shape=[jax.ShapeDtypeStruct(s, t) for (s, t), _ in outs],
        compiler_params=pltpu.CompilerParams(vmem_limit_bytes=VMEM_BYTES),
        cost_estimate=pl.CostEstimate(flops=flops, bytes_accessed=int(moved), transcendentals=0),
    )(*prefetch, *[a for a, _ in ins])


def widen(src_ref, dst):
    devices, cols = src_ref.shape[0], src_ref.shape[-1]
    per = dst.shape[0] // devices
    for d in range(devices):
        dst[d * per : (d + 1) * per, :] = src_ref[d].astype(F32).reshape(per, cols)


def narrow(src, dst_ref):
    devices = dst_ref.shape[0]
    per = src.shape[0] // devices
    for d in range(devices):
        dst_ref[d, :per, :] = src[d * per : (d + 1) * per, :].astype(BF16)


def get_channel(src, ch, sub, subs, dims):
    row_devs, col_devs, rows, cpd, cols = dims
    halves = []
    for s in range(col_devs):
        parts = []
        for r in range(row_devs):
            base = ((r * col_devs + s) * subs + sub) * rows * cpd
            parts.append(src[pl.ds(base + ch, rows, stride=cpd), :])
        halves.append(jnp.concatenate(parts, 0))
    return jnp.concatenate(halves, 1).astype(BF16)


def put_channel(dst, value, ch, sub, subs, dims):
    row_devs, col_devs, rows, cpd, cols = dims
    for s in range(col_devs):
        for r in range(row_devs):
            base = ((r * col_devs + s) * subs + sub) * rows * cpd
            dst[pl.ds(base + ch, rows, stride=cpd), :] = value[
                r * rows : (r + 1) * rows, s * cols : (s + 1) * cols
            ]


def product_kernel(dims, outgoing, edges_ref, out_ref, edges, result):
    widen(edges_ref, edges)
    for ch in range(dims[3]):
        left = get_channel(edges, ch, 0, 2, dims)
        right = get_channel(edges, ch, 1, 2, dims)
        value = dot(left, right, 1, 1) if outgoing else dot(left, right, 0, 0)
        put_channel(result, value, ch, 0, 1, dims)
    narrow(result, out_ref)


def assemble_kernel(dims, edges_ref, out_ref, edges):
    widen(edges_ref, edges)
    for ch in range(dims[3]):
        for sub in range(2):
            out_ref[ch, sub] = get_channel(edges, ch, sub, 2, dims)


def product_grad_kernel(dims, outgoing, sides_ref, grad_ref, *rest):
    out_ref, grad, result = rest[-3:]
    widen(grad_ref, grad)
    for ch in range(dims[3]):
        left, right = sides_ref[ch, 0], sides_ref[ch, 1]
        gp = get_channel(grad, ch, 0, 1, dims)
        if outgoing:
            grad_left = dot(gp, right, 1, 0)
            grad_right = dot(gp, left, 0, 0)
        else:
            grad_left = dot(right, gp, 1, 1)
            grad_right = dot(left, gp, 1, 0)
        put_channel(result, grad_left, ch, 0, 2, dims)
        put_channel(result, grad_right, ch, 1, 2, dims)
    narrow(result, out_ref)
    for terms_ref in rest[:-3]:
        out_ref[:, out_ref.shape[1] - terms_ref.shape[1] :, :] = terms_ref[...]


def whole_call(kernel, ins, outs, scratch, flops):
    moved = sum(a.size * a.dtype.itemsize for a in ins)
    moved += sum(functools.reduce(lambda x, y: x * y, s, 1) * jnp.dtype(t).itemsize for s, t in outs)
    specs = [pl.BlockSpec(memory_space=pltpu.VMEM)] * len(outs)
    shapes = [jax.ShapeDtypeStruct(s, t) for s, t in outs]
    return pl.pallas_call(
        kernel,
        in_specs=[pl.BlockSpec(memory_space=pltpu.VMEM)] * len(ins),
        out_specs=specs if len(outs) > 1 else specs[0],
        out_shape=shapes if len(outs) > 1 else shapes[0],
        scratch_shapes=scratch,
        compiler_params=pltpu.CompilerParams(vmem_limit_bytes=VMEM_BYTES),
        cost_estimate=pl.CostEstimate(flops=flops, bytes_accessed=int(moved), transcendentals=0),
    )(*ins)


def exchange(array):
    return lax.all_to_all(array, AXES, split_axis=0, concat_axis=0, tiled=True)


def after(array, *others):
    return lax.optimization_barrier((array, *others))[0]


def shards(
    pair_rep, cotangent, residue_mask, chain_ids, proj_weight, out_weight,
    input_gain, input_bias, hidden_gain, hidden_bias, chain_bias,
):
    rows, cols, width = pair_rep.shape
    hidden = out_weight.shape[1]
    row_devs, col_devs = lax.axis_size("row"), lax.axis_size("col")
    devices = row_devs * col_devs
    length = rows * row_devs
    cpd = hidden // devices
    q = max(1, 16 // cpd)
    tiles = rows // q
    lanes = q * cols
    steps = max(1, tiles // 4)
    dims = (row_devs, col_devs, rows, cpd, cols)
    side = rows * cpd

    starts = jnp.stack([lax.axis_index("row") * rows, lax.axis_index("col")]).astype(jnp.int32)
    wt = [proj_weight[n].T for n in range(2)]
    owt = [out_weight[n].T for n in range(2)]
    weight = [proj_weight[n] for n in range(2)]
    mixer = [out_weight[n] for n in range(2)]
    mask_cols, chain_cols = residue_mask.reshape(col_devs, cols), chain_ids.reshape(col_devs, cols)
    scalars = (residue_mask, chain_ids, starts)
    tile = (tiles, width, lanes)
    fac_tile = (tiles, 4 * hidden, lanes)
    edge_shape = (devices, 2, side, cols)
    cell_shape = (devices, side, cols)
    vec = lambda n: pltpu.VMEM((n, width, lanes), F32)
    acc = lambda n, m=width: pltpu.VMEM((m, n), F32)
    wide = lambda n: pltpu.VMEM((n * devices * side, cols), F32)
    cell_flops = 2 * rows * cols * width * hidden
    tri_flops = 2 * cpd * length**3
    rows_for = lambda n: -(-n // (devices * 16)) * 16
    early_rows, late_rows = rows_for(7 * hidden + 8), rows_for(5 * hidden + 2)
    terms_shape = (hidden + 8, hidden)

    def product(edges, outgoing):
        return whole_call(
            functools.partial(product_kernel, dims, outgoing), [edges], [(cell_shape, BF16)],
            [wide(2), wide(1)], tri_flops,
        )

    def assemble(edges):
        return whole_call(
            functools.partial(assemble_kernel, dims), [edges], [((cpd, 2, length, length), BF16)], [wide(2)], 0
        )

    def product_grad(sides, grad, outgoing, *terms):
        out_rows = 2 * side + sum(t.shape[1] for t in terms)
        return whole_call(
            functools.partial(product_grad_kernel, dims, outgoing), [sides, grad, *terms],
            [((devices, out_rows, cols), BF16)], [wide(1), wide(2)], 2 * tri_flops,
        )

    def halves(grads):
        per = side // steps
        return [(grads, (1, 0, per)), (grads, (1, steps, per))]

    (edges0,) = cell_call(
        functools.partial(edge_first_kernel, cpd, q), steps,
        [
            (pair_rep, 0), (mask_cols, None), (chain_cols, None), (wt[0], None), (input_gain, None),
            (input_bias, None),
        ],
        [((edge_shape, BF16), 2)], [vec(2)], prefetch=scalars, flops=4 * cell_flops,
    )
    got0 = exchange(edges0)
    z0, up, gate0, flags, fac0 = cell_call(
        functools.partial(first_keep_kernel, q), steps,
        [
            (after(pair_rep, edges0), 0), (cotangent, 0), (mask_cols, None), (chain_cols, None), (wt[0], None),
            (input_gain, None), (input_bias, None), (chain_bias, None),
        ],
        [
            ((tile, BF16), 0), ((tile, BF16), 0), ((tile, F32), 0), (((tiles, 2, lanes), F32), 0),
            ((fac_tile, BF16), 0),
        ],
        [vec(3)], prefetch=scalars, flops=5 * cell_flops,
    )
    made0 = product(got0, True)
    prod0 = exchange(made0)
    sides0 = assemble(after(got0, made0))
    edges1, z1 = cell_call(
        functools.partial(mix_edge_kernel, cpd, q, 0), steps,
        [
            (prod0, 1), (z0, 0), (gate0, 0), (flags, 0), (owt[0], None), (hidden_gain, None),
            (hidden_bias, None), (wt[1], None), (input_gain, None), (input_bias, None),
        ],
        [((edge_shape, BF16), 2), ((tile, F32), 0)], [vec(4)], flops=5 * cell_flops,
    )
    got1 = exchange(edges1)
    gate1, fac1 = cell_call(
        functools.partial(keep_kernel, 1), steps,
        [
            (z1, 0), (flags, 0), (wt[1], None), (input_gain, None), (input_bias, None), (chain_bias, None),
        ],
        [((tile, F32), 0), ((fac_tile, BF16), 0)], [vec(3)], flops=5 * cell_flops,
    )
    made1 = product(got1, False)
    prod1 = exchange(made1)
    sides1 = assemble(after(got1, made1))

    (grad1,) = cell_call(
        functools.partial(mix_back_kernel, cpd, q, 1), steps,
        [(prod1, 1), (up, 0), (gate1, 0), (mixer[1], None), (hidden_gain, None)],
        [((cell_shape, BF16), 1)], [vec(1)], flops=cell_flops,
    )
    got_grad1 = exchange(grad1)
    glog1, terms1 = cell_call(
        functools.partial(mix_terms_kernel, cpd, q, 1), steps,
        [
            (after(prod1, grad1), 1), (up, 0), (gate1, 0), (flags, 0), (mixer[1], None), (owt[1], None),
            (hidden_gain, None), (hidden_bias, None),
        ],
        [((tile, BF16), 0), ((terms_shape, F32), None)],
        [vec(2), acc(hidden), acc(cols), acc(cols), acc(cols)], flops=3 * cell_flops,
    )
    grads1 = exchange(product_grad(sides1, got_grad1, False))
    up0, grad0, gproj1 = cell_call(
        functools.partial(edge_mix_back_kernel, cpd, q, 1), steps,
        halves(grads1)
        + [
            (fac1, 0), (z1, 0), (glog1, 0), (up, 0), (weight[1], None), (input_gain, None),
            (prod0, 1), (gate0, 0), (mixer[0], None), (hidden_gain, None),
        ],
        [((tile, F32), 0), ((cell_shape, BF16), 1), ((fac_tile, BF16), 0)],
        [vec(2)], flops=6 * cell_flops,
    )
    got_grad0 = exchange(grad0)
    glog0, early = cell_call(
        functools.partial(late_terms_kernel, cpd, q, 1), steps,
        [
            (z1, 0), (after(gproj1, grad0), 0), (glog1, 0), (weight[1], None), (input_gain, None),
            (input_bias, None), (terms1, None), (prod0, 1), (up0, 0), (gate0, 0), (flags, 0),
            (mixer[0], None), (owt[0], None), (hidden_gain, None), (hidden_bias, None),
        ],
        [((tile, BF16), 0), (((devices * early_rows, hidden), BF16), None)],
        [vec(4), acc(5 * hidden, 2 * width + 16), acc(hidden), acc(cols), acc(cols), acc(cols)],
        flops=13 * cell_flops,
    )

    grads0 = exchange(
        product_grad(sides0, got_grad0, True, early.reshape(devices, early_rows, hidden))
    )
    gproj0, late = cell_call(
        functools.partial(last_terms_kernel, cpd, q, 0), steps,
        halves(grads0)
        + [
            (fac0, 0), (z0, 0), (glog0, 0), (weight[0], None), (input_gain, None), (input_bias, None),
        ],
        [((fac_tile, BF16), 0), (((devices * late_rows, hidden), BF16), None)],
        [vec(2), acc(5 * hidden, 2 * width + 16)], flops=10 * cell_flops,
    )
    late = exchange(late.reshape(devices, late_rows, hidden))
    (grad_pair,) = cell_call(
        functools.partial(pair_grad_kernel, q, 0), steps,
        [(gproj0, 0), (glog0, 0), (z0, 0), (up0, 0), (weight[0], None), (input_gain, None)],
        [((pair_rep.shape, BF16), 0)], [vec(1)], flops=5 * cell_flops,
    )
    (spread,) = cell_call(
        functools.partial(spread_kernel, 1.0 / length), 1,
        [(grads0, (1, 2 * side // early_rows, early_rows)), (late, None)],
        [(((devices, early_rows + late_rows, hidden), BF16), None)], [],
    )
    proj, out, inorm, hnorm, chain = whole_call(
        functools.partial(unpack_kernel, early_rows), [exchange(spread)],
        [
            ((2, width, 5 * hidden), F32), ((2, hidden, hidden), F32), ((2, 2, hidden), F32),
            ((2, 2, hidden), F32), ((2, hidden), F32),
        ],
        [], 0,
    )
    return grad_pair, proj, out, inorm, hnorm, chain


def solution(mesh):
    cells = P(("grp", "row"), "col", None)
    return jax.shard_map(
        shards,
        mesh=mesh,
        in_specs=(cells, cells, P("grp"), P("grp")) + (P(),) * 7,
        out_specs=(
            cells, P("grp", None, None), P("grp", None, None), P("grp", None, None),
            P("grp", None, None), P("grp", None),
        ),
        check_vma=False,
    )
```

time: 447 us -> 426 us (0.953)
  blocking collectives: 268 us -> 183 us
  starting transfers between devices: 15.4 us -> 39.3 us
  Pallas kernels: 61 us -> 80.5 us
  waiting for transfers between devices: 84.6 us -> 97.7 us
  local copies, waits for them, and re-layouts: 15.4 us -> 23.1 us
    all_to_all x6 -> x4, blocking collectives: 247 us -> 183 us  [exchange(): return lax.all_to_all(array, AXES, split_axis=0, concat_axis=0, tiled=True)]
    all_to_all x3 -> x6, starting transfers between devices: 15.4 us -> 39.3 us  [exchange(): return lax.all_to_all(array, AXES, split_axis=0, concat_axis=0, tiled=True)]
    all_gather x1 -> x0, blocking collectives: 20.9 us -> none  [shards(): lax.all_gather(mine, AXES, axis=0, tiled=True).reshape(2, -1, hidden)]
    pallas_call x5 -> x11, Pallas kernels: 48.1 us -> 62.2 us  [cell_call(): pl.pallas_call(kernel, grid_spec=pltpu.PrefetchScalarGridSpec(num_scalar_...]
    all_to_all x3 -> x6, waiting for transfers between devices: 84.6 us -> 97.7 us  [exchange(): return lax.all_to_all(array, AXES, split_axis=0, concat_axis=0, tiled=True)]
    unnamed x45 -> x88, local copies, waits for them, and re-layouts: 11.9 us -> 18.1 us
    pallas_call x4 -> x7, Pallas kernels: 12.9 us -> 18.3 us  [whole_call(): pl.pallas_call(kernel, in_specs=[pl.BlockSpec(memory_space=pltpu.VMEM)] *...]
  transfers between devices with their start and end apart: 3 -> 6, of which waited for: 3 -> 6; matrix products, arithmetic and copies ran while one was open for 1% -> 1% of each run, Pallas kernels for 0% -> 8%
where the time goes in v2:
time: 426 us; the launch traced here: 424 us
  blocking collectives  183 us (43%)
  waiting for transfers between devices  97.7 us (23%)
  Pallas kernels  80.5 us (19%)
  starting transfers between devices  39.3 us (9%)
  local copies, waits for them, and re-layouts  23.1 us (5%)
    all_to_all x4, blocking collectives, exchange(): return lax.all_to_all(array, AXES, split_axis=0, concat_axis=0, tiled=True)  183 us
    all_to_all x6, waiting for transfers between devices, exchange(): return lax.all_to_all(array, AXES, split_axis=0, concat_axis=0, tiled=True)  97.7 us
    pallas_call x11, Pallas kernels, cell_call(): pl.pallas_call(kernel, grid_spec=pltpu.PrefetchScalarGridSpec(num_scalar_...  62.2 us
    all_to_all x6, starting transfers between devices, exchange(): return lax.all_to_all(array, AXES, split_axis=0, concat_axis=0, tiled=True)  39.3 us
    pallas_call x7, Pallas kernels, whole_call(): pl.pallas_call(kernel, in_specs=[pl.BlockSpec(memory_space=pltpu.VMEM)] *...  18.3 us
    unnamed x88, local copies, waits for them, and re-layouts  18.1 us
  transfers between devices with their start and end apart: 6, of which 6 were waited for; matrix products, arithmetic and copies ran while one was open for 1% of the time, Pallas kernels for 8%

profile of v2, /device:TPU:0, one launch (start us, length us, event | category | flops | bytes accessed | tf_op | source)
XLA Modules:
  0.0 424.3 jit_solution(9005322364202905317)
XLA Ops:
  0.6 1.7 slice_bitcast_fusion.3
  6.5 3.6 shard_map.154
  10.2 54.5 %all_to_all.50.edges_ref = bf16[16,2,256,128]{3,2,1,0:T(8,128)(2,1)S(1)} all-to-all(bf16[16,2,256,128]{3,2,1,0:T(8,128)(2,1)S(1)} %shard_map.154), channel_id=1, replica_groups=mesh['grp'=2,'row'=8,'col'=2] {'row','col'}, dimensions={0} | all-to-all | bytes 4194304 | tf_op jit(solution)/shard_map/all_to_all | solution.py:518
  67.0 5.3 %all-to-all-start.1 = ((bf16[16,256,128]{2,1,0:T(8,128)(2,1)}), bf16[16,256,128]{2,1,0:T(8,128)(2,1)S(1)}, u32[]{:S(2)}, u32[]{:S(2)}) async-start(bf16[16,256,128]{2,1,0:T(8,128)(2,1)} %copy-done.11), calls=%async_computation.1 | async-start | bytes 2097152 | tf_op jit(solution)/shard_map/all_to_all | solution.py:518
  73.8 1.7 copy.20.wt_ref
  80.3 6.8 %shard_map.157 = (bf16[16,128,256]{2,1,0:T(8,128)(2,1)S(1)}, bf16[16,128,256]{2,1,0:T(8,128)(2,1)S(1)}, f32[16,128,256]{2,1,0:T(8,128)}, f32[16,2,256]{2,1,0:T(2,128)S(1)}, bf16[16,512,256]{2,1,0:T(8,128)(2,1)}) custom-call(s32[256]{0:T(256)S(1)} %copy-done.35, s32[256]{0:T(256)S(1)} %copy-done.37, s32[2]{0:T(128)S(1)} %copy-done.39, ...), custom_call_target="tpu_custom_call" | custom-call | flops 671088640 | bytes 10687488 | tf_op jit(solution)/shard_map/pallas_call | solution.py:414
  87.1 8.0 %all-to-all-done.1.prod_ref = bf16[16,256,128]{2,1,0:T(8,128)(2,1)S(1)} async-done(((bf16[16,256,128]{2,1,0:T(8,128)(2,1)}), bf16[16,256,128]{2,1,0:T(8,128)(2,1)S(1)}, u32[]{:S(2)}, u32[]{:S(2)}) %all-to-all-start.1) | async-done | bytes 1048608 | tf_op jit(solution)/shard_map/all_to_all | solution.py:518
  96.2 6.9 %shard_map.158 = (bf16[16,2,256,128]{3,2,1,0:T(8,128)(2,1)}, f32[16,128,256]{2,1,0:T(8,128)}) custom-call(bf16[16,256,128]{2,1,0:T(8,128)(2,1)S(1)} %all-to-all-done.1.prod_ref, bf16[16,128,256]{2,1,0:T(8,128)(2,1)S(1)} %get-tuple-element.36.z_ref, f32[16,128,256]{2,1,0:T(8,128)} %get-tuple-element.37.gate_ref, ...), custom_call_target="tpu_custom_call" | custom-call | flops 671088640 | bytes 8622080 | tf_op jit(solution)/shard_map/pallas_call | solution.py:414
  103.1 54.2 %all_to_all.51.edges_ref = bf16[16,2,256,128]{3,2,1,0:T(8,128)(2,1)S(1)} all-to-all(bf16[16,2,256,128]{3,2,1,0:T(8,128)(2,1)} %get-tuple-element.39), channel_id=1, replica_groups=mesh['grp'=2,'row'=8,'col'=2] {'row','col'}, dimensions={0} | all-to-all | bytes 4194304 | tf_op jit(solution)/shard_map/all_to_all | solution.py:518
  159.7 5.3 %all-to-all-start.3 = ((bf16[16,256,128]{2,1,0:T(8,128)(2,1)}), bf16[16,256,128]{2,1,0:T(8,128)(2,1)}, u32[]{:S(2)}, u32[]{:S(2)}) async-start(bf16[16,256,128]{2,1,0:T(8,128)(2,1)} %copy-done.12), calls=%async_computation.3 | async-start | bytes 2097152 | tf_op jit(solution)/shard_map/all_to_all | solution.py:518
  166.6 5.8 %shard_map.161 = (f32[16,128,256]{2,1,0:T(8,128)S(1)}, bf16[16,512,256]{2,1,0:T(8,128)(2,1)}) custom-call(f32[16,128,256]{2,1,0:T(8,128)} %get-tuple-element.42.z_ref, f32[16,2,256]{2,1,0:T(2,128)S(1)} %get-tuple-element.38.flags_ref, bf16[640,128]{1,0:T(8,128)(2,1)S(1)} %copy-done.20, f32[2,128]{1,0:T(2,128)S(1)} %copy-done.29, f32[2,128]{1,0:T(2,128)S(1)} %copy-done.32, ...), custom_call_target="tpu_custom_call" | custom-call | flops 671088640 | bytes 8588288 | tf_op jit(solution)/shard_map/pallas_call | solution.py:414
  173.7 14.3 %all-to-all-done.3.prod_ref = bf16[16,256,128]{2,1,0:T(8,128)(2,1)} async-done(((bf16[16,256,128]{2,1,0:T(8,128)(2,1)}), bf16[16,256,128]{2,1,0:T(8,128)(2,1)}, u32[]{:S(2)}, u32[]{:S(2)}) %all-to-all-start.3) | async-done | bytes 1048608 | tf_op jit(solution)/shard_map/all_to_all | solution.py:518
  188.0 4.6 %shard_map.162 = bf16[16,256,128]{2,1,0:T(8,128)(2,1)} custom-call(bf16[16,256,128]{2,1,0:T(8,128)(2,1)} %all-to-all-done.3.prod_ref, bf16[16,128,256]{2,1,0:T(8,128)(2,1)S(1)} %copy-done.8, f32[16,128,256]{2,1,0:T(8,128)} %copy-done.9, bf16[128,128]{1,0:T(8,128)(2,1)S(1)} %copy-done.23, f32[2,128]{1,0:T(2,128)S(1)} %copy-done.30), custom_call_target="tpu_custom_call" | custom-call | flops 134217728 | bytes 5276672 | tf_op jit(solution)/shard_map/pallas_call | solution.py:414
  192.6 6.9 %all-to-all-start.4 = ((bf16[16,256,128]{2,1,0:T(8,128)(2,1)}), bf16[16,256,128]{2,1,0:T(8,128)(2,1)S(1)}, u32[]{:S(2)}, u32[]{:S(2)}) async-start(bf16[16,256,128]{2,1,0:T(8,128)(2,1)} %shard_map.162), calls=%async_computation.4 | async-start | bytes 2097152 | tf_op jit(solution)/shard_map/all_to_all | solution.py:518
  199.5 2.9 shard_map.160.sides_ref
  203.8 18.6 %all-to-all-done.4.grad_ref = bf16[16,256,128]{2,1,0:T(8,128)(2,1)S(1)} async-done(((bf16[16,256,128]{2,1,0:T(8,128)(2,1)}), bf16[16,256,128]{2,1,0:T(8,128)(2,1)S(1)}, u32[]{:S(2)}, u32[]{:S(2)}) %all-to-all-start.4) | async-done | bytes 1048608 | tf_op jit(solution)/shard_map/all_to_all | solution.py:518
  222.4 4.6 %shard_map.163 = bf16[16,512,128]{2,1,0:T(8,128)(2,1)} custom-call(bf16[8,2,256,256]{3,2,1,0:T(8,128)(2,1)} %copy-done.10, bf16[16,256,128]{2,1,0:T(8,128)(2,1)S(1)} %all-to-all-done.4.grad_ref), custom_call_target="tpu_custom_call" | custom-call | flops 536870912 | bytes 5242880 | tf_op jit(solution)/shard_map/pallas_call | solution.py:506
  227.1 7.1 %all-to-all-start.5 = ((bf16[16,512,128]{2,1,0:T(8,128)(2,1)}), bf16[16,512,128]{2,1,0:T(8,128)(2,1)}, u32[]{:S(2)}, u32[]{:S(2)}) async-start(bf16[16,512,128]{2,1,0:T(8,128)(2,1)} %shard_map.163), calls=%async_computation.5 | async-start | bytes 4194304 | tf_op jit(solution)/shard_map/all_to_all | solution.py:518
  234.3 4.1 shard_map.164
  238.4 36.9 %all-to-all-done.5.left_ref.right_ref = bf16[16,512,128]{2,1,0:T(8,128)(2,1)} async-done(((bf16[16,512,128]{2,1,0:T(8,128)(2,1)}), bf16[16,512,128]{2,1,0:T(8,128)(2,1)}, u32[]{:S(2)}, u32[]{:S(2)}) %all-to-all-start.5) | async-done | bytes 2097184 | tf_op jit(solution)/shard_map/all_to_all | solution.py:518
  275.3 9.8 %shard_map.165 = (f32[16,128,256]{2,1,0:T(8,128)}, bf16[16,256,128]{2,1,0:T(8,128)(2,1)}, bf16[16,512,256]{2,1,0:T(8,128)(2,1)}) custom-call(bf16[16,512,128]{2,1,0:T(8,128)(2,1)} %all-to-all-done.5.left_ref.right_ref, bf16[16,512,128]{2,1,0:T(8,128)(2,1)} %all-to-all-done.5.left_ref.right_ref, bf16[16,512,256]{2,1,0:T(8,128)(2,1)} %get-tuple-element.44.fac_ref, ...), custom_call_target="tpu_custom_call" | custom-call | flops 805306368 | bytes 23267328 | tf_op jit(solution)/shard_map/pallas_call | solution.py:414
  285.1 11.3 %all-to-all-start.6 = ((bf16[16,256,128]{2,1,0:T(8,128)(2,1)}), bf16[16,256,128]{2,1,0:T(8,128)(2,1)}, u32[]{:S(2)}, u32[]{:S(2)}) async-start(bf16[16,256,128]{2,1,0:T(8,128)(2,1)} %get-tuple-element.47), calls=%async_computation.6 | async-start | bytes 2097152 | tf_op jit(solution)/shard_map/all_to_all | solution.py:518
  296.4 3.0 shard_map.156.sides_ref
  299.5 7.0 %shard_map.166 = (bf16[16,128,256]{2,1,0:T(8,128)(2,1)S(1)}, bf16[1024,128]{1,0:T(8,128)(2,1)S(1)}) custom-call(f32[16,128,256]{2,1,0:T(8,128)} %get-tuple-element.42.z_ref, bf16[16,512,256]{2,1,0:T(8,128)(2,1)} %get-tuple-element.49.gproj_ref, bf16[16,128,256]{2,1,0:T(8,128)(2,1)S(1)} %copy-done.14, bf16[128,640]{1,0:T(8,128)(2,1)S(1)} %get-tuple-element.65.w_ref, ...), custom_call_target="tpu_custom_call" | custom-call | flops 1744830464 | bytes 14229504 | tf_op jit(solution)/shard_map/pallas_call | solution.py:414
  307.1 12.2 %all-to-all-done.6.grad_ref = bf16[16,256,128]{2,1,0:T(8,128)(2,1)} async-done(((bf16[16,256,128]{2,1,0:T(8,128)(2,1)}), bf16[16,256,128]{2,1,0:T(8,128)(2,1)}, u32[]{:S(2)}, u32[]{:S(2)}) %all-to-all-start.6) | async-done | bytes 1048608 | tf_op jit(solution)/shard_map/all_to_all | solution.py:518
  320.3 4.2 shard_map.167
  324.5 61.1 %all_to_all.52.left_ref.right_ref.early_ref = bf16[16,576,128]{2,1,0:T(8,128)(2,1)} all-to-all(bf16[16,576,128]{2,1,0:T(8,128)(2,1)} %shard_map.167), channel_id=1, replica_groups=mesh['grp'=2,'row'=8,'col'=2] {'row','col'}, dimensions={0} | all-to-all | bytes 4718592 | tf_op jit(solution)/shard_map/all_to_all | solution.py:518
  385.6 7.3 %shard_map.168 = (bf16[16,512,256]{2,1,0:T(8,128)(2,1)}, bf16[768,128]{1,0:T(8,128)(2,1)S(1)}) custom-call(bf16[16,576,128]{2,1,0:T(8,128)(2,1)} %all_to_all.52.left_ref.right_ref.early_ref, bf16[16,576,128]{2,1,0:T(8,128)(2,1)} %all_to_all.52.left_ref.right_ref.early_ref, bf16[16,512,256]{2,1,0:T(8,128)(2,1)} %get-tuple-element.53.fac_ref, ...), custom_call_target="tpu_custom_call" | custom-call | flops 1342177280 | bytes 15566848 | tf_op jit(solution)/shard_map/pallas_call | solution.py:414
  392.9 12.8 %all_to_all.53.late_ref = bf16[16,48,128]{2,1,0:T(8,128)(2,1)S(1)} all-to-all(bf16[16,48,128]{2,1,0:T(8,128)(2,1)S(1)} %bitcast.29), channel_id=1, replica_groups=mesh['grp'=2,'row'=8,'col'=2] {'row','col'}, dimensions={0} | all-to-all | bytes 393216 | tf_op jit(solution)/shard_map/all_to_all | solution.py:518
  406.6 3.6 all-to-all-start.9
  410.1 5.6 %shard_map.169 = bf16[32,128,128]{2,1,0:T(8,128)(2,1)} custom-call(bf16[16,512,256]{2,1,0:T(8,128)(2,1)} %get-tuple-element.55.gproj_ref, bf16[16,128,256]{2,1,0:T(8,128)(2,1)S(1)} %get-tuple-element.54.glog_ref, bf16[16,128,256]{2,1,0:T(8,128)(2,1)S(1)} %copy-done.6, f32[16,128,256]{2,1,0:T(8,128)} %get-tuple-element.51.up_ref, ...), custom_call_target="tpu_custom_call" | custom-call | flops 671088640 | bytes 9602048 | tf_op jit(solution)/shard_map/pallas_call | solution.py:414
  415.7 7.6 %all-to-all-done.9.got_ref = bf16[16,112,128]{2,1,0:T(8,128)(2,1)S(1)} async-done(((bf16[16,112,128]{2,1,0:T(8,128)(2,1)}), bf16[16,112,128]{2,1,0:T(8,128)(2,1)S(1)}, u32[]{:S(2)}, u32[]{:S(2)}) %all-to-all-start.9) | async-done | bytes 458784 | tf_op jit(solution)/shard_map/all_to_all | solution.py:518
  (95 shorter events, 24.2 us)
Async XLA Ops:
  2.5 62.2 %copy-start.17 = (bf16[640,128]{1,0:T(8,128)(2,1)}, bf16[640,128]{1,0:T(8,128)(2,1)S(1)}, u32[]{:S(2)}) copy-start(bf16[640,128]{1,0:T(8,128)(2,1)S(1)} %copy.17.wt_ref) | copy-start | bytes 491524
  2.6 62.1 %copy-start.38 = (s32[2]{0:T(128)}, s32[2]{0:T(128)S(1)}, u32[]{:S(2)}) copy-start(s32[2]{0:T(128)S(1)} %pad_add_fusion.start_smem) | copy-start | bytes 28
  2.6 1.2 copy-start.15
  64.7 2.3 copy-start.1
  66.9 8.5 %copy-start.29 = (f32[2,128]{1,0:T(2,128)S(1)}, f32[2,128]{1,0:T(2,128)}, u32[]{:S(2)}) copy-start(f32[2,128]{1,0:T(2,128)} %gain_ref.15) | copy-start | bytes 3076
  66.9 8.5 %copy-start.32 = (f32[2,128]{1,0:T(2,128)S(1)}, f32[2,128]{1,0:T(2,128)}, u32[]{:S(2)}) copy-start(f32[2,128]{1,0:T(2,128)} %bias_ref.11) | copy-start | bytes 3076
  66.9 28.2 %copy-start.30 = (f32[2,128]{1,0:T(2,128)S(1)}, f32[2,128]{1,0:T(2,128)}, u32[]{:S(2)}) copy-start(f32[2,128]{1,0:T(2,128)} %hgain_ref.9) | copy-start | bytes 3076
  66.9 28.2 %copy-start.33 = (f32[2,128]{1,0:T(2,128)S(1)}, f32[2,128]{1,0:T(2,128)}, u32[]{:S(2)}) copy-start(f32[2,128]{1,0:T(2,128)} %hbias_ref.5) | copy-start | bytes 3076
  67.0 28.2 %all-to-all-start.1 = ((bf16[16,256,128]{2,1,0:T(8,128)(2,1)}), bf16[16,256,128]{2,1,0:T(8,128)(2,1)S(1)}, u32[]{:S(2)}, u32[]{:S(2)}) async-start(bf16[16,256,128]{2,1,0:T(8,128)(2,1)} %copy-done.11), calls=%async_computation.1 | async-start | bytes 2097152 | tf_op jit(solution)/shard_map/all_to_all | solution.py:518
  87.1 16.0 %copy-start.5 = (bf16[16,128,256]{2,1,0:T(8,128)(2,1)}, bf16[16,128,256]{2,1,0:T(8,128)(2,1)S(1)}, u32[]{:S(2)}) copy-start(bf16[16,128,256]{2,1,0:T(8,128)(2,1)S(1)} %get-tuple-element.36.z_ref) | copy-start | bytes 3145732
  87.1 16.0 %copy-start.7 = (bf16[16,128,256]{2,1,0:T(8,128)(2,1)}, bf16[16,128,256]{2,1,0:T(8,128)(2,1)S(1)}, u32[]{:S(2)}) copy-start(bf16[16,128,256]{2,1,0:T(8,128)(2,1)S(1)} %get-tuple-element.41.up_ref) | copy-start | bytes 3145732
  95.2 8.0 %copy-start.3 = (bf16[16,256,128]{2,1,0:T(8,128)(2,1)}, bf16[16,256,128]{2,1,0:T(8,128)(2,1)S(1)}, u32[]{:S(2)}) copy-start(bf16[16,256,128]{2,1,0:T(8,128)(2,1)S(1)} %all-to-all-done.1.prod_ref) | copy-start | bytes 3145732
  157.3 2.3 copy-start.2
  159.7 28.3 %copy-start.8 = (bf16[16,128,256]{2,1,0:T(8,128)(2,1)S(1)}, bf16[16,128,256]{2,1,0:T(8,128)(2,1)}, u32[]{:S(2)}) copy-start(bf16[16,128,256]{2,1,0:T(8,128)(2,1)} %copy-done.7) | copy-start | bytes 3145732
  159.7 28.3 %all-to-all-start.3 = ((bf16[16,256,128]{2,1,0:T(8,128)(2,1)}), bf16[16,256,128]{2,1,0:T(8,128)(2,1)}, u32[]{:S(2)}, u32[]{:S(2)}) async-start(bf16[16,256,128]{2,1,0:T(8,128)(2,1)} %copy-done.12), calls=%async_computation.3 | async-start | bytes 2097152 | tf_op jit(solution)/shard_map/all_to_all | solution.py:518
  166.6 21.4 %copy-start.23 = (bf16[128,128]{1,0:T(8,128)(2,1)S(1)}, bf16[128,128]{1,0:T(8,128)(2,1)}, u32[]{:S(2)}) copy-start(bf16[128,128]{1,0:T(8,128)(2,1)} %get-tuple-element.67.ow_ref) | copy-start | bytes 98308
  172.3 1.4 copy-start.9
  192.6 29.8 %all-to-all-start.4 = ((bf16[16,256,128]{2,1,0:T(8,128)(2,1)}), bf16[16,256,128]{2,1,0:T(8,128)(2,1)S(1)}, u32[]{:S(2)}, u32[]{:S(2)}) async-start(bf16[16,256,128]{2,1,0:T(8,128)(2,1)} %shard_map.162), calls=%async_computation.4 | async-start | bytes 2097152 | tf_op jit(solution)/shard_map/all_to_all | solution.py:518
  202.4 1.4 copy-start.10
  227.1 7.1 %copy-start.42 = (bf16[1,128,128]{2,1,0:T(8,128)(2,1)S(1)}, bf16[1,128,128]{2,1,0:T(8,128)(2,1)}, u32[]{:S(2)}) copy-start(bf16[1,128,128]{2,1,0:T(8,128)(2,1)} %get-tuple-element.69) | copy-start | bytes 98308
  227.1 48.2 %all-to-all-start.5 = ((bf16[16,512,128]{2,1,0:T(8,128)(2,1)}), bf16[16,512,128]{2,1,0:T(8,128)(2,1)}, u32[]{:S(2)}, u32[]{:S(2)}) async-start(bf16[16,512,128]{2,1,0:T(8,128)(2,1)} %shard_map.163), calls=%async_computation.5 | async-start | bytes 4194304 | tf_op jit(solution)/shard_map/all_to_all | solution.py:518
  234.3 41.0 %copy-start.21 = (bf16[128,128]{1,0:T(8,128)(2,1)S(1)}, bf16[128,128]{1,0:T(8,128)(2,1)}, u32[]{:S(2)}) copy-start(bf16[128,128]{1,0:T(8,128)(2,1)} %get-tuple-element.66.ow_ref) | copy-start | bytes 98308
  238.3 46.7 %copy-start.13 = (bf16[16,128,256]{2,1,0:T(8,128)(2,1)}, bf16[16,128,256]{2,1,0:T(8,128)(2,1)S(1)}, u32[]{:S(2)}) copy-start(bf16[16,128,256]{2,1,0:T(8,128)(2,1)S(1)} %get-tuple-element.46.glog_ref) | copy-start | bytes 3145732
  238.4 46.7 %copy-start.26 = (f32[136,128]{1,0:T(8,128)}, f32[136,128]{1,0:T(8,128)S(1)}, u32[]{:S(2)}) copy-start(f32[136,128]{1,0:T(8,128)S(1)} %get-tuple-element.50.terms_ref) | copy-start | bytes 208900
  285.1 34.3 %all-to-all-start.6 = ((bf16[16,256,128]{2,1,0:T(8,128)(2,1)}), bf16[16,256,128]{2,1,0:T(8,128)(2,1)}, u32[]{:S(2)}, u32[]{:S(2)}) async-start(bf16[16,256,128]{2,1,0:T(8,128)(2,1)} %get-tuple-element.47), calls=%async_computation.6 | async-start | bytes 2097152 | tf_op jit(solution)/shard_map/all_to_all | solution.py:518
  296.4 3.1 copy-start.4
  296.4 3.1 copy-start.14
  296.4 3.1 copy-start.22
  296.4 3.1 copy-start.27
  324.5 61.1 %copy-start.6 = (bf16[16,128,256]{2,1,0:T(8,128)(2,1)S(1)}, bf16[16,128,256]{2,1,0:T(8,128)(2,1)}, u32[]{:S(2)}) copy-start(bf16[16,128,256]{2,1,0:T(8,128)(2,1)} %copy-done.5) | copy-start | bytes 3145732
  385.6 20.1 %copy-start = (bf16[16,576,128]{2,1,0:T(8,128)(2,1)S(1)}, bf16[16,576,128]{2,1,0:T(8,128)(2,1)}, u32[]{:S(2)}) copy-start(bf16[16,576,128]{2,1,0:T(8,128)(2,1)} %all_to_all.52.left_ref.right_ref.early_ref) | copy-start | bytes 7077892
  406.6 16.8 %all-to-all-start.9 = ((bf16[16,112,128]{2,1,0:T(8,128)(2,1)}), bf16[16,112,128]{2,1,0:T(8,128)(2,1)S(1)}, u32[]{:S(2)}, u32[]{:S(2)}) async-start(bf16[16,112,128]{2,1,0:T(8,128)(2,1)} %shard_map.170), calls=%async_computation.9 | async-start | bytes 917504 | tf_op jit(solution)/shard_map/all_to_all | solution.py:518
  (17 other events, 13.8 us)

commit v3 on v2

--- a/solution.py
+++ b/solution.py
@@ -12,6 +12,7 @@
 F32 = jnp.float32
 BF16 = jnp.bfloat16
 VMEM_BYTES = 50 * 1024 * 1024
+LARGE_VMEM_BYTES = 60 * 1024 * 1024
 
 
 def dot(a, b, ca, cb):
@@ -73,16 +74,19 @@
     return sum(tile[:, a : a + width] for a in range(0, tile.shape[1], width))
 
 
-def project(cells, wt_ref, gain, bias, first, last):
-    normed, _ = norm(cells)
-    lowered = (normed * gain + bias).astype(BF16)
+def project(lowered, wt_ref, first, last):
     hidden = wt_ref.shape[0] // 5
     projected = dot(wt_ref[first * hidden : last * hidden, :], lowered, 1, 0)
     return [projected[n * hidden : (n + 1) * hidden] for n in range(last - first)]
 
 
+def lower(cells, gain, bias):
+    normed, inv = norm(cells)
+    return normed, inv, (normed * gain + bias).astype(BF16)
+
+
 def emit_edges(edges_ref, here, cells, wt_ref, gain, bias, mask, cpd, cols):
-    part = project(cells, wt_ref, gain, bias, 0, 4)
+    part = project(lower(cells, gain, bias)[2], wt_ref, 0, 4)
     edges_ref[:, 0, here, :] = pack(part[0] * sigmoid(part[1]) * mask, cpd, cols)
     edges_ref[:, 1, here, :] = pack(part[2] * sigmoid(part[3]) * mask, cpd, cols)
 
@@ -121,11 +125,18 @@
 
 
 def edge_first_kernel(
-    cpd, q, mask_smem, chain_smem, start_smem, pair_ref, maskc_ref, chainc_ref, wt_ref, gain_ref, bias_ref,
-    edges_ref, vec,
-):
-    rows, cols, _ = pair_ref.shape
+    cpd, q, mask_smem, chain_smem, start_smem, pair_ref, maskc_ref, chainc_ref, w_ref, gain_ref, bias_ref,
+    edges_ref, vec, turned_weight,
+):
+    rows, cols, width = pair_ref.shape
     load_columns(vec, (gain_ref, 0), (bias_ref, 0))
+
+    @first_step
+    def _():
+        for n in range(turned_weight.shape[0] // width):
+            block = slice(n * width, (n + 1) * width)
+            turned_weight[block, :] = w_ref[0, :, block].astype(F32).T.astype(BF16)
+
     for t in range(rows // q):
         first = pl.program_id(0) * rows + t * q
         mask = jnp.concatenate(
@@ -136,24 +147,12 @@
             1,
         )
         here = slice(t * q * cpd, (t + 1) * q * cpd)
-        emit_edges(edges_ref, here, turned(pair_ref, t, q), wt_ref, vec[0], vec[1], mask, cpd, cols)
-
-
-def keep_factors(fac_ref, gate_ref, t, cells, wt_ref, gain, bias, chain, mask, same):
-    hidden = wt_ref.shape[0] // 5
-    part = project(cells, wt_ref, gain, bias, 0, 5)
-    for n in (0, 2):
-        sig = sigmoid(part[n + 1]) * mask
-        fac_ref[t, n * hidden : (n + 1) * hidden, :] = sig.astype(BF16)
-        fac_ref[t, (n + 1) * hidden : (n + 2) * hidden, :] = (
-            part[n] * sig * (1.0 - sig)
-        ).astype(BF16)
-    gate_ref[t] = sigmoid(part[4] + same * chain)
+        emit_edges(edges_ref, here, turned(pair_ref, t, q), turned_weight, vec[0], vec[1], mask, cpd, cols)
 
 
 def first_keep_kernel(
     q, mask_smem, chain_smem, start_smem, pair_ref, cot_ref, maskc_ref, chainc_ref, wt_ref, gain_ref,
-    bias_ref, chain_ref, z_ref, up_ref, gate_ref, flags_ref, fac_ref, vec,
+    bias_ref, chain_ref, z_ref, up_ref, gate_ref, flags_ref, vec,
 ):
     load_columns(vec, (gain_ref, 0), (bias_ref, 0), (chain_ref, 0))
     tiles = z_ref.shape[0]
@@ -170,16 +169,35 @@
         z_ref[t] = cells.astype(BF16)
         up_ref[t] = turned(cot_ref, t, q).astype(BF16)
         flags_ref[t] = jnp.concatenate([mask, same], 0)
-        keep_factors(fac_ref, gate_ref, t, cells, wt_ref, vec[0], vec[1], vec[2], mask, same)
-
-
-def keep_kernel(layer, z_ref, flags_ref, wt_ref, gain_ref, bias_ref, chain_ref, gate_ref, fac_ref, vec):
+        (logits,) = project(lower(cells, vec[0], vec[1])[2], wt_ref, 4, 5)
+        gate_ref[t] = sigmoid(logits + same * vec[2]).astype(BF16)
+
+
+def keep_kernel(layer, z_ref, flags_ref, wt_ref, gain_ref, bias_ref, chain_ref, fac_ref, low_ref, nrm_ref, inv_ref, *rest):
+    vec = rest[-1]
+    hidden = wt_ref.shape[0] // 5
     load_columns(vec, (gain_ref, layer), (bias_ref, layer), (chain_ref, layer))
     for t in range(z_ref.shape[0]):
-        keep_factors(
-            fac_ref, gate_ref, t, z_ref[t], wt_ref, vec[0], vec[1], vec[2],
-            flags_ref[t, 0:1, :], flags_ref[t, 1:2, :],
-        )
+        mask, same = flags_ref[t, 0:1, :], flags_ref[t, 1:2, :]
+        normed, inv_ref[t], lowered = lower(z_ref[t].astype(F32), vec[0], vec[1])
+        low_ref[t] = lowered
+        nrm_ref[t] = normed.astype(BF16)
+        part = project(lowered, wt_ref, 0, 3 + len(rest))
+        for n in (0, 2):
+            sig = sigmoid(part[n + 1]) * mask
+            fac_ref[t, n * hidden : (n + 1) * hidden, :] = sig.astype(BF16)
+            fac_ref[t, (n + 1) * hidden : (n + 2) * hidden, :] = (
+                part[n] * sig * (1.0 - sig)
+            ).astype(BF16)
+        for gate_ref in rest[:-1]:
+            gate_ref[t] = sigmoid(part[4] + same * vec[2]).astype(BF16)
+
+
+def keep_product_kernel(cpd, q, prod_ref, nrm_ref, inv_ref):
+    rows = q * cpd
+    for t in range(nrm_ref.shape[0]):
+        normed, inv_ref[t] = norm(unpack(prod_ref[:, t * rows : (t + 1) * rows, :], cpd))
+        nrm_ref[t] = normed.astype(BF16)
 
 
 def mix_edge_kernel(
@@ -193,17 +211,16 @@
         here = slice(t * rows, (t + 1) * rows)
         hnormed, _ = norm(unpack(prod_ref[:, here, :], cpd))
         hscaled = (hnormed * vec[0] + vec[1]).astype(BF16)
-        cells = z_ref[t].astype(F32) + gate_ref[t] * dot(owt_ref[...], hscaled, 1, 0)
+        cells = z_ref[t].astype(F32) + gate_ref[t].astype(F32) * dot(owt_ref[...], hscaled, 1, 0)
         znext_ref[t] = cells
         emit_edges(
             edges_ref, here, cells, wt_ref, vec[2], vec[3], flags_ref[t, 0:1, :], cpd, lanes // q
         )
 
 
-def mix_grad(upstream, product, gate, ow_ref, hgain):
-    hnormed, hinv = norm(product)
-    grad_hscaled = dot(ow_ref[...], (upstream * gate).astype(BF16), 1, 0)
-    return norm_grad(grad_hscaled, hnormed, hinv, hgain)
+def mix_grad(upstream, hnormed, hinv, gate_ref, t, ow_ref, hgain):
+    grad_mixed = (upstream * gate_ref[t].astype(F32)).astype(BF16)
+    return norm_grad(dot(ow_ref[...], grad_mixed, 1, 0), hnormed, hinv, hgain)
 
 
 def mix_back_kernel(cpd, q, layer, prod_ref, up_ref, gate_ref, ow_ref, hgain_ref, gp_ref, vec):
@@ -212,9 +229,8 @@
     load_columns(vec, (hgain_ref, layer))
     for t in range(tiles):
         here = slice(t * rows, (t + 1) * rows)
-        grad = mix_grad(
-            up_ref[t].astype(F32), unpack(prod_ref[:, here, :], cpd), gate_ref[t], ow_ref, vec[0]
-        )
+        hnormed, hinv = norm(unpack(prod_ref[:, here, :], cpd))
+        grad = mix_grad(up_ref[t].astype(F32), hnormed, hinv, gate_ref, t, ow_ref, vec[0])
         gp_ref[:, here, :] = pack(grad, cpd, lanes // q)
 
 
@@ -248,7 +264,7 @@
     for t in range(up_ref.shape[0]):
         grad_logits = mix_terms(
             up_ref[t].astype(F32), unpack(prod_ref[:, t * rows : (t + 1) * rows, :], cpd),
-            gate_ref[t], flags_ref[t, 1:2, :], ow_ref, owt_ref, vec[0], vec[1],
+            gate_ref[t].astype(F32), flags_ref[t, 1:2, :], ow_ref, owt_ref, vec[0], vec[1],
             acc_ow, acc_hg, acc_hb, acc_ch,
         )
         glog_ref[t] = grad_logits.astype(BF16)
@@ -262,47 +278,39 @@
         terms_ref[hidden:, :] = jnp.concatenate(vectors, 0)
 
 
-def project_grad(grads, fac_ref, t, gproj_ref):
+def project_grad(left_ref, right_ref, fac_ref, glog_ref, t, cpd, rows):
     hidden = fac_ref.shape[1] // 4
-    for n in range(4):
-        block = slice(n * hidden, (n + 1) * hidden)
-        gproj_ref[t, block, :] = (grads[n // 2] * fac_ref[t, block, :].astype(F32)).astype(BF16)
-
-
-def input_grad(cells, gproj_ref, glog_ref, t, w_ref, gain):
-    hidden = gproj_ref.shape[1] // 4
-    normed, inv = norm(cells)
-    grad_scaled = dot(w_ref[:, : 4 * hidden], gproj_ref[t], 1, 0) + dot(
-        w_ref[:, 4 * hidden :], glog_ref[t], 1, 0
-    )
-    return norm_grad(grad_scaled, normed, inv, gain)
+    here = slice(t * rows, (t + 1) * rows)
+    grads = (unpack(left_ref[:, here, :], cpd), unpack(right_ref[:, here, :], cpd))
+    blocks = [
+        (grads[n // 2] * fac_ref[t, n * hidden : (n + 1) * hidden, :].astype(F32)).astype(BF16)
+        for n in range(4)
+    ]
+    return jnp.concatenate(blocks + [glog_ref[t]], 0)
+
+
+def input_grad(gproj, nrm_ref, inv_ref, t, w_ref, gain):
+    return norm_grad(dot(w_ref[...], gproj, 1, 0), nrm_ref[t].astype(F32), inv_ref[t], gain)
 
 
 def edge_mix_back_kernel(
-    cpd, q, layer, left_ref, right_ref, fac_ref, z_ref, glog_ref, up_ref, w_ref, gain_ref,
-    prod_ref, gate_ref, ow_ref, hgain_ref, upnext_ref, gp_ref, gproj_ref, vec,
-):
-    tiles, _, lanes = z_ref.shape
+    cpd, q, layer, left_ref, right_ref, fac_ref, nrm_ref, inv_ref, glog_ref, up_ref, w_ref, gain_ref,
+    hnrm_ref, hinv_ref, gate_ref, ow_ref, hgain_ref, upnext_ref, gp_ref, vec,
+):
+    tiles, _, lanes = up_ref.shape
     rows = q * cpd
     load_columns(vec, (gain_ref, layer), (hgain_ref, layer - 1))
     for t in range(tiles):
-        here = slice(t * rows, (t + 1) * rows)
-        grads = (unpack(left_ref[:, here, :], cpd), unpack(right_ref[:, here, :], cpd))
-        project_grad(grads, fac_ref, t, gproj_ref)
-        upstream = up_ref[t].astype(F32) + input_grad(z_ref[t], gproj_ref, glog_ref, t, w_ref, vec[0])
+        gproj = project_grad(left_ref, right_ref, fac_ref, glog_ref, t, cpd, rows)
+        upstream = up_ref[t].astype(F32) + input_grad(gproj, nrm_ref, inv_ref, t, w_ref, vec[0])
         upnext_ref[t] = upstream
-        grad = mix_grad(upstream, unpack(prod_ref[:, here, :], cpd), gate_ref[t], ow_ref, vec[1])
-        gp_ref[:, here, :] = pack(grad, cpd, lanes // q)
-
-
-def edge_terms(cells, gproj_ref, glog_ref, t, gain, bias, acc_w):
-    hidden = gproj_ref.shape[1] // 4
-    normed, _ = norm(cells)
-    lowered = (normed * gain + bias).astype(BF16)
-    ones = jnp.ones((16, cells.shape[1]), BF16)
-    sides = jnp.concatenate([lowered, normed.astype(BF16), ones], 0)
-    acc_w[:, : 4 * hidden] += dot(sides, gproj_ref[t], 1, 1)
-    acc_w[:, 4 * hidden :] += dot(sides, glog_ref[t], 1, 1)
+        grad = mix_grad(upstream, hnrm_ref[t].astype(F32), hinv_ref[t], gate_ref, t, ow_ref, vec[1])
+        gp_ref[:, t * rows : (t + 1) * rows, :] = pack(grad, cpd, lanes // q)
+
+
+def edge_terms(gproj, low_ref, nrm_ref, t, acc_w):
+    ones = jnp.ones((16, gproj.shape[1]), BF16)
+    acc_w[...] += dot(jnp.concatenate([low_ref[t], nrm_ref[t], ones], 0), gproj, 1, 1)
 
 
 def finish_edge(out_ref, acc_w, w_ref):
@@ -321,18 +329,19 @@
 
 
 def late_terms_kernel(
-    cpd, q, layer, z_ref, gproj_ref, glog_ref, w_ref, gain_ref, bias_ref, terms_ref,
+    cpd, q, layer, left_ref, right_ref, fac_ref, low_ref, nrm_ref, glog_ref, w_ref, terms_ref,
     prod_ref, up_ref, gate_ref, flags_ref, ow_ref, owt_ref, hgain_ref, hbias_ref,
     glognext_ref, all_ref, vec, acc_w, acc_ow, acc_hg, acc_hb, acc_ch,
 ):
     rows = q * cpd
-    load_columns(vec, (gain_ref, layer), (bias_ref, layer), (hgain_ref, layer - 1), (hbias_ref, layer - 1))
+    load_columns(vec, (hgain_ref, layer - 1), (hbias_ref, layer - 1))
     clear(acc_w, acc_ow, acc_hg, acc_hb, acc_ch)
-    for t in range(z_ref.shape[0]):
-        edge_terms(z_ref[t], gproj_ref, glog_ref, t, vec[0], vec[1], acc_w)
+    for t in range(up_ref.shape[0]):
+        gproj = project_grad(left_ref, right_ref, fac_ref, glog_ref, t, cpd, rows)
+        edge_terms(gproj, low_ref, nrm_ref, t, acc_w)
         grad_logits = mix_terms(
-            up_ref[t], unpack(prod_ref[:, t * rows : (t + 1) * rows, :], cpd), gate_ref[t],
-            flags_ref[t, 1:2, :], ow_ref, owt_ref, vec[2], vec[3], acc_ow, acc_hg, acc_hb, acc_ch,
+            up_ref[t], unpack(prod_ref[:, t * rows : (t + 1) * rows, :], cpd), gate_ref[t].astype(F32),
+            flags_ref[t, 1:2, :], ow_ref, owt_ref, vec[0], vec[1], acc_ow, acc_hg, acc_hb, acc_ch,
         )
         glognext_ref[t] = grad_logits.astype(BF16)
 
@@ -348,29 +357,27 @@
 
 
 def last_terms_kernel(
-    cpd, q, layer, left_ref, right_ref, fac_ref, z_ref, glog_ref, w_ref, gain_ref, bias_ref,
-    gproj_ref, all_ref, vec, acc_w,
-):
-    rows = q * cpd
-    load_columns(vec, (gain_ref, layer), (bias_ref, layer))
+    cpd, q, left_ref, right_ref, fac_ref, low_ref, nrm_ref, glog_ref, w_ref, all_ref, acc_w,
+):
     clear(acc_w)
-    for t in range(z_ref.shape[0]):
-        here = slice(t * rows, (t + 1) * rows)
-        grads = (unpack(left_ref[:, here, :], cpd), unpack(right_ref[:, here, :], cpd))
-        project_grad(grads, fac_ref, t, gproj_ref)
-        edge_terms(z_ref[t].astype(F32), gproj_ref, glog_ref, t, vec[0], vec[1], acc_w)
+    for t in range(low_ref.shape[0]):
+        gproj = project_grad(left_ref, right_ref, fac_ref, glog_ref, t, cpd, q * cpd)
+        edge_terms(gproj, low_ref, nrm_ref, t, acc_w)
 
     @last_step
     def _():
         finish_rows(all_ref, acc_w.shape[1], finish_edge(all_ref, acc_w, w_ref))
 
 
-def pair_grad_kernel(q, layer, gproj_ref, glog_ref, z_ref, up_ref, w_ref, gain_ref, pair_ref, vec):
-    tiles, _, lanes = z_ref.shape
+def pair_grad_kernel(
+    cpd, q, layer, left_ref, right_ref, fac_ref, nrm_ref, inv_ref, glog_ref, up_ref, w_ref, gain_ref, pair_ref, vec,
+):
+    tiles, _, lanes = up_ref.shape
     cols = lanes // q
     load_columns(vec, (gain_ref, layer))
     for t in range(tiles):
-        upstream = up_ref[t] + input_grad(z_ref[t].astype(F32), gproj_ref, glog_ref, t, w_ref, vec[0])
+        gproj = project_grad(left_ref, right_ref, fac_ref, glog_ref, t, cpd, q * cpd)
+        upstream = up_ref[t] + input_grad(gproj, nrm_ref, inv_ref, t, w_ref, vec[0])
         for a in range(q):
             pair_ref[t * q + a] = upstream[:, a * cols : (a + 1) * cols].T.astype(BF16)
 
@@ -399,14 +406,16 @@
     chain_ref[...] = jnp.concatenate([vectors[7:8], vectors[4:5]], 0)
 
 
-def cell_call(kernel, steps, ins, outs, scratch, prefetch=(), flops=0):
+def cell_call(kernel, steps, ins, outs, scratch, prefetch=(), flops=0, vmem=VMEM_BYTES):
     def spec(shape, how):
         if how is None:
             return pl.BlockSpec(shape, lambda *s: (0,) * len(shape))
         axis, first, size = how if isinstance(how, tuple) else (how, 0, shape[how] // steps)
         block = tuple(size if n == axis else length for n, length in enumerate(shape))
+        moves = shape[axis] >= size * steps
         return pl.BlockSpec(
-            block, lambda *s: tuple(s[0] + first if n == axis else 0 for n in range(len(shape)))
+            block,
+            lambda *s: tuple((s[0] if moves else 0) + first if n == axis else 0 for n in range(len(shape))),
         )
 
     moved = sum(a.size * a.dtype.itemsize for a, _ in ins)
@@ -421,7 +430,7 @@
             scratch_shapes=scratch,
         ),
         out_shape=[jax.ShapeDtypeStruct(s, t) for (s, t), _ in outs],
-        compiler_params=pltpu.CompilerParams(vmem_limit_bytes=VMEM_BYTES),
+        compiler_params=pltpu.CompilerParams(vmem_limit_bytes=vmem),
         cost_estimate=pl.CostEstimate(flops=flops, bytes_accessed=int(moved), transcendentals=0),
     )(*prefetch, *[a for a, _ in ins])
 
@@ -581,110 +590,118 @@
         per = side // steps
         return [(grads, (1, 0, per)), (grads, (1, steps, per))]
 
+    def keep(layer, z, with_gate):
+        norm_outs = [((tile, BF16), 0), ((tile, BF16), 0), (((tiles, 1, lanes), F32), 0)]
+        return cell_call(
+            functools.partial(keep_kernel, layer), steps,
+            [
+                (z, 0), (flags, 0), (wt[layer], None), (input_gain, None), (input_bias, None), (chain_bias, None),
+            ],
+            [((fac_tile, BF16), 0)] + norm_outs + [((tile, BF16), 0)] * with_gate,
+            [vec(3)], flops=5 * cell_flops,
+        )
+
     (edges0,) = cell_call(
         functools.partial(edge_first_kernel, cpd, q), steps,
         [
-            (pair_rep, 0), (mask_cols, None), (chain_cols, None), (wt[0], None), (input_gain, None),
-            (input_bias, None),
+            (pair_rep, 0), (mask_cols, None), (chain_cols, None), (proj_weight, (0, 0, 1)),
+            (input_gain, None), (input_bias, None),
         ],
-        [((edge_shape, BF16), 2)], [vec(2)], prefetch=scalars, flops=4 * cell_flops,
+        [((edge_shape, BF16), 2)], [vec(2), pltpu.VMEM((5 * hidden, width), BF16)],
+        prefetch=scalars, flops=4 * cell_flops, vmem=LARGE_VMEM_BYTES,
     )
     got0 = exchange(edges0)
-    z0, up, gate0, flags, fac0 = cell_call(
+    z0, up, gate0, flags = cell_call(
         functools.partial(first_keep_kernel, q), steps,
         [
             (after(pair_rep, edges0), 0), (cotangent, 0), (mask_cols, None), (chain_cols, None), (wt[0], None),
             (input_gain, None), (input_bias, None), (chain_bias, None),
         ],
-        [
-            ((tile, BF16), 0), ((tile, BF16), 0), ((tile, F32), 0), (((tiles, 2, lanes), F32), 0),
-            ((fac_tile, BF16), 0),
-        ],
-        [vec(3)], prefetch=scalars, flops=5 * cell_flops,
-    )
-    made0 = product(got0, True)
+        [((tile, BF16), 0), ((tile, BF16), 0), ((tile, BF16), 0), (((tiles, 2, lanes), F32), 0)],
+        [vec(3)], prefetch=scalars, flops=2 * cell_flops,
+    )
+    made0 = product(after(got0, z0), True)
     prod0 = exchange(made0)
     sides0 = assemble(after(got0, made0))
     edges1, z1 = cell_call(
         functools.partial(mix_edge_kernel, cpd, q, 0), steps,
         [
-            (prod0, 1), (z0, 0), (gate0, 0), (flags, 0), (owt[0], None), (hidden_gain, None),
+            (after(prod0, sides0), 1), (z0, 0), (gate0, 0), (flags, 0), (owt[0], None), (hidden_gain, None),
             (hidden_bias, None), (wt[1], None), (input_gain, None), (input_bias, None),
         ],
         [((edge_shape, BF16), 2), ((tile, F32), 0)], [vec(4)], flops=5 * cell_flops,
     )
     got1 = exchange(edges1)
-    gate1, fac1 = cell_call(
-        functools.partial(keep_kernel, 1), steps,
-        [
-            (z1, 0), (flags, 0), (wt[1], None), (input_gain, None), (input_bias, None), (chain_bias, None),
-        ],
-        [((tile, F32), 0), ((fac_tile, BF16), 0)], [vec(3)], flops=5 * cell_flops,
-    )
-    made1 = product(got1, False)
+    fac1, low1, nrm1, inv1, gate1 = keep(1, after(z1, edges1), True)
+    made1 = product(after(got1, gate1), False)
     prod1 = exchange(made1)
     sides1 = assemble(after(got1, made1))
 
     (grad1,) = cell_call(
         functools.partial(mix_back_kernel, cpd, q, 1), steps,
-        [(prod1, 1), (up, 0), (gate1, 0), (mixer[1], None), (hidden_gain, None)],
+        [(after(prod1, sides1), 1), (up, 0), (gate1, 0), (mixer[1], None), (hidden_gain, None)],
         [((cell_shape, BF16), 1)], [vec(1)], flops=cell_flops,
     )
     got_grad1 = exchange(grad1)
+    hnrm0, hinv0 = cell_call(
+        functools.partial(keep_product_kernel, cpd, q), steps, [(after(prod0, grad1), 1)],
+        [((tile, BF16), 0), (((tiles, 1, lanes), F32), 0)], [],
+    )
+    made_grads1 = product_grad(sides1, after(got_grad1, hnrm0), False)
+    grads1 = exchange(made_grads1)
     glog1, terms1 = cell_call(
         functools.partial(mix_terms_kernel, cpd, q, 1), steps,
         [
-            (after(prod1, grad1), 1), (up, 0), (gate1, 0), (flags, 0), (mixer[1], None), (owt[1], None),
+            (after(prod1, made_grads1), 1), (up, 0), (gate1, 0), (flags, 0), (mixer[1], None), (owt[1], None),
             (hidden_gain, None), (hidden_bias, None),
         ],
         [((tile, BF16), 0), ((terms_shape, F32), None)],
         [vec(2), acc(hidden), acc(cols), acc(cols), acc(cols)], flops=3 * cell_flops,
     )
-    grads1 = exchange(product_grad(sides1, got_grad1, False))
-    up0, grad0, gproj1 = cell_call(
+    up0, grad0 = cell_call(
         functools.partial(edge_mix_back_kernel, cpd, q, 1), steps,
-        halves(grads1)
+        halves(after(grads1, glog1))
         + [
-            (fac1, 0), (z1, 0), (glog1, 0), (up, 0), (weight[1], None), (input_gain, None),
-            (prod0, 1), (gate0, 0), (mixer[0], None), (hidden_gain, None),
+            (fac1, 0), (nrm1, 0), (inv1, 0), (glog1, 0), (up, 0), (weight[1], None), (input_gain, None),
+            (hnrm0, 0), (hinv0, 0), (gate0, 0), (mixer[0], None), (hidden_gain, None),
         ],
-        [((tile, F32), 0), ((cell_shape, BF16), 1), ((fac_tile, BF16), 0)],
+        [((tile, F32), 0), ((cell_shape, BF16), 1)],
         [vec(2)], flops=6 * cell_flops,
     )
     got_grad0 = exchange(grad0)
     glog0, early = cell_call(
         functools.partial(late_terms_kernel, cpd, q, 1), steps,
-        [
-            (z1, 0), (after(gproj1, grad0), 0), (glog1, 0), (weight[1], None), (input_gain, None),
-            (input_bias, None), (terms1, None), (prod0, 1), (up0, 0), (gate0, 0), (flags, 0),
-            (mixer[0], None), (owt[0], None), (hidden_gain, None), (hidden_bias, None),
+        halves(after(grads1, grad0))
+        + [
+            (fac1, 0), (low1, 0), (nrm1, 0), (glog1, 0), (weight[1], None), (terms1, None), (prod0, 1),
+            (up0, 0), (gate0, 0), (flags, 0), (mixer[0], None), (owt[0], None), (hidden_gain, None),
+            (hidden_bias, None),
         ],
         [((tile, BF16), 0), (((devices * early_rows, hidden), BF16), None)],
-        [vec(4), acc(5 * hidden, 2 * width + 16), acc(hidden), acc(cols), acc(cols), acc(cols)],
+        [vec(2), acc(5 * hidden, 2 * width + 16), acc(hidden), acc(cols), acc(cols), acc(cols)],
         flops=13 * cell_flops,
     )
 
-    grads0 = exchange(
-        product_grad(sides0, got_grad0, True, early.reshape(devices, early_rows, hidden))
-    )
-    gproj0, late = cell_call(
-        functools.partial(last_terms_kernel, cpd, q, 0), steps,
-        halves(grads0)
-        + [
-            (fac0, 0), (z0, 0), (glog0, 0), (weight[0], None), (input_gain, None), (input_bias, None),
-        ],
-        [((fac_tile, BF16), 0), (((devices * late_rows, hidden), BF16), None)],
-        [vec(2), acc(5 * hidden, 2 * width + 16)], flops=10 * cell_flops,
-    )
-    late = exchange(late.reshape(devices, late_rows, hidden))
+    made_grads0 = product_grad(sides0, got_grad0, True, early.reshape(devices, early_rows, hidden))
+    grads0 = exchange(made_grads0)
+    fac0, low0, nrm0, inv0 = keep(0, after(z0, made_grads0), False)
+    grads0 = after(grads0, nrm0)
+    (late,) = cell_call(
+        functools.partial(last_terms_kernel, cpd, q), steps,
+        halves(grads0) + [(fac0, 0), (low0, 0), (nrm0, 0), (glog0, 0), (weight[0], None)],
+        [(((devices * late_rows, hidden), BF16), None)],
+        [acc(5 * hidden, 2 * width + 16)], flops=10 * cell_flops,
+    )
+    got_late = exchange(late.reshape(devices, late_rows, hidden))
     (grad_pair,) = cell_call(
-        functools.partial(pair_grad_kernel, q, 0), steps,
-        [(gproj0, 0), (glog0, 0), (z0, 0), (up0, 0), (weight[0], None), (input_gain, None)],
+        functools.partial(pair_grad_kernel, cpd, q, 0), steps,
+        halves(after(grads0, late))
+        + [(fac0, 0), (nrm0, 0), (inv0, 0), (glog0, 0), (up0, 0), (weight[0], None), (input_gain, None)],
         [((pair_rep.shape, BF16), 0)], [vec(1)], flops=5 * cell_flops,
     )
     (spread,) = cell_call(
         functools.partial(spread_kernel, 1.0 / length), 1,
-        [(grads0, (1, 2 * side // early_rows, early_rows)), (late, None)],
+        [(grads0, (1, 2 * side // early_rows, early_rows)), (got_late, None)],
         [(((devices, early_rows + late_rows, hidden), BF16), None)], [],
     )
     proj, out, inorm, hnorm, chain = whole_call(

time: 426 us -> 424 us (level)
  blocking collectives: 183 us -> 21.2 us
  waiting for transfers between devices: 97.7 us -> 214 us
  starting transfers between devices: 39.3 us -> 72.8 us
  local copies, waits for them, and re-layouts: 23.1 us -> 31.5 us
    all_to_all x4 -> x1, blocking collectives: 183 us -> 21.2 us  [exchange(): return lax.all_to_all(array, AXES, split_axis=0, concat_axis=0, tiled=True)]
    all_to_all x6 -> x9, waiting for transfers between devices: 97.7 us -> 214 us  [exchange(): return lax.all_to_all(array, AXES, split_axis=0, concat_axis=0, tiled=True)]
    all_to_all x6 -> x9, starting transfers between devices: 39.3 us -> 72.8 us  [exchange(): return lax.all_to_all(array, AXES, split_axis=0, concat_axis=0, tiled=True)]
    unnamed x88 -> x114, local copies, waits for them, and re-layouts: 18.1 us -> 29 us
    pallas_call x11 -> x13, Pallas kernels: 62.2 us -> 62 us  [cell_call(): pl.pallas_call(kernel, grid_spec=pltpu.PrefetchScalarGridSpec(num_scalar_...]
  transfers between devices with their start and end apart: 6 -> 9, of which waited for: 6 -> 9; matrix products, arithmetic and copies ran while one was open for 1% -> 1% of each run, Pallas kernels for 8% -> 9%
where the time goes in v3:
time: 424 us; the launch traced here: 422 us
  waiting for transfers between devices  214 us (50%)
  Pallas kernels  80.4 us (19%)
  starting transfers between devices  72.8 us (17%)
  local copies, waits for them, and re-layouts  31.5 us (7%)
  blocking collectives  21.2 us (5%)
    all_to_all x9, waiting for transfers between devices, exchange(): return lax.all_to_all(array, AXES, split_axis=0, concat_axis=0, tiled=True)  214 us
    all_to_all x9, starting transfers between devices, exchange(): return lax.all_to_all(array, AXES, split_axis=0, concat_axis=0, tiled=True)  72.8 us
    pallas_call x13, Pallas kernels, cell_call(): pl.pallas_call(kernel, grid_spec=pltpu.PrefetchScalarGridSpec(num_scalar_...  62 us
    unnamed x114, local copies, waits for them, and re-layouts  29 us
    all_to_all x1, blocking collectives, exchange(): return lax.all_to_all(array, AXES, split_axis=0, concat_axis=0, tiled=True)  21.2 us
    pallas_call x7, Pallas kernels, whole_call(): pl.pallas_call(kernel, in_specs=[pl.BlockSpec(memory_space=pltpu.VMEM)] *...  18.4 us
  transfers between devices with their start and end apart: 9, of which 9 were waited for; matrix products, arithmetic and copies ran while one was open for 1% of the time, Pallas kernels for 9%

profile of v3, /device:TPU:0, one launch (start us, length us, event | category | flops | bytes accessed | tf_op | source)
XLA Modules:
  0.0 421.7 jit_solution(14811731472007508888)
XLA Ops:
  1.2 6.1 %shard_map.154 = bf16[16,2,256,128]{3,2,1,0:T(8,128)(2,1)} custom-call(s32[256]{0:T(256)} %mask_smem.3, s32[256]{0:T(256)} %chain_smem.3, s32[2]{0:T(128)} %pad_add_fusion.start_smem, bf16[32,128,128]{2,1,0:T(8,128)(2,1)} %pair_ref.2, s32[2,128]{1,0:T(2,128)} %bitcast.31, s32[2,128]{1,0:T(2,128)} %bitcast.33, bf16[2,128,640]{2,1,0:T(8,128)(2,1)} %w_ref.1, ...), custom_call_target="tpu_custom_call" | custom-call | flops 536870912 | bytes 3477504 | tf_op jit(solution)/shard_map/pallas_call | solution.py:423
  7.4 7.5 %all-to-all-start = ((bf16[16,2,256,128]{3,2,1,0:T(8,128)(2,1)}), bf16[16,2,256,128]{3,2,1,0:T(8,128)(2,1)S(1)}, u32[]{:S(2)}, u32[]{:S(2)}) async-start(bf16[16,2,256,128]{3,2,1,0:T(8,128)(2,1)} %shard_map.154), calls=%async_computation | async-start | bytes 4194304 | tf_op jit(solution)/shard_map/all_to_all | solution.py:527
  15.9 4.4 %shard_map.155 = (bf16[16,128,256]{2,1,0:T(8,128)(2,1)S(1)}, bf16[16,128,256]{2,1,0:T(8,128)(2,1)S(1)}, bf16[16,128,256]{2,1,0:T(8,128)(2,1)S(1)}, f32[16,2,256]{2,1,0:T(2,128)S(1)}) custom-call(s32[256]{0:T(256)S(1)} %copy-done.44, s32[256]{0:T(256)S(1)} %copy-done.45, s32[2]{0:T(128)S(1)} %copy-done.50, bf16[32,128,128]{2,1,0:T(8,128)(2,1)} %pair_ref.2, ...), custom_call_target="tpu_custom_call" | custom-call | flops 268435456 | bytes 5444608 | tf_op jit(solution)/shard_map/pallas_call | solution.py:423
  23.3 32.7 %all-to-all-done.edges_ref = bf16[16,2,256,128]{3,2,1,0:T(8,128)(2,1)S(1)} async-done(((bf16[16,2,256,128]{3,2,1,0:T(8,128)(2,1)}), bf16[16,2,256,128]{3,2,1,0:T(8,128)(2,1)S(1)}, u32[]{:S(2)}, u32[]{:S(2)}) %all-to-all-start) | async-done | bytes 2097184 | tf_op jit(solution)/shard_map/all_to_all | solution.py:527
  58.3 11.2 %all-to-all-start.1 = ((bf16[16,256,128]{2,1,0:T(8,128)(2,1)}), bf16[16,256,128]{2,1,0:T(8,128)(2,1)S(1)}, u32[]{:S(2)}, u32[]{:S(2)}) async-start(bf16[16,256,128]{2,1,0:T(8,128)(2,1)} %copy-done.20), calls=%async_computation.1 | async-start | bytes 2097152 | tf_op jit(solution)/shard_map/all_to_all | solution.py:527
  75.6 16.8 %all-to-all-done.1.prod_ref = bf16[16,256,128]{2,1,0:T(8,128)(2,1)S(1)} async-done(((bf16[16,256,128]{2,1,0:T(8,128)(2,1)}), bf16[16,256,128]{2,1,0:T(8,128)(2,1)S(1)}, u32[]{:S(2)}, u32[]{:S(2)}) %all-to-all-start.1) | async-done | bytes 1048608 | tf_op jit(solution)/shard_map/all_to_all | solution.py:527
  92.5 5.6 %shard_map.158 = (bf16[16,2,256,128]{3,2,1,0:T(8,128)(2,1)}, f32[16,128,256]{2,1,0:T(8,128)}) custom-call(bf16[16,256,128]{2,1,0:T(8,128)(2,1)S(1)} %all-to-all-done.1.prod_ref, bf16[16,128,256]{2,1,0:T(8,128)(2,1)S(1)} %copy-done.32, bf16[16,128,256]{2,1,0:T(8,128)(2,1)S(1)} %copy-done.6, f32[16,2,256]{2,1,0:T(2,128)S(1)} %get-tuple-element.56.flags_ref, ...), custom_call_target="tpu_custom_call" | custom-call | flops 671088640 | bytes 7573504 | tf_op jit(solution)/shard_map/pallas_call | solution.py:423
  98.1 6.9 %all-to-all-start.2 = ((bf16[16,2,256,128]{3,2,1,0:T(8,128)(2,1)}), bf16[16,2,256,128]{3,2,1,0:T(8,128)(2,1)S(1)}, u32[]{:S(2)}, u32[]{:S(2)}) async-start(bf16[16,2,256,128]{3,2,1,0:T(8,128)(2,1)} %get-tuple-element.57), calls=%async_computation.2 | async-start | bytes 4194304 | tf_op jit(solution)/shard_map/all_to_all | solution.py:527
  105.6 5.8 %shard_map.159 = (bf16[16,512,256]{2,1,0:T(8,128)(2,1)}, bf16[16,128,256]{2,1,0:T(8,128)(2,1)S(1)}, bf16[16,128,256]{2,1,0:T(8,128)(2,1)S(1)}, f32[16,1,256]{2,1,0:T(1,128)S(1)}, bf16[16,128,256]{2,1,0:T(8,128)(2,1)S(1)}) custom-call(f32[16,128,256]{2,1,0:T(8,128)} %get-tuple-element.59.z_ref, f32[16,2,256]{2,1,0:T(2,128)S(1)} %get-tuple-element.56.flags_ref, ...), custom_call_target="tpu_custom_call" | custom-call | flops 671088640 | bytes 9653248 | tf_op jit(solution)/shard_map/pallas_call | solution.py:423
  114.9 31.1 %all-to-all-done.2.edges_ref = bf16[16,2,256,128]{3,2,1,0:T(8,128)(2,1)S(1)} async-done(((bf16[16,2,256,128]{3,2,1,0:T(8,128)(2,1)}), bf16[16,2,256,128]{3,2,1,0:T(8,128)(2,1)S(1)}, u32[]{:S(2)}, u32[]{:S(2)}) %all-to-all-start.2) | async-done | bytes 2097184 | tf_op jit(solution)/shard_map/all_to_all | solution.py:527
  148.4 11.3 %all-to-all-start.3 = ((bf16[16,256,128]{2,1,0:T(8,128)(2,1)}), bf16[16,256,128]{2,1,0:T(8,128)(2,1)}, u32[]{:S(2)}, u32[]{:S(2)}) async-start(bf16[16,256,128]{2,1,0:T(8,128)(2,1)} %copy-done.22), calls=%async_computation.3 | async-start | bytes 2097152 | tf_op jit(solution)/shard_map/all_to_all | solution.py:527
  164.0 18.7 %all-to-all-done.3.prod_ref = bf16[16,256,128]{2,1,0:T(8,128)(2,1)} async-done(((bf16[16,256,128]{2,1,0:T(8,128)(2,1)}), bf16[16,256,128]{2,1,0:T(8,128)(2,1)}, u32[]{:S(2)}, u32[]{:S(2)}) %all-to-all-start.3) | async-done | bytes 1048608 | tf_op jit(solution)/shard_map/all_to_all | solution.py:527
  182.7 3.6 shard_map.162
  187.2 6.9 %all-to-all-start.4 = ((bf16[16,256,128]{2,1,0:T(8,128)(2,1)}), bf16[16,256,128]{2,1,0:T(8,128)(2,1)S(1)}, u32[]{:S(2)}, u32[]{:S(2)}) async-start(bf16[16,256,128]{2,1,0:T(8,128)(2,1)} %copy-done.21), calls=%async_computation.4 | async-start | bytes 2097152 | tf_op jit(solution)/shard_map/all_to_all | solution.py:527
  196.0 21.1 %all-to-all-done.4.grad_ref = bf16[16,256,128]{2,1,0:T(8,128)(2,1)S(1)} async-done(((bf16[16,256,128]{2,1,0:T(8,128)(2,1)}), bf16[16,256,128]{2,1,0:T(8,128)(2,1)S(1)}, u32[]{:S(2)}, u32[]{:S(2)}) %all-to-all-start.4) | async-done | bytes 1048608 | tf_op jit(solution)/shard_map/all_to_all | solution.py:527
  217.0 4.7 %shard_map.164 = bf16[16,512,128]{2,1,0:T(8,128)(2,1)} custom-call(bf16[8,2,256,256]{3,2,1,0:T(8,128)(2,1)} %copy-done.9, bf16[16,256,128]{2,1,0:T(8,128)(2,1)S(1)} %all-to-all-done.4.grad_ref), custom_call_target="tpu_custom_call" | custom-call | flops 536870912 | bytes 5242880 | tf_op jit(solution)/shard_map/pallas_call | solution.py:515
  221.8 7.0 %all-to-all-start.5 = ((bf16[16,512,128]{2,1,0:T(8,128)(2,1)}), bf16[16,512,128]{2,1,0:T(8,128)(2,1)}, u32[]{:S(2)}, u32[]{:S(2)}) async-start(bf16[16,512,128]{2,1,0:T(8,128)(2,1)} %shard_map.164), calls=%async_computation.5 | async-start | bytes 4194304 | tf_op jit(solution)/shard_map/all_to_all | solution.py:527
  229.0 4.0 shard_map.165
  233.6 36.4 %all-to-all-done.5.left_ref.right_ref = bf16[16,512,128]{2,1,0:T(8,128)(2,1)} async-done(((bf16[16,512,128]{2,1,0:T(8,128)(2,1)}), bf16[16,512,128]{2,1,0:T(8,128)(2,1)}, u32[]{:S(2)}, u32[]{:S(2)}) %all-to-all-start.5) | async-done | bytes 2097184 | tf_op jit(solution)/shard_map/all_to_all | solution.py:527
  270.0 8.1 %shard_map.166 = (f32[16,128,256]{2,1,0:T(8,128)}, bf16[16,256,128]{2,1,0:T(8,128)(2,1)}) custom-call(bf16[16,512,128]{2,1,0:T(8,128)(2,1)} %all-to-all-done.5.left_ref.right_ref, bf16[16,512,128]{2,1,0:T(8,128)(2,1)} %all-to-all-done.5.left_ref.right_ref, bf16[16,512,256]{2,1,0:T(8,128)(2,1)} %get-tuple-element.71.fac_ref, ...), custom_call_target="tpu_custom_call" | custom-call | flops 805306368 | bytes 17008640 | tf_op jit(solution)/shard_map/pallas_call | solution.py:423
  278.1 11.4 %all-to-all-start.6 = ((bf16[16,256,128]{2,1,0:T(8,128)(2,1)}), bf16[16,256,128]{2,1,0:T(8,128)(2,1)}, u32[]{:S(2)}, u32[]{:S(2)}) async-start(bf16[16,256,128]{2,1,0:T(8,128)(2,1)} %get-tuple-element.75), calls=%async_computation.6 | async-start | bytes 2097152 | tf_op jit(solution)/shard_map/all_to_all | solution.py:527
  290.8 7.3 %shard_map.167 = (bf16[16,128,256]{2,1,0:T(8,128)(2,1)S(1)}, bf16[1024,128]{1,0:T(8,128)(2,1)S(1)}) custom-call(bf16[16,512,128]{2,1,0:T(8,128)(2,1)} %all-to-all-done.5.left_ref.right_ref, bf16[16,512,128]{2,1,0:T(8,128)(2,1)} %all-to-all-done.5.left_ref.right_ref, bf16[16,512,256]{2,1,0:T(8,128)(2,1)} %get-tuple-element.71.fac_ref, ...), custom_call_target="tpu_custom_call" | custom-call | flops 1744830464 | bytes 17373184 | tf_op jit(solution)/shard_map/pallas_call | solution.py:423
  299.8 12.8 %all-to-all-done.6.grad_ref = bf16[16,256,128]{2,1,0:T(8,128)(2,1)} async-done(((bf16[16,256,128]{2,1,0:T(8,128)(2,1)}), bf16[16,256,128]{2,1,0:T(8,128)(2,1)}, u32[]{:S(2)}, u32[]{:S(2)}) %all-to-all-start.6) | async-done | bytes 1048608 | tf_op jit(solution)/shard_map/all_to_all | solution.py:527
  313.5 4.2 shard_map.168
  317.7 7.0 %all-to-all-start.7 = ((bf16[16,576,128]{2,1,0:T(8,128)(2,1)}), bf16[16,576,128]{2,1,0:T(8,128)(2,1)S(1)}, u32[]{:S(2)}, u32[]{:S(2)}) async-start(bf16[16,576,128]{2,1,0:T(8,128)(2,1)} %shard_map.168), calls=%async_computation.7 | async-start | bytes 4718592 | tf_op jit(solution)/shard_map/all_to_all | solution.py:527
  326.8 4.1 shard_map.169
  332.9 37.5 %all-to-all-done.7.left_ref.right_ref.early_ref = bf16[16,576,128]{2,1,0:T(8,128)(2,1)S(1)} async-done(((bf16[16,576,128]{2,1,0:T(8,128)(2,1)}), bf16[16,576,128]{2,1,0:T(8,128)(2,1)S(1)}, u32[]{:S(2)}, u32[]{:S(2)}) %all-to-all-start.7) | async-done | bytes 2359328 | tf_op jit(solution)/shard_map/all_to_all | solution.py:527
  375.1 5.1 %shard_map.170 = bf16[768,128]{1,0:T(8,128)(2,1)S(1)} custom-call(bf16[16,576,128]{2,1,0:T(8,128)(2,1)} %copy-done, bf16[16,576,128]{2,1,0:T(8,128)(2,1)} %copy-done, bf16[16,512,256]{2,1,0:T(8,128)(2,1)} %get-tuple-element.84.fac_ref, bf16[16,128,256]{2,1,0:T(8,128)(2,1)S(1)} %copy-done.30, bf16[16,128,256]{2,1,0:T(8,128)(2,1)S(1)} %copy-done.18, ...), custom_call_target="tpu_custom_call" | custom-call | flops 1342177280 | bytes 12419072 | tf_op jit(solution)/shard_map/pallas_call | solution.py:423
  380.2 21.2 %all_to_all.50.late_ref = bf16[16,48,128]{2,1,0:T(8,128)(2,1)S(1)} all-to-all(bf16[16,48,128]{2,1,0:T(8,128)(2,1)S(1)} %bitcast.26), channel_id=1, replica_groups=mesh['grp'=2,'row'=8,'col'=2] {'row','col'}, dimensions={0} | all-to-all | bytes 393216 | tf_op jit(solution)/shard_map/all_to_all | solution.py:527
  404.0 3.6 all-to-all-start.9
  407.6 6.2 %shard_map.171 = bf16[32,128,128]{2,1,0:T(8,128)(2,1)} custom-call(bf16[16,576,128]{2,1,0:T(8,128)(2,1)} %copy-done, bf16[16,576,128]{2,1,0:T(8,128)(2,1)} %copy-done, bf16[16,512,256]{2,1,0:T(8,128)(2,1)} %get-tuple-element.84.fac_ref, bf16[16,128,256]{2,1,0:T(8,128)(2,1)S(1)} %copy-done.19, f32[16,1,256]{2,1,0:T(1,128)S(1)} %get-tuple-element.88.inv_ref, ...), custom_call_target="tpu_custom_call" | custom-call | flops 671088640 | bytes 14337024 | tf_op jit(solution)/shard_map/pallas_call | solution.py:423
  413.7 7.0 %all-to-all-done.9.got_ref = bf16[16,112,128]{2,1,0:T(8,128)(2,1)S(1)} async-done(((bf16[16,112,128]{2,1,0:T(8,128)(2,1)}), bf16[16,112,128]{2,1,0:T(8,128)(2,1)S(1)}, u32[]{:S(2)}, u32[]{:S(2)}) %all-to-all-start.9) | async-done | bytes 458784 | tf_op jit(solution)/shard_map/all_to_all | solution.py:527
  (126 shorter events, 43.3 us)
Async XLA Ops:
  7.3 7.6 %copy-start.54 = (bf16[2,128,640]{2,1,0:T(8,128)(2,1)S(1)}, bf16[2,128,640]{2,1,0:T(8,128)(2,1)}, u32[]{:S(2)}) copy-start(bf16[2,128,640]{2,1,0:T(8,128)(2,1)} %w_ref.1) | copy-start | bytes 983044
  7.3 8.5 %copy-start.42 = (f32[2,128]{1,0:T(2,128)S(1)}, f32[2,128]{1,0:T(2,128)}, u32[]{:S(2)}) copy-start(f32[2,128]{1,0:T(2,128)} %gain_ref.13) | copy-start | bytes 3076
  7.3 8.5 %copy-start.44 = (s32[256]{0:T(256)S(1)}, s32[256]{0:T(256)}, u32[]{:S(2)}) copy-start(s32[256]{0:T(256)} %mask_smem.3) | copy-start | bytes 3076
  7.3 8.5 %copy-start.45 = (s32[256]{0:T(256)S(1)}, s32[256]{0:T(256)}, u32[]{:S(2)}) copy-start(s32[256]{0:T(256)} %chain_smem.3) | copy-start | bytes 3076
  7.3 8.5 %copy-start.48 = (f32[2,128]{1,0:T(2,128)S(1)}, f32[2,128]{1,0:T(2,128)}, u32[]{:S(2)}) copy-start(f32[2,128]{1,0:T(2,128)} %bias_ref.9) | copy-start | bytes 3076
  7.4 8.5 %copy-start.50 = (s32[2]{0:T(128)S(1)}, s32[2]{0:T(128)}, u32[]{:S(2)}) copy-start(s32[2]{0:T(128)} %pad_add_fusion.start_smem) | copy-start | bytes 28
  7.4 8.5 %copy-start.51 = (f32[2,128]{1,0:T(2,128)S(1)}, f32[2,128]{1,0:T(2,128)}, u32[]{:S(2)}) copy-start(f32[2,128]{1,0:T(2,128)} %chain_ref.5) | copy-start | bytes 3076
  7.4 48.6 %all-to-all-start = ((bf16[16,2,256,128]{3,2,1,0:T(8,128)(2,1)}), bf16[16,2,256,128]{3,2,1,0:T(8,128)(2,1)S(1)}, u32[]{:S(2)}, u32[]{:S(2)}) async-start(bf16[16,2,256,128]{3,2,1,0:T(8,128)(2,1)} %shard_map.154), calls=%async_computation | async-start | bytes 4194304 | tf_op jit(solution)/shard_map/all_to_all | solution.py:527
  15.9 41.4 %copy-start.34 = (bf16[640,128]{1,0:T(8,128)(2,1)}, bf16[640,128]{1,0:T(8,128)(2,1)S(1)}, u32[]{:S(2)}) copy-start(bf16[640,128]{1,0:T(8,128)(2,1)S(1)} %copy.17.wt_ref) | copy-start | bytes 491524
  58.3 34.2 %all-to-all-start.1 = ((bf16[16,256,128]{2,1,0:T(8,128)(2,1)}), bf16[16,256,128]{2,1,0:T(8,128)(2,1)S(1)}, u32[]{:S(2)}, u32[]{:S(2)}) async-start(bf16[16,256,128]{2,1,0:T(8,128)(2,1)} %copy-done.20), calls=%async_computation.1 | async-start | bytes 2097152 | tf_op jit(solution)/shard_map/all_to_all | solution.py:527
  71.2 21.2 %copy-start.6 = (bf16[16,128,256]{2,1,0:T(8,128)(2,1)S(1)}, bf16[16,128,256]{2,1,0:T(8,128)(2,1)}, u32[]{:S(2)}) copy-start(bf16[16,128,256]{2,1,0:T(8,128)(2,1)} %copy-done.5) | copy-start | bytes 3145732
  71.2 21.2 %copy-start.32 = (bf16[16,128,256]{2,1,0:T(8,128)(2,1)S(1)}, bf16[16,128,256]{2,1,0:T(8,128)(2,1)}, u32[]{:S(2)}) copy-start(bf16[16,128,256]{2,1,0:T(8,128)(2,1)} %copy-done.31) | copy-start | bytes 3145732
  71.2 21.2 %copy-start.43 = (f32[2,128]{1,0:T(2,128)S(1)}, f32[2,128]{1,0:T(2,128)}, u32[]{:S(2)}) copy-start(f32[2,128]{1,0:T(2,128)} %hgain_ref.9) | copy-start | bytes 3076
  71.2 21.2 %copy-start.49 = (f32[2,128]{1,0:T(2,128)S(1)}, f32[2,128]{1,0:T(2,128)}, u32[]{:S(2)}) copy-start(f32[2,128]{1,0:T(2,128)} %hbias_ref.5) | copy-start | bytes 3076
  92.4 101.7 %copy-start.4 = (bf16[16,256,128]{2,1,0:T(8,128)(2,1)}, bf16[16,256,128]{2,1,0:T(8,128)(2,1)S(1)}, u32[]{:S(2)}) copy-start(bf16[16,256,128]{2,1,0:T(8,128)(2,1)S(1)} %all-to-all-done.1.prod_ref) | copy-start | bytes 3145732
  98.1 48.0 %all-to-all-start.2 = ((bf16[16,2,256,128]{3,2,1,0:T(8,128)(2,1)}), bf16[16,2,256,128]{3,2,1,0:T(8,128)(2,1)S(1)}, u32[]{:S(2)}, u32[]{:S(2)}) async-start(bf16[16,2,256,128]{3,2,1,0:T(8,128)(2,1)} %get-tuple-element.57), calls=%async_computation.2 | async-start | bytes 4194304 | tf_op jit(solution)/shard_map/all_to_all | solution.py:527
  148.4 34.3 %all-to-all-start.3 = ((bf16[16,256,128]{2,1,0:T(8,128)(2,1)}), bf16[16,256,128]{2,1,0:T(8,128)(2,1)}, u32[]{:S(2)}, u32[]{:S(2)}) async-start(bf16[16,256,128]{2,1,0:T(8,128)(2,1)} %copy-done.22), calls=%async_computation.3 | async-start | bytes 2097152 | tf_op jit(solution)/shard_map/all_to_all | solution.py:527
  159.7 23.0 %copy-start.8 = (bf16[16,128,256]{2,1,0:T(8,128)(2,1)S(1)}, bf16[16,128,256]{2,1,0:T(8,128)(2,1)}, u32[]{:S(2)}) copy-start(bf16[16,128,256]{2,1,0:T(8,128)(2,1)} %copy-done.7) | copy-start | bytes 3145732
  159.7 23.0 %copy-start.37 = (bf16[128,128]{1,0:T(8,128)(2,1)S(1)}, bf16[128,128]{1,0:T(8,128)(2,1)}, u32[]{:S(2)}) copy-start(bf16[128,128]{1,0:T(8,128)(2,1)} %get-tuple-element.99.ow_ref) | copy-start | bytes 98308
  187.2 29.8 %all-to-all-start.4 = ((bf16[16,256,128]{2,1,0:T(8,128)(2,1)}), bf16[16,256,128]{2,1,0:T(8,128)(2,1)S(1)}, u32[]{:S(2)}, u32[]{:S(2)}) async-start(bf16[16,256,128]{2,1,0:T(8,128)(2,1)} %copy-done.21), calls=%async_computation.4 | async-start | bytes 2097152 | tf_op jit(solution)/shard_map/all_to_all | solution.py:527
  221.8 48.2 %all-to-all-start.5 = ((bf16[16,512,128]{2,1,0:T(8,128)(2,1)}), bf16[16,512,128]{2,1,0:T(8,128)(2,1)}, u32[]{:S(2)}, u32[]{:S(2)}) async-start(bf16[16,512,128]{2,1,0:T(8,128)(2,1)} %shard_map.164), calls=%async_computation.5 | async-start | bytes 4194304 | tf_op jit(solution)/shard_map/all_to_all | solution.py:527
  228.8 41.2 %copy-start.13 = (bf16[16,128,256]{2,1,0:T(8,128)(2,1)S(1)}, bf16[16,128,256]{2,1,0:T(8,128)(2,1)}, u32[]{:S(2)}) copy-start(bf16[16,128,256]{2,1,0:T(8,128)(2,1)} %copy-done.12) | copy-start | bytes 3145732
  228.8 41.2 %copy-start.36 = (bf16[128,128]{1,0:T(8,128)(2,1)S(1)}, bf16[128,128]{1,0:T(8,128)(2,1)}, u32[]{:S(2)}) copy-start(bf16[128,128]{1,0:T(8,128)(2,1)} %get-tuple-element.98.ow_ref) | copy-start | bytes 98308
  228.8 41.1 %copy-start.47 = (f32[16,1,256]{2,1,0:T(1,128)S(1)}, f32[16,1,256]{2,1,0:T(1,128)}, u32[]{:S(2)}) copy-start(f32[16,1,256]{2,1,0:T(1,128)} %copy-done.46) | copy-start | bytes 49156
  233.6 44.5 %copy-start.16 = (bf16[16,128,256]{2,1,0:T(8,128)(2,1)}, bf16[16,128,256]{2,1,0:T(8,128)(2,1)S(1)}, u32[]{:S(2)}) copy-start(bf16[16,128,256]{2,1,0:T(8,128)(2,1)S(1)} %get-tuple-element.69.glog_ref) | copy-start | bytes 3145732
  278.1 11.4 %copy-start.41 = (f32[136,128]{1,0:T(8,128)S(1)}, f32[136,128]{1,0:T(8,128)}, u32[]{:S(2)}) copy-start(f32[136,128]{1,0:T(8,128)} %copy-done.40) | copy-start | bytes 208900
  278.1 34.4 %all-to-all-start.6 = ((bf16[16,256,128]{2,1,0:T(8,128)(2,1)}), bf16[16,256,128]{2,1,0:T(8,128)(2,1)}, u32[]{:S(2)}, u32[]{:S(2)}) async-start(bf16[16,256,128]{2,1,0:T(8,128)(2,1)} %get-tuple-element.75), calls=%async_computation.6 | async-start | bytes 2097152 | tf_op jit(solution)/shard_map/all_to_all | solution.py:527
  290.8 21.8 %copy-start.11 = (bf16[8,2,256,256]{3,2,1,0:T(8,128)(2,1)S(1)}, bf16[8,2,256,256]{3,2,1,0:T(8,128)(2,1)}, u32[]{:S(2)}) copy-start(bf16[8,2,256,256]{3,2,1,0:T(8,128)(2,1)} %copy-done.10) | copy-start | bytes 6291460
  317.7 52.7 %all-to-all-start.7 = ((bf16[16,576,128]{2,1,0:T(8,128)(2,1)}), bf16[16,576,128]{2,1,0:T(8,128)(2,1)S(1)}, u32[]{:S(2)}, u32[]{:S(2)}) async-start(bf16[16,576,128]{2,1,0:T(8,128)(2,1)} %shard_map.168), calls=%async_computation.7 | async-start | bytes 4718592 | tf_op jit(solution)/shard_map/all_to_all | solution.py:527
  326.8 44.9 %copy-start.15 = (bf16[16,128,256]{2,1,0:T(8,128)(2,1)S(1)}, bf16[16,128,256]{2,1,0:T(8,128)(2,1)}, u32[]{:S(2)}) copy-start(bf16[16,128,256]{2,1,0:T(8,128)(2,1)} %copy-done.14) | copy-start | bytes 3145732
  380.2 27.3 %copy-start.25 = (bf16[128,640]{1,0:T(8,128)(2,1)S(1)}, bf16[128,640]{1,0:T(8,128)(2,1)}, u32[]{:S(2)}) copy-start(bf16[128,640]{1,0:T(8,128)(2,1)} %get-tuple-element.94.w_ref) | copy-start | bytes 491524
  404.0 16.8 %all-to-all-start.9 = ((bf16[16,112,128]{2,1,0:T(8,128)(2,1)}), bf16[16,112,128]{2,1,0:T(8,128)(2,1)S(1)}, u32[]{:S(2)}, u32[]{:S(2)}) async-start(bf16[16,112,128]{2,1,0:T(8,128)(2,1)} %shard_map.172), calls=%async_computation.9 | async-start | bytes 917504 | tf_op jit(solution)/shard_map/all_to_all | solution.py:527
  (33 other events, 51.9 us)

commit v4 on v3

--- a/solution.py
+++ b/solution.py
@@ -11,7 +11,7 @@
 AXES = ("row", "col")
 F32 = jnp.float32
 BF16 = jnp.bfloat16
-VMEM_BYTES = 50 * 1024 * 1024
+VMEM_BYTES = 24 * 1024 * 1024
 LARGE_VMEM_BYTES = 60 * 1024 * 1024
 
 
@@ -382,16 +382,15 @@
             pair_ref[t * q + a] = upstream[:, a * cols : (a + 1) * cols].T.astype(BF16)
 
 
-def spread_kernel(factor, early_ref, late_ref, out_ref):
-    early = (jnp.sum(early_ref[...].astype(F32), 0) * factor).astype(BF16)
-    late = (jnp.sum(late_ref[...].astype(F32), 0) * factor).astype(BF16)
-    out_ref[...] = jnp.broadcast_to(jnp.concatenate([early, late], 0)[None], out_ref.shape)
-
-
-def unpack_kernel(early_rows, got_ref, proj_ref, ow_ref, inorm_ref, hnorm_ref, chain_ref):
+def spread_kernel(got_ref, out_ref):
+    total = jnp.sum(got_ref[...].astype(F32), 0).astype(BF16)
+    out_ref[...] = jnp.broadcast_to(total[None], out_ref.shape)
+
+
+def unpack_kernel(factor, early_ref, late_ref, proj_ref, ow_ref, inorm_ref, hnorm_ref, chain_ref):
     width = ow_ref.shape[1]
-    early = got_ref[:, :early_rows, :].astype(F32).reshape(-1, width)
-    late = got_ref[:, early_rows:, :].astype(F32).reshape(-1, width)
+    early = early_ref[...].astype(F32) * factor
+    late = late_ref[...].astype(F32).reshape(-1, width) * factor
     for n in range(5):
         rows, lanes = slice(n * width, (n + 1) * width), slice(n * width, (n + 1) * width)
         proj_ref[0, :, lanes] = late[rows]
@@ -406,7 +405,7 @@
     chain_ref[...] = jnp.concatenate([vectors[7:8], vectors[4:5]], 0)
 
 
-def cell_call(kernel, steps, ins, outs, scratch, prefetch=(), flops=0, vmem=VMEM_BYTES):
+def cell_call(kernel, steps, ins, outs, scratch, prefetch=(), flops=0):
     def spec(shape, how):
         if how is None:
             return pl.BlockSpec(shape, lambda *s: (0,) * len(shape))
@@ -430,7 +429,7 @@
             scratch_shapes=scratch,
         ),
         out_shape=[jax.ShapeDtypeStruct(s, t) for (s, t), _ in outs],
-        compiler_params=pltpu.CompilerParams(vmem_limit_bytes=vmem),
+        compiler_params=pltpu.CompilerParams(vmem_limit_bytes=LARGE_VMEM_BYTES),
         cost_estimate=pl.CostEstimate(flops=flops, bytes_accessed=int(moved), transcendentals=0),
     )(*prefetch, *[a for a, _ in ins])
 
@@ -488,8 +487,7 @@
             out_ref[ch, sub] = get_channel(edges, ch, sub, 2, dims)
 
 
-def product_grad_kernel(dims, outgoing, sides_ref, grad_ref, *rest):
-    out_ref, grad, result = rest[-3:]
+def product_grad_kernel(dims, outgoing, sides_ref, grad_ref, out_ref, grad, result):
     widen(grad_ref, grad)
     for ch in range(dims[3]):
         left, right = sides_ref[ch, 0], sides_ref[ch, 1]
@@ -503,8 +501,6 @@
         put_channel(result, grad_left, ch, 0, 2, dims)
         put_channel(result, grad_right, ch, 1, 2, dims)
     narrow(result, out_ref)
-    for terms_ref in rest[:-3]:
-        out_ref[:, out_ref.shape[1] - terms_ref.shape[1] :, :] = terms_ref[...]
 
 
 def whole_call(kernel, ins, outs, scratch, flops):
@@ -579,11 +575,10 @@
             functools.partial(assemble_kernel, dims), [edges], [((cpd, 2, length, length), BF16)], [wide(2)], 0
         )
 
-    def product_grad(sides, grad, outgoing, *terms):
-        out_rows = 2 * side + sum(t.shape[1] for t in terms)
+    def product_grad(sides, grad, outgoing):
         return whole_call(
-            functools.partial(product_grad_kernel, dims, outgoing), [sides, grad, *terms],
-            [((devices, out_rows, cols), BF16)], [wide(1), wide(2)], 2 * tri_flops,
+            functools.partial(product_grad_kernel, dims, outgoing), [sides, grad],
+            [((devices, 2 * side, cols), BF16)], [wide(1), wide(2)], 2 * tri_flops,
         )
 
     def halves(grads):
@@ -608,7 +603,7 @@
             (input_gain, None), (input_bias, None),
         ],
         [((edge_shape, BF16), 2)], [vec(2), pltpu.VMEM((5 * hidden, width), BF16)],
-        prefetch=scalars, flops=4 * cell_flops, vmem=LARGE_VMEM_BYTES,
+        prefetch=scalars, flops=4 * cell_flops,
     )
     got0 = exchange(edges0)
     z0, up, gate0, flags = cell_call(
@@ -682,7 +677,8 @@
         flops=13 * cell_flops,
     )
 
-    made_grads0 = product_grad(sides0, got_grad0, True, early.reshape(devices, early_rows, hidden))
+    early = lax.psum(early, AXES)
+    made_grads0 = product_grad(sides0, got_grad0, True)
     grads0 = exchange(made_grads0)
     fac0, low0, nrm0, inv0 = keep(0, after(z0, made_grads0), False)
     grads0 = after(grads0, nrm0)
@@ -699,13 +695,9 @@
         + [(fac0, 0), (nrm0, 0), (inv0, 0), (glog0, 0), (up0, 0), (weight[0], None), (input_gain, None)],
         [((pair_rep.shape, BF16), 0)], [vec(1)], flops=5 * cell_flops,
     )
-    (spread,) = cell_call(
-        functools.partial(spread_kernel, 1.0 / length), 1,
-        [(grads0, (1, 2 * side // early_rows, early_rows)), (got_late, None)],
-        [(((devices, early_rows + late_rows, hidden), BF16), None)], [],
-    )
+    spread = whole_call(spread_kernel, [after(got_late, grad_pair)], [((devices, late_rows, hidden), BF16)], [], 0)
     proj, out, inorm, hnorm, chain = whole_call(
-        functools.partial(unpack_kernel, early_rows), [exchange(spread)],
+        functools.partial(unpack_kernel, 1.0 / length), [early, exchange(spread)],
         [
             ((2, width, 5 * hidden), F32), ((2, hidden, hidden), F32), ((2, 2, hidden), F32),
             ((2, 2, hidden), F32), ((2, hidden), F32),

time: 424 us -> 511 us (1.21)
  waiting for transfers between devices: 214 us -> 286 us
  local copies, waits for them, and re-layouts: 31.5 us -> 14.3 us
  blocking collectives: 21.2 us -> 36.2 us
  between operations: 1.19 us -> 14.2 us
  Pallas kernels: 80.4 us -> 87.3 us
    psum x0 -> x1, waiting for transfers between devices: none -> 94.1 us  [shards(): early = lax.psum(early, AXES)]
    all_to_all x9, waiting for transfers between devices: 214 us -> 191 us  [exchange(): return lax.all_to_all(array, AXES, split_axis=0, concat_axis=0, tiled=True)]
    unnamed x114 -> x26, local copies, waits for them, and re-layouts: 29 us -> 11.3 us
    all_to_all x1, blocking collectives: 21.2 us -> 36.2 us  [exchange(): return lax.all_to_all(array, AXES, split_axis=0, concat_axis=0, tiled=True)]
    pallas_call x13 -> x12, Pallas kernels: 62 us -> 73.9 us  [cell_call(): pl.pallas_call(kernel, grid_spec=pltpu.PrefetchScalarGridSpec(num_scalar_...]
    pallas_call x7 -> x8, Pallas kernels: 18.4 us -> 13.4 us  [whole_call(): pl.pallas_call(kernel, in_specs=[pl.BlockSpec(memory_space=pltpu.VMEM)] *...]
  transfers between devices with their start and end apart: 9 -> 10, of which waited for: 9 -> 9; matrix products, arithmetic and copies ran while one was open for 1% -> 1% of each run, Pallas kernels for 9% -> 9%
where the time goes in v4:
time: 511 us; the launch traced here: 509 us
  waiting for transfers between devices  286 us (56%)
  Pallas kernels  87.3 us (17%)
  starting transfers between devices  70.6 us (14%)
  blocking collectives  36.2 us (7%)
  local copies, waits for them, and re-layouts  14.3 us (3%)
  between operations  14.2 us (3%)
    all_to_all x9, waiting for transfers between devices, exchange(): return lax.all_to_all(array, AXES, split_axis=0, concat_axis=0, tiled=True)  191 us
    psum x1, waiting for transfers between devices, shards(): early = lax.psum(early, AXES)  94.1 us
    pallas_call x12, Pallas kernels, cell_call(): pl.pallas_call(kernel, grid_spec=pltpu.PrefetchScalarGridSpec(num_scalar_...  73.9 us
    all_to_all x9, starting transfers between devices, exchange(): return lax.all_to_all(array, AXES, split_axis=0, concat_axis=0, tiled=True)  70.6 us
    all_to_all x1, blocking collectives, exchange(): return lax.all_to_all(array, AXES, split_axis=0, concat_axis=0, tiled=True)  36.2 us
    pallas_call x8, Pallas kernels, whole_call(): pl.pallas_call(kernel, in_specs=[pl.BlockSpec(memory_space=pltpu.VMEM)] *...  13.4 us
    unnamed x26, local copies, waits for them, and re-layouts  11.3 us
  transfers between devices with their start and end apart: 10, of which 9 were waited for; matrix products, arithmetic and copies ran while one was open for 1% of the time, Pallas kernels for 9%

profile of v4, /device:TPU:0, one launch (start us, length us, event | category | flops | bytes accessed | tf_op | source)
XLA Modules:
  0.0 509.2 jit_solution(15583722361906322260)
XLA Ops:
  7.8 6.1 %shard_map.154 = bf16[16,2,256,128]{3,2,1,0:T(8,128)(2,1)} custom-call(s32[256]{0:T(256)} %mask_smem.3, s32[256]{0:T(256)} %chain_smem.3, s32[2]{0:T(128)} %pad_add_fusion.start_smem, bf16[32,128,128]{2,1,0:T(8,128)(2,1)} %pair_ref.2, s32[2,128]{1,0:T(2,128)} %bitcast.29, s32[2,128]{1,0:T(2,128)} %bitcast.31, bf16[2,128,640]{2,1,0:T(8,128)(2,1)} %w_ref.1, ...), custom_call_target="tpu_custom_call" | custom-call | flops 536870912 | bytes 3477504 | tf_op jit(solution)/shard_map/pallas_call | solution.py:422
  13.8 7.5 %all-to-all-start = ((bf16[16,2,256,128]{3,2,1,0:T(8,128)(2,1)}), bf16[16,2,256,128]{3,2,1,0:T(8,128)(2,1)S(1)}, u32[]{:S(2)}, u32[]{:S(2)}) async-start(bf16[16,2,256,128]{3,2,1,0:T(8,128)(2,1)} %shard_map.154), calls=%async_computation | async-start | bytes 4194304 | tf_op jit(solution)/shard_map/all_to_all | solution.py:523
  23.0 5.7 %shard_map.155 = (bf16[16,128,256]{2,1,0:T(8,128)(2,1)}, bf16[16,128,256]{2,1,0:T(8,128)(2,1)}, bf16[16,128,256]{2,1,0:T(8,128)(2,1)}, f32[16,2,256]{2,1,0:T(2,128)}) custom-call(s32[256]{0:T(256)} %mask_smem.3, s32[256]{0:T(256)} %chain_smem.3, s32[2]{0:T(128)} %pad_add_fusion.start_smem, bf16[32,128,128]{2,1,0:T(8,128)(2,1)} %pair_ref.2, ...), custom_call_target="tpu_custom_call" | custom-call | flops 268435456 | bytes 5444608 | tf_op jit(solution)/shard_map/pallas_call | solution.py:422
  28.7 33.8 %all-to-all-done.edges_ref = bf16[16,2,256,128]{3,2,1,0:T(8,128)(2,1)S(1)} async-done(((bf16[16,2,256,128]{3,2,1,0:T(8,128)(2,1)}), bf16[16,2,256,128]{3,2,1,0:T(8,128)(2,1)S(1)}, u32[]{:S(2)}, u32[]{:S(2)}) %all-to-all-start) | async-done | bytes 2097184 | tf_op jit(solution)/shard_map/all_to_all | solution.py:523
  64.7 11.2 %all-to-all-start.1 = ((bf16[16,256,128]{2,1,0:T(8,128)(2,1)}), bf16[16,256,128]{2,1,0:T(8,128)(2,1)S(1)}, u32[]{:S(2)}, u32[]{:S(2)}) async-start(bf16[16,256,128]{2,1,0:T(8,128)(2,1)} %shard_map.156), calls=%async_computation.1 | async-start | bytes 2097152 | tf_op jit(solution)/shard_map/all_to_all | solution.py:523
  80.7 18.1 %all-to-all-done.1.prod_ref = bf16[16,256,128]{2,1,0:T(8,128)(2,1)S(1)} async-done(((bf16[16,256,128]{2,1,0:T(8,128)(2,1)}), bf16[16,256,128]{2,1,0:T(8,128)(2,1)S(1)}, u32[]{:S(2)}, u32[]{:S(2)}) %all-to-all-start.1) | async-done | bytes 1048608 | tf_op jit(solution)/shard_map/all_to_all | solution.py:523
  99.8 7.2 %shard_map.158 = (bf16[16,2,256,128]{3,2,1,0:T(8,128)(2,1)}, f32[16,128,256]{2,1,0:T(8,128)}) custom-call(bf16[16,256,128]{2,1,0:T(8,128)(2,1)} %copy-done.8, bf16[16,128,256]{2,1,0:T(8,128)(2,1)} %get-tuple-element.77.z_ref, bf16[16,128,256]{2,1,0:T(8,128)(2,1)} %get-tuple-element.56.gate_ref, f32[16,2,256]{2,1,0:T(2,128)} %get-tuple-element.57.flags_ref, ...), custom_call_target="tpu_custom_call" | custom-call | flops 671088640 | bytes 7573504 | tf_op jit(solution)/shard_map/pallas_call | solution.py:422
  107.0 6.9 %all-to-all-start.2 = ((bf16[16,2,256,128]{3,2,1,0:T(8,128)(2,1)}), bf16[16,2,256,128]{3,2,1,0:T(8,128)(2,1)S(1)}, u32[]{:S(2)}, u32[]{:S(2)}) async-start(bf16[16,2,256,128]{3,2,1,0:T(8,128)(2,1)} %get-tuple-element.58), calls=%async_computation.2 | async-start | bytes 4194304 | tf_op jit(solution)/shard_map/all_to_all | solution.py:523
  113.9 6.2 %shard_map.159 = (bf16[16,512,256]{2,1,0:T(8,128)(2,1)}, bf16[16,128,256]{2,1,0:T(8,128)(2,1)}, bf16[16,128,256]{2,1,0:T(8,128)(2,1)}, f32[16,1,256]{2,1,0:T(1,128)}, bf16[16,128,256]{2,1,0:T(8,128)(2,1)}) custom-call(f32[16,128,256]{2,1,0:T(8,128)} %get-tuple-element.60.z_ref, f32[16,2,256]{2,1,0:T(2,128)} %get-tuple-element.57.flags_ref, ...), custom_call_target="tpu_custom_call" | custom-call | flops 671088640 | bytes 9653248 | tf_op jit(solution)/shard_map/pallas_call | solution.py:422
  120.0 34.9 %all-to-all-done.2.edges_ref = bf16[16,2,256,128]{3,2,1,0:T(8,128)(2,1)S(1)} async-done(((bf16[16,2,256,128]{3,2,1,0:T(8,128)(2,1)}), bf16[16,2,256,128]{3,2,1,0:T(8,128)(2,1)S(1)}, u32[]{:S(2)}, u32[]{:S(2)}) %all-to-all-start.2) | async-done | bytes 2097184 | tf_op jit(solution)/shard_map/all_to_all | solution.py:523
  155.0 2.3 shard_map.160
  157.3 11.2 %all-to-all-start.3 = ((bf16[16,256,128]{2,1,0:T(8,128)(2,1)}), bf16[16,256,128]{2,1,0:T(8,128)(2,1)S(1)}, u32[]{:S(2)}, u32[]{:S(2)}) async-start(bf16[16,256,128]{2,1,0:T(8,128)(2,1)} %shard_map.160), calls=%async_computation.3 | async-start | bytes 2097152 | tf_op jit(solution)/shard_map/all_to_all | solution.py:523
  171.2 20.2 %all-to-all-done.3.prod_ref = bf16[16,256,128]{2,1,0:T(8,128)(2,1)S(1)} async-done(((bf16[16,256,128]{2,1,0:T(8,128)(2,1)}), bf16[16,256,128]{2,1,0:T(8,128)(2,1)S(1)}, u32[]{:S(2)}, u32[]{:S(2)}) %all-to-all-start.3) | async-done | bytes 1048608 | tf_op jit(solution)/shard_map/all_to_all | solution.py:523
  192.4 4.7 shard_map.162
  197.1 7.0 %all-to-all-start.4 = ((bf16[16,256,128]{2,1,0:T(8,128)(2,1)}), bf16[16,256,128]{2,1,0:T(8,128)(2,1)S(1)}, u32[]{:S(2)}, u32[]{:S(2)}) async-start(bf16[16,256,128]{2,1,0:T(8,128)(2,1)} %shard_map.162), calls=%async_computation.4 | async-start | bytes 2097152 | tf_op jit(solution)/shard_map/all_to_all | solution.py:523
  204.1 3.7 shard_map.163
  207.8 19.2 %all-to-all-done.4.grad_ref = bf16[16,256,128]{2,1,0:T(8,128)(2,1)S(1)} async-done(((bf16[16,256,128]{2,1,0:T(8,128)(2,1)}), bf16[16,256,128]{2,1,0:T(8,128)(2,1)S(1)}, u32[]{:S(2)}, u32[]{:S(2)}) %all-to-all-start.4) | async-done | bytes 1048608 | tf_op jit(solution)/shard_map/all_to_all | solution.py:523
  230.2 6.9 %all-to-all-start.5 = ((bf16[16,512,128]{2,1,0:T(8,128)(2,1)}), bf16[16,512,128]{2,1,0:T(8,128)(2,1)S(1)}, u32[]{:S(2)}, u32[]{:S(2)}) async-start(bf16[16,512,128]{2,1,0:T(8,128)(2,1)} %copy-done.4), calls=%async_computation.5 | async-start | bytes 4194304 | tf_op jit(solution)/shard_map/all_to_all | solution.py:523
  237.8 4.9 shard_map.165
  242.7 35.5 %all-to-all-done.5.left_ref.right_ref = bf16[16,512,128]{2,1,0:T(8,128)(2,1)S(1)} async-done(((bf16[16,512,128]{2,1,0:T(8,128)(2,1)}), bf16[16,512,128]{2,1,0:T(8,128)(2,1)S(1)}, u32[]{:S(2)}, u32[]{:S(2)}) %all-to-all-start.5) | async-done | bytes 2097184 | tf_op jit(solution)/shard_map/all_to_all | solution.py:523
  279.6 8.6 %shard_map.166 = (f32[16,128,256]{2,1,0:T(8,128)}, bf16[16,256,128]{2,1,0:T(8,128)(2,1)}) custom-call(bf16[16,512,128]{2,1,0:T(8,128)(2,1)} %copy-done.6, bf16[16,512,128]{2,1,0:T(8,128)(2,1)} %copy-done.6, bf16[16,512,256]{2,1,0:T(8,128)(2,1)} %get-tuple-element.72.fac_ref, bf16[16,128,256]{2,1,0:T(8,128)(2,1)} %get-tuple-element.73.nrm_ref, ...), custom_call_target="tpu_custom_call" | custom-call | flops 805306368 | bytes 17008640 | tf_op jit(solution)/shard_map/pallas_call | solution.py:422
  288.1 36.2 %all_to_all.50.grad_ref = bf16[16,256,128]{2,1,0:T(8,128)(2,1)S(1)} all-to-all(bf16[16,256,128]{2,1,0:T(8,128)(2,1)} %get-tuple-element.76), channel_id=1, replica_groups=mesh['grp'=2,'row'=8,'col'=2] {'row','col'}, dimensions={0} | all-to-all | bytes 2097152 | tf_op jit(solution)/shard_map/all_to_all | solution.py:523
  324.3 2.9 shard_map.167
  327.3 5.0 all-to-all-start.7
  332.3 8.5 %shard_map.169 = (bf16[16,128,256]{2,1,0:T(8,128)(2,1)}, bf16[1024,128]{1,0:T(8,128)(2,1)}) custom-call(bf16[16,512,128]{2,1,0:T(8,128)(2,1)} %copy-done.6, bf16[16,512,128]{2,1,0:T(8,128)(2,1)} %copy-done.6, bf16[16,512,256]{2,1,0:T(8,128)(2,1)} %get-tuple-element.72.fac_ref, bf16[16,128,256]{2,1,0:T(8,128)(2,1)} %get-tuple-element.83.low_ref, ...), custom_call_target="tpu_custom_call" | custom-call | flops 1744830464 | bytes 17373184 | tf_op jit(solution)/shard_map/pallas_call | solution.py:422
  340.7 5.5 %shard_map.168 = (bf16[16,512,256]{2,1,0:T(8,128)(2,1)}, bf16[16,128,256]{2,1,0:T(8,128)(2,1)}, bf16[16,128,256]{2,1,0:T(8,128)(2,1)}, f32[16,1,256]{2,1,0:T(1,128)}) custom-call(bf16[16,128,256]{2,1,0:T(8,128)(2,1)} %get-tuple-element.77.z_ref, f32[16,2,256]{2,1,0:T(2,128)} %get-tuple-element.57.flags_ref, bf16[640,128]{1,0:T(8,128)(2,1)} %copy.17.wt_ref, ...), custom_call_target="tpu_custom_call" | custom-call | flops 671088640 | bytes 7556096 | tf_op jit(solution)/shard_map/pallas_call | solution.py:422
  346.3 27.1 %all-to-all-done.7.left_ref.right_ref = bf16[16,512,128]{2,1,0:T(8,128)(2,1)S(1)} async-done(((bf16[16,512,128]{2,1,0:T(8,128)(2,1)}), bf16[16,512,128]{2,1,0:T(8,128)(2,1)S(1)}, u32[]{:S(2)}, u32[]{:S(2)}) %all-to-all-start.7) | async-done | bytes 2097184 | tf_op jit(solution)/shard_map/all_to_all | solution.py:523
  374.7 6.2 %shard_map.170 = bf16[768,128]{1,0:T(8,128)(2,1)} custom-call(bf16[16,512,128]{2,1,0:T(8,128)(2,1)} %copy-done.7, bf16[16,512,128]{2,1,0:T(8,128)(2,1)} %copy-done.7, bf16[16,512,256]{2,1,0:T(8,128)(2,1)} %get-tuple-element.80.fac_ref, bf16[16,128,256]{2,1,0:T(8,128)(2,1)} %get-tuple-element.81.low_ref, bf16[16,128,256]{2,1,0:T(8,128)(2,1)} %get-tuple-element.78.nrm_ref, ...), custom_call_target="tpu_custom_call" | custom-call | flops 1342177280 | bytes 11894784 | tf_op jit(solution)/shard_map/pallas_call | solution.py:422
  380.9 11.2 %all-to-all-start.8 = ((bf16[16,48,128]{2,1,0:T(8,128)(2,1)}), bf16[16,48,128]{2,1,0:T(8,128)(2,1)S(1)}, u32[]{:S(2)}, u32[]{:S(2)}) async-start(bf16[16,48,128]{2,1,0:T(8,128)(2,1)} %bitcast.25), calls=%async_computation.8 | async-start | bytes 393216 | tf_op jit(solution)/shard_map/all_to_all | solution.py:523
  392.2 6.7 %shard_map.171 = bf16[32,128,128]{2,1,0:T(8,128)(2,1)} custom-call(bf16[16,512,128]{2,1,0:T(8,128)(2,1)} %copy-done.7, bf16[16,512,128]{2,1,0:T(8,128)(2,1)} %copy-done.7, bf16[16,512,256]{2,1,0:T(8,128)(2,1)} %get-tuple-element.80.fac_ref, bf16[16,128,256]{2,1,0:T(8,128)(2,1)} %get-tuple-element.78.nrm_ref, f32[16,1,256]{2,1,0:T(1,128)} %get-tuple-element.88.inv_ref, ...), custom_call_target="tpu_custom_call" | custom-call | flops 671088640 | bytes 13812736 | tf_op jit(solution)/shard_map/pallas_call | solution.py:422
  401.9 3.7 all-to-all-start.9
  406.3 94.1 %all-reduce.2.cloned.1.call-done.early_ref = bf16[1024,128]{1,0:T(8,128)(2,1)} async-done(((bf16[1024,128]{1,0:T(8,128)(2,1)}), bf16[1024,128]{1,0:T(8,128)(2,1)}) %all-reduce.2.cloned.1.call-update) | async-done | bytes 262160 | tf_op jit(solution)/shard_map/psum | solution.py:680
  (41 shorter events, 26.1 us)
Async XLA Ops:
  13.8 7.5 %copy-start.10 = (bf16[2,128,640]{2,1,0:T(8,128)(2,1)S(1)}, bf16[2,128,640]{2,1,0:T(8,128)(2,1)}, u32[]{:S(2)}) copy-start(bf16[2,128,640]{2,1,0:T(8,128)(2,1)} %w_ref.1) | copy-start | bytes 983044
  13.8 48.6 %all-to-all-start = ((bf16[16,2,256,128]{3,2,1,0:T(8,128)(2,1)}), bf16[16,2,256,128]{3,2,1,0:T(8,128)(2,1)S(1)}, u32[]{:S(2)}, u32[]{:S(2)}) async-start(bf16[16,2,256,128]{3,2,1,0:T(8,128)(2,1)} %shard_map.154), calls=%async_computation | async-start | bytes 4194304 | tf_op jit(solution)/shard_map/all_to_all | solution.py:523
  62.5 13.5 %copy-start.11 = (bf16[2,128,128]{2,1,0:T(8,128)(2,1)S(1)}, bf16[2,128,128]{2,1,0:T(8,128)(2,1)}, u32[]{:S(2)}) copy-start(bf16[2,128,128]{2,1,0:T(8,128)(2,1)} %param.16) | copy-start | bytes 196612
  64.7 34.2 %all-to-all-start.1 = ((bf16[16,256,128]{2,1,0:T(8,128)(2,1)}), bf16[16,256,128]{2,1,0:T(8,128)(2,1)S(1)}, u32[]{:S(2)}, u32[]{:S(2)}) async-start(bf16[16,256,128]{2,1,0:T(8,128)(2,1)} %shard_map.156), calls=%async_computation.1 | async-start | bytes 2097152 | tf_op jit(solution)/shard_map/all_to_all | solution.py:523
  79.4 1.4 copy-start
  98.9 1.0 copy-start.8
  107.0 48.0 %all-to-all-start.2 = ((bf16[16,2,256,128]{3,2,1,0:T(8,128)(2,1)}), bf16[16,2,256,128]{3,2,1,0:T(8,128)(2,1)S(1)}, u32[]{:S(2)}, u32[]{:S(2)}) async-start(bf16[16,2,256,128]{3,2,1,0:T(8,128)(2,1)} %get-tuple-element.58), calls=%async_computation.2 | async-start | bytes 4194304 | tf_op jit(solution)/shard_map/all_to_all | solution.py:523
  157.3 34.2 %all-to-all-start.3 = ((bf16[16,256,128]{2,1,0:T(8,128)(2,1)}), bf16[16,256,128]{2,1,0:T(8,128)(2,1)S(1)}, u32[]{:S(2)}, u32[]{:S(2)}) async-start(bf16[16,256,128]{2,1,0:T(8,128)(2,1)} %shard_map.160), calls=%async_computation.3 | async-start | bytes 2097152 | tf_op jit(solution)/shard_map/all_to_all | solution.py:523
  169.8 1.4 copy-start.2
  191.5 1.0 copy-start.9
  197.1 29.9 %copy-start.3 = (bf16[8,2,256,256]{3,2,1,0:T(8,128)(2,1)S(1)}, bf16[8,2,256,256]{3,2,1,0:T(8,128)(2,1)}, u32[]{:S(2)}) copy-start(bf16[8,2,256,256]{3,2,1,0:T(8,128)(2,1)} %copy-done.2) | copy-start | bytes 6291460
  197.1 29.9 %all-to-all-start.4 = ((bf16[16,256,128]{2,1,0:T(8,128)(2,1)}), bf16[16,256,128]{2,1,0:T(8,128)(2,1)S(1)}, u32[]{:S(2)}, u32[]{:S(2)}) async-start(bf16[16,256,128]{2,1,0:T(8,128)(2,1)} %shard_map.162), calls=%async_computation.4 | async-start | bytes 2097152 | tf_op jit(solution)/shard_map/all_to_all | solution.py:523
  228.8 1.4 copy-start.4
  230.2 48.0 %all-to-all-start.5 = ((bf16[16,512,128]{2,1,0:T(8,128)(2,1)}), bf16[16,512,128]{2,1,0:T(8,128)(2,1)S(1)}, u32[]{:S(2)}, u32[]{:S(2)}) async-start(bf16[16,512,128]{2,1,0:T(8,128)(2,1)} %copy-done.4), calls=%async_computation.5 | async-start | bytes 4194304 | tf_op jit(solution)/shard_map/all_to_all | solution.py:523
  278.2 1.4 copy-start.6
  288.1 36.2 %copy-start.1 = (bf16[8,2,256,256]{3,2,1,0:T(8,128)(2,1)S(1)}, bf16[8,2,256,256]{3,2,1,0:T(8,128)(2,1)}, u32[]{:S(2)}) copy-start(bf16[8,2,256,256]{3,2,1,0:T(8,128)(2,1)} %copy-done) | copy-start | bytes 6291460
  327.3 46.1 %all-to-all-start.7 = ((bf16[16,512,128]{2,1,0:T(8,128)(2,1)}), bf16[16,512,128]{2,1,0:T(8,128)(2,1)S(1)}, u32[]{:S(2)}, u32[]{:S(2)}) async-start(bf16[16,512,128]{2,1,0:T(8,128)(2,1)} %shard_map.167), calls=%async_computation.7 | async-start | bytes 4194304 | tf_op jit(solution)/shard_map/all_to_all | solution.py:523
  373.4 1.4 copy-start.7
  380.9 20.2 %all-to-all-start.8 = ((bf16[16,48,128]{2,1,0:T(8,128)(2,1)}), bf16[16,48,128]{2,1,0:T(8,128)(2,1)S(1)}, u32[]{:S(2)}, u32[]{:S(2)}) async-start(bf16[16,48,128]{2,1,0:T(8,128)(2,1)} %bitcast.25), calls=%async_computation.8 | async-start | bytes 393216 | tf_op jit(solution)/shard_map/all_to_all | solution.py:523
  401.9 98.6 %all-to-all-start.9 = ((bf16[16,48,128]{2,1,0:T(8,128)(2,1)}), bf16[16,48,128]{2,1,0:T(8,128)(2,1)S(1)}, u32[]{:S(2)}, u32[]{:S(2)}) async-start(bf16[16,48,128]{2,1,0:T(8,128)(2,1)} %shard_map.172), calls=%async_computation.9 | async-start | bytes 393216 | tf_op jit(solution)/shard_map/all_to_all | solution.py:523
  405.6 94.9 %all-reduce.2.cloned.1.call-start = ((), (), s32[]{:S(2)}) async-start(), calls=%async_computation.10 | async-start | bytes 524288 | tf_op jit(solution)/shard_map/psum | solution.py:680
  500.5 1.0 copy-start.5
Sparse Core Ops, SparseCore 0:
  410.4 90.0 all-reduce.1

commit v5 on v3

--- a/solution.py
+++ b/solution.py
@@ -11,8 +11,9 @@
 AXES = ("row", "col")
 F32 = jnp.float32
 BF16 = jnp.bfloat16
-VMEM_BYTES = 50 * 1024 * 1024
-LARGE_VMEM_BYTES = 60 * 1024 * 1024
+CHANNEL_VMEM = 24 * 1024 * 1024
+CELL_VMEM = 50 * 1024 * 1024
+ALL_VMEM = 60 * 1024 * 1024
 
 
 def dot(a, b, ca, cb):
@@ -382,16 +383,16 @@
             pair_ref[t * q + a] = upstream[:, a * cols : (a + 1) * cols].T.astype(BF16)
 
 
-def spread_kernel(factor, early_ref, late_ref, out_ref):
-    early = (jnp.sum(early_ref[...].astype(F32), 0) * factor).astype(BF16)
-    late = (jnp.sum(late_ref[...].astype(F32), 0) * factor).astype(BF16)
+def spread_kernel(early_ref, late_ref, out_ref):
+    early = jnp.sum(early_ref[...].astype(F32), 0).astype(BF16)
+    late = jnp.sum(late_ref[...].astype(F32), 0).astype(BF16)
     out_ref[...] = jnp.broadcast_to(jnp.concatenate([early, late], 0)[None], out_ref.shape)
 
 
-def unpack_kernel(early_rows, got_ref, proj_ref, ow_ref, inorm_ref, hnorm_ref, chain_ref):
+def unpack_kernel(factor, early_rows, got_ref, proj_ref, ow_ref, inorm_ref, hnorm_ref, chain_ref):
     width = ow_ref.shape[1]
-    early = got_ref[:, :early_rows, :].astype(F32).reshape(-1, width)
-    late = got_ref[:, early_rows:, :].astype(F32).reshape(-1, width)
+    early = got_ref[:, :early_rows, :].astype(F32).reshape(-1, width) * factor
+    late = got_ref[:, early_rows:, :].astype(F32).reshape(-1, width) * factor
     for n in range(5):
         rows, lanes = slice(n * width, (n + 1) * width), slice(n * width, (n + 1) * width)
         proj_ref[0, :, lanes] = late[rows]
@@ -406,7 +407,7 @@
     chain_ref[...] = jnp.concatenate([vectors[7:8], vectors[4:5]], 0)
 
 
-def cell_call(kernel, steps, ins, outs, scratch, prefetch=(), flops=0, vmem=VMEM_BYTES):
+def cell_call(kernel, steps, ins, outs, scratch, prefetch=(), flops=0, vmem=CELL_VMEM):
     def spec(shape, how):
         if how is None:
             return pl.BlockSpec(shape, lambda *s: (0,) * len(shape))
@@ -518,7 +519,7 @@
         out_specs=specs if len(outs) > 1 else specs[0],
         out_shape=shapes if len(outs) > 1 else shapes[0],
         scratch_shapes=scratch,
-        compiler_params=pltpu.CompilerParams(vmem_limit_bytes=VMEM_BYTES),
+        compiler_params=pltpu.CompilerParams(vmem_limit_bytes=CHANNEL_VMEM),
         cost_estimate=pl.CostEstimate(flops=flops, bytes_accessed=int(moved), transcendentals=0),
     )(*ins)
 
@@ -608,7 +609,7 @@
             (input_gain, None), (input_bias, None),
         ],
         [((edge_shape, BF16), 2)], [vec(2), pltpu.VMEM((5 * hidden, width), BF16)],
-        prefetch=scalars, flops=4 * cell_flops, vmem=LARGE_VMEM_BYTES,
+        prefetch=scalars, flops=4 * cell_flops, vmem=ALL_VMEM,
     )
     got0 = exchange(edges0)
     z0, up, gate0, flags = cell_call(
@@ -690,22 +691,22 @@
         functools.partial(last_terms_kernel, cpd, q), steps,
         halves(grads0) + [(fac0, 0), (low0, 0), (nrm0, 0), (glog0, 0), (weight[0], None)],
         [(((devices * late_rows, hidden), BF16), None)],
-        [acc(5 * hidden, 2 * width + 16)], flops=10 * cell_flops,
+        [acc(5 * hidden, 2 * width + 16)], flops=10 * cell_flops, vmem=ALL_VMEM,
     )
     got_late = exchange(late.reshape(devices, late_rows, hidden))
     (grad_pair,) = cell_call(
         functools.partial(pair_grad_kernel, cpd, q, 0), steps,
         halves(after(grads0, late))
         + [(fac0, 0), (nrm0, 0), (inv0, 0), (glog0, 0), (up0, 0), (weight[0], None), (input_gain, None)],
-        [((pair_rep.shape, BF16), 0)], [vec(1)], flops=5 * cell_flops,
+        [((pair_rep.shape, BF16), 0)], [vec(1)], flops=5 * cell_flops, vmem=ALL_VMEM,
     )
     (spread,) = cell_call(
-        functools.partial(spread_kernel, 1.0 / length), 1,
-        [(grads0, (1, 2 * side // early_rows, early_rows)), (got_late, None)],
-        [(((devices, early_rows + late_rows, hidden), BF16), None)], [],
+        spread_kernel, 1,
+        [(grads0, (1, 2 * side // early_rows, early_rows)), (after(got_late, grad_pair), None)],
+        [(((devices, early_rows + late_rows, hidden), BF16), None)], [], vmem=ALL_VMEM,
     )
     proj, out, inorm, hnorm, chain = whole_call(
-        functools.partial(unpack_kernel, early_rows), [exchange(spread)],
+        functools.partial(unpack_kernel, 1.0 / length, early_rows), [exchange(spread)],
         [
             ((2, width, 5 * hidden), F32), ((2, hidden, hidden), F32), ((2, 2, hidden), F32),
             ((2, 2, hidden), F32), ((2, hidden), F32),

time: 424 us -> 424 us (level)
  starting transfers between devices: 72.8 us -> 81.7 us
    all_to_all x9, starting transfers between devices: 72.8 us -> 81.7 us  [exchange(): return lax.all_to_all(array, AXES, split_axis=0, concat_axis=0, tiled=True)]
    pallas_call x7, Pallas kernels: 18.4 us -> 13.3 us  [whole_call(): pl.pallas_call(kernel, in_specs=[pl.BlockSpec(memory_space=pltpu.VMEM)] *...]
    unnamed x114 -> x106, local copies, waits for them, and re-layouts: 29 us -> 26.7 us
  transfers between devices with their start and end apart: 9 -> 9, of which waited for: 9 -> 9; matrix products, arithmetic and copies ran while one was open for 1% -> 1% of each run, Pallas kernels for 9% -> 8%
where the time goes in v5:
time: 424 us; the launch traced here: 422 us
  waiting for transfers between devices  215 us (51%)
  starting transfers between devices  81.7 us (19%)
  Pallas kernels  77.8 us (18%)
  local copies, waits for them, and re-layouts  29.3 us (7%)
  blocking collectives  17 us (4%)
    all_to_all x9, waiting for transfers between devices, exchange(): return lax.all_to_all(array, AXES, split_axis=0, concat_axis=0, tiled=True)  215 us
    all_to_all x9, starting transfers between devices, exchange(): return lax.all_to_all(array, AXES, split_axis=0, concat_axis=0, tiled=True)  81.7 us
    pallas_call x13, Pallas kernels, cell_call(): pl.pallas_call(kernel, grid_spec=pltpu.PrefetchScalarGridSpec(num_scalar_...  64.5 us
    unnamed x106, local copies, waits for them, and re-layouts  26.7 us
    all_to_all x1, blocking collectives, exchange(): return lax.all_to_all(array, AXES, split_axis=0, concat_axis=0, tiled=True)  17 us
    pallas_call x7, Pallas kernels, whole_call(): pl.pallas_call(kernel, in_specs=[pl.BlockSpec(memory_space=pltpu.VMEM)] *...  13.3 us
  transfers between devices with their start and end apart: 9, of which 9 were waited for; matrix products, arithmetic and copies ran while one was open for 1% of the time, Pallas kernels for 8%

profile of v5, /device:TPU:0, one launch (start us, length us, event | category | flops | bytes accessed | tf_op | source)
XLA Modules:
  0.0 422.1 jit_solution(17909917083542494071)
XLA Ops:
  1.2 6.1 %shard_map.154 = bf16[16,2,256,128]{3,2,1,0:T(8,128)(2,1)} custom-call(s32[256]{0:T(256)} %mask_smem.3, s32[256]{0:T(256)} %chain_smem.3, s32[2]{0:T(128)} %pad_add_fusion.start_smem, bf16[32,128,128]{2,1,0:T(8,128)(2,1)} %pair_ref.2, s32[2,128]{1,0:T(2,128)} %bitcast.30, s32[2,128]{1,0:T(2,128)} %bitcast.32, bf16[2,128,640]{2,1,0:T(8,128)(2,1)} %w_ref.1, ...), custom_call_target="tpu_custom_call" | custom-call | flops 536870912 | bytes 3477504 | tf_op jit(solution)/shard_map/pallas_call | solution.py:424
  7.4 7.5 %all-to-all-start = ((bf16[16,2,256,128]{3,2,1,0:T(8,128)(2,1)}), bf16[16,2,256,128]{3,2,1,0:T(8,128)(2,1)S(1)}, u32[]{:S(2)}, u32[]{:S(2)}) async-start(bf16[16,2,256,128]{3,2,1,0:T(8,128)(2,1)} %shard_map.154), calls=%async_computation | async-start | bytes 4194304 | tf_op jit(solution)/shard_map/all_to_all | solution.py:528
  15.9 4.4 %shard_map.155 = (bf16[16,128,256]{2,1,0:T(8,128)(2,1)S(1)}, bf16[16,128,256]{2,1,0:T(8,128)(2,1)S(1)}, bf16[16,128,256]{2,1,0:T(8,128)(2,1)S(1)}, f32[16,2,256]{2,1,0:T(2,128)S(1)}) custom-call(s32[256]{0:T(256)S(1)} %copy-done.37, s32[256]{0:T(256)S(1)} %copy-done.38, s32[2]{0:T(128)S(1)} %copy-done.44, bf16[32,128,128]{2,1,0:T(8,128)(2,1)} %pair_ref.2, ...), custom_call_target="tpu_custom_call" | custom-call | flops 268435456 | bytes 5444608 | tf_op jit(solution)/shard_map/pallas_call | solution.py:424
  23.4 32.7 %all-to-all-done.edges_ref = bf16[16,2,256,128]{3,2,1,0:T(8,128)(2,1)S(1)} async-done(((bf16[16,2,256,128]{3,2,1,0:T(8,128)(2,1)}), bf16[16,2,256,128]{3,2,1,0:T(8,128)(2,1)S(1)}, u32[]{:S(2)}, u32[]{:S(2)}) %all-to-all-start) | async-done | bytes 2097184 | tf_op jit(solution)/shard_map/all_to_all | solution.py:528
  58.3 11.2 %all-to-all-start.1 = ((bf16[16,256,128]{2,1,0:T(8,128)(2,1)}), bf16[16,256,128]{2,1,0:T(8,128)(2,1)S(1)}, u32[]{:S(2)}, u32[]{:S(2)}) async-start(bf16[16,256,128]{2,1,0:T(8,128)(2,1)} %copy-done.16), calls=%async_computation.1 | async-start | bytes 2097152 | tf_op jit(solution)/shard_map/all_to_all | solution.py:528
  74.0 18.4 %all-to-all-done.1.prod_ref = bf16[16,256,128]{2,1,0:T(8,128)(2,1)S(1)} async-done(((bf16[16,256,128]{2,1,0:T(8,128)(2,1)}), bf16[16,256,128]{2,1,0:T(8,128)(2,1)S(1)}, u32[]{:S(2)}, u32[]{:S(2)}) %all-to-all-start.1) | async-done | bytes 1048608 | tf_op jit(solution)/shard_map/all_to_all | solution.py:528
  95.3 5.6 %shard_map.158 = (bf16[16,2,256,128]{3,2,1,0:T(8,128)(2,1)}, f32[16,128,256]{2,1,0:T(8,128)}) custom-call(bf16[16,256,128]{2,1,0:T(8,128)(2,1)S(1)} %all-to-all-done.1.prod_ref, bf16[16,128,256]{2,1,0:T(8,128)(2,1)S(1)} %copy-done.25, bf16[16,128,256]{2,1,0:T(8,128)(2,1)S(1)} %copy-done.2, f32[16,2,256]{2,1,0:T(2,128)S(1)} %get-tuple-element.57.flags_ref, ...), custom_call_target="tpu_custom_call" | custom-call | flops 671088640 | bytes 7573504 | tf_op jit(solution)/shard_map/pallas_call | solution.py:424
  100.9 6.9 %all-to-all-start.2 = ((bf16[16,2,256,128]{3,2,1,0:T(8,128)(2,1)}), bf16[16,2,256,128]{3,2,1,0:T(8,128)(2,1)S(1)}, u32[]{:S(2)}, u32[]{:S(2)}) async-start(bf16[16,2,256,128]{3,2,1,0:T(8,128)(2,1)} %get-tuple-element.58), calls=%async_computation.2 | async-start | bytes 4194304 | tf_op jit(solution)/shard_map/all_to_all | solution.py:528
  108.4 5.8 %shard_map.159 = (bf16[16,512,256]{2,1,0:T(8,128)(2,1)}, bf16[16,128,256]{2,1,0:T(8,128)(2,1)S(1)}, bf16[16,128,256]{2,1,0:T(8,128)(2,1)S(1)}, f32[16,1,256]{2,1,0:T(1,128)S(1)}, bf16[16,128,256]{2,1,0:T(8,128)(2,1)S(1)}) custom-call(f32[16,128,256]{2,1,0:T(8,128)} %get-tuple-element.60.z_ref, f32[16,2,256]{2,1,0:T(2,128)S(1)} %get-tuple-element.57.flags_ref, ...), custom_call_target="tpu_custom_call" | custom-call | flops 671088640 | bytes 9653248 | tf_op jit(solution)/shard_map/pallas_call | solution.py:424
  117.8 31.0 %all-to-all-done.2.edges_ref = bf16[16,2,256,128]{3,2,1,0:T(8,128)(2,1)S(1)} async-done(((bf16[16,2,256,128]{3,2,1,0:T(8,128)(2,1)}), bf16[16,2,256,128]{3,2,1,0:T(8,128)(2,1)S(1)}, u32[]{:S(2)}, u32[]{:S(2)}) %all-to-all-start.2) | async-done | bytes 2097184 | tf_op jit(solution)/shard_map/all_to_all | solution.py:528
  151.2 11.3 %all-to-all-start.3 = ((bf16[16,256,128]{2,1,0:T(8,128)(2,1)}), bf16[16,256,128]{2,1,0:T(8,128)(2,1)}, u32[]{:S(2)}, u32[]{:S(2)}) async-start(bf16[16,256,128]{2,1,0:T(8,128)(2,1)} %copy-done.18), calls=%async_computation.3 | async-start | bytes 2097152 | tf_op jit(solution)/shard_map/all_to_all | solution.py:528
  165.1 20.3 %all-to-all-done.3.prod_ref = bf16[16,256,128]{2,1,0:T(8,128)(2,1)} async-done(((bf16[16,256,128]{2,1,0:T(8,128)(2,1)}), bf16[16,256,128]{2,1,0:T(8,128)(2,1)}, u32[]{:S(2)}, u32[]{:S(2)}) %all-to-all-start.3) | async-done | bytes 1048608 | tf_op jit(solution)/shard_map/all_to_all | solution.py:528
  186.7 3.6 shard_map.162
  191.2 7.1 %all-to-all-start.4 = ((bf16[16,256,128]{2,1,0:T(8,128)(2,1)}), bf16[16,256,128]{2,1,0:T(8,128)(2,1)}, u32[]{:S(2)}, u32[]{:S(2)}) async-start(bf16[16,256,128]{2,1,0:T(8,128)(2,1)} %copy-done.17), calls=%async_computation.4 | async-start | bytes 2097152 | tf_op jit(solution)/shard_map/all_to_all | solution.py:528
  200.2 21.1 %all-to-all-done.4.grad_ref = bf16[16,256,128]{2,1,0:T(8,128)(2,1)} async-done(((bf16[16,256,128]{2,1,0:T(8,128)(2,1)}), bf16[16,256,128]{2,1,0:T(8,128)(2,1)}, u32[]{:S(2)}, u32[]{:S(2)}) %all-to-all-start.4) | async-done | bytes 1048608 | tf_op jit(solution)/shard_map/all_to_all | solution.py:528
  221.3 2.9 shard_map.164
  225.5 7.0 %all-to-all-start.5 = ((bf16[16,512,128]{2,1,0:T(8,128)(2,1)}), bf16[16,512,128]{2,1,0:T(8,128)(2,1)}, u32[]{:S(2)}, u32[]{:S(2)}) async-start(bf16[16,512,128]{2,1,0:T(8,128)(2,1)} %copy-done.8), calls=%async_computation.5 | async-start | bytes 4194304 | tf_op jit(solution)/shard_map/all_to_all | solution.py:528
  232.8 4.0 shard_map.165
  237.4 36.3 %all-to-all-done.5.left_ref.right_ref = bf16[16,512,128]{2,1,0:T(8,128)(2,1)} async-done(((bf16[16,512,128]{2,1,0:T(8,128)(2,1)}), bf16[16,512,128]{2,1,0:T(8,128)(2,1)}, u32[]{:S(2)}, u32[]{:S(2)}) %all-to-all-start.5) | async-done | bytes 2097184 | tf_op jit(solution)/shard_map/all_to_all | solution.py:528
  273.8 8.1 %shard_map.166 = (f32[16,128,256]{2,1,0:T(8,128)}, bf16[16,256,128]{2,1,0:T(8,128)(2,1)}) custom-call(bf16[16,512,128]{2,1,0:T(8,128)(2,1)} %all-to-all-done.5.left_ref.right_ref, bf16[16,512,128]{2,1,0:T(8,128)(2,1)} %all-to-all-done.5.left_ref.right_ref, bf16[16,512,256]{2,1,0:T(8,128)(2,1)} %get-tuple-element.72.fac_ref, ...), custom_call_target="tpu_custom_call" | custom-call | flops 805306368 | bytes 17008640 | tf_op jit(solution)/shard_map/pallas_call | solution.py:424
  281.9 11.4 %all-to-all-start.6 = ((bf16[16,256,128]{2,1,0:T(8,128)(2,1)}), bf16[16,256,128]{2,1,0:T(8,128)(2,1)}, u32[]{:S(2)}, u32[]{:S(2)}) async-start(bf16[16,256,128]{2,1,0:T(8,128)(2,1)} %get-tuple-element.76), calls=%async_computation.6 | async-start | bytes 2097152 | tf_op jit(solution)/shard_map/all_to_all | solution.py:528
  294.5 7.2 %shard_map.167 = (bf16[16,128,256]{2,1,0:T(8,128)(2,1)S(1)}, bf16[1024,128]{1,0:T(8,128)(2,1)S(1)}) custom-call(bf16[16,512,128]{2,1,0:T(8,128)(2,1)} %all-to-all-done.5.left_ref.right_ref, bf16[16,512,128]{2,1,0:T(8,128)(2,1)} %all-to-all-done.5.left_ref.right_ref, bf16[16,512,256]{2,1,0:T(8,128)(2,1)} %get-tuple-element.72.fac_ref, ...), custom_call_target="tpu_custom_call" | custom-call | flops 1744830464 | bytes 17373184 | tf_op jit(solution)/shard_map/pallas_call | solution.py:424
  303.4 12.9 %all-to-all-done.6.grad_ref = bf16[16,256,128]{2,1,0:T(8,128)(2,1)} async-done(((bf16[16,256,128]{2,1,0:T(8,128)(2,1)}), bf16[16,256,128]{2,1,0:T(8,128)(2,1)}, u32[]{:S(2)}, u32[]{:S(2)}) %all-to-all-start.6) | async-done | bytes 1048608 | tf_op jit(solution)/shard_map/all_to_all | solution.py:528
  317.2 4.2 %shard_map.168 = bf16[16,576,128]{2,1,0:T(8,128)(2,1)} custom-call(bf16[8,2,256,256]{3,2,1,0:T(8,128)(2,1)S(1)} %copy-done.10, bf16[16,256,128]{2,1,0:T(8,128)(2,1)} %all-to-all-done.6.grad_ref, bf16[16,64,128]{2,1,0:T(8,128)(2,1)S(1)} %bitcast.28), custom_call_target="tpu_custom_call" | custom-call | flops 536870912 | bytes 5767168 | tf_op jit(solution)/shard_map/pallas_call | solution.py:516
  321.5 7.0 %all-to-all-start.7 = ((bf16[16,576,128]{2,1,0:T(8,128)(2,1)}), bf16[16,576,128]{2,1,0:T(8,128)(2,1)}, u32[]{:S(2)}, u32[]{:S(2)}) async-start(bf16[16,576,128]{2,1,0:T(8,128)(2,1)} %shard_map.168), calls=%async_computation.7 | async-start | bytes 4718592 | tf_op jit(solution)/shard_map/all_to_all | solution.py:528
  328.6 4.1 shard_map.169
  334.7 39.6 %all-to-all-done.7.left_ref.right_ref.early_ref = bf16[16,576,128]{2,1,0:T(8,128)(2,1)} async-done(((bf16[16,576,128]{2,1,0:T(8,128)(2,1)}), bf16[16,576,128]{2,1,0:T(8,128)(2,1)}, u32[]{:S(2)}, u32[]{:S(2)}) %all-to-all-start.7) | async-done | bytes 2359328 | tf_op jit(solution)/shard_map/all_to_all | solution.py:528
  374.3 6.2 %shard_map.170 = bf16[768,128]{1,0:T(8,128)(2,1)} custom-call(bf16[16,576,128]{2,1,0:T(8,128)(2,1)} %all-to-all-done.7.left_ref.right_ref.early_ref, bf16[16,576,128]{2,1,0:T(8,128)(2,1)} %all-to-all-done.7.left_ref.right_ref.early_ref, bf16[16,512,256]{2,1,0:T(8,128)(2,1)} %get-tuple-element.85.fac_ref, bf16[16,128,256]{2,1,0:T(8,128)(2,1)} %copy-done.23, ...), custom_call_target="tpu_custom_call" | custom-call | flops 1342177280 | bytes 12419072 | tf_op jit(solution)/shard_map/pallas_call | solution.py:424
  380.5 12.3 %all-to-all-start.8 = ((bf16[16,48,128]{2,1,0:T(8,128)(2,1)}), bf16[16,48,128]{2,1,0:T(8,128)(2,1)S(1)}, u32[]{:S(2)}, u32[]{:S(2)}) async-start(bf16[16,48,128]{2,1,0:T(8,128)(2,1)} %bitcast.34), calls=%async_computation.8 | async-start | bytes 393216 | tf_op jit(solution)/shard_map/all_to_all | solution.py:528
  392.7 6.7 %shard_map.171 = bf16[32,128,128]{2,1,0:T(8,128)(2,1)} custom-call(bf16[16,576,128]{2,1,0:T(8,128)(2,1)} %all-to-all-done.7.left_ref.right_ref.early_ref, bf16[16,576,128]{2,1,0:T(8,128)(2,1)} %all-to-all-done.7.left_ref.right_ref.early_ref, bf16[16,512,256]{2,1,0:T(8,128)(2,1)} %get-tuple-element.85.fac_ref, bf16[16,128,256]{2,1,0:T(8,128)(2,1)} %copy-done.15, ...), custom_call_target="tpu_custom_call" | custom-call | flops 671088640 | bytes 14337024 | tf_op jit(solution)/shard_map/pallas_call | solution.py:424
  399.4 2.3 all-to-all-done.8.late_ref
  404.3 17.0 %all_to_all.50.got_ref = bf16[16,112,128]{2,1,0:T(8,128)(2,1)S(1)} all-to-all(bf16[16,112,128]{2,1,0:T(8,128)(2,1)} %shard_map.172), channel_id=1, replica_groups=mesh['grp'=2,'row'=8,'col'=2] {'row','col'}, dimensions={0} | all-to-all | bytes 917504 | tf_op jit(solution)/shard_map/all_to_all | solution.py:528
  (118 shorter events, 38.7 us)
Async XLA Ops:
  7.3 7.6 %copy-start.48 = (bf16[2,128,640]{2,1,0:T(8,128)(2,1)S(1)}, bf16[2,128,640]{2,1,0:T(8,128)(2,1)}, u32[]{:S(2)}) copy-start(bf16[2,128,640]{2,1,0:T(8,128)(2,1)} %w_ref.1) | copy-start | bytes 983044
  7.3 8.5 %copy-start.35 = (f32[2,128]{1,0:T(2,128)S(1)}, f32[2,128]{1,0:T(2,128)}, u32[]{:S(2)}) copy-start(f32[2,128]{1,0:T(2,128)} %gain_ref.13) | copy-start | bytes 3076
  7.3 8.6 %copy-start.37 = (s32[256]{0:T(256)S(1)}, s32[256]{0:T(256)}, u32[]{:S(2)}) copy-start(s32[256]{0:T(256)} %mask_smem.3) | copy-start | bytes 3076
  7.3 8.6 %copy-start.38 = (s32[256]{0:T(256)S(1)}, s32[256]{0:T(256)}, u32[]{:S(2)}) copy-start(s32[256]{0:T(256)} %chain_smem.3) | copy-start | bytes 3076
  7.4 8.6 %copy-start.42 = (f32[2,128]{1,0:T(2,128)S(1)}, f32[2,128]{1,0:T(2,128)}, u32[]{:S(2)}) copy-start(f32[2,128]{1,0:T(2,128)} %bias_ref.9) | copy-start | bytes 3076
  7.4 8.5 %copy-start.44 = (s32[2]{0:T(128)S(1)}, s32[2]{0:T(128)}, u32[]{:S(2)}) copy-start(s32[2]{0:T(128)} %pad_add_fusion.start_smem) | copy-start | bytes 28
  7.4 8.5 %copy-start.45 = (f32[2,128]{1,0:T(2,128)S(1)}, f32[2,128]{1,0:T(2,128)}, u32[]{:S(2)}) copy-start(f32[2,128]{1,0:T(2,128)} %chain_ref.5) | copy-start | bytes 3076
  7.4 48.6 %all-to-all-start = ((bf16[16,2,256,128]{3,2,1,0:T(8,128)(2,1)}), bf16[16,2,256,128]{3,2,1,0:T(8,128)(2,1)S(1)}, u32[]{:S(2)}, u32[]{:S(2)}) async-start(bf16[16,2,256,128]{3,2,1,0:T(8,128)(2,1)} %shard_map.154), calls=%async_computation | async-start | bytes 4194304 | tf_op jit(solution)/shard_map/all_to_all | solution.py:528
  15.9 41.4 %copy-start.27 = (bf16[640,128]{1,0:T(8,128)(2,1)}, bf16[640,128]{1,0:T(8,128)(2,1)S(1)}, u32[]{:S(2)}) copy-start(bf16[640,128]{1,0:T(8,128)(2,1)S(1)} %copy.17.wt_ref) | copy-start | bytes 491524
  56.0 13.5 %copy-start.51 = (bf16[2,128,128]{2,1,0:T(8,128)(2,1)S(1)}, bf16[2,128,128]{2,1,0:T(8,128)(2,1)}, u32[]{:S(2)}) copy-start(bf16[2,128,128]{2,1,0:T(8,128)(2,1)} %param.16) | copy-start | bytes 196612
  58.3 34.2 %all-to-all-start.1 = ((bf16[16,256,128]{2,1,0:T(8,128)(2,1)}), bf16[16,256,128]{2,1,0:T(8,128)(2,1)S(1)}, u32[]{:S(2)}, u32[]{:S(2)}) async-start(bf16[16,256,128]{2,1,0:T(8,128)(2,1)} %copy-done.16), calls=%async_computation.1 | async-start | bytes 2097152 | tf_op jit(solution)/shard_map/all_to_all | solution.py:528
  71.4 21.1 %copy-start.36 = (f32[2,128]{1,0:T(2,128)S(1)}, f32[2,128]{1,0:T(2,128)}, u32[]{:S(2)}) copy-start(f32[2,128]{1,0:T(2,128)} %hgain_ref.9) | copy-start | bytes 3076
  71.4 21.1 %copy-start.43 = (f32[2,128]{1,0:T(2,128)S(1)}, f32[2,128]{1,0:T(2,128)}, u32[]{:S(2)}) copy-start(f32[2,128]{1,0:T(2,128)} %hbias_ref.5) | copy-start | bytes 3076
  92.4 105.8 %copy-start = (bf16[16,256,128]{2,1,0:T(8,128)(2,1)}, bf16[16,256,128]{2,1,0:T(8,128)(2,1)S(1)}, u32[]{:S(2)}) copy-start(bf16[16,256,128]{2,1,0:T(8,128)(2,1)S(1)} %all-to-all-done.1.prod_ref) | copy-start | bytes 3145732
  100.9 48.0 %all-to-all-start.2 = ((bf16[16,2,256,128]{3,2,1,0:T(8,128)(2,1)}), bf16[16,2,256,128]{3,2,1,0:T(8,128)(2,1)S(1)}, u32[]{:S(2)}, u32[]{:S(2)}) async-start(bf16[16,2,256,128]{3,2,1,0:T(8,128)(2,1)} %get-tuple-element.58), calls=%async_computation.2 | async-start | bytes 4194304 | tf_op jit(solution)/shard_map/all_to_all | solution.py:528
  151.2 34.3 %all-to-all-start.3 = ((bf16[16,256,128]{2,1,0:T(8,128)(2,1)}), bf16[16,256,128]{2,1,0:T(8,128)(2,1)}, u32[]{:S(2)}, u32[]{:S(2)}) async-start(bf16[16,256,128]{2,1,0:T(8,128)(2,1)} %copy-done.18), calls=%async_computation.3 | async-start | bytes 2097152 | tf_op jit(solution)/shard_map/all_to_all | solution.py:528
  162.4 23.0 %copy-start.30 = (bf16[128,128]{1,0:T(8,128)(2,1)S(1)}, bf16[128,128]{1,0:T(8,128)(2,1)}, u32[]{:S(2)}) copy-start(bf16[128,128]{1,0:T(8,128)(2,1)} %get-tuple-element.101.ow_ref) | copy-start | bytes 98308
  191.2 30.1 %copy-start.7 = (bf16[8,2,256,256]{3,2,1,0:T(8,128)(2,1)S(1)}, bf16[8,2,256,256]{3,2,1,0:T(8,128)(2,1)}, u32[]{:S(2)}) copy-start(bf16[8,2,256,256]{3,2,1,0:T(8,128)(2,1)} %copy-done.6) | copy-start | bytes 6291460
  191.2 30.0 %all-to-all-start.4 = ((bf16[16,256,128]{2,1,0:T(8,128)(2,1)}), bf16[16,256,128]{2,1,0:T(8,128)(2,1)}, u32[]{:S(2)}, u32[]{:S(2)}) async-start(bf16[16,256,128]{2,1,0:T(8,128)(2,1)} %copy-done.17), calls=%async_computation.4 | async-start | bytes 2097152 | tf_op jit(solution)/shard_map/all_to_all | solution.py:528
  225.5 7.1 %copy-start.50 = (bf16[1,128,128]{2,1,0:T(8,128)(2,1)S(1)}, bf16[1,128,128]{2,1,0:T(8,128)(2,1)}, u32[]{:S(2)}) copy-start(bf16[1,128,128]{2,1,0:T(8,128)(2,1)} %get-tuple-element.103) | copy-start | bytes 98308
  225.5 7.2 %copy-start.5 = (bf16[16,128,256]{2,1,0:T(8,128)(2,1)S(1)}, bf16[16,128,256]{2,1,0:T(8,128)(2,1)}, u32[]{:S(2)}) copy-start(bf16[16,128,256]{2,1,0:T(8,128)(2,1)} %copy-done.3) | copy-start | bytes 3145732
  225.5 48.2 %all-to-all-start.5 = ((bf16[16,512,128]{2,1,0:T(8,128)(2,1)}), bf16[16,512,128]{2,1,0:T(8,128)(2,1)}, u32[]{:S(2)}, u32[]{:S(2)}) async-start(bf16[16,512,128]{2,1,0:T(8,128)(2,1)} %copy-done.8), calls=%async_computation.5 | async-start | bytes 4194304 | tf_op jit(solution)/shard_map/all_to_all | solution.py:528
  232.6 41.2 %copy-start.12 = (bf16[16,128,256]{2,1,0:T(8,128)(2,1)S(1)}, bf16[16,128,256]{2,1,0:T(8,128)(2,1)}, u32[]{:S(2)}) copy-start(bf16[16,128,256]{2,1,0:T(8,128)(2,1)} %copy-done.11) | copy-start | bytes 3145732
  232.6 41.2 %copy-start.29 = (bf16[128,128]{1,0:T(8,128)(2,1)S(1)}, bf16[128,128]{1,0:T(8,128)(2,1)}, u32[]{:S(2)}) copy-start(bf16[128,128]{1,0:T(8,128)(2,1)} %get-tuple-element.100.ow_ref) | copy-start | bytes 98308
  232.6 41.1 %copy-start.40 = (f32[16,1,256]{2,1,0:T(1,128)S(1)}, f32[16,1,256]{2,1,0:T(1,128)}, u32[]{:S(2)}) copy-start(f32[16,1,256]{2,1,0:T(1,128)} %copy-done.39) | copy-start | bytes 49156
  237.4 44.5 %copy-start.14 = (bf16[16,128,256]{2,1,0:T(8,128)(2,1)}, bf16[16,128,256]{2,1,0:T(8,128)(2,1)S(1)}, u32[]{:S(2)}) copy-start(bf16[16,128,256]{2,1,0:T(8,128)(2,1)S(1)} %get-tuple-element.70.glog_ref) | copy-start | bytes 3145732
  281.9 11.4 %copy-start.34 = (f32[136,128]{1,0:T(8,128)S(1)}, f32[136,128]{1,0:T(8,128)}, u32[]{:S(2)}) copy-start(f32[136,128]{1,0:T(8,128)} %copy-done.33) | copy-start | bytes 208900
  281.9 34.4 %all-to-all-start.6 = ((bf16[16,256,128]{2,1,0:T(8,128)(2,1)}), bf16[16,256,128]{2,1,0:T(8,128)(2,1)}, u32[]{:S(2)}, u32[]{:S(2)}) async-start(bf16[16,256,128]{2,1,0:T(8,128)(2,1)} %get-tuple-element.76), calls=%async_computation.6 | async-start | bytes 2097152 | tf_op jit(solution)/shard_map/all_to_all | solution.py:528
  294.5 21.8 %copy-start.10 = (bf16[8,2,256,256]{3,2,1,0:T(8,128)(2,1)S(1)}, bf16[8,2,256,256]{3,2,1,0:T(8,128)(2,1)}, u32[]{:S(2)}) copy-start(bf16[8,2,256,256]{3,2,1,0:T(8,128)(2,1)} %copy-done.9) | copy-start | bytes 6291460
  321.5 52.8 %all-to-all-start.7 = ((bf16[16,576,128]{2,1,0:T(8,128)(2,1)}), bf16[16,576,128]{2,1,0:T(8,128)(2,1)}, u32[]{:S(2)}, u32[]{:S(2)}) async-start(bf16[16,576,128]{2,1,0:T(8,128)(2,1)} %shard_map.168), calls=%async_computation.7 | async-start | bytes 4718592 | tf_op jit(solution)/shard_map/all_to_all | solution.py:528
  334.7 45.8 %copy-start.41 = (f32[16,1,256]{2,1,0:T(1,128)}, f32[16,1,256]{2,1,0:T(1,128)S(1)}, u32[]{:S(2)}) copy-start(f32[16,1,256]{2,1,0:T(1,128)S(1)} %get-tuple-element.89.inv_ref) | copy-start | bytes 49156
  380.5 21.3 %all-to-all-start.8 = ((bf16[16,48,128]{2,1,0:T(8,128)(2,1)}), bf16[16,48,128]{2,1,0:T(8,128)(2,1)S(1)}, u32[]{:S(2)}, u32[]{:S(2)}) async-start(bf16[16,48,128]{2,1,0:T(8,128)(2,1)} %bitcast.34), calls=%async_computation.8 | async-start | bytes 393216 | tf_op jit(solution)/shard_map/all_to_all | solution.py:528
  (29 other events, 47.6 us)

commit v6 on v5

--- a/solution.py
+++ b/solution.py
@@ -12,7 +12,8 @@
 F32 = jnp.float32
 BF16 = jnp.bfloat16
 CHANNEL_VMEM = 24 * 1024 * 1024
-CELL_VMEM = 50 * 1024 * 1024
+CELL_VMEM = 30 * 1024 * 1024
+LOOP_VMEM = 32 * 1024 * 1024
 ALL_VMEM = 60 * 1024 * 1024
 
 
@@ -92,12 +93,36 @@
     edges_ref[:, 1, here, :] = pack(part[2] * sigmoid(part[3]) * mask, cpd, cols)
 
 
+STEP = []
+
+
+def step_now():
+    return STEP[-1] if STEP else (pl.program_id(0), pl.num_programs(0))
+
+
 def first_step(fill):
-    pl.when(pl.program_id(0) == 0)(fill)
+    pl.when(step_now()[0] == 0)(fill)
 
 
 def last_step(fill):
-    pl.when(pl.program_id(0) == pl.num_programs(0) - 1)(fill)
+    index, count = step_now()
+    pl.when(index == count - 1)(fill)
+
+
+def looped_kernel(kernel, steps, hows, *refs):
+    @pl.loop(0, steps)
+    def _(step):
+        views = []
+        for ref, how in zip(refs, hows):
+            if how is None:
+                views.append(ref)
+                continue
+            axis, first, size = how
+            here = pl.ds(pl.multiple_of((step + first) * size, size), size)
+            views.append(ref.at[tuple(here if n == axis else slice(None) for n in range(axis + 1))])
+        STEP.append((step, steps))
+        kernel(*views, *refs[len(hows) :])
+        STEP.pop()
 
 
 def load_columns(vec, *rows):
@@ -361,9 +386,11 @@
     cpd, q, left_ref, right_ref, fac_ref, low_ref, nrm_ref, glog_ref, w_ref, all_ref, acc_w,
 ):
     clear(acc_w)
-    for t in range(low_ref.shape[0]):
-        gproj = project_grad(left_ref, right_ref, fac_ref, glog_ref, t, cpd, q * cpd)
-        edge_terms(gproj, low_ref, nrm_ref, t, acc_w)
+    tiles = range(low_ref.shape[0])
+    gproj = [project_grad(left_ref, right_ref, fac_ref, glog_ref, t, cpd, q * cpd) for t in tiles]
+    ones = jnp.ones((16, low_ref.shape[2]), BF16)
+    sides = [jnp.concatenate([low_ref[t], nrm_ref[t], ones], 0) for t in tiles]
+    acc_w[...] += dot(jnp.concatenate(sides, 1), jnp.concatenate(gproj, 1), 1, 1)
 
     @last_step
     def _():
@@ -508,7 +535,19 @@
         out_ref[:, out_ref.shape[1] - terms_ref.shape[1] :, :] = terms_ref[...]
 
 
-def whole_call(kernel, ins, outs, scratch, flops):
+def loop_call(kernel, steps, ins, outs, scratch, flops=0):
+    def part(shape, how):
+        return how if how is None or isinstance(how, tuple) else (how, 0, shape[how] // steps)
+
+    hows = [part(a.shape, how) for a, how in ins] + [part(shape, how) for (shape, _), how in outs]
+    made = whole_call(
+        functools.partial(looped_kernel, kernel, steps, hows), [a for a, _ in ins], [o for o, _ in outs],
+        scratch, flops, LOOP_VMEM,
+    )
+    return made if len(outs) > 1 else (made,)
+
+
+def whole_call(kernel, ins, outs, scratch, flops, vmem=None):
     moved = sum(a.size * a.dtype.itemsize for a in ins)
     moved += sum(functools.reduce(lambda x, y: x * y, s, 1) * jnp.dtype(t).itemsize for s, t in outs)
     specs = [pl.BlockSpec(memory_space=pltpu.VMEM)] * len(outs)
@@ -519,7 +558,7 @@
         out_specs=specs if len(outs) > 1 else specs[0],
         out_shape=shapes if len(outs) > 1 else shapes[0],
         scratch_shapes=scratch,
-        compiler_params=pltpu.CompilerParams(vmem_limit_bytes=CHANNEL_VMEM),
+        compiler_params=pltpu.CompilerParams(vmem_limit_bytes=vmem or CHANNEL_VMEM),
         cost_estimate=pl.CostEstimate(flops=flops, bytes_accessed=int(moved), transcendentals=0),
     )(*ins)
 
@@ -624,7 +663,7 @@
     made0 = product(after(got0, z0), True)
     prod0 = exchange(made0)
     sides0 = assemble(after(got0, made0))
-    edges1, z1 = cell_call(
+    edges1, z1 = loop_call(
         functools.partial(mix_edge_kernel, cpd, q, 0), steps,
         [
             (after(prod0, sides0), 1), (z0, 0), (gate0, 0), (flags, 0), (owt[0], None), (hidden_gain, None),
@@ -638,7 +677,7 @@
     prod1 = exchange(made1)
     sides1 = assemble(after(got1, made1))
 
-    (grad1,) = cell_call(
+    (grad1,) = loop_call(
         functools.partial(mix_back_kernel, cpd, q, 1), steps,
         [(after(prod1, sides1), 1), (up, 0), (gate1, 0), (mixer[1], None), (hidden_gain, None)],
         [((cell_shape, BF16), 1)], [vec(1)], flops=cell_flops,
@@ -659,7 +698,7 @@
         [((tile, BF16), 0), ((terms_shape, F32), None)],
         [vec(2), acc(hidden), acc(cols), acc(cols), acc(cols)], flops=3 * cell_flops,
     )
-    up0, grad0 = cell_call(
+    up0, grad0 = loop_call(
         functools.partial(edge_mix_back_kernel, cpd, q, 1), steps,
         halves(after(grads1, glog1))
         + [
@@ -687,11 +726,11 @@
     grads0 = exchange(made_grads0)
     fac0, low0, nrm0, inv0 = keep(0, after(z0, made_grads0), False)
     grads0 = after(grads0, nrm0)
-    (late,) = cell_call(
+    (late,) = loop_call(
         functools.partial(last_terms_kernel, cpd, q), steps,
         halves(grads0) + [(fac0, 0), (low0, 0), (nrm0, 0), (glog0, 0), (weight[0], None)],
         [(((devices * late_rows, hidden), BF16), None)],
-        [acc(5 * hidden, 2 * width + 16)], flops=10 * cell_flops, vmem=ALL_VMEM,
+        [acc(5 * hidden, 2 * width + 16)], flops=10 * cell_flops,
     )
     got_late = exchange(late.reshape(devices, late_rows, hidden))
     (grad_pair,) = cell_call(

time: 424 us -> 439 us (1.035)
  local copies, waits for them, and re-layouts: 29.3 us -> 76 us
  Pallas kernels: 77.8 us -> 59.8 us
  waiting for transfers between devices: 215 us -> 201 us
    unnamed x106 -> x158, local copies, waits for them, and re-layouts: 26.7 us -> 70.6 us
    pallas_call x13 -> x9, Pallas kernels: 64.5 us -> 32.6 us  [cell_call(): pl.pallas_call(kernel, grid_spec=pltpu.PrefetchScalarGridSpec(num_scalar_...]
    all_to_all x9, waiting for transfers between devices: 215 us -> 201 us  [exchange(): return lax.all_to_all(array, AXES, split_axis=0, concat_axis=0, tiled=True)]
    pallas_call x7 -> x11, Pallas kernels: 13.3 us -> 27.2 us  [whole_call(): pl.pallas_call(kernel, in_specs=[pl.BlockSpec(memory_space=pltpu.VMEM)] *...]
  transfers between devices with their start and end apart: 9 -> 9, of which waited for: 9 -> 9; matrix products, arithmetic and copies ran while one was open for 1% -> 1% of each run, Pallas kernels for 8% -> 6%
where the time goes in v6:
time: 439 us; the launch traced here: 437 us
  waiting for transfers between devices  201 us (46%)
  starting transfers between devices  81.6 us (19%)
  local copies, waits for them, and re-layouts  76 us (17%)
  Pallas kernels  59.8 us (14%)
  blocking collectives  17 us (4%)
    all_to_all x9, waiting for transfers between devices, exchange(): return lax.all_to_all(array, AXES, split_axis=0, concat_axis=0, tiled=True)  201 us
    all_to_all x9, starting transfers between devices, exchange(): return lax.all_to_all(array, AXES, split_axis=0, concat_axis=0, tiled=True)  81.6 us
    unnamed x158, local copies, waits for them, and re-layouts  70.6 us
    pallas_call x9, Pallas kernels, cell_call(): pl.pallas_call(kernel, grid_spec=pltpu.PrefetchScalarGridSpec(num_scalar_...  32.6 us
    pallas_call x11, Pallas kernels, whole_call(): pl.pallas_call(kernel, in_specs=[pl.BlockSpec(memory_space=pltpu.VMEM)] *...  27.2 us
    all_to_all x1, blocking collectives, exchange(): return lax.all_to_all(array, AXES, split_axis=0, concat_axis=0, tiled=True)  17 us
  transfers between devices with their start and end apart: 9, of which 9 were waited for; matrix products, arithmetic and copies ran while one was open for 1% of the time, Pallas kernels for 6%

profile of v6, /device:TPU:0, one launch (start us, length us, event | category | flops | bytes accessed | tf_op | source)
XLA Modules:
  0.0 436.7 jit_solution(11266609517838620457)
XLA Ops:
  1.2 6.1 %shard_map.154 = bf16[16,2,256,128]{3,2,1,0:T(8,128)(2,1)} custom-call(s32[256]{0:T(256)} %mask_smem.3, s32[256]{0:T(256)} %chain_smem.3, s32[2]{0:T(128)} %pad_add_fusion.start_smem, bf16[32,128,128]{2,1,0:T(8,128)(2,1)} %pair_ref.2, s32[2,128]{1,0:T(2,128)} %bitcast.31, s32[2,128]{1,0:T(2,128)} %bitcast.33, bf16[2,128,640]{2,1,0:T(8,128)(2,1)} %w_ref.1, ...), custom_call_target="tpu_custom_call" | custom-call | flops 536870912 | bytes 3477504 | tf_op jit(solution)/shard_map/pallas_call | solution.py:451
  7.4 7.5 %all-to-all-start = ((bf16[16,2,256,128]{3,2,1,0:T(8,128)(2,1)}), bf16[16,2,256,128]{3,2,1,0:T(8,128)(2,1)S(1)}, u32[]{:S(2)}, u32[]{:S(2)}) async-start(bf16[16,2,256,128]{3,2,1,0:T(8,128)(2,1)} %shard_map.154), calls=%async_computation | async-start | bytes 4194304 | tf_op jit(solution)/shard_map/all_to_all | solution.py:567
  19.1 2.8 shard_map.155
  24.9 31.1 %all-to-all-done.edges_ref = bf16[16,2,256,128]{3,2,1,0:T(8,128)(2,1)S(1)} async-done(((bf16[16,2,256,128]{3,2,1,0:T(8,128)(2,1)}), bf16[16,2,256,128]{3,2,1,0:T(8,128)(2,1)S(1)}, u32[]{:S(2)}, u32[]{:S(2)}) %all-to-all-start) | async-done | bytes 2097184 | tf_op jit(solution)/shard_map/all_to_all | solution.py:567
  58.2 11.2 %all-to-all-start.1 = ((bf16[16,256,128]{2,1,0:T(8,128)(2,1)}), bf16[16,256,128]{2,1,0:T(8,128)(2,1)S(1)}, u32[]{:S(2)}, u32[]{:S(2)}) async-start(bf16[16,256,128]{2,1,0:T(8,128)(2,1)} %copy-done.32), calls=%async_computation.1 | async-start | bytes 2097152 | tf_op jit(solution)/shard_map/all_to_all | solution.py:567
  74.7 17.7 %all-to-all-done.1.refs_0_.prod_ref = bf16[16,256,128]{2,1,0:T(8,128)(2,1)S(1)} async-done(((bf16[16,256,128]{2,1,0:T(8,128)(2,1)}), bf16[16,256,128]{2,1,0:T(8,128)(2,1)S(1)}, u32[]{:S(2)}, u32[]{:S(2)}) %all-to-all-start.1) | async-done | bytes 1048608 | tf_op jit(solution)/shard_map/all_to_all | solution.py:567
  94.9 4.4 %shard_map.158 = (bf16[16,2,256,128]{3,2,1,0:T(8,128)(2,1)S(1)}, f32[16,128,256]{2,1,0:T(8,128)S(1)}) custom-call(bf16[16,256,128]{2,1,0:T(8,128)(2,1)S(1)} %all-to-all-done.1.refs_0_.prod_ref, bf16[16,128,256]{2,1,0:T(8,128)(2,1)S(1)} %copy-done.48, bf16[16,128,256]{2,1,0:T(8,128)(2,1)S(1)} %copy-done.7, ...), custom_call_target="tpu_custom_call" | custom-call | flops 671088640 | bytes 7573504 | tf_op jit(solution)/shard_map/pallas_call | solution.py:555
  102.0 6.9 %all-to-all-start.2 = ((bf16[16,2,256,128]{3,2,1,0:T(8,128)(2,1)}), bf16[16,2,256,128]{3,2,1,0:T(8,128)(2,1)S(1)}, u32[]{:S(2)}, u32[]{:S(2)}) async-start(bf16[16,2,256,128]{3,2,1,0:T(8,128)(2,1)} %copy-done.39), calls=%async_computation.2 | async-start | bytes 4194304 | tf_op jit(solution)/shard_map/all_to_all | solution.py:567
  111.1 3.2 shard_map.159
  119.9 30.0 %all-to-all-done.2.edges_ref = bf16[16,2,256,128]{3,2,1,0:T(8,128)(2,1)S(1)} async-done(((bf16[16,2,256,128]{3,2,1,0:T(8,128)(2,1)}), bf16[16,2,256,128]{3,2,1,0:T(8,128)(2,1)S(1)}, u32[]{:S(2)}, u32[]{:S(2)}) %all-to-all-start.2) | async-done | bytes 2097184 | tf_op jit(solution)/shard_map/all_to_all | solution.py:567
  152.3 11.3 %all-to-all-start.3 = ((bf16[16,256,128]{2,1,0:T(8,128)(2,1)}), bf16[16,256,128]{2,1,0:T(8,128)(2,1)}, u32[]{:S(2)}, u32[]{:S(2)}) async-start(bf16[16,256,128]{2,1,0:T(8,128)(2,1)} %copy-done.34), calls=%async_computation.3 | async-start | bytes 2097152 | tf_op jit(solution)/shard_map/all_to_all | solution.py:567
  166.2 20.3 %all-to-all-done.3.refs_0_.prod_ref = bf16[16,256,128]{2,1,0:T(8,128)(2,1)} async-done(((bf16[16,256,128]{2,1,0:T(8,128)(2,1)}), bf16[16,256,128]{2,1,0:T(8,128)(2,1)}, u32[]{:S(2)}, u32[]{:S(2)}) %all-to-all-start.3) | async-done | bytes 1048608 | tf_op jit(solution)/shard_map/all_to_all | solution.py:567
  189.0 3.0 shard_map.162
  193.0 7.0 %all-to-all-start.4 = ((bf16[16,256,128]{2,1,0:T(8,128)(2,1)}), bf16[16,256,128]{2,1,0:T(8,128)(2,1)}, u32[]{:S(2)}, u32[]{:S(2)}) async-start(bf16[16,256,128]{2,1,0:T(8,128)(2,1)} %copy-done.33), calls=%async_computation.4 | async-start | bytes 2097152 | tf_op jit(solution)/shard_map/all_to_all | solution.py:567
  201.9 21.1 %all-to-all-done.4.grad_ref = bf16[16,256,128]{2,1,0:T(8,128)(2,1)} async-done(((bf16[16,256,128]{2,1,0:T(8,128)(2,1)}), bf16[16,256,128]{2,1,0:T(8,128)(2,1)}, u32[]{:S(2)}, u32[]{:S(2)}) %all-to-all-start.4) | async-done | bytes 1048608 | tf_op jit(solution)/shard_map/all_to_all | solution.py:567
  223.0 2.9 shard_map.164
  227.3 7.0 %all-to-all-start.5 = ((bf16[16,512,128]{2,1,0:T(8,128)(2,1)}), bf16[16,512,128]{2,1,0:T(8,128)(2,1)S(1)}, u32[]{:S(2)}, u32[]{:S(2)}) async-start(bf16[16,512,128]{2,1,0:T(8,128)(2,1)} %copy-done.19), calls=%async_computation.5 | async-start | bytes 4194304 | tf_op jit(solution)/shard_map/all_to_all | solution.py:567
  236.9 3.7 shard_map.165
  242.3 33.2 %all-to-all-done.5.refs_0_.refs_1_.left_ref.right_ref = bf16[16,512,128]{2,1,0:T(8,128)(2,1)S(1)} async-done(((bf16[16,512,128]{2,1,0:T(8,128)(2,1)}), bf16[16,512,128]{2,1,0:T(8,128)(2,1)S(1)}, u32[]{:S(2)}, u32[]{:S(2)}) %all-to-all-start.5) | async-done | bytes 2097184 | tf_op jit(solution)/shard_map/all_to_all | solution.py:567
  283.8 5.2 %shard_map.166 = (f32[16,128,256]{2,1,0:T(8,128)S(1)}, bf16[16,256,128]{2,1,0:T(8,128)(2,1)S(1)}) custom-call(bf16[16,512,128]{2,1,0:T(8,128)(2,1)S(1)} %all-to-all-done.5.refs_0_.refs_1_.left_ref.right_ref, bf16[16,512,128]{2,1,0:T(8,128)(2,1)S(1)} %all-to-all-done.5.refs_0_.refs_1_.left_ref.right_ref, bf16[16,512,256]{2,1,0:T(8,128)(2,1)S(1)} %copy-done.4, ...), custom_call_target="tpu_custom_call" | custom-call | flops 805306368 | bytes 17008640 | tf_op jit(solution)/shard_map/pallas_call | solution.py:555
  291.3 11.4 %all-to-all-start.6 = ((bf16[16,256,128]{2,1,0:T(8,128)(2,1)}), bf16[16,256,128]{2,1,0:T(8,128)(2,1)}, u32[]{:S(2)}, u32[]{:S(2)}) async-start(bf16[16,256,128]{2,1,0:T(8,128)(2,1)} %copy-done.50), calls=%async_computation.6 | async-start | bytes 2097152 | tf_op jit(solution)/shard_map/all_to_all | solution.py:567
  311.4 4.7 %shard_map.167 = (bf16[16,128,256]{2,1,0:T(8,128)(2,1)S(1)}, bf16[1024,128]{1,0:T(8,128)(2,1)S(1)}) custom-call(bf16[16,512,128]{2,1,0:T(8,128)(2,1)S(1)} %all-to-all-done.5.refs_0_.refs_1_.left_ref.right_ref, bf16[16,512,128]{2,1,0:T(8,128)(2,1)S(1)} %all-to-all-done.5.refs_0_.refs_1_.left_ref.right_ref, bf16[16,512,256]{2,1,0:T(8,128)(2,1)S(1)} %copy-done.5, ...), custom_call_target="tpu_custom_call" | custom-call | flops 1744830464 | bytes 17373184 | tf_op jit(solution)/shard_map/pallas_call | solution.py:451
  317.7 8.0 %all-to-all-done.6.grad_ref = bf16[16,256,128]{2,1,0:T(8,128)(2,1)} async-done(((bf16[16,256,128]{2,1,0:T(8,128)(2,1)}), bf16[16,256,128]{2,1,0:T(8,128)(2,1)}, u32[]{:S(2)}, u32[]{:S(2)}) %all-to-all-start.6) | async-done | bytes 1048608 | tf_op jit(solution)/shard_map/all_to_all | solution.py:567
  328.2 2.8 shard_map.168
  332.5 7.0 %all-to-all-start.7 = ((bf16[16,576,128]{2,1,0:T(8,128)(2,1)}), bf16[16,576,128]{2,1,0:T(8,128)(2,1)S(1)}, u32[]{:S(2)}, u32[]{:S(2)}) async-start(bf16[16,576,128]{2,1,0:T(8,128)(2,1)} %copy-done.14), calls=%async_computation.7 | async-start | bytes 4718592 | tf_op jit(solution)/shard_map/all_to_all | solution.py:567
  341.6 2.8 shard_map.169
  348.3 36.8 %all-to-all-done.7.refs_0_.refs_1_.left_ref.right_ref.early_ref = bf16[16,576,128]{2,1,0:T(8,128)(2,1)S(1)} async-done(((bf16[16,576,128]{2,1,0:T(8,128)(2,1)}), bf16[16,576,128]{2,1,0:T(8,128)(2,1)S(1)}, u32[]{:S(2)}, u32[]{:S(2)}) %all-to-all-start.7) | async-done | bytes 2359328 | tf_op jit(solution)/shard_map/all_to_all | solution.py:567
  385.2 3.0 copy-done.2
  391.6 2.8 shard_map.170
  395.1 12.3 %all-to-all-start.8 = ((bf16[16,48,128]{2,1,0:T(8,128)(2,1)}), bf16[16,48,128]{2,1,0:T(8,128)(2,1)S(1)}, u32[]{:S(2)}, u32[]{:S(2)}) async-start(bf16[16,48,128]{2,1,0:T(8,128)(2,1)} %bitcast.26), calls=%async_computation.8 | async-start | bytes 393216 | tf_op jit(solution)/shard_map/all_to_all | solution.py:567
  407.4 6.7 %shard_map.171 = bf16[32,128,128]{2,1,0:T(8,128)(2,1)} custom-call(bf16[16,576,128]{2,1,0:T(8,128)(2,1)} %copy-done, bf16[16,576,128]{2,1,0:T(8,128)(2,1)} %copy-done, bf16[16,512,256]{2,1,0:T(8,128)(2,1)} %copy-done.1, bf16[16,128,256]{2,1,0:T(8,128)(2,1)} %copy-done.30, f32[16,1,256]{2,1,0:T(1,128)} %copy-done.67, bf16[16,128,256]{2,1,0:T(8,128)(2,1)} %copy-done.25, ...), custom_call_target="tpu_custom_call" | custom-call | flops 671088640 | bytes 14337024 | tf_op jit(solution)/shard_map/pallas_call | solution.py:451
  418.9 17.0 %all_to_all.50.got_ref = bf16[16,112,128]{2,1,0:T(8,128)(2,1)S(1)} all-to-all(bf16[16,112,128]{2,1,0:T(8,128)(2,1)} %shard_map.172), channel_id=1, replica_groups=mesh['grp'=2,'row'=8,'col'=2] {'row','col'}, dimensions={0} | all-to-all | bytes 917504 | tf_op jit(solution)/shard_map/all_to_all | solution.py:567
  (170 shorter events, 84.6 us)
Async XLA Ops:
  7.3 10.5 %copy-start.38 = (bf16[32,128,128]{2,1,0:T(8,128)(2,1)S(1)}, bf16[32,128,128]{2,1,0:T(8,128)(2,1)}, u32[]{:S(2)}) copy-start(bf16[32,128,128]{2,1,0:T(8,128)(2,1)} %pair_ref.2) | copy-start | bytes 3145732
  7.3 10.5 %copy-start.61 = (f32[2,128]{1,0:T(2,128)S(1)}, f32[2,128]{1,0:T(2,128)}, u32[]{:S(2)}) copy-start(f32[2,128]{1,0:T(2,128)} %gain_ref.9) | copy-start | bytes 3076
  7.3 10.5 %copy-start.63 = (s32[256]{0:T(256)S(1)}, s32[256]{0:T(256)}, u32[]{:S(2)}) copy-start(s32[256]{0:T(256)} %mask_smem.3) | copy-start | bytes 3076
  7.3 10.5 %copy-start.64 = (s32[256]{0:T(256)S(1)}, s32[256]{0:T(256)}, u32[]{:S(2)}) copy-start(s32[256]{0:T(256)} %chain_smem.3) | copy-start | bytes 3076
  7.3 10.5 %copy-start.68 = (f32[2,128]{1,0:T(2,128)S(1)}, f32[2,128]{1,0:T(2,128)}, u32[]{:S(2)}) copy-start(f32[2,128]{1,0:T(2,128)} %bias_ref.7) | copy-start | bytes 3076
  7.3 10.5 %copy-start.70 = (s32[2]{0:T(128)S(1)}, s32[2]{0:T(128)}, u32[]{:S(2)}) copy-start(s32[2]{0:T(128)} %pad_add_fusion.start_smem) | copy-start | bytes 28
  7.3 10.5 %copy-start.71 = (f32[2,128]{1,0:T(2,128)S(1)}, f32[2,128]{1,0:T(2,128)}, u32[]{:S(2)}) copy-start(f32[2,128]{1,0:T(2,128)} %chain_ref.5) | copy-start | bytes 3076
  7.4 48.6 %all-to-all-start = ((bf16[16,2,256,128]{3,2,1,0:T(8,128)(2,1)}), bf16[16,2,256,128]{3,2,1,0:T(8,128)(2,1)S(1)}, u32[]{:S(2)}, u32[]{:S(2)}) async-start(bf16[16,2,256,128]{3,2,1,0:T(8,128)(2,1)} %shard_map.154), calls=%async_computation | async-start | bytes 4194304 | tf_op jit(solution)/shard_map/all_to_all | solution.py:567
  19.0 38.2 %copy-start.53 = (bf16[640,128]{1,0:T(8,128)(2,1)}, bf16[640,128]{1,0:T(8,128)(2,1)S(1)}, u32[]{:S(2)}) copy-start(bf16[640,128]{1,0:T(8,128)(2,1)S(1)} %copy.17.wt_ref) | copy-start | bytes 491524
  58.2 34.2 %all-to-all-start.1 = ((bf16[16,256,128]{2,1,0:T(8,128)(2,1)}), bf16[16,256,128]{2,1,0:T(8,128)(2,1)S(1)}, u32[]{:S(2)}, u32[]{:S(2)}) async-start(bf16[16,256,128]{2,1,0:T(8,128)(2,1)} %copy-done.32), calls=%async_computation.1 | async-start | bytes 2097152 | tf_op jit(solution)/shard_map/all_to_all | solution.py:567
  72.1 20.3 %copy-start.62 = (f32[2,128]{1,0:T(2,128)S(1)}, f32[2,128]{1,0:T(2,128)}, u32[]{:S(2)}) copy-start(f32[2,128]{1,0:T(2,128)} %hgain_ref.3) | copy-start | bytes 3076
  72.1 20.3 %copy-start.69 = (f32[2,128]{1,0:T(2,128)S(1)}, f32[2,128]{1,0:T(2,128)}, u32[]{:S(2)}) copy-start(f32[2,128]{1,0:T(2,128)} %hbias_ref.3) | copy-start | bytes 3076
  102.0 48.0 %all-to-all-start.2 = ((bf16[16,2,256,128]{3,2,1,0:T(8,128)(2,1)}), bf16[16,2,256,128]{3,2,1,0:T(8,128)(2,1)S(1)}, u32[]{:S(2)}, u32[]{:S(2)}) async-start(bf16[16,2,256,128]{3,2,1,0:T(8,128)(2,1)} %copy-done.39), calls=%async_computation.2 | async-start | bytes 4194304 | tf_op jit(solution)/shard_map/all_to_all | solution.py:567
  152.3 34.3 %all-to-all-start.3 = ((bf16[16,256,128]{2,1,0:T(8,128)(2,1)}), bf16[16,256,128]{2,1,0:T(8,128)(2,1)}, u32[]{:S(2)}, u32[]{:S(2)}) async-start(bf16[16,256,128]{2,1,0:T(8,128)(2,1)} %copy-done.34), calls=%async_computation.3 | async-start | bytes 2097152 | tf_op jit(solution)/shard_map/all_to_all | solution.py:567
  163.5 23.0 %copy-start.56 = (bf16[128,128]{1,0:T(8,128)(2,1)S(1)}, bf16[128,128]{1,0:T(8,128)(2,1)}, u32[]{:S(2)}) copy-start(bf16[128,128]{1,0:T(8,128)(2,1)} %get-tuple-element.101.refs_3_.ow_ref) | copy-start | bytes 98308
  193.0 30.0 %copy-start.18 = (bf16[8,2,256,256]{3,2,1,0:T(8,128)(2,1)S(1)}, bf16[8,2,256,256]{3,2,1,0:T(8,128)(2,1)}, u32[]{:S(2)}) copy-start(bf16[8,2,256,256]{3,2,1,0:T(8,128)(2,1)} %copy-done.17) | copy-start | bytes 6291460
  193.0 30.0 %all-to-all-start.4 = ((bf16[16,256,128]{2,1,0:T(8,128)(2,1)}), bf16[16,256,128]{2,1,0:T(8,128)(2,1)}, u32[]{:S(2)}, u32[]{:S(2)}) async-start(bf16[16,256,128]{2,1,0:T(8,128)(2,1)} %copy-done.33), calls=%async_computation.4 | async-start | bytes 2097152 | tf_op jit(solution)/shard_map/all_to_all | solution.py:567
  227.3 7.0 %copy-start.77 = (bf16[1,128,128]{2,1,0:T(8,128)(2,1)S(1)}, bf16[1,128,128]{2,1,0:T(8,128)(2,1)}, u32[]{:S(2)}) copy-start(bf16[1,128,128]{2,1,0:T(8,128)(2,1)} %get-tuple-element.103) | copy-start | bytes 98308
  227.3 48.1 %all-to-all-start.5 = ((bf16[16,512,128]{2,1,0:T(8,128)(2,1)}), bf16[16,512,128]{2,1,0:T(8,128)(2,1)S(1)}, u32[]{:S(2)}, u32[]{:S(2)}) async-start(bf16[16,512,128]{2,1,0:T(8,128)(2,1)} %copy-done.19), calls=%async_computation.5 | async-start | bytes 4194304 | tf_op jit(solution)/shard_map/all_to_all | solution.py:567
  234.3 41.1 %copy-start.55 = (bf16[128,128]{1,0:T(8,128)(2,1)S(1)}, bf16[128,128]{1,0:T(8,128)(2,1)}, u32[]{:S(2)}) copy-start(bf16[128,128]{1,0:T(8,128)(2,1)} %get-tuple-element.100.refs_12_.ow_ref) | copy-start | bytes 98308
  234.3 41.1 %copy-start.66 = (f32[16,1,256]{2,1,0:T(1,128)S(1)}, f32[16,1,256]{2,1,0:T(1,128)}, u32[]{:S(2)}) copy-start(f32[16,1,256]{2,1,0:T(1,128)} %copy-done.65) | copy-start | bytes 49156
  275.4 2.2 copy-start.4
  291.3 11.4 %copy-start.60 = (f32[136,128]{1,0:T(8,128)S(1)}, f32[136,128]{1,0:T(8,128)}, u32[]{:S(2)}) copy-start(f32[136,128]{1,0:T(8,128)} %copy-done.59) | copy-start | bytes 208900
  291.3 34.4 %all-to-all-start.6 = ((bf16[16,256,128]{2,1,0:T(8,128)(2,1)}), bf16[16,256,128]{2,1,0:T(8,128)(2,1)}, u32[]{:S(2)}, u32[]{:S(2)}) async-start(bf16[16,256,128]{2,1,0:T(8,128)(2,1)} %copy-done.50), calls=%async_computation.6 | async-start | bytes 2097152 | tf_op jit(solution)/shard_map/all_to_all | solution.py:567
  302.7 2.2 copy-start.5
  332.5 7.0 %copy-start.73 = (f32[2,128]{1,0:T(2,128)S(1)}, f32[2,128]{1,0:T(2,128)}, u32[]{:S(2)}) copy-start(f32[2,128]{1,0:T(2,128)} %chain_ref.5) | copy-start | bytes 3076
  332.5 52.7 %all-to-all-start.7 = ((bf16[16,576,128]{2,1,0:T(8,128)(2,1)}), bf16[16,576,128]{2,1,0:T(8,128)(2,1)S(1)}, u32[]{:S(2)}, u32[]{:S(2)}) async-start(bf16[16,576,128]{2,1,0:T(8,128)(2,1)} %copy-done.14), calls=%async_computation.7 | async-start | bytes 4718592 | tf_op jit(solution)/shard_map/all_to_all | solution.py:567
  341.6 43.5 %copy-start.26 = (bf16[16,128,256]{2,1,0:T(8,128)(2,1)S(1)}, bf16[16,128,256]{2,1,0:T(8,128)(2,1)}, u32[]{:S(2)}) copy-start(bf16[16,128,256]{2,1,0:T(8,128)(2,1)} %copy-done.25) | copy-start | bytes 3145732
  348.3 46.1 %copy-start.67 = (f32[16,1,256]{2,1,0:T(1,128)}, f32[16,1,256]{2,1,0:T(1,128)S(1)}, u32[]{:S(2)}) copy-start(f32[16,1,256]{2,1,0:T(1,128)S(1)} %get-tuple-element.89.inv_ref) | copy-start | bytes 49156
  385.1 9.3 %copy-start = (bf16[16,576,128]{2,1,0:T(8,128)(2,1)}, bf16[16,576,128]{2,1,0:T(8,128)(2,1)S(1)}, u32[]{:S(2)}) copy-start(bf16[16,576,128]{2,1,0:T(8,128)(2,1)S(1)} %all-to-all-done.7.refs_0_.refs_1_.left_ref.right_ref.early_ref) | copy-start | bytes 7077892
  385.1 3.0 copy-start.2
  395.1 21.3 %all-to-all-start.8 = ((bf16[16,48,128]{2,1,0:T(8,128)(2,1)}), bf16[16,48,128]{2,1,0:T(8,128)(2,1)S(1)}, u32[]{:S(2)}, u32[]{:S(2)}) async-start(bf16[16,48,128]{2,1,0:T(8,128)(2,1)} %bitcast.26), calls=%async_computation.8 | async-start | bytes 393216 | tf_op jit(solution)/shard_map/all_to_all | solution.py:567
  (55 other events, 63.0 us)

commit v7 on v6

--- a/solution.py
+++ b/solution.py
@@ -12,8 +12,7 @@
 F32 = jnp.float32
 BF16 = jnp.bfloat16
 CHANNEL_VMEM = 24 * 1024 * 1024
-CELL_VMEM = 30 * 1024 * 1024
-LOOP_VMEM = 32 * 1024 * 1024
+CELL_VMEM = 50 * 1024 * 1024
 ALL_VMEM = 60 * 1024 * 1024
 
 
@@ -109,20 +108,65 @@
     pl.when(index == count - 1)(fill)
 
 
-def looped_kernel(kernel, steps, hows, *refs):
+def looped_kernel(kernel, steps, in_hows, out_hows, scratches, *refs):
+    n_in, n_out = len(in_hows), len(out_hows)
+    ins, outs, scratch = refs[:n_in], refs[n_in : n_in + n_out], refs[n_in + n_out : n_in + n_out + scratches]
+    bufs = list(refs[n_in + n_out + scratches : -3])
+    whole_sems, in_sems, out_sems = refs[-3:]
+
+    def part(ref, how, step, first):
+        axis, _, size = how
+        start = (step + first) * size
+        here = pl.ds(start if isinstance(start, int) else pl.multiple_of(start, size), size)
+        return ref.at[tuple(here if n == axis else slice(None) for n in range(axis + 1))]
+
+    def copy_in(k, step):
+        how = in_hows[k]
+        if how is None:
+            return pltpu.make_async_copy(ins[k], bufs[k], whole_sems.at[k])
+        return pltpu.make_async_copy(
+            part(ins[k], how, step, how[1]), part(bufs[k], how, step, 0), in_sems.at[k, step]
+        )
+
+    def copy_out(k, step):
+        how = out_hows[k]
+        return pltpu.make_async_copy(
+            part(bufs[n_in + k], how, step, 0), part(outs[k], how, step, 0), out_sems.at[k, step]
+        )
+
+    wholes = [k for k in range(n_in) if in_hows[k] is None]
+    parts = [k for k in range(n_in) if in_hows[k] is not None]
+    moved = [k for k in range(n_out) if out_hows[k] is not None]
+    for k in parts:
+        copy_in(k, 0).start()
+    for k in wholes:
+        copy_in(k, 0).start()
+    for step in range(1, steps):
+        for k in parts:
+            copy_in(k, step).start()
+    for k in wholes:
+        copy_in(k, 0).wait()
+
     @pl.loop(0, steps)
     def _(step):
         views = []
-        for ref, how in zip(refs, hows):
-            if how is None:
-                views.append(ref)
-                continue
-            axis, first, size = how
-            here = pl.ds(pl.multiple_of((step + first) * size, size), size)
-            views.append(ref.at[tuple(here if n == axis else slice(None) for n in range(axis + 1))])
+        for k in range(n_in):
+            if in_hows[k] is None:
+                views.append(bufs[k])
+            else:
+                copy_in(k, step).wait()
+                views.append(part(bufs[k], in_hows[k], step, 0))
+        for k in range(n_out):
+            views.append(outs[k] if out_hows[k] is None else part(bufs[n_in + k], out_hows[k], step, 0))
         STEP.append((step, steps))
-        kernel(*views, *refs[len(hows) :])
+        kernel(*views, *scratch)
         STEP.pop()
+        for k in moved:
+            copy_out(k, step).start()
+
+    for step in range(steps):
+        for k in moved:
+            copy_out(k, step).wait()
 
 
 def load_columns(vec, *rows):
@@ -516,12 +560,30 @@
             out_ref[ch, sub] = get_channel(edges, ch, sub, 2, dims)
 
 
-def product_grad_kernel(dims, outgoing, sides_ref, grad_ref, *rest):
-    out_ref, grad, result = rest[-3:]
+def product_grad_kernel(dims, outgoing, count, sides_hbm, grad_ref, *refs):
+    terms, (out_hbm, grad, result, sides_ref, out_ref, side_sems, out_sems, term_sems) = refs[:count], refs[count:]
+    channels, devices = sides_ref.shape[0], out_ref.shape[0]
+    rows = out_ref.shape[1]
+
+    def side_copy(ch):
+        return pltpu.make_async_copy(sides_hbm.at[ch], sides_ref.at[ch], side_sems.at[ch])
+
+    def out_copy(d):
+        return pltpu.make_async_copy(out_ref.at[d], out_hbm.at[d, pl.ds(0, rows)], out_sems.at[d])
+
+    def term_copy(n):
+        extra = terms[n].shape[1]
+        return pltpu.make_async_copy(terms[n], out_hbm.at[:, pl.ds(rows, extra)], term_sems.at[n])
+
+    for ch in range(channels):
+        side_copy(ch).start()
+    for n in range(count):
+        term_copy(n).start()
     widen(grad_ref, grad)
-    for ch in range(dims[3]):
+    for ch in range(channels):
+        gp = get_channel(grad, ch, 0, 1, dims)
+        side_copy(ch).wait()
         left, right = sides_ref[ch, 0], sides_ref[ch, 1]
-        gp = get_channel(grad, ch, 0, 1, dims)
         if outgoing:
             grad_left = dot(gp, right, 1, 0)
             grad_right = dot(gp, left, 0, 0)
@@ -530,31 +592,50 @@
             grad_right = dot(left, gp, 1, 0)
         put_channel(result, grad_left, ch, 0, 2, dims)
         put_channel(result, grad_right, ch, 1, 2, dims)
-    narrow(result, out_ref)
-    for terms_ref in rest[:-3]:
-        out_ref[:, out_ref.shape[1] - terms_ref.shape[1] :, :] = terms_ref[...]
+    for d in range(devices):
+        out_ref[d] = result[d * rows : (d + 1) * rows, :].astype(BF16)
+        out_copy(d).start()
+    for n in range(count):
+        term_copy(n).wait()
+    for d in range(devices):
+        out_copy(d).wait()
 
 
 def loop_call(kernel, steps, ins, outs, scratch, flops=0):
     def part(shape, how):
         return how if how is None or isinstance(how, tuple) else (how, 0, shape[how] // steps)
 
-    hows = [part(a.shape, how) for a, how in ins] + [part(shape, how) for (shape, _), how in outs]
+    in_hows = [part(a.shape, how) for a, how in ins]
+    out_hows = [part(shape, how) for (shape, _), how in outs]
+
+    def buffer(shape, dtype, how):
+        if how is None:
+            return pltpu.VMEM(shape, dtype)
+        return pltpu.VMEM(tuple(how[2] * steps if n == how[0] else m for n, m in enumerate(shape)), dtype)
+
+    buffers = [buffer(a.shape, a.dtype, how) for (a, _), how in zip(ins, in_hows)]
+    for ((shape, dtype), _), how in zip(outs, out_hows):
+        buffers.append(pltpu.VMEM((8, 128), F32) if how is None else buffer(shape, dtype, how))
+    sems = [
+        pltpu.SemaphoreType.DMA((len(ins),)), pltpu.SemaphoreType.DMA((len(ins), steps)),
+        pltpu.SemaphoreType.DMA((len(outs), steps)),
+    ]
     made = whole_call(
-        functools.partial(looped_kernel, kernel, steps, hows), [a for a, _ in ins], [o for o, _ in outs],
-        scratch, flops, LOOP_VMEM,
+        functools.partial(looped_kernel, kernel, steps, in_hows, out_hows, len(scratch)),
+        [a for a, _ in ins], [o for o, _ in outs], list(scratch) + buffers + sems, flops, CELL_VMEM,
+        [pltpu.HBM] * len(ins), [pltpu.VMEM if how is None else pltpu.HBM for how in out_hows],
     )
     return made if len(outs) > 1 else (made,)
 
 
-def whole_call(kernel, ins, outs, scratch, flops, vmem=None):
+def whole_call(kernel, ins, outs, scratch, flops, vmem=None, in_spaces=None, out_spaces=None):
     moved = sum(a.size * a.dtype.itemsize for a in ins)
     moved += sum(functools.reduce(lambda x, y: x * y, s, 1) * jnp.dtype(t).itemsize for s, t in outs)
-    specs = [pl.BlockSpec(memory_space=pltpu.VMEM)] * len(outs)
+    specs = [pl.BlockSpec(memory_space=m) for m in out_spaces or [pltpu.VMEM] * len(outs)]
     shapes = [jax.ShapeDtypeStruct(s, t) for s, t in outs]
     return pl.pallas_call(
         kernel,
-        in_specs=[pl.BlockSpec(memory_space=pltpu.VMEM)] * len(ins),
+        in_specs=[pl.BlockSpec(memory_space=m) for m in in_spaces or [pltpu.VMEM] * len(ins)],
         out_specs=specs if len(outs) > 1 else specs[0],
         out_shape=shapes if len(outs) > 1 else shapes[0],
         scratch_shapes=scratch,
@@ -622,8 +703,14 @@
     def product_grad(sides, grad, outgoing, *terms):
         out_rows = 2 * side + sum(t.shape[1] for t in terms)
         return whole_call(
-            functools.partial(product_grad_kernel, dims, outgoing), [sides, grad, *terms],
-            [((devices, out_rows, cols), BF16)], [wide(1), wide(2)], 2 * tri_flops,
+            functools.partial(product_grad_kernel, dims, outgoing, len(terms)), [sides, grad, *terms],
+            [((devices, out_rows, cols), BF16)],
+            [
+                wide(1), wide(2), pltpu.VMEM(sides.shape, BF16), pltpu.VMEM((devices, 2 * side, cols), BF16),
+                pltpu.SemaphoreType.DMA((cpd,)), pltpu.SemaphoreType.DMA((devices,)),
+                pltpu.SemaphoreType.DMA((max(1, len(terms)),)),
+            ],
+            2 * tri_flops, None, [pltpu.HBM, pltpu.VMEM] + [pltpu.HBM] * len(terms), [pltpu.HBM],
         )
 
     def halves(grads):

time: 439 us -> 434 us (0.989)
  local copies, waits for them, and re-layouts: 76 us -> 39.8 us
  Pallas kernels: 59.8 us -> 83.2 us
  waiting for transfers between devices: 201 us -> 208 us
    unnamed x158 -> x120, local copies, waits for them, and re-layouts: 70.6 us -> 35.7 us
    pallas_call x11, Pallas kernels: 27.2 us -> 42.3 us  [whole_call(): pl.pallas_call(kernel, in_specs=[pl.BlockSpec(memory_space=m) for m in in...]
    pallas_call x9, Pallas kernels: 32.6 us -> 40.9 us  [cell_call(): pl.pallas_call(kernel, grid_spec=pltpu.PrefetchScalarGridSpec(num_scalar_...]
    all_to_all x9, waiting for transfers between devices: 201 us -> 208 us  [exchange(): return lax.all_to_all(array, AXES, split_axis=0, concat_axis=0, tiled=True)]
  transfers between devices with their start and end apart: 9 -> 9, of which waited for: 9 -> 9; matrix products, arithmetic and copies ran while one was open for 1% -> 1% of each run, Pallas kernels for 6% -> 8%
where the time goes in v7:
time: 434 us; the launch traced here: 431 us
  waiting for transfers between devices  208 us (48%)
  Pallas kernels  83.2 us (19%)
  starting transfers between devices  81.6 us (19%)
  local copies, waits for them, and re-layouts  39.8 us (9%)
  blocking collectives  17 us (4%)
    all_to_all x9, waiting for transfers between devices, exchange(): return lax.all_to_all(array, AXES, split_axis=0, concat_axis=0, tiled=True)  208 us
    all_to_all x9, starting transfers between devices, exchange(): return lax.all_to_all(array, AXES, split_axis=0, concat_axis=0, tiled=True)  81.6 us
    pallas_call x11, Pallas kernels, whole_call(): pl.pallas_call(kernel, in_specs=[pl.BlockSpec(memory_space=m) for m in in...  42.3 us
    pallas_call x9, Pallas kernels, cell_call(): pl.pallas_call(kernel, grid_spec=pltpu.PrefetchScalarGridSpec(num_scalar_...  40.9 us
    unnamed x120, local copies, waits for them, and re-layouts  35.7 us
    all_to_all x1, blocking collectives, exchange(): return lax.all_to_all(array, AXES, split_axis=0, concat_axis=0, tiled=True)  17 us
  transfers between devices with their start and end apart: 9, of which 9 were waited for; matrix products, arithmetic and copies ran while one was open for 1% of the time, Pallas kernels for 8%

profile of v7, /device:TPU:0, one launch (start us, length us, event | category | flops | bytes accessed | tf_op | source)
XLA Modules:
  0.0 431.5 jit_solution(18430982390177750073)
XLA Ops:
  1.2 6.1 %shard_map.154 = bf16[16,2,256,128]{3,2,1,0:T(8,128)(2,1)} custom-call(s32[256]{0:T(256)} %mask_smem.3, s32[256]{0:T(256)} %chain_smem.3, s32[2]{0:T(128)} %pad_add_fusion.start_smem, bf16[32,128,128]{2,1,0:T(8,128)(2,1)} %pair_ref.2, s32[2,128]{1,0:T(2,128)} %bitcast.30, s32[2,128]{1,0:T(2,128)} %bitcast.32, bf16[2,128,640]{2,1,0:T(8,128)(2,1)} %w_ref.1, ...), custom_call_target="tpu_custom_call" | custom-call | flops 536870912 | bytes 3477504 | tf_op jit(solution)/shard_map/pallas_call | solution.py:495
  7.3 7.5 %all-to-all-start = ((bf16[16,2,256,128]{3,2,1,0:T(8,128)(2,1)}), bf16[16,2,256,128]{3,2,1,0:T(8,128)(2,1)S(1)}, u32[]{:S(2)}, u32[]{:S(2)}) async-start(bf16[16,2,256,128]{3,2,1,0:T(8,128)(2,1)} %shard_map.154), calls=%async_computation | async-start | bytes 4194304 | tf_op jit(solution)/shard_map/all_to_all | solution.py:648
  15.8 4.4 %shard_map.155 = (bf16[16,128,256]{2,1,0:T(8,128)(2,1)S(1)}, bf16[16,128,256]{2,1,0:T(8,128)(2,1)S(1)}, bf16[16,128,256]{2,1,0:T(8,128)(2,1)S(1)}, f32[16,2,256]{2,1,0:T(2,128)S(1)}) custom-call(s32[256]{0:T(256)S(1)} %copy-done.43, s32[256]{0:T(256)S(1)} %copy-done.44, s32[2]{0:T(128)S(1)} %copy-done.52, bf16[32,128,128]{2,1,0:T(8,128)(2,1)} %pair_ref.2, ...), custom_call_target="tpu_custom_call" | custom-call | flops 268435456 | bytes 5444608 | tf_op jit(solution)/shard_map/pallas_call | solution.py:495
  23.3 32.7 %all-to-all-done.edges_ref = bf16[16,2,256,128]{3,2,1,0:T(8,128)(2,1)S(1)} async-done(((bf16[16,2,256,128]{3,2,1,0:T(8,128)(2,1)}), bf16[16,2,256,128]{3,2,1,0:T(8,128)(2,1)S(1)}, u32[]{:S(2)}, u32[]{:S(2)}) %all-to-all-start) | async-done | bytes 2097184 | tf_op jit(solution)/shard_map/all_to_all | solution.py:648
  58.2 11.2 %all-to-all-start.1 = ((bf16[16,256,128]{2,1,0:T(8,128)(2,1)}), bf16[16,256,128]{2,1,0:T(8,128)(2,1)S(1)}, u32[]{:S(2)}, u32[]{:S(2)}) async-start(bf16[16,256,128]{2,1,0:T(8,128)(2,1)} %copy-done.17), calls=%async_computation.1 | async-start | bytes 2097152 | tf_op jit(solution)/shard_map/all_to_all | solution.py:648
  76.1 16.3 %all-to-all-done.1.refs_0_.prod_ref = bf16[16,256,128]{2,1,0:T(8,128)(2,1)S(1)} async-done(((bf16[16,256,128]{2,1,0:T(8,128)(2,1)}), bf16[16,256,128]{2,1,0:T(8,128)(2,1)S(1)}, u32[]{:S(2)}, u32[]{:S(2)}) %all-to-all-start.1) | async-done | bytes 1048608 | tf_op jit(solution)/shard_map/all_to_all | solution.py:648
  96.1 6.4 %shard_map.158 = (bf16[16,2,256,128]{3,2,1,0:T(8,128)(2,1)}, f32[16,128,256]{2,1,0:T(8,128)}) custom-call(bf16[16,256,128]{2,1,0:T(8,128)(2,1)S(1)} %all-to-all-done.1.refs_0_.prod_ref, bf16[16,128,256]{2,1,0:T(8,128)(2,1)S(1)} %copy-done.26, bf16[16,128,256]{2,1,0:T(8,128)(2,1)S(1)} %copy-done.2, f32[16,2,256]{2,1,0:T(2,128)S(1)} %get-tuple-element.57.refs_3_.flags_ref, ...), custom_call_target="tpu_custom_call" | custom-call | flops 671088640 | bytes 7573504 | tf_op jit(solution)/shard_map/pallas_call | solution.py:636
  102.6 6.9 %all-to-all-start.2 = ((bf16[16,2,256,128]{3,2,1,0:T(8,128)(2,1)}), bf16[16,2,256,128]{3,2,1,0:T(8,128)(2,1)S(1)}, u32[]{:S(2)}, u32[]{:S(2)}) async-start(bf16[16,2,256,128]{3,2,1,0:T(8,128)(2,1)} %get-tuple-element.58), calls=%async_computation.2 | async-start | bytes 4194304 | tf_op jit(solution)/shard_map/all_to_all | solution.py:648
  111.0 5.8 %shard_map.159 = (bf16[16,512,256]{2,1,0:T(8,128)(2,1)}, bf16[16,128,256]{2,1,0:T(8,128)(2,1)S(1)}, bf16[16,128,256]{2,1,0:T(8,128)(2,1)S(1)}, f32[16,1,256]{2,1,0:T(1,128)S(1)}, bf16[16,128,256]{2,1,0:T(8,128)(2,1)S(1)}) custom-call(f32[16,128,256]{2,1,0:T(8,128)} %get-tuple-element.60.z_ref, f32[16,2,256]{2,1,0:T(2,128)S(1)} %get-tuple-element.57.refs_3_.flags_ref, ...), custom_call_target="tpu_custom_call" | custom-call | flops 671088640 | bytes 9653248 | tf_op jit(solution)/shard_map/pallas_call | solution.py:495
  120.4 30.1 %all-to-all-done.2.edges_ref = bf16[16,2,256,128]{3,2,1,0:T(8,128)(2,1)S(1)} async-done(((bf16[16,2,256,128]{3,2,1,0:T(8,128)(2,1)}), bf16[16,2,256,128]{3,2,1,0:T(8,128)(2,1)S(1)}, u32[]{:S(2)}, u32[]{:S(2)}) %all-to-all-start.2) | async-done | bytes 2097184 | tf_op jit(solution)/shard_map/all_to_all | solution.py:648
  152.9 11.3 %all-to-all-start.3 = ((bf16[16,256,128]{2,1,0:T(8,128)(2,1)}), bf16[16,256,128]{2,1,0:T(8,128)(2,1)}, u32[]{:S(2)}, u32[]{:S(2)}) async-start(bf16[16,256,128]{2,1,0:T(8,128)(2,1)} %copy-done.19), calls=%async_computation.3 | async-start | bytes 2097152 | tf_op jit(solution)/shard_map/all_to_all | solution.py:648
  166.8 20.3 %all-to-all-done.3.refs_0_.prod_ref = bf16[16,256,128]{2,1,0:T(8,128)(2,1)} async-done(((bf16[16,256,128]{2,1,0:T(8,128)(2,1)}), bf16[16,256,128]{2,1,0:T(8,128)(2,1)}, u32[]{:S(2)}, u32[]{:S(2)}) %all-to-all-start.3) | async-done | bytes 1048608 | tf_op jit(solution)/shard_map/all_to_all | solution.py:648
  189.1 3.2 shard_map.162
  193.3 7.1 %all-to-all-start.4 = ((bf16[16,256,128]{2,1,0:T(8,128)(2,1)}), bf16[16,256,128]{2,1,0:T(8,128)(2,1)}, u32[]{:S(2)}, u32[]{:S(2)}) async-start(bf16[16,256,128]{2,1,0:T(8,128)(2,1)} %copy-done.18), calls=%async_computation.4 | async-start | bytes 2097152 | tf_op jit(solution)/shard_map/all_to_all | solution.py:648
  202.8 20.5 %all-to-all-done.4.grad_ref = bf16[16,256,128]{2,1,0:T(8,128)(2,1)} async-done(((bf16[16,256,128]{2,1,0:T(8,128)(2,1)}), bf16[16,256,128]{2,1,0:T(8,128)(2,1)}, u32[]{:S(2)}, u32[]{:S(2)}) %all-to-all-start.4) | async-done | bytes 1048608 | tf_op jit(solution)/shard_map/all_to_all | solution.py:648
  223.3 7.3 %shard_map.164 = bf16[16,512,128]{2,1,0:T(8,128)(2,1)S(1)} custom-call(bf16[8,2,256,256]{3,2,1,0:T(8,128)(2,1)S(1)} %copy-done.7, bf16[16,256,128]{2,1,0:T(8,128)(2,1)} %all-to-all-done.4.grad_ref), custom_call_target="tpu_custom_call" | custom-call | flops 536870912 | bytes 5242880 | tf_op jit(solution)/shard_map/pallas_call | solution.py:636
  231.9 7.0 %all-to-all-start.5 = ((bf16[16,512,128]{2,1,0:T(8,128)(2,1)}), bf16[16,512,128]{2,1,0:T(8,128)(2,1)}, u32[]{:S(2)}, u32[]{:S(2)}) async-start(bf16[16,512,128]{2,1,0:T(8,128)(2,1)} %copy-done.8), calls=%async_computation.5 | async-start | bytes 4194304 | tf_op jit(solution)/shard_map/all_to_all | solution.py:648
  241.3 3.9 shard_map.165
  245.8 34.3 %all-to-all-done.5.refs_0_.refs_1_.left_ref.right_ref = bf16[16,512,128]{2,1,0:T(8,128)(2,1)} async-done(((bf16[16,512,128]{2,1,0:T(8,128)(2,1)}), bf16[16,512,128]{2,1,0:T(8,128)(2,1)}, u32[]{:S(2)}, u32[]{:S(2)}) %all-to-all-start.5) | async-done | bytes 2097184 | tf_op jit(solution)/shard_map/all_to_all | solution.py:648
  282.4 8.0 %shard_map.166 = (f32[16,128,256]{2,1,0:T(8,128)}, bf16[16,256,128]{2,1,0:T(8,128)(2,1)}) custom-call(bf16[16,512,128]{2,1,0:T(8,128)(2,1)} %all-to-all-done.5.refs_0_.refs_1_.left_ref.right_ref, bf16[16,512,128]{2,1,0:T(8,128)(2,1)} %all-to-all-done.5.refs_0_.refs_1_.left_ref.right_ref, bf16[16,512,256]{2,1,0:T(8,128)(2,1)} %get-tuple-element.72.refs_2_.fac_ref, ...), custom_call_target="tpu_custom_call" | custom-call | flops 805306368 | bytes 17008640 | tf_op jit(solution)/shard_map/pallas_call | solution.py:636
  290.3 11.3 %all-to-all-start.6 = ((bf16[16,256,128]{2,1,0:T(8,128)(2,1)}), bf16[16,256,128]{2,1,0:T(8,128)(2,1)}, u32[]{:S(2)}, u32[]{:S(2)}) async-start(bf16[16,256,128]{2,1,0:T(8,128)(2,1)} %get-tuple-element.76), calls=%async_computation.6 | async-start | bytes 2097152 | tf_op jit(solution)/shard_map/all_to_all | solution.py:648
  304.5 7.2 %shard_map.167 = (bf16[16,128,256]{2,1,0:T(8,128)(2,1)S(1)}, bf16[1024,128]{1,0:T(8,128)(2,1)S(1)}) custom-call(bf16[16,512,128]{2,1,0:T(8,128)(2,1)} %all-to-all-done.5.refs_0_.refs_1_.left_ref.right_ref, bf16[16,512,128]{2,1,0:T(8,128)(2,1)} %all-to-all-done.5.refs_0_.refs_1_.left_ref.right_ref, bf16[16,512,256]{2,1,0:T(8,128)(2,1)} %get-tuple-element.72.refs_2_.fac_ref, ...), custom_call_target="tpu_custom_call" | custom-call | flops 1744830464 | bytes 17373184 | tf_op jit(solution)/shard_map/pallas_call | solution.py:495
  313.4 11.2 %all-to-all-done.6.grad_ref = bf16[16,256,128]{2,1,0:T(8,128)(2,1)} async-done(((bf16[16,256,128]{2,1,0:T(8,128)(2,1)}), bf16[16,256,128]{2,1,0:T(8,128)(2,1)}, u32[]{:S(2)}, u32[]{:S(2)}) %all-to-all-start.6) | async-done | bytes 1048608 | tf_op jit(solution)/shard_map/all_to_all | solution.py:648
  325.6 5.9 %shard_map.168 = bf16[16,576,128]{2,1,0:T(8,128)(2,1)} custom-call(bf16[8,2,256,256]{3,2,1,0:T(8,128)(2,1)S(1)} %copy-done.10, bf16[16,256,128]{2,1,0:T(8,128)(2,1)} %all-to-all-done.6.grad_ref, bf16[16,64,128]{2,1,0:T(8,128)(2,1)S(1)} %bitcast.28), custom_call_target="tpu_custom_call" | custom-call | flops 536870912 | bytes 5767168 | tf_op jit(solution)/shard_map/pallas_call | solution.py:636
  331.6 7.1 %all-to-all-start.7 = ((bf16[16,576,128]{2,1,0:T(8,128)(2,1)}), bf16[16,576,128]{2,1,0:T(8,128)(2,1)}, u32[]{:S(2)}, u32[]{:S(2)}) async-start(bf16[16,576,128]{2,1,0:T(8,128)(2,1)} %shard_map.168), calls=%async_computation.7 | async-start | bytes 4718592 | tf_op jit(solution)/shard_map/all_to_all | solution.py:648
  339.9 4.1 shard_map.169
  343.9 40.4 %all-to-all-done.7.refs_0_.refs_1_.left_ref.right_ref.early_ref = bf16[16,576,128]{2,1,0:T(8,128)(2,1)} async-done(((bf16[16,576,128]{2,1,0:T(8,128)(2,1)}), bf16[16,576,128]{2,1,0:T(8,128)(2,1)}, u32[]{:S(2)}, u32[]{:S(2)}) %all-to-all-start.7) | async-done | bytes 2359328 | tf_op jit(solution)/shard_map/all_to_all | solution.py:648
  384.4 5.4 %shard_map.170 = bf16[768,128]{1,0:T(8,128)(2,1)} custom-call(bf16[16,576,128]{2,1,0:T(8,128)(2,1)} %all-to-all-done.7.refs_0_.refs_1_.left_ref.right_ref.early_ref, bf16[16,576,128]{2,1,0:T(8,128)(2,1)} %all-to-all-done.7.refs_0_.refs_1_.left_ref.right_ref.early_ref, bf16[16,512,256]{2,1,0:T(8,128)(2,1)} %get-tuple-element.85.refs_2_.fac_ref, ...), custom_call_target="tpu_custom_call" | custom-call | flops 1342177280 | bytes 12419072 | tf_op jit(solution)/shard_map/pallas_call | solution.py:636
  389.8 12.3 %all-to-all-start.8 = ((bf16[16,48,128]{2,1,0:T(8,128)(2,1)}), bf16[16,48,128]{2,1,0:T(8,128)(2,1)S(1)}, u32[]{:S(2)}, u32[]{:S(2)}) async-start(bf16[16,48,128]{2,1,0:T(8,128)(2,1)} %bitcast.14), calls=%async_computation.8 | async-start | bytes 393216 | tf_op jit(solution)/shard_map/all_to_all | solution.py:648
  402.1 6.7 %shard_map.171 = bf16[32,128,128]{2,1,0:T(8,128)(2,1)} custom-call(bf16[16,576,128]{2,1,0:T(8,128)(2,1)} %all-to-all-done.7.refs_0_.refs_1_.left_ref.right_ref.early_ref, bf16[16,576,128]{2,1,0:T(8,128)(2,1)} %all-to-all-done.7.refs_0_.refs_1_.left_ref.right_ref.early_ref, bf16[16,512,256]{2,1,0:T(8,128)(2,1)} %get-tuple-element.85.refs_2_.fac_ref, ...), custom_call_target="tpu_custom_call" | custom-call | flops 671088640 | bytes 14337024 | tf_op jit(solution)/shard_map/pallas_call | solution.py:495
  408.8 2.3 all-to-all-done.8.late_ref
  413.6 17.0 %all_to_all.50.got_ref = bf16[16,112,128]{2,1,0:T(8,128)(2,1)S(1)} all-to-all(bf16[16,112,128]{2,1,0:T(8,128)(2,1)} %shard_map.172), channel_id=1, replica_groups=mesh['grp'=2,'row'=8,'col'=2] {'row','col'}, dimensions={0} | all-to-all | bytes 917504 | tf_op jit(solution)/shard_map/all_to_all | solution.py:648
  (132 shorter events, 49.1 us)
Async XLA Ops:
  7.3 7.6 %copy-start.56 = (bf16[2,128,640]{2,1,0:T(8,128)(2,1)S(1)}, bf16[2,128,640]{2,1,0:T(8,128)(2,1)}, u32[]{:S(2)}) copy-start(bf16[2,128,640]{2,1,0:T(8,128)(2,1)} %w_ref.1) | copy-start | bytes 983044
  7.3 8.5 %copy-start.41 = (f32[2,128]{1,0:T(2,128)S(1)}, f32[2,128]{1,0:T(2,128)}, u32[]{:S(2)}) copy-start(f32[2,128]{1,0:T(2,128)} %gain_ref.9) | copy-start | bytes 3076
  7.3 8.5 %copy-start.43 = (s32[256]{0:T(256)S(1)}, s32[256]{0:T(256)}, u32[]{:S(2)}) copy-start(s32[256]{0:T(256)} %mask_smem.3) | copy-start | bytes 3076
  7.3 8.5 %copy-start.44 = (s32[256]{0:T(256)S(1)}, s32[256]{0:T(256)}, u32[]{:S(2)}) copy-start(s32[256]{0:T(256)} %chain_smem.3) | copy-start | bytes 3076
  7.3 8.5 %copy-start.50 = (f32[2,128]{1,0:T(2,128)S(1)}, f32[2,128]{1,0:T(2,128)}, u32[]{:S(2)}) copy-start(f32[2,128]{1,0:T(2,128)} %bias_ref.7) | copy-start | bytes 3076
  7.3 8.5 %copy-start.52 = (s32[2]{0:T(128)S(1)}, s32[2]{0:T(128)}, u32[]{:S(2)}) copy-start(s32[2]{0:T(128)} %pad_add_fusion.start_smem) | copy-start | bytes 28
  7.3 8.5 %copy-start.53 = (f32[2,128]{1,0:T(2,128)S(1)}, f32[2,128]{1,0:T(2,128)}, u32[]{:S(2)}) copy-start(f32[2,128]{1,0:T(2,128)} %chain_ref.5) | copy-start | bytes 3076
  7.3 48.6 %all-to-all-start = ((bf16[16,2,256,128]{3,2,1,0:T(8,128)(2,1)}), bf16[16,2,256,128]{3,2,1,0:T(8,128)(2,1)S(1)}, u32[]{:S(2)}, u32[]{:S(2)}) async-start(bf16[16,2,256,128]{3,2,1,0:T(8,128)(2,1)} %shard_map.154), calls=%async_computation | async-start | bytes 4194304 | tf_op jit(solution)/shard_map/all_to_all | solution.py:648
  15.6 368.7 %copy-start.21 = (bf16[128,640]{1,0:T(8,128)(2,1)}, bf16[128,640]{1,0:T(8,128)(2,1)S(1)}, u32[]{:S(2)}) copy-start(bf16[128,640]{1,0:T(8,128)(2,1)S(1)} %get-tuple-element.96.refs_6_.w_ref) | copy-start | bytes 491524
  15.8 41.4 %copy-start.30 = (bf16[640,128]{1,0:T(8,128)(2,1)}, bf16[640,128]{1,0:T(8,128)(2,1)S(1)}, u32[]{:S(2)}) copy-start(bf16[640,128]{1,0:T(8,128)(2,1)S(1)} %copy.17.wt_ref) | copy-start | bytes 491524
  58.2 34.2 %all-to-all-start.1 = ((bf16[16,256,128]{2,1,0:T(8,128)(2,1)}), bf16[16,256,128]{2,1,0:T(8,128)(2,1)S(1)}, u32[]{:S(2)}, u32[]{:S(2)}) async-start(bf16[16,256,128]{2,1,0:T(8,128)(2,1)} %copy-done.17), calls=%async_computation.1 | async-start | bytes 2097152 | tf_op jit(solution)/shard_map/all_to_all | solution.py:648
  73.5 18.9 %copy-start.42 = (f32[2,128]{1,0:T(2,128)S(1)}, f32[2,128]{1,0:T(2,128)}, u32[]{:S(2)}) copy-start(f32[2,128]{1,0:T(2,128)} %hgain_ref.3) | copy-start | bytes 3076
  73.5 18.9 %copy-start.51 = (f32[2,128]{1,0:T(2,128)S(1)}, f32[2,128]{1,0:T(2,128)}, u32[]{:S(2)}) copy-start(f32[2,128]{1,0:T(2,128)} %hbias_ref.3) | copy-start | bytes 3076
  92.4 108.0 %copy-start = (bf16[16,256,128]{2,1,0:T(8,128)(2,1)}, bf16[16,256,128]{2,1,0:T(8,128)(2,1)S(1)}, u32[]{:S(2)}) copy-start(bf16[16,256,128]{2,1,0:T(8,128)(2,1)S(1)} %all-to-all-done.1.refs_0_.prod_ref) | copy-start | bytes 3145732
  102.6 48.0 %all-to-all-start.2 = ((bf16[16,2,256,128]{3,2,1,0:T(8,128)(2,1)}), bf16[16,2,256,128]{3,2,1,0:T(8,128)(2,1)S(1)}, u32[]{:S(2)}, u32[]{:S(2)}) async-start(bf16[16,2,256,128]{3,2,1,0:T(8,128)(2,1)} %get-tuple-element.58), calls=%async_computation.2 | async-start | bytes 4194304 | tf_op jit(solution)/shard_map/all_to_all | solution.py:648
  152.9 34.3 %all-to-all-start.3 = ((bf16[16,256,128]{2,1,0:T(8,128)(2,1)}), bf16[16,256,128]{2,1,0:T(8,128)(2,1)}, u32[]{:S(2)}, u32[]{:S(2)}) async-start(bf16[16,256,128]{2,1,0:T(8,128)(2,1)} %copy-done.19), calls=%async_computation.3 | async-start | bytes 2097152 | tf_op jit(solution)/shard_map/all_to_all | solution.py:648
  193.3 30.1 %copy-start.7 = (bf16[8,2,256,256]{3,2,1,0:T(8,128)(2,1)S(1)}, bf16[8,2,256,256]{3,2,1,0:T(8,128)(2,1)}, u32[]{:S(2)}) copy-start(bf16[8,2,256,256]{3,2,1,0:T(8,128)(2,1)} %copy-done.6) | copy-start | bytes 6291460
  193.3 30.0 %all-to-all-start.4 = ((bf16[16,256,128]{2,1,0:T(8,128)(2,1)}), bf16[16,256,128]{2,1,0:T(8,128)(2,1)}, u32[]{:S(2)}, u32[]{:S(2)}) async-start(bf16[16,256,128]{2,1,0:T(8,128)(2,1)} %copy-done.18), calls=%async_computation.4 | async-start | bytes 2097152 | tf_op jit(solution)/shard_map/all_to_all | solution.py:648
  231.9 7.1 %copy-start.58 = (bf16[1,128,128]{2,1,0:T(8,128)(2,1)S(1)}, bf16[1,128,128]{2,1,0:T(8,128)(2,1)}, u32[]{:S(2)}) copy-start(bf16[1,128,128]{2,1,0:T(8,128)(2,1)} %get-tuple-element.103) | copy-start | bytes 98308
  231.9 7.8 %copy-start.5 = (bf16[16,128,256]{2,1,0:T(8,128)(2,1)S(1)}, bf16[16,128,256]{2,1,0:T(8,128)(2,1)}, u32[]{:S(2)}) copy-start(bf16[16,128,256]{2,1,0:T(8,128)(2,1)} %copy-done.3) | copy-start | bytes 3145732
  231.9 48.2 %all-to-all-start.5 = ((bf16[16,512,128]{2,1,0:T(8,128)(2,1)}), bf16[16,512,128]{2,1,0:T(8,128)(2,1)}, u32[]{:S(2)}, u32[]{:S(2)}) async-start(bf16[16,512,128]{2,1,0:T(8,128)(2,1)} %copy-done.8), calls=%async_computation.5 | async-start | bytes 4194304 | tf_op jit(solution)/shard_map/all_to_all | solution.py:648
  239.0 41.2 %copy-start.12 = (bf16[16,128,256]{2,1,0:T(8,128)(2,1)S(1)}, bf16[16,128,256]{2,1,0:T(8,128)(2,1)}, u32[]{:S(2)}) copy-start(bf16[16,128,256]{2,1,0:T(8,128)(2,1)} %copy-done.11) | copy-start | bytes 3145732
  245.8 44.5 %copy-start.15 = (bf16[16,128,256]{2,1,0:T(8,128)(2,1)}, bf16[16,128,256]{2,1,0:T(8,128)(2,1)S(1)}, u32[]{:S(2)}) copy-start(bf16[16,128,256]{2,1,0:T(8,128)(2,1)S(1)} %get-tuple-element.70.refs_5_.glog_ref) | copy-start | bytes 3145732
  290.3 34.3 %all-to-all-start.6 = ((bf16[16,256,128]{2,1,0:T(8,128)(2,1)}), bf16[16,256,128]{2,1,0:T(8,128)(2,1)}, u32[]{:S(2)}, u32[]{:S(2)}) async-start(bf16[16,256,128]{2,1,0:T(8,128)(2,1)} %get-tuple-element.76), calls=%async_computation.6 | async-start | bytes 2097152 | tf_op jit(solution)/shard_map/all_to_all | solution.py:648
  304.5 20.1 %copy-start.10 = (bf16[8,2,256,256]{3,2,1,0:T(8,128)(2,1)S(1)}, bf16[8,2,256,256]{3,2,1,0:T(8,128)(2,1)}, u32[]{:S(2)}) copy-start(bf16[8,2,256,256]{3,2,1,0:T(8,128)(2,1)} %copy-done.9) | copy-start | bytes 6291460
  331.5 7.1 %copy-start.31 = (bf16[640,128]{1,0:T(8,128)(2,1)S(1)}, bf16[640,128]{1,0:T(8,128)(2,1)}, u32[]{:S(2)}) copy-start(bf16[640,128]{1,0:T(8,128)(2,1)} %copy-done.30) | copy-start | bytes 491524
  331.5 7.1 %copy-start.55 = (f32[2,128]{1,0:T(2,128)S(1)}, f32[2,128]{1,0:T(2,128)}, u32[]{:S(2)}) copy-start(f32[2,128]{1,0:T(2,128)} %chain_ref.5) | copy-start | bytes 3076
  331.6 52.8 %all-to-all-start.7 = ((bf16[16,576,128]{2,1,0:T(8,128)(2,1)}), bf16[16,576,128]{2,1,0:T(8,128)(2,1)}, u32[]{:S(2)}, u32[]{:S(2)}) async-start(bf16[16,576,128]{2,1,0:T(8,128)(2,1)} %shard_map.168), calls=%async_computation.7 | async-start | bytes 4718592 | tf_op jit(solution)/shard_map/all_to_all | solution.py:648
  339.9 44.5 %copy-start.14 = (bf16[16,128,256]{2,1,0:T(8,128)(2,1)S(1)}, bf16[16,128,256]{2,1,0:T(8,128)(2,1)}, u32[]{:S(2)}) copy-start(bf16[16,128,256]{2,1,0:T(8,128)(2,1)} %copy-done.13) | copy-start | bytes 3145732
  343.9 45.8 %copy-start.16 = (bf16[16,128,256]{2,1,0:T(8,128)(2,1)}, bf16[16,128,256]{2,1,0:T(8,128)(2,1)S(1)}, u32[]{:S(2)}) copy-start(bf16[16,128,256]{2,1,0:T(8,128)(2,1)S(1)} %get-tuple-element.83.refs_4_.nrm_ref) | copy-start | bytes 3145732
  343.9 45.8 %copy-start.49 = (f32[16,1,256]{2,1,0:T(1,128)}, f32[16,1,256]{2,1,0:T(1,128)S(1)}, u32[]{:S(2)}) copy-start(f32[16,1,256]{2,1,0:T(1,128)S(1)} %get-tuple-element.89.inv_ref) | copy-start | bytes 49156
  389.8 21.3 %all-to-all-start.8 = ((bf16[16,48,128]{2,1,0:T(8,128)(2,1)}), bf16[16,48,128]{2,1,0:T(8,128)(2,1)S(1)}, u32[]{:S(2)}, u32[]{:S(2)}) async-start(bf16[16,48,128]{2,1,0:T(8,128)(2,1)} %bitcast.14), calls=%async_computation.8 | async-start | bytes 393216 | tf_op jit(solution)/shard_map/all_to_all | solution.py:648
  (36 other events, 34.2 us)

commit v8 on v5

--- a/solution.py
+++ b/solution.py
@@ -11,7 +11,7 @@
 AXES = ("row", "col")
 F32 = jnp.float32
 BF16 = jnp.bfloat16
-CHANNEL_VMEM = 24 * 1024 * 1024
+CHANNEL_VMEM = 50 * 1024 * 1024
 CELL_VMEM = 50 * 1024 * 1024
 ALL_VMEM = 60 * 1024 * 1024
 
@@ -118,15 +118,15 @@
     return jnp.concatenate([ref[t * q + a].astype(F32).T for a in range(q)], 1)
 
 
-def row_flags(row, mask_smem, chain_smem, start_smem, maskc_ref, chainc_ref):
-    whole = start_smem[0] + row
-    here = pl.ds(start_smem[1], 1)
+def row_flags(row, device_rows, mask_smem, chain_smem, maskc_ref, chainc_ref):
+    whole = lax.axis_index("row") * device_rows + row
+    here = pl.ds(lax.axis_index("col"), 1)
     mask = (maskc_ref[here, :] * mask_smem[whole]).astype(F32)
     return mask, (chainc_ref[here, :] == chain_smem[whole]).astype(F32)
 
 
 def edge_first_kernel(
-    cpd, q, mask_smem, chain_smem, start_smem, pair_ref, maskc_ref, chainc_ref, w_ref, gain_ref, bias_ref,
+    cpd, q, device_rows, mask_smem, chain_smem, pair_ref, maskc_ref, chainc_ref, w_ref, gain_ref, bias_ref,
     edges_ref, vec, turned_weight,
 ):
     rows, cols, width = pair_ref.shape
@@ -142,7 +142,7 @@
         first = pl.program_id(0) * rows + t * q
         mask = jnp.concatenate(
             [
-                row_flags(first + a, mask_smem, chain_smem, start_smem, maskc_ref, chainc_ref)[0]
+                row_flags(first + a, device_rows, mask_smem, chain_smem, maskc_ref, chainc_ref)[0]
                 for a in range(q)
             ],
             1,
@@ -152,7 +152,7 @@
 
 
 def first_keep_kernel(
-    q, mask_smem, chain_smem, start_smem, pair_ref, cot_ref, maskc_ref, chainc_ref, wt_ref, gain_ref,
+    q, device_rows, mask_smem, chain_smem, pair_ref, cot_ref, maskc_ref, chainc_ref, wt_ref, gain_ref,
     bias_ref, chain_ref, z_ref, up_ref, gate_ref, flags_ref, vec,
 ):
     load_columns(vec, (gain_ref, 0), (bias_ref, 0), (chain_ref, 0))
@@ -160,7 +160,7 @@
     for t in range(tiles):
         flags = [
             row_flags(
-                (pl.program_id(0) * tiles + t) * q + a, mask_smem, chain_smem, start_smem, maskc_ref, chainc_ref
+                (pl.program_id(0) * tiles + t) * q + a, device_rows, mask_smem, chain_smem, maskc_ref, chainc_ref
             )
             for a in range(q)
         ]
@@ -361,9 +361,11 @@
     cpd, q, left_ref, right_ref, fac_ref, low_ref, nrm_ref, glog_ref, w_ref, all_ref, acc_w,
 ):
     clear(acc_w)
-    for t in range(low_ref.shape[0]):
-        gproj = project_grad(left_ref, right_ref, fac_ref, glog_ref, t, cpd, q * cpd)
-        edge_terms(gproj, low_ref, nrm_ref, t, acc_w)
+    tiles = range(low_ref.shape[0])
+    gproj = [project_grad(left_ref, right_ref, fac_ref, glog_ref, t, cpd, q * cpd) for t in tiles]
+    ones = jnp.ones((16, low_ref.shape[2]), BF16)
+    sides = [jnp.concatenate([low_ref[t], nrm_ref[t], ones], 0) for t in tiles]
+    acc_w[...] += dot(jnp.concatenate(sides, 1), jnp.concatenate(gproj, 1), 1, 1)
 
     @last_step
     def _():
@@ -549,13 +551,12 @@
     dims = (row_devs, col_devs, rows, cpd, cols)
     side = rows * cpd
 
-    starts = jnp.stack([lax.axis_index("row") * rows, lax.axis_index("col")]).astype(jnp.int32)
     wt = [proj_weight[n].T for n in range(2)]
     owt = [out_weight[n].T for n in range(2)]
     weight = [proj_weight[n] for n in range(2)]
     mixer = [out_weight[n] for n in range(2)]
     mask_cols, chain_cols = residue_mask.reshape(col_devs, cols), chain_ids.reshape(col_devs, cols)
-    scalars = (residue_mask, chain_ids, starts)
+    scalars = (residue_mask, chain_ids)
     tile = (tiles, width, lanes)
     fac_tile = (tiles, 4 * hidden, lanes)
     edge_shape = (devices, 2, side, cols)
@@ -603,7 +604,7 @@
         )
 
     (edges0,) = cell_call(
-        functools.partial(edge_first_kernel, cpd, q), steps,
+        functools.partial(edge_first_kernel, cpd, q, rows), steps,
         [
             (pair_rep, 0), (mask_cols, None), (chain_cols, None), (proj_weight, (0, 0, 1)),
             (input_gain, None), (input_bias, None),
@@ -613,7 +614,7 @@
     )
     got0 = exchange(edges0)
     z0, up, gate0, flags = cell_call(
-        functools.partial(first_keep_kernel, q), steps,
+        functools.partial(first_keep_kernel, q, rows), steps,
         [
             (after(pair_rep, edges0), 0), (cotangent, 0), (mask_cols, None), (chain_cols, None), (wt[0], None),
             (input_gain, None), (input_bias, None), (chain_bias, None),

time: 424 us -> 423 us (level)
  waiting for transfers between devices: 215 us -> 205 us
  Pallas kernels: 77.8 us -> 83 us
  local copies, waits for them, and re-layouts: 29.3 us -> 34 us
    all_to_all x9, waiting for transfers between devices: 215 us -> 205 us  [exchange(): return lax.all_to_all(array, AXES, split_axis=0, concat_axis=0, tiled=True)]
    pallas_call x7, Pallas kernels: 13.3 us -> 18.4 us  [whole_call(): pl.pallas_call(kernel, in_specs=[pl.BlockSpec(memory_space=pltpu.VMEM)] *...]
    unnamed x106 -> x110, local copies, waits for them, and re-layouts: 26.7 us -> 29.9 us
  transfers between devices with their start and end apart: 9 -> 9, of which waited for: 9 -> 9; matrix products, arithmetic and copies ran while one was open for 1% -> 1% of each run, Pallas kernels for 8% -> 9%
where the time goes in v8:
time: 423 us; the launch traced here: 421 us
  waiting for transfers between devices  205 us (48%)
  Pallas kernels  83 us (20%)
  starting transfers between devices  81.4 us (19%)
  local copies, waits for them, and re-layouts  34 us (8%)
  blocking collectives  17 us (4%)
    all_to_all x9, waiting for transfers between devices, exchange(): return lax.all_to_all(array, AXES, split_axis=0, concat_axis=0, tiled=True)  205 us
    all_to_all x9, starting transfers between devices, exchange(): return lax.all_to_all(array, AXES, split_axis=0, concat_axis=0, tiled=True)  81.4 us
    pallas_call x13, Pallas kernels, cell_call(): pl.pallas_call(kernel, grid_spec=pltpu.PrefetchScalarGridSpec(num_scalar_...  64.6 us
    unnamed x110, local copies, waits for them, and re-layouts  29.9 us
    pallas_call x7, Pallas kernels, whole_call(): pl.pallas_call(kernel, in_specs=[pl.BlockSpec(memory_space=pltpu.VMEM)] *...  18.4 us
    all_to_all x1, blocking collectives, exchange(): return lax.all_to_all(array, AXES, split_axis=0, concat_axis=0, tiled=True)  17 us
  transfers between devices with their start and end apart: 9, of which 9 were waited for; matrix products, arithmetic and copies ran while one was open for 1% of the time, Pallas kernels for 9%

profile of v8, /device:TPU:0, one launch (start us, length us, event | category | flops | bytes accessed | tf_op | source)
XLA Modules:
  0.0 421.0 jit_solution(4831495712768877105)
XLA Ops:
  0.6 6.0 %shard_map.154 = bf16[16,2,256,128]{3,2,1,0:T(8,128)(2,1)} custom-call(s32[256]{0:T(256)} %mask_smem.3, s32[256]{0:T(256)} %chain_smem.3, bf16[32,128,128]{2,1,0:T(8,128)(2,1)} %pair_ref.2, s32[2,128]{1,0:T(2,128)} %bitcast.28, s32[2,128]{1,0:T(2,128)} %bitcast.30, bf16[2,128,640]{2,1,0:T(8,128)(2,1)} %w_ref.1, f32[2,128]{1,0:T(2,128)} %gain_ref.13, ...), custom_call_target="tpu_custom_call" | custom-call | flops 536870912 | bytes 3477504 | tf_op jit(solution)/shard_map/pallas_call | solution.py:426
  6.7 7.5 %all-to-all-start = ((bf16[16,2,256,128]{3,2,1,0:T(8,128)(2,1)}), bf16[16,2,256,128]{3,2,1,0:T(8,128)(2,1)S(1)}, u32[]{:S(2)}, u32[]{:S(2)}) async-start(bf16[16,2,256,128]{3,2,1,0:T(8,128)(2,1)} %shard_map.154), calls=%async_computation | async-start | bytes 4194304 | tf_op jit(solution)/shard_map/all_to_all | solution.py:530
  15.3 4.4 %shard_map.155 = (bf16[16,128,256]{2,1,0:T(8,128)(2,1)S(1)}, bf16[16,128,256]{2,1,0:T(8,128)(2,1)S(1)}, bf16[16,128,256]{2,1,0:T(8,128)(2,1)S(1)}, f32[16,2,256]{2,1,0:T(2,128)S(1)}) custom-call(s32[256]{0:T(256)S(1)} %copy-done.43, s32[256]{0:T(256)S(1)} %copy-done.44, bf16[32,128,128]{2,1,0:T(8,128)(2,1)} %pair_ref.2, bf16[32,128,128]{2,1,0:T(8,128)(2,1)} %cot_ref.1, ...), custom_call_target="tpu_custom_call" | custom-call | flops 268435456 | bytes 5444608 | tf_op jit(solution)/shard_map/pallas_call | solution.py:426
  22.7 32.7 %all-to-all-done.edges_ref = bf16[16,2,256,128]{3,2,1,0:T(8,128)(2,1)S(1)} async-done(((bf16[16,2,256,128]{3,2,1,0:T(8,128)(2,1)}), bf16[16,2,256,128]{3,2,1,0:T(8,128)(2,1)S(1)}, u32[]{:S(2)}, u32[]{:S(2)}) %all-to-all-start) | async-done | bytes 2097184 | tf_op jit(solution)/shard_map/all_to_all | solution.py:530
  57.6 11.2 %all-to-all-start.1 = ((bf16[16,256,128]{2,1,0:T(8,128)(2,1)}), bf16[16,256,128]{2,1,0:T(8,128)(2,1)S(1)}, u32[]{:S(2)}, u32[]{:S(2)}) async-start(bf16[16,256,128]{2,1,0:T(8,128)(2,1)} %copy-done.15), calls=%async_computation.1 | async-start | bytes 2097152 | tf_op jit(solution)/shard_map/all_to_all | solution.py:530
  72.1 3.0 shard_map.157.sides_ref
  76.5 15.3 %all-to-all-done.1.prod_ref = bf16[16,256,128]{2,1,0:T(8,128)(2,1)S(1)} async-done(((bf16[16,256,128]{2,1,0:T(8,128)(2,1)}), bf16[16,256,128]{2,1,0:T(8,128)(2,1)S(1)}, u32[]{:S(2)}, u32[]{:S(2)}) %all-to-all-start.1) | async-done | bytes 1048608 | tf_op jit(solution)/shard_map/all_to_all | solution.py:530
  92.9 5.6 %shard_map.158 = (bf16[16,2,256,128]{3,2,1,0:T(8,128)(2,1)}, f32[16,128,256]{2,1,0:T(8,128)}) custom-call(bf16[16,256,128]{2,1,0:T(8,128)(2,1)S(1)} %all-to-all-done.1.prod_ref, bf16[16,128,256]{2,1,0:T(8,128)(2,1)S(1)} %copy-done.24, bf16[16,128,256]{2,1,0:T(8,128)(2,1)S(1)} %copy-done.4, f32[16,2,256]{2,1,0:T(2,128)S(1)} %get-tuple-element.57.flags_ref, ...), custom_call_target="tpu_custom_call" | custom-call | flops 671088640 | bytes 7573504 | tf_op jit(solution)/shard_map/pallas_call | solution.py:426
  98.6 6.9 %all-to-all-start.2 = ((bf16[16,2,256,128]{3,2,1,0:T(8,128)(2,1)}), bf16[16,2,256,128]{3,2,1,0:T(8,128)(2,1)S(1)}, u32[]{:S(2)}, u32[]{:S(2)}) async-start(bf16[16,2,256,128]{3,2,1,0:T(8,128)(2,1)} %get-tuple-element.58), calls=%async_computation.2 | async-start | bytes 4194304 | tf_op jit(solution)/shard_map/all_to_all | solution.py:530
  107.0 5.8 %shard_map.159 = (bf16[16,512,256]{2,1,0:T(8,128)(2,1)}, bf16[16,128,256]{2,1,0:T(8,128)(2,1)S(1)}, bf16[16,128,256]{2,1,0:T(8,128)(2,1)S(1)}, f32[16,1,256]{2,1,0:T(1,128)S(1)}, bf16[16,128,256]{2,1,0:T(8,128)(2,1)S(1)}) custom-call(f32[16,128,256]{2,1,0:T(8,128)} %get-tuple-element.60.z_ref, f32[16,2,256]{2,1,0:T(2,128)S(1)} %get-tuple-element.57.flags_ref, ...), custom_call_target="tpu_custom_call" | custom-call | flops 671088640 | bytes 9653248 | tf_op jit(solution)/shard_map/pallas_call | solution.py:426
  116.4 30.2 %all-to-all-done.2.edges_ref = bf16[16,2,256,128]{3,2,1,0:T(8,128)(2,1)S(1)} async-done(((bf16[16,2,256,128]{3,2,1,0:T(8,128)(2,1)}), bf16[16,2,256,128]{3,2,1,0:T(8,128)(2,1)S(1)}, u32[]{:S(2)}, u32[]{:S(2)}) %all-to-all-start.2) | async-done | bytes 2097184 | tf_op jit(solution)/shard_map/all_to_all | solution.py:530
  148.9 11.3 %all-to-all-start.3 = ((bf16[16,256,128]{2,1,0:T(8,128)(2,1)}), bf16[16,256,128]{2,1,0:T(8,128)(2,1)}, u32[]{:S(2)}, u32[]{:S(2)}) async-start(bf16[16,256,128]{2,1,0:T(8,128)(2,1)} %copy-done.17), calls=%async_computation.3 | async-start | bytes 2097152 | tf_op jit(solution)/shard_map/all_to_all | solution.py:530
  164.5 18.6 %all-to-all-done.3.prod_ref = bf16[16,256,128]{2,1,0:T(8,128)(2,1)} async-done(((bf16[16,256,128]{2,1,0:T(8,128)(2,1)}), bf16[16,256,128]{2,1,0:T(8,128)(2,1)}, u32[]{:S(2)}, u32[]{:S(2)}) %all-to-all-start.3) | async-done | bytes 1048608 | tf_op jit(solution)/shard_map/all_to_all | solution.py:530
  183.1 3.6 shard_map.162
  187.7 6.9 %all-to-all-start.4 = ((bf16[16,256,128]{2,1,0:T(8,128)(2,1)}), bf16[16,256,128]{2,1,0:T(8,128)(2,1)S(1)}, u32[]{:S(2)}, u32[]{:S(2)}) async-start(bf16[16,256,128]{2,1,0:T(8,128)(2,1)} %copy-done.16), calls=%async_computation.4 | async-start | bytes 2097152 | tf_op jit(solution)/shard_map/all_to_all | solution.py:530
  197.1 20.5 %all-to-all-done.4.grad_ref = bf16[16,256,128]{2,1,0:T(8,128)(2,1)S(1)} async-done(((bf16[16,256,128]{2,1,0:T(8,128)(2,1)}), bf16[16,256,128]{2,1,0:T(8,128)(2,1)S(1)}, u32[]{:S(2)}, u32[]{:S(2)}) %all-to-all-start.4) | async-done | bytes 1048608 | tf_op jit(solution)/shard_map/all_to_all | solution.py:530
  217.5 4.6 %shard_map.164 = bf16[16,512,128]{2,1,0:T(8,128)(2,1)} custom-call(bf16[8,2,256,256]{3,2,1,0:T(8,128)(2,1)} %copy-done.7, bf16[16,256,128]{2,1,0:T(8,128)(2,1)S(1)} %all-to-all-done.4.grad_ref), custom_call_target="tpu_custom_call" | custom-call | flops 536870912 | bytes 5242880 | tf_op jit(solution)/shard_map/pallas_call | solution.py:518
  222.2 7.0 %all-to-all-start.5 = ((bf16[16,512,128]{2,1,0:T(8,128)(2,1)}), bf16[16,512,128]{2,1,0:T(8,128)(2,1)}, u32[]{:S(2)}, u32[]{:S(2)}) async-start(bf16[16,512,128]{2,1,0:T(8,128)(2,1)} %shard_map.164), calls=%async_computation.5 | async-start | bytes 4194304 | tf_op jit(solution)/shard_map/all_to_all | solution.py:530
  231.5 3.9 shard_map.165
  236.0 34.3 %all-to-all-done.5.left_ref.right_ref = bf16[16,512,128]{2,1,0:T(8,128)(2,1)} async-done(((bf16[16,512,128]{2,1,0:T(8,128)(2,1)}), bf16[16,512,128]{2,1,0:T(8,128)(2,1)}, u32[]{:S(2)}, u32[]{:S(2)}) %all-to-all-start.5) | async-done | bytes 2097184 | tf_op jit(solution)/shard_map/all_to_all | solution.py:530
  272.6 8.2 %shard_map.166 = (f32[16,128,256]{2,1,0:T(8,128)}, bf16[16,256,128]{2,1,0:T(8,128)(2,1)}) custom-call(bf16[16,512,128]{2,1,0:T(8,128)(2,1)} %all-to-all-done.5.left_ref.right_ref, bf16[16,512,128]{2,1,0:T(8,128)(2,1)} %all-to-all-done.5.left_ref.right_ref, bf16[16,512,256]{2,1,0:T(8,128)(2,1)} %get-tuple-element.72.fac_ref, ...), custom_call_target="tpu_custom_call" | custom-call | flops 805306368 | bytes 17008640 | tf_op jit(solution)/shard_map/pallas_call | solution.py:426
  280.8 11.3 %all-to-all-start.6 = ((bf16[16,256,128]{2,1,0:T(8,128)(2,1)}), bf16[16,256,128]{2,1,0:T(8,128)(2,1)}, u32[]{:S(2)}, u32[]{:S(2)}) async-start(bf16[16,256,128]{2,1,0:T(8,128)(2,1)} %get-tuple-element.76), calls=%async_computation.6 | async-start | bytes 2097152 | tf_op jit(solution)/shard_map/all_to_all | solution.py:530
  294.9 7.2 %shard_map.167 = (bf16[16,128,256]{2,1,0:T(8,128)(2,1)S(1)}, bf16[1024,128]{1,0:T(8,128)(2,1)S(1)}) custom-call(bf16[16,512,128]{2,1,0:T(8,128)(2,1)} %all-to-all-done.5.left_ref.right_ref, bf16[16,512,128]{2,1,0:T(8,128)(2,1)} %all-to-all-done.5.left_ref.right_ref, bf16[16,512,256]{2,1,0:T(8,128)(2,1)} %get-tuple-element.72.fac_ref, ...), custom_call_target="tpu_custom_call" | custom-call | flops 1744830464 | bytes 17373184 | tf_op jit(solution)/shard_map/pallas_call | solution.py:426
  303.8 11.2 %all-to-all-done.6.grad_ref = bf16[16,256,128]{2,1,0:T(8,128)(2,1)} async-done(((bf16[16,256,128]{2,1,0:T(8,128)(2,1)}), bf16[16,256,128]{2,1,0:T(8,128)(2,1)}, u32[]{:S(2)}, u32[]{:S(2)}) %all-to-all-start.6) | async-done | bytes 1048608 | tf_op jit(solution)/shard_map/all_to_all | solution.py:530
  316.0 4.2 %shard_map.168 = bf16[16,576,128]{2,1,0:T(8,128)(2,1)} custom-call(bf16[8,2,256,256]{3,2,1,0:T(8,128)(2,1)S(1)} %copy-done.9, bf16[16,256,128]{2,1,0:T(8,128)(2,1)} %all-to-all-done.6.grad_ref, bf16[16,64,128]{2,1,0:T(8,128)(2,1)S(1)} %bitcast.26), custom_call_target="tpu_custom_call" | custom-call | flops 536870912 | bytes 5767168 | tf_op jit(solution)/shard_map/pallas_call | solution.py:518
  320.2 7.0 %all-to-all-start.7 = ((bf16[16,576,128]{2,1,0:T(8,128)(2,1)}), bf16[16,576,128]{2,1,0:T(8,128)(2,1)}, u32[]{:S(2)}, u32[]{:S(2)}) async-start(bf16[16,576,128]{2,1,0:T(8,128)(2,1)} %shard_map.168), calls=%async_computation.7 | async-start | bytes 4718592 | tf_op jit(solution)/shard_map/all_to_all | solution.py:530
  327.3 4.1 shard_map.169
  333.4 39.6 %all-to-all-done.7.left_ref.right_ref.early_ref = bf16[16,576,128]{2,1,0:T(8,128)(2,1)} async-done(((bf16[16,576,128]{2,1,0:T(8,128)(2,1)}), bf16[16,576,128]{2,1,0:T(8,128)(2,1)}, u32[]{:S(2)}, u32[]{:S(2)}) %all-to-all-start.7) | async-done | bytes 2359328 | tf_op jit(solution)/shard_map/all_to_all | solution.py:530
  373.0 6.3 %shard_map.170 = bf16[768,128]{1,0:T(8,128)(2,1)} custom-call(bf16[16,576,128]{2,1,0:T(8,128)(2,1)} %all-to-all-done.7.left_ref.right_ref.early_ref, bf16[16,576,128]{2,1,0:T(8,128)(2,1)} %all-to-all-done.7.left_ref.right_ref.early_ref, bf16[16,512,256]{2,1,0:T(8,128)(2,1)} %get-tuple-element.85.fac_ref, bf16[16,128,256]{2,1,0:T(8,128)(2,1)} %copy-done.22, ...), custom_call_target="tpu_custom_call" | custom-call | flops 1342177280 | bytes 12419072 | tf_op jit(solution)/shard_map/pallas_call | solution.py:426
  379.3 12.2 %all-to-all-start.8 = ((bf16[16,48,128]{2,1,0:T(8,128)(2,1)}), bf16[16,48,128]{2,1,0:T(8,128)(2,1)S(1)}, u32[]{:S(2)}, u32[]{:S(2)}) async-start(bf16[16,48,128]{2,1,0:T(8,128)(2,1)} %bitcast.32), calls=%async_computation.8 | async-start | bytes 393216 | tf_op jit(solution)/shard_map/all_to_all | solution.py:530
  391.6 6.7 %shard_map.171 = bf16[32,128,128]{2,1,0:T(8,128)(2,1)} custom-call(bf16[16,576,128]{2,1,0:T(8,128)(2,1)} %all-to-all-done.7.left_ref.right_ref.early_ref, bf16[16,576,128]{2,1,0:T(8,128)(2,1)} %all-to-all-done.7.left_ref.right_ref.early_ref, bf16[16,512,256]{2,1,0:T(8,128)(2,1)} %get-tuple-element.85.fac_ref, bf16[16,128,256]{2,1,0:T(8,128)(2,1)} %copy-done.14, ...), custom_call_target="tpu_custom_call" | custom-call | flops 671088640 | bytes 14337024 | tf_op jit(solution)/shard_map/pallas_call | solution.py:426
  403.1 17.0 %all_to_all.50.got_ref = bf16[16,112,128]{2,1,0:T(8,128)(2,1)S(1)} all-to-all(bf16[16,112,128]{2,1,0:T(8,128)(2,1)} %shard_map.172), channel_id=1, replica_groups=mesh['grp'=2,'row'=8,'col'=2] {'row','col'}, dimensions={0} | all-to-all | bytes 917504 | tf_op jit(solution)/shard_map/all_to_all | solution.py:530
  (121 shorter events, 45.4 us)
Async XLA Ops:
  6.7 7.6 %copy-start.51 = (bf16[2,128,640]{2,1,0:T(8,128)(2,1)S(1)}, bf16[2,128,640]{2,1,0:T(8,128)(2,1)}, u32[]{:S(2)}) copy-start(bf16[2,128,640]{2,1,0:T(8,128)(2,1)} %w_ref.1) | copy-start | bytes 983044
  6.7 8.5 %copy-start.38 = (f32[2,128]{1,0:T(2,128)S(1)}, f32[2,128]{1,0:T(2,128)}, u32[]{:S(2)}) copy-start(f32[2,128]{1,0:T(2,128)} %gain_ref.13) | copy-start | bytes 3076
  6.7 8.5 %copy-start.43 = (s32[256]{0:T(256)S(1)}, s32[256]{0:T(256)}, u32[]{:S(2)}) copy-start(s32[256]{0:T(256)} %mask_smem.3) | copy-start | bytes 3076
  6.7 8.5 %copy-start.44 = (s32[256]{0:T(256)S(1)}, s32[256]{0:T(256)}, u32[]{:S(2)}) copy-start(s32[256]{0:T(256)} %chain_smem.3) | copy-start | bytes 3076
  6.7 8.5 %copy-start.47 = (f32[2,128]{1,0:T(2,128)S(1)}, f32[2,128]{1,0:T(2,128)}, u32[]{:S(2)}) copy-start(f32[2,128]{1,0:T(2,128)} %bias_ref.9) | copy-start | bytes 3076
  6.7 8.5 %copy-start.48 = (f32[2,128]{1,0:T(2,128)S(1)}, f32[2,128]{1,0:T(2,128)}, u32[]{:S(2)}) copy-start(f32[2,128]{1,0:T(2,128)} %chain_ref.5) | copy-start | bytes 3076
  6.7 48.6 %all-to-all-start = ((bf16[16,2,256,128]{3,2,1,0:T(8,128)(2,1)}), bf16[16,2,256,128]{3,2,1,0:T(8,128)(2,1)S(1)}, u32[]{:S(2)}, u32[]{:S(2)}) async-start(bf16[16,2,256,128]{3,2,1,0:T(8,128)(2,1)} %shard_map.154), calls=%async_computation | async-start | bytes 4194304 | tf_op jit(solution)/shard_map/all_to_all | solution.py:530
  55.4 2.2 copy-start
  57.6 34.2 %all-to-all-start.1 = ((bf16[16,256,128]{2,1,0:T(8,128)(2,1)}), bf16[16,256,128]{2,1,0:T(8,128)(2,1)S(1)}, u32[]{:S(2)}, u32[]{:S(2)}) async-start(bf16[16,256,128]{2,1,0:T(8,128)(2,1)} %copy-done.15), calls=%async_computation.1 | async-start | bytes 2097152 | tf_op jit(solution)/shard_map/all_to_all | solution.py:530
  72.1 19.7 %copy-start.4 = (bf16[16,128,256]{2,1,0:T(8,128)(2,1)S(1)}, bf16[16,128,256]{2,1,0:T(8,128)(2,1)}, u32[]{:S(2)}) copy-start(bf16[16,128,256]{2,1,0:T(8,128)(2,1)} %copy-done.3) | copy-start | bytes 3145732
  72.1 19.7 %copy-start.24 = (bf16[16,128,256]{2,1,0:T(8,128)(2,1)S(1)}, bf16[16,128,256]{2,1,0:T(8,128)(2,1)}, u32[]{:S(2)}) copy-start(bf16[16,128,256]{2,1,0:T(8,128)(2,1)} %copy-done.23) | copy-start | bytes 3145732
  72.1 19.7 %copy-start.37 = (f32[2,128]{1,0:T(2,128)S(1)}, f32[2,128]{1,0:T(2,128)}, u32[]{:S(2)}) copy-start(f32[2,128]{1,0:T(2,128)} %hgain_ref.9) | copy-start | bytes 3076
  72.1 19.7 %copy-start.46 = (f32[2,128]{1,0:T(2,128)S(1)}, f32[2,128]{1,0:T(2,128)}, u32[]{:S(2)}) copy-start(f32[2,128]{1,0:T(2,128)} %hbias_ref.5) | copy-start | bytes 3076
  91.8 102.8 %copy-start.2 = (bf16[16,256,128]{2,1,0:T(8,128)(2,1)}, bf16[16,256,128]{2,1,0:T(8,128)(2,1)S(1)}, u32[]{:S(2)}) copy-start(bf16[16,256,128]{2,1,0:T(8,128)(2,1)S(1)} %all-to-all-done.1.prod_ref) | copy-start | bytes 3145732
  98.6 48.0 %all-to-all-start.2 = ((bf16[16,2,256,128]{3,2,1,0:T(8,128)(2,1)}), bf16[16,2,256,128]{3,2,1,0:T(8,128)(2,1)S(1)}, u32[]{:S(2)}, u32[]{:S(2)}) async-start(bf16[16,2,256,128]{3,2,1,0:T(8,128)(2,1)} %get-tuple-element.58), calls=%async_computation.2 | async-start | bytes 4194304 | tf_op jit(solution)/shard_map/all_to_all | solution.py:530
  146.5 2.3 copy-start.1
  148.9 34.3 %all-to-all-start.3 = ((bf16[16,256,128]{2,1,0:T(8,128)(2,1)}), bf16[16,256,128]{2,1,0:T(8,128)(2,1)}, u32[]{:S(2)}, u32[]{:S(2)}) async-start(bf16[16,256,128]{2,1,0:T(8,128)(2,1)} %copy-done.17), calls=%async_computation.3 | async-start | bytes 2097152 | tf_op jit(solution)/shard_map/all_to_all | solution.py:530
  160.1 23.0 %copy-start.6 = (bf16[16,128,256]{2,1,0:T(8,128)(2,1)S(1)}, bf16[16,128,256]{2,1,0:T(8,128)(2,1)}, u32[]{:S(2)}) copy-start(bf16[16,128,256]{2,1,0:T(8,128)(2,1)} %copy-done.5) | copy-start | bytes 3145732
  160.2 23.0 %copy-start.30 = (bf16[128,128]{1,0:T(8,128)(2,1)S(1)}, bf16[128,128]{1,0:T(8,128)(2,1)}, u32[]{:S(2)}) copy-start(bf16[128,128]{1,0:T(8,128)(2,1)} %get-tuple-element.101.ow_ref) | copy-start | bytes 98308
  163.1 1.4 copy-start.7
  187.7 29.8 %all-to-all-start.4 = ((bf16[16,256,128]{2,1,0:T(8,128)(2,1)}), bf16[16,256,128]{2,1,0:T(8,128)(2,1)S(1)}, u32[]{:S(2)}, u32[]{:S(2)}) async-start(bf16[16,256,128]{2,1,0:T(8,128)(2,1)} %copy-done.16), calls=%async_computation.4 | async-start | bytes 2097152 | tf_op jit(solution)/shard_map/all_to_all | solution.py:530
  222.2 7.1 %copy-start.53 = (bf16[1,128,128]{2,1,0:T(8,128)(2,1)S(1)}, bf16[1,128,128]{2,1,0:T(8,128)(2,1)}, u32[]{:S(2)}) copy-start(bf16[1,128,128]{2,1,0:T(8,128)(2,1)} %get-tuple-element.103) | copy-start | bytes 98308
  222.2 48.2 %all-to-all-start.5 = ((bf16[16,512,128]{2,1,0:T(8,128)(2,1)}), bf16[16,512,128]{2,1,0:T(8,128)(2,1)}, u32[]{:S(2)}, u32[]{:S(2)}) async-start(bf16[16,512,128]{2,1,0:T(8,128)(2,1)} %shard_map.164), calls=%async_computation.5 | async-start | bytes 4194304 | tf_op jit(solution)/shard_map/all_to_all | solution.py:530
  229.2 41.2 %copy-start.11 = (bf16[16,128,256]{2,1,0:T(8,128)(2,1)S(1)}, bf16[16,128,256]{2,1,0:T(8,128)(2,1)}, u32[]{:S(2)}) copy-start(bf16[16,128,256]{2,1,0:T(8,128)(2,1)} %copy-done.10) | copy-start | bytes 3145732
  236.0 44.7 %copy-start.13 = (bf16[16,128,256]{2,1,0:T(8,128)(2,1)}, bf16[16,128,256]{2,1,0:T(8,128)(2,1)S(1)}, u32[]{:S(2)}) copy-start(bf16[16,128,256]{2,1,0:T(8,128)(2,1)S(1)} %get-tuple-element.70.glog_ref) | copy-start | bytes 3145732
  280.8 34.3 %all-to-all-start.6 = ((bf16[16,256,128]{2,1,0:T(8,128)(2,1)}), bf16[16,256,128]{2,1,0:T(8,128)(2,1)}, u32[]{:S(2)}, u32[]{:S(2)}) async-start(bf16[16,256,128]{2,1,0:T(8,128)(2,1)} %get-tuple-element.76), calls=%async_computation.6 | async-start | bytes 2097152 | tf_op jit(solution)/shard_map/all_to_all | solution.py:530
  294.9 20.1 %copy-start.9 = (bf16[8,2,256,256]{3,2,1,0:T(8,128)(2,1)S(1)}, bf16[8,2,256,256]{3,2,1,0:T(8,128)(2,1)}, u32[]{:S(2)}) copy-start(bf16[8,2,256,256]{3,2,1,0:T(8,128)(2,1)} %copy-done.8) | copy-start | bytes 6291460
  320.2 7.1 %copy-start.25 = (bf16[16,128,256]{2,1,0:T(8,128)(2,1)S(1)}, bf16[16,128,256]{2,1,0:T(8,128)(2,1)}, u32[]{:S(2)}) copy-start(bf16[16,128,256]{2,1,0:T(8,128)(2,1)} %copy-done.23) | copy-start | bytes 3145732
  320.2 7.1 %copy-start.50 = (f32[2,128]{1,0:T(2,128)S(1)}, f32[2,128]{1,0:T(2,128)}, u32[]{:S(2)}) copy-start(f32[2,128]{1,0:T(2,128)} %chain_ref.5) | copy-start | bytes 3076
  320.2 52.8 %all-to-all-start.7 = ((bf16[16,576,128]{2,1,0:T(8,128)(2,1)}), bf16[16,576,128]{2,1,0:T(8,128)(2,1)}, u32[]{:S(2)}, u32[]{:S(2)}) async-start(bf16[16,576,128]{2,1,0:T(8,128)(2,1)} %shard_map.168), calls=%async_computation.7 | async-start | bytes 4718592 | tf_op jit(solution)/shard_map/all_to_all | solution.py:530
  333.4 45.9 %copy-start.45 = (f32[16,1,256]{2,1,0:T(1,128)}, f32[16,1,256]{2,1,0:T(1,128)S(1)}, u32[]{:S(2)}) copy-start(f32[16,1,256]{2,1,0:T(1,128)S(1)} %get-tuple-element.89.inv_ref) | copy-start | bytes 49156
  379.3 21.2 %all-to-all-start.8 = ((bf16[16,48,128]{2,1,0:T(8,128)(2,1)}), bf16[16,48,128]{2,1,0:T(8,128)(2,1)S(1)}, u32[]{:S(2)}, u32[]{:S(2)}) async-start(bf16[16,48,128]{2,1,0:T(8,128)(2,1)} %bitcast.32), calls=%async_computation.8 | async-start | bytes 393216 | tf_op jit(solution)/shard_map/all_to_all | solution.py:530
  (31 other events, 27.7 us)

commit v9 on v8

--- a/solution.py
+++ b/solution.py
@@ -76,7 +76,7 @@
 
 
 def project(lowered, wt_ref, first, last):
-    hidden = wt_ref.shape[0] // 5
+    hidden = lowered.shape[0]
     projected = dot(wt_ref[first * hidden : last * hidden, :], lowered, 1, 0)
     return [projected[n * hidden : (n + 1) * hidden] for n in range(last - first)]
 
@@ -510,7 +510,7 @@
         out_ref[:, out_ref.shape[1] - terms_ref.shape[1] :, :] = terms_ref[...]
 
 
-def whole_call(kernel, ins, outs, scratch, flops):
+def whole_call(kernel, ins, outs, scratch, flops, vmem=CHANNEL_VMEM):
     moved = sum(a.size * a.dtype.itemsize for a in ins)
     moved += sum(functools.reduce(lambda x, y: x * y, s, 1) * jnp.dtype(t).itemsize for s, t in outs)
     specs = [pl.BlockSpec(memory_space=pltpu.VMEM)] * len(outs)
@@ -521,7 +521,7 @@
         out_specs=specs if len(outs) > 1 else specs[0],
         out_shape=shapes if len(outs) > 1 else shapes[0],
         scratch_shapes=scratch,
-        compiler_params=pltpu.CompilerParams(vmem_limit_bytes=CHANNEL_VMEM),
+        compiler_params=pltpu.CompilerParams(vmem_limit_bytes=vmem),
         cost_estimate=pl.CostEstimate(flops=flops, bytes_accessed=int(moved), transcendentals=0),
     )(*ins)
 
@@ -585,7 +585,7 @@
         out_rows = 2 * side + sum(t.shape[1] for t in terms)
         return whole_call(
             functools.partial(product_grad_kernel, dims, outgoing), [sides, grad, *terms],
-            [((devices, out_rows, cols), BF16)], [wide(1), wide(2)], 2 * tri_flops,
+            [((devices, out_rows, cols), BF16)], [wide(1), wide(2)], 2 * tri_flops, 24 * 1024 * 1024,
         )
 
     def halves(grads):
@@ -609,7 +609,7 @@
             (pair_rep, 0), (mask_cols, None), (chain_cols, None), (proj_weight, (0, 0, 1)),
             (input_gain, None), (input_bias, None),
         ],
-        [((edge_shape, BF16), 2)], [vec(2), pltpu.VMEM((5 * hidden, width), BF16)],
+        [((edge_shape, BF16), 2)], [vec(2), pltpu.VMEM((4 * hidden, width), BF16)],
         prefetch=scalars, flops=4 * cell_flops, vmem=ALL_VMEM,
     )
     got0 = exchange(edges0)

time: 423 us -> 423 us (level)
    unnamed x110 -> x112, local copies, waits for them, and re-layouts: 29.9 us -> 31.4 us
where the time goes in v9:
time: 423 us; the launch traced here: 421 us
  waiting for transfers between devices  205 us (48%)
  starting transfers between devices  81.4 us (19%)
  Pallas kernels  81.3 us (19%)
  local copies, waits for them, and re-layouts  35.5 us (8%)
  blocking collectives  17 us (4%)
    all_to_all x9, waiting for transfers between devices, exchange(): return lax.all_to_all(array, AXES, split_axis=0, concat_axis=0, tiled=True)  205 us
    all_to_all x9, starting transfers between devices, exchange(): return lax.all_to_all(array, AXES, split_axis=0, concat_axis=0, tiled=True)  81.4 us
    pallas_call x13, Pallas kernels, cell_call(): pl.pallas_call(kernel, grid_spec=pltpu.PrefetchScalarGridSpec(num_scalar_...  64.5 us
    unnamed x112, local copies, waits for them, and re-layouts  31.4 us
    all_to_all x1, blocking collectives, exchange(): return lax.all_to_all(array, AXES, split_axis=0, concat_axis=0, tiled=True)  17 us
    pallas_call x7, Pallas kernels, whole_call(): pl.pallas_call(kernel, in_specs=[pl.BlockSpec(memory_space=pltpu.VMEM)] *...  16.8 us
  transfers between devices with their start and end apart: 9, of which 9 were waited for; matrix products, arithmetic and copies ran while one was open for 1% of the time, Pallas kernels for 9%

profile of v9, /device:TPU:0, one launch (start us, length us, event | category | flops | bytes accessed | tf_op | source)
XLA Modules:
  0.0 420.9 jit_solution(3261581745084328327)
XLA Ops:
  0.6 6.0 %shard_map.154 = bf16[16,2,256,128]{3,2,1,0:T(8,128)(2,1)} custom-call(s32[256]{0:T(256)} %mask_smem.3, s32[256]{0:T(256)} %chain_smem.3, bf16[32,128,128]{2,1,0:T(8,128)(2,1)} %pair_ref.2, s32[2,128]{1,0:T(2,128)} %bitcast.28, s32[2,128]{1,0:T(2,128)} %bitcast.30, bf16[2,128,640]{2,1,0:T(8,128)(2,1)} %w_ref.1, f32[2,128]{1,0:T(2,128)} %gain_ref.13, ...), custom_call_target="tpu_custom_call" | custom-call | flops 536870912 | bytes 3477504 | tf_op jit(solution)/shard_map/pallas_call | solution.py:426
  6.7 7.5 %all-to-all-start = ((bf16[16,2,256,128]{3,2,1,0:T(8,128)(2,1)}), bf16[16,2,256,128]{3,2,1,0:T(8,128)(2,1)S(1)}, u32[]{:S(2)}, u32[]{:S(2)}) async-start(bf16[16,2,256,128]{3,2,1,0:T(8,128)(2,1)} %shard_map.154), calls=%async_computation | async-start | bytes 4194304 | tf_op jit(solution)/shard_map/all_to_all | solution.py:530
  15.3 4.4 %shard_map.155 = (bf16[16,128,256]{2,1,0:T(8,128)(2,1)S(1)}, bf16[16,128,256]{2,1,0:T(8,128)(2,1)S(1)}, bf16[16,128,256]{2,1,0:T(8,128)(2,1)S(1)}, f32[16,2,256]{2,1,0:T(2,128)S(1)}) custom-call(s32[256]{0:T(256)S(1)} %copy-done.44, s32[256]{0:T(256)S(1)} %copy-done.45, bf16[32,128,128]{2,1,0:T(8,128)(2,1)} %pair_ref.2, bf16[32,128,128]{2,1,0:T(8,128)(2,1)} %cot_ref.1, ...), custom_call_target="tpu_custom_call" | custom-call | flops 268435456 | bytes 5444608 | tf_op jit(solution)/shard_map/pallas_call | solution.py:426
  22.6 32.7 %all-to-all-done.edges_ref = bf16[16,2,256,128]{3,2,1,0:T(8,128)(2,1)S(1)} async-done(((bf16[16,2,256,128]{3,2,1,0:T(8,128)(2,1)}), bf16[16,2,256,128]{3,2,1,0:T(8,128)(2,1)S(1)}, u32[]{:S(2)}, u32[]{:S(2)}) %all-to-all-start) | async-done | bytes 2097184 | tf_op jit(solution)/shard_map/all_to_all | solution.py:530
  57.6 11.2 %all-to-all-start.1 = ((bf16[16,256,128]{2,1,0:T(8,128)(2,1)}), bf16[16,256,128]{2,1,0:T(8,128)(2,1)S(1)}, u32[]{:S(2)}, u32[]{:S(2)}) async-start(bf16[16,256,128]{2,1,0:T(8,128)(2,1)} %copy-done.16), calls=%async_computation.1 | async-start | bytes 2097152 | tf_op jit(solution)/shard_map/all_to_all | solution.py:530
  72.1 3.0 shard_map.157.sides_ref
  76.5 15.3 %all-to-all-done.1.prod_ref = bf16[16,256,128]{2,1,0:T(8,128)(2,1)S(1)} async-done(((bf16[16,256,128]{2,1,0:T(8,128)(2,1)}), bf16[16,256,128]{2,1,0:T(8,128)(2,1)S(1)}, u32[]{:S(2)}, u32[]{:S(2)}) %all-to-all-start.1) | async-done | bytes 1048608 | tf_op jit(solution)/shard_map/all_to_all | solution.py:530
  92.9 5.6 %shard_map.158 = (bf16[16,2,256,128]{3,2,1,0:T(8,128)(2,1)}, f32[16,128,256]{2,1,0:T(8,128)}) custom-call(bf16[16,256,128]{2,1,0:T(8,128)(2,1)S(1)} %all-to-all-done.1.prod_ref, bf16[16,128,256]{2,1,0:T(8,128)(2,1)S(1)} %copy-done.25, bf16[16,128,256]{2,1,0:T(8,128)(2,1)S(1)} %copy-done.4, f32[16,2,256]{2,1,0:T(2,128)S(1)} %get-tuple-element.57.flags_ref, ...), custom_call_target="tpu_custom_call" | custom-call | flops 671088640 | bytes 7573504 | tf_op jit(solution)/shard_map/pallas_call | solution.py:426
  98.5 6.9 %all-to-all-start.2 = ((bf16[16,2,256,128]{3,2,1,0:T(8,128)(2,1)}), bf16[16,2,256,128]{3,2,1,0:T(8,128)(2,1)S(1)}, u32[]{:S(2)}, u32[]{:S(2)}) async-start(bf16[16,2,256,128]{3,2,1,0:T(8,128)(2,1)} %get-tuple-element.58), calls=%async_computation.2 | async-start | bytes 4194304 | tf_op jit(solution)/shard_map/all_to_all | solution.py:530
  107.0 5.8 %shard_map.159 = (bf16[16,512,256]{2,1,0:T(8,128)(2,1)}, bf16[16,128,256]{2,1,0:T(8,128)(2,1)S(1)}, bf16[16,128,256]{2,1,0:T(8,128)(2,1)S(1)}, f32[16,1,256]{2,1,0:T(1,128)S(1)}, bf16[16,128,256]{2,1,0:T(8,128)(2,1)S(1)}) custom-call(f32[16,128,256]{2,1,0:T(8,128)} %get-tuple-element.60.z_ref, f32[16,2,256]{2,1,0:T(2,128)S(1)} %get-tuple-element.57.flags_ref, ...), custom_call_target="tpu_custom_call" | custom-call | flops 671088640 | bytes 9653248 | tf_op jit(solution)/shard_map/pallas_call | solution.py:426
  116.3 30.2 %all-to-all-done.2.edges_ref = bf16[16,2,256,128]{3,2,1,0:T(8,128)(2,1)S(1)} async-done(((bf16[16,2,256,128]{3,2,1,0:T(8,128)(2,1)}), bf16[16,2,256,128]{3,2,1,0:T(8,128)(2,1)S(1)}, u32[]{:S(2)}, u32[]{:S(2)}) %all-to-all-start.2) | async-done | bytes 2097184 | tf_op jit(solution)/shard_map/all_to_all | solution.py:530
  148.8 11.3 %all-to-all-start.3 = ((bf16[16,256,128]{2,1,0:T(8,128)(2,1)}), bf16[16,256,128]{2,1,0:T(8,128)(2,1)}, u32[]{:S(2)}, u32[]{:S(2)}) async-start(bf16[16,256,128]{2,1,0:T(8,128)(2,1)} %copy-done.18), calls=%async_computation.3 | async-start | bytes 2097152 | tf_op jit(solution)/shard_map/all_to_all | solution.py:530
  164.5 18.6 %all-to-all-done.3.prod_ref = bf16[16,256,128]{2,1,0:T(8,128)(2,1)} async-done(((bf16[16,256,128]{2,1,0:T(8,128)(2,1)}), bf16[16,256,128]{2,1,0:T(8,128)(2,1)}, u32[]{:S(2)}, u32[]{:S(2)}) %all-to-all-start.3) | async-done | bytes 1048608 | tf_op jit(solution)/shard_map/all_to_all | solution.py:530
  183.1 3.6 shard_map.162
  187.7 6.9 %all-to-all-start.4 = ((bf16[16,256,128]{2,1,0:T(8,128)(2,1)}), bf16[16,256,128]{2,1,0:T(8,128)(2,1)S(1)}, u32[]{:S(2)}, u32[]{:S(2)}) async-start(bf16[16,256,128]{2,1,0:T(8,128)(2,1)} %copy-done.17), calls=%async_computation.4 | async-start | bytes 2097152 | tf_op jit(solution)/shard_map/all_to_all | solution.py:530
  197.0 20.5 %all-to-all-done.4.grad_ref = bf16[16,256,128]{2,1,0:T(8,128)(2,1)S(1)} async-done(((bf16[16,256,128]{2,1,0:T(8,128)(2,1)}), bf16[16,256,128]{2,1,0:T(8,128)(2,1)S(1)}, u32[]{:S(2)}, u32[]{:S(2)}) %all-to-all-start.4) | async-done | bytes 1048608 | tf_op jit(solution)/shard_map/all_to_all | solution.py:530
  219.1 3.0 shard_map.164
  222.1 7.0 %all-to-all-start.5 = ((bf16[16,512,128]{2,1,0:T(8,128)(2,1)}), bf16[16,512,128]{2,1,0:T(8,128)(2,1)}, u32[]{:S(2)}, u32[]{:S(2)}) async-start(bf16[16,512,128]{2,1,0:T(8,128)(2,1)} %shard_map.164), calls=%async_computation.5 | async-start | bytes 4194304 | tf_op jit(solution)/shard_map/all_to_all | solution.py:530
  231.4 3.9 shard_map.165
  236.0 34.3 %all-to-all-done.5.left_ref.right_ref = bf16[16,512,128]{2,1,0:T(8,128)(2,1)} async-done(((bf16[16,512,128]{2,1,0:T(8,128)(2,1)}), bf16[16,512,128]{2,1,0:T(8,128)(2,1)}, u32[]{:S(2)}, u32[]{:S(2)}) %all-to-all-start.5) | async-done | bytes 2097184 | tf_op jit(solution)/shard_map/all_to_all | solution.py:530
  272.5 8.1 %shard_map.166 = (f32[16,128,256]{2,1,0:T(8,128)}, bf16[16,256,128]{2,1,0:T(8,128)(2,1)}) custom-call(bf16[16,512,128]{2,1,0:T(8,128)(2,1)} %all-to-all-done.5.left_ref.right_ref, bf16[16,512,128]{2,1,0:T(8,128)(2,1)} %all-to-all-done.5.left_ref.right_ref, bf16[16,512,256]{2,1,0:T(8,128)(2,1)} %get-tuple-element.72.fac_ref, ...), custom_call_target="tpu_custom_call" | custom-call | flops 805306368 | bytes 17008640 | tf_op jit(solution)/shard_map/pallas_call | solution.py:426
  280.6 11.3 %all-to-all-start.6 = ((bf16[16,256,128]{2,1,0:T(8,128)(2,1)}), bf16[16,256,128]{2,1,0:T(8,128)(2,1)}, u32[]{:S(2)}, u32[]{:S(2)}) async-start(bf16[16,256,128]{2,1,0:T(8,128)(2,1)} %get-tuple-element.76), calls=%async_computation.6 | async-start | bytes 2097152 | tf_op jit(solution)/shard_map/all_to_all | solution.py:530
  294.8 7.2 %shard_map.167 = (bf16[16,128,256]{2,1,0:T(8,128)(2,1)S(1)}, bf16[1024,128]{1,0:T(8,128)(2,1)S(1)}) custom-call(bf16[16,512,128]{2,1,0:T(8,128)(2,1)} %all-to-all-done.5.left_ref.right_ref, bf16[16,512,128]{2,1,0:T(8,128)(2,1)} %all-to-all-done.5.left_ref.right_ref, bf16[16,512,256]{2,1,0:T(8,128)(2,1)} %get-tuple-element.72.fac_ref, ...), custom_call_target="tpu_custom_call" | custom-call | flops 1744830464 | bytes 17373184 | tf_op jit(solution)/shard_map/pallas_call | solution.py:426
  303.7 11.2 %all-to-all-done.6.grad_ref = bf16[16,256,128]{2,1,0:T(8,128)(2,1)} async-done(((bf16[16,256,128]{2,1,0:T(8,128)(2,1)}), bf16[16,256,128]{2,1,0:T(8,128)(2,1)}, u32[]{:S(2)}, u32[]{:S(2)}) %all-to-all-start.6) | async-done | bytes 1048608 | tf_op jit(solution)/shard_map/all_to_all | solution.py:530
  315.9 4.2 %shard_map.168 = bf16[16,576,128]{2,1,0:T(8,128)(2,1)} custom-call(bf16[8,2,256,256]{3,2,1,0:T(8,128)(2,1)S(1)} %copy-done.10, bf16[16,256,128]{2,1,0:T(8,128)(2,1)} %all-to-all-done.6.grad_ref, bf16[16,64,128]{2,1,0:T(8,128)(2,1)S(1)} %bitcast.26), custom_call_target="tpu_custom_call" | custom-call | flops 536870912 | bytes 5767168 | tf_op jit(solution)/shard_map/pallas_call | solution.py:518
  320.1 7.0 %all-to-all-start.7 = ((bf16[16,576,128]{2,1,0:T(8,128)(2,1)}), bf16[16,576,128]{2,1,0:T(8,128)(2,1)}, u32[]{:S(2)}, u32[]{:S(2)}) async-start(bf16[16,576,128]{2,1,0:T(8,128)(2,1)} %shard_map.168), calls=%async_computation.7 | async-start | bytes 4718592 | tf_op jit(solution)/shard_map/all_to_all | solution.py:530
  327.2 4.1 shard_map.169
  333.3 39.6 %all-to-all-done.7.left_ref.right_ref.early_ref = bf16[16,576,128]{2,1,0:T(8,128)(2,1)} async-done(((bf16[16,576,128]{2,1,0:T(8,128)(2,1)}), bf16[16,576,128]{2,1,0:T(8,128)(2,1)}, u32[]{:S(2)}, u32[]{:S(2)}) %all-to-all-start.7) | async-done | bytes 2359328 | tf_op jit(solution)/shard_map/all_to_all | solution.py:530
  372.9 6.3 %shard_map.170 = bf16[768,128]{1,0:T(8,128)(2,1)} custom-call(bf16[16,576,128]{2,1,0:T(8,128)(2,1)} %all-to-all-done.7.left_ref.right_ref.early_ref, bf16[16,576,128]{2,1,0:T(8,128)(2,1)} %all-to-all-done.7.left_ref.right_ref.early_ref, bf16[16,512,256]{2,1,0:T(8,128)(2,1)} %get-tuple-element.85.fac_ref, bf16[16,128,256]{2,1,0:T(8,128)(2,1)} %copy-done.23, ...), custom_call_target="tpu_custom_call" | custom-call | flops 1342177280 | bytes 12419072 | tf_op jit(solution)/shard_map/pallas_call | solution.py:426
  379.2 12.2 %all-to-all-start.8 = ((bf16[16,48,128]{2,1,0:T(8,128)(2,1)}), bf16[16,48,128]{2,1,0:T(8,128)(2,1)S(1)}, u32[]{:S(2)}, u32[]{:S(2)}) async-start(bf16[16,48,128]{2,1,0:T(8,128)(2,1)} %bitcast.32), calls=%async_computation.8 | async-start | bytes 393216 | tf_op jit(solution)/shard_map/all_to_all | solution.py:530
  391.5 6.7 %shard_map.171 = bf16[32,128,128]{2,1,0:T(8,128)(2,1)} custom-call(bf16[16,576,128]{2,1,0:T(8,128)(2,1)} %all-to-all-done.7.left_ref.right_ref.early_ref, bf16[16,576,128]{2,1,0:T(8,128)(2,1)} %all-to-all-done.7.left_ref.right_ref.early_ref, bf16[16,512,256]{2,1,0:T(8,128)(2,1)} %get-tuple-element.85.fac_ref, bf16[16,128,256]{2,1,0:T(8,128)(2,1)} %copy-done.15, ...), custom_call_target="tpu_custom_call" | custom-call | flops 671088640 | bytes 14337024 | tf_op jit(solution)/shard_map/pallas_call | solution.py:426
  403.0 17.0 %all_to_all.50.got_ref = bf16[16,112,128]{2,1,0:T(8,128)(2,1)S(1)} all-to-all(bf16[16,112,128]{2,1,0:T(8,128)(2,1)} %shard_map.172), channel_id=1, replica_groups=mesh['grp'=2,'row'=8,'col'=2] {'row','col'}, dimensions={0} | all-to-all | bytes 917504 | tf_op jit(solution)/shard_map/all_to_all | solution.py:530
  (123 shorter events, 47.0 us)
Async XLA Ops:
  6.7 7.6 %copy-start.52 = (bf16[2,128,640]{2,1,0:T(8,128)(2,1)S(1)}, bf16[2,128,640]{2,1,0:T(8,128)(2,1)}, u32[]{:S(2)}) copy-start(bf16[2,128,640]{2,1,0:T(8,128)(2,1)} %w_ref.1) | copy-start | bytes 983044
  6.7 8.5 %copy-start.39 = (f32[2,128]{1,0:T(2,128)S(1)}, f32[2,128]{1,0:T(2,128)}, u32[]{:S(2)}) copy-start(f32[2,128]{1,0:T(2,128)} %gain_ref.13) | copy-start | bytes 3076
  6.7 8.5 %copy-start.44 = (s32[256]{0:T(256)S(1)}, s32[256]{0:T(256)}, u32[]{:S(2)}) copy-start(s32[256]{0:T(256)} %mask_smem.3) | copy-start | bytes 3076
  6.7 8.5 %copy-start.45 = (s32[256]{0:T(256)S(1)}, s32[256]{0:T(256)}, u32[]{:S(2)}) copy-start(s32[256]{0:T(256)} %chain_smem.3) | copy-start | bytes 3076
  6.7 8.5 %copy-start.48 = (f32[2,128]{1,0:T(2,128)S(1)}, f32[2,128]{1,0:T(2,128)}, u32[]{:S(2)}) copy-start(f32[2,128]{1,0:T(2,128)} %bias_ref.9) | copy-start | bytes 3076
  6.7 8.5 %copy-start.49 = (f32[2,128]{1,0:T(2,128)S(1)}, f32[2,128]{1,0:T(2,128)}, u32[]{:S(2)}) copy-start(f32[2,128]{1,0:T(2,128)} %chain_ref.5) | copy-start | bytes 3076
  6.7 48.6 %all-to-all-start = ((bf16[16,2,256,128]{3,2,1,0:T(8,128)(2,1)}), bf16[16,2,256,128]{3,2,1,0:T(8,128)(2,1)S(1)}, u32[]{:S(2)}, u32[]{:S(2)}) async-start(bf16[16,2,256,128]{3,2,1,0:T(8,128)(2,1)} %shard_map.154), calls=%async_computation | async-start | bytes 4194304 | tf_op jit(solution)/shard_map/all_to_all | solution.py:530
  55.4 2.2 copy-start
  57.6 34.2 %all-to-all-start.1 = ((bf16[16,256,128]{2,1,0:T(8,128)(2,1)}), bf16[16,256,128]{2,1,0:T(8,128)(2,1)S(1)}, u32[]{:S(2)}, u32[]{:S(2)}) async-start(bf16[16,256,128]{2,1,0:T(8,128)(2,1)} %copy-done.16), calls=%async_computation.1 | async-start | bytes 2097152 | tf_op jit(solution)/shard_map/all_to_all | solution.py:530
  72.1 19.7 %copy-start.4 = (bf16[16,128,256]{2,1,0:T(8,128)(2,1)S(1)}, bf16[16,128,256]{2,1,0:T(8,128)(2,1)}, u32[]{:S(2)}) copy-start(bf16[16,128,256]{2,1,0:T(8,128)(2,1)} %copy-done.3) | copy-start | bytes 3145732
  72.1 19.7 %copy-start.25 = (bf16[16,128,256]{2,1,0:T(8,128)(2,1)S(1)}, bf16[16,128,256]{2,1,0:T(8,128)(2,1)}, u32[]{:S(2)}) copy-start(bf16[16,128,256]{2,1,0:T(8,128)(2,1)} %copy-done.24) | copy-start | bytes 3145732
  72.1 19.7 %copy-start.38 = (f32[2,128]{1,0:T(2,128)S(1)}, f32[2,128]{1,0:T(2,128)}, u32[]{:S(2)}) copy-start(f32[2,128]{1,0:T(2,128)} %hgain_ref.9) | copy-start | bytes 3076
  72.1 19.7 %copy-start.47 = (f32[2,128]{1,0:T(2,128)S(1)}, f32[2,128]{1,0:T(2,128)}, u32[]{:S(2)}) copy-start(f32[2,128]{1,0:T(2,128)} %hbias_ref.5) | copy-start | bytes 3076
  91.8 102.8 %copy-start.2 = (bf16[16,256,128]{2,1,0:T(8,128)(2,1)}, bf16[16,256,128]{2,1,0:T(8,128)(2,1)S(1)}, u32[]{:S(2)}) copy-start(bf16[16,256,128]{2,1,0:T(8,128)(2,1)S(1)} %all-to-all-done.1.prod_ref) | copy-start | bytes 3145732
  98.5 48.0 %all-to-all-start.2 = ((bf16[16,2,256,128]{3,2,1,0:T(8,128)(2,1)}), bf16[16,2,256,128]{3,2,1,0:T(8,128)(2,1)S(1)}, u32[]{:S(2)}, u32[]{:S(2)}) async-start(bf16[16,2,256,128]{3,2,1,0:T(8,128)(2,1)} %get-tuple-element.58), calls=%async_computation.2 | async-start | bytes 4194304 | tf_op jit(solution)/shard_map/all_to_all | solution.py:530
  146.5 2.3 copy-start.1
  148.8 34.3 %all-to-all-start.3 = ((bf16[16,256,128]{2,1,0:T(8,128)(2,1)}), bf16[16,256,128]{2,1,0:T(8,128)(2,1)}, u32[]{:S(2)}, u32[]{:S(2)}) async-start(bf16[16,256,128]{2,1,0:T(8,128)(2,1)} %copy-done.18), calls=%async_computation.3 | async-start | bytes 2097152 | tf_op jit(solution)/shard_map/all_to_all | solution.py:530
  160.1 23.0 %copy-start.6 = (bf16[16,128,256]{2,1,0:T(8,128)(2,1)S(1)}, bf16[16,128,256]{2,1,0:T(8,128)(2,1)}, u32[]{:S(2)}) copy-start(bf16[16,128,256]{2,1,0:T(8,128)(2,1)} %copy-done.5) | copy-start | bytes 3145732
  160.1 23.0 %copy-start.31 = (bf16[128,128]{1,0:T(8,128)(2,1)S(1)}, bf16[128,128]{1,0:T(8,128)(2,1)}, u32[]{:S(2)}) copy-start(bf16[128,128]{1,0:T(8,128)(2,1)} %get-tuple-element.101.ow_ref) | copy-start | bytes 98308
  187.7 29.8 %all-to-all-start.4 = ((bf16[16,256,128]{2,1,0:T(8,128)(2,1)}), bf16[16,256,128]{2,1,0:T(8,128)(2,1)S(1)}, u32[]{:S(2)}, u32[]{:S(2)}) async-start(bf16[16,256,128]{2,1,0:T(8,128)(2,1)} %copy-done.17), calls=%async_computation.4 | async-start | bytes 2097152 | tf_op jit(solution)/shard_map/all_to_all | solution.py:530
  217.5 1.6 copy-start.8
  222.1 7.1 %copy-start.54 = (bf16[1,128,128]{2,1,0:T(8,128)(2,1)S(1)}, bf16[1,128,128]{2,1,0:T(8,128)(2,1)}, u32[]{:S(2)}) copy-start(bf16[1,128,128]{2,1,0:T(8,128)(2,1)} %get-tuple-element.103) | copy-start | bytes 98308
  222.1 48.2 %all-to-all-start.5 = ((bf16[16,512,128]{2,1,0:T(8,128)(2,1)}), bf16[16,512,128]{2,1,0:T(8,128)(2,1)}, u32[]{:S(2)}, u32[]{:S(2)}) async-start(bf16[16,512,128]{2,1,0:T(8,128)(2,1)} %shard_map.164), calls=%async_computation.5 | async-start | bytes 4194304 | tf_op jit(solution)/shard_map/all_to_all | solution.py:530
  229.2 41.2 %copy-start.12 = (bf16[16,128,256]{2,1,0:T(8,128)(2,1)S(1)}, bf16[16,128,256]{2,1,0:T(8,128)(2,1)}, u32[]{:S(2)}) copy-start(bf16[16,128,256]{2,1,0:T(8,128)(2,1)} %copy-done.11) | copy-start | bytes 3145732
  236.0 44.7 %copy-start.14 = (bf16[16,128,256]{2,1,0:T(8,128)(2,1)}, bf16[16,128,256]{2,1,0:T(8,128)(2,1)S(1)}, u32[]{:S(2)}) copy-start(bf16[16,128,256]{2,1,0:T(8,128)(2,1)S(1)} %get-tuple-element.70.glog_ref) | copy-start | bytes 3145732
  280.6 34.3 %all-to-all-start.6 = ((bf16[16,256,128]{2,1,0:T(8,128)(2,1)}), bf16[16,256,128]{2,1,0:T(8,128)(2,1)}, u32[]{:S(2)}, u32[]{:S(2)}) async-start(bf16[16,256,128]{2,1,0:T(8,128)(2,1)} %get-tuple-element.76), calls=%async_computation.6 | async-start | bytes 2097152 | tf_op jit(solution)/shard_map/all_to_all | solution.py:530
  294.8 20.1 %copy-start.10 = (bf16[8,2,256,256]{3,2,1,0:T(8,128)(2,1)S(1)}, bf16[8,2,256,256]{3,2,1,0:T(8,128)(2,1)}, u32[]{:S(2)}) copy-start(bf16[8,2,256,256]{3,2,1,0:T(8,128)(2,1)} %copy-done.9) | copy-start | bytes 6291460
  320.1 7.1 %copy-start.26 = (bf16[16,128,256]{2,1,0:T(8,128)(2,1)S(1)}, bf16[16,128,256]{2,1,0:T(8,128)(2,1)}, u32[]{:S(2)}) copy-start(bf16[16,128,256]{2,1,0:T(8,128)(2,1)} %copy-done.24) | copy-start | bytes 3145732
  320.1 7.1 %copy-start.51 = (f32[2,128]{1,0:T(2,128)S(1)}, f32[2,128]{1,0:T(2,128)}, u32[]{:S(2)}) copy-start(f32[2,128]{1,0:T(2,128)} %chain_ref.5) | copy-start | bytes 3076
  320.1 52.8 %all-to-all-start.7 = ((bf16[16,576,128]{2,1,0:T(8,128)(2,1)}), bf16[16,576,128]{2,1,0:T(8,128)(2,1)}, u32[]{:S(2)}, u32[]{:S(2)}) async-start(bf16[16,576,128]{2,1,0:T(8,128)(2,1)} %shard_map.168), calls=%async_computation.7 | async-start | bytes 4718592 | tf_op jit(solution)/shard_map/all_to_all | solution.py:530
  333.3 45.9 %copy-start.46 = (f32[16,1,256]{2,1,0:T(1,128)}, f32[16,1,256]{2,1,0:T(1,128)S(1)}, u32[]{:S(2)}) copy-start(f32[16,1,256]{2,1,0:T(1,128)S(1)} %get-tuple-element.89.inv_ref) | copy-start | bytes 49156
  379.2 21.2 %all-to-all-start.8 = ((bf16[16,48,128]{2,1,0:T(8,128)(2,1)}), bf16[16,48,128]{2,1,0:T(8,128)(2,1)S(1)}, u32[]{:S(2)}, u32[]{:S(2)}) async-start(bf16[16,48,128]{2,1,0:T(8,128)(2,1)} %bitcast.32), calls=%async_computation.8 | async-start | bytes 393216 | tf_op jit(solution)/shard_map/all_to_all | solution.py:530
  (32 other events, 29.0 us)
